TPU v7x, 512 devices: a whole 4x4x16 slice. The times are simulated.
512 devices in a mesh: wide: 32 (over z_lo, x, core), narrow: 16 (over z_hi, y).
Axes of the slice: x: 4, y: 4, z: 16 (z_hi: 4, z_lo: 4; z = z_hi * 4 + z_lo), core: 2. Of those that a mesh axis runs over, the one named last changes fastest.
Arguments:
- hidden_in: bfloat16 [65536, 4096], P(('wide', 'narrow')), may hold values from -6 to 6
- queries: bfloat16 [65536, 4096], P(('wide', 'narrow')), may hold values from -256 to 256, as said below
- keys: bfloat16 [65536, 512], P(('wide', 'narrow')), may hold values from -8 to 8, as said below
- lengths: int32 [512, 4], P(('wide', 'narrow')), may hold values from 1 to 64, 128 in all within a row
- master: float32 [4096, 512], P(('narrow', 'wide')), may hold values from -0.09375 to 0.09375
- moment: float32 [4096, 512], P(('narrow', 'wide')), may hold values from -0.0625 to 0.0625
- second: float32 [4096, 512], P(('narrow', 'wide')), may hold values from 1e-05 to 0.1
Outputs:
- attended: bfloat16 [65536, 4096], P(('wide', 'narrow'))
- grad_hidden: bfloat16 [65536, 4096], P(('wide', 'narrow'))
- master_new: float32 [4096, 512], P(('narrow', 'wide'))
- moment_new: float32 [4096, 512], P(('narrow', 'wide'))
- second_new: float32 [4096, 512], P(('narrow', 'wide'))
Inputs may be any that keep to these rules, and one draw needn't show every extreme that they name: `queries`: queries are real-valued activations. `keys`: keys are real-valued activations. `lengths`: each row sums to 128; its largest entry is 64.
All inputs are finite; a program needn't handle non-finite values.
Results may differ from a plain program's by a relative error of at most 0.009.
Values may be sent and summed in bfloat16 or wider, within the bound.
No kernel may reach another device: no remote copies, remote signals or barrier semaphores. Data moves between devices by JAX's collectives and lax.ppermute only.
A program may use at most 64 MiB of HBM per device.

v0:
```python
import jax
import jax.numpy as jnp
from jax import lax
from jax.sharding import PartitionSpec as P

HD = 128
VH = 4
QH = 32


beta_one = 0.9
beta_two = 0.95
adam_eps = 1e-08
learn_rate = 0.001
decay_rate = 0.1


def attend_local(queries, keys, values, length_row):
    tok_rows = queries.shape[0]
    groups = QH // VH
    query_blk = queries.reshape(tok_rows, VH, groups, HD)
    key_blk = keys.reshape(tok_rows, VH, HD)
    value_blk = values.reshape(tok_rows, VH, HD)
    positions = jnp.arange(tok_rows, dtype=jnp.int32)
    seg_ends = jnp.cumsum(length_row)
    segment_ids = jnp.sum((positions[:, None] >= seg_ends[None, :]).astype(jnp.int32), axis=1)
    allowed = (segment_ids[:, None] == segment_ids[None, :]) & (
        positions[None, :] <= positions[:, None]
    )
    scores = jnp.einsum(
        "tkgd,skd->kgts", query_blk, key_blk, preferred_element_type=jnp.float32
    ) / jnp.sqrt(jnp.float32(HD))
    scores = jnp.where(allowed[None, None], scores, jnp.float32(-1000000000.0))
    top_score = jnp.max(scores, axis=-1, keepdims=True)
    expos = jnp.exp(scores - top_score)
    probs = (expos / jnp.sum(expos, axis=-1, keepdims=True)).astype(jnp.bfloat16)
    attended = jnp.einsum(
        "kgts,skd->tkgd", probs, value_blk, preferred_element_type=jnp.float32
    ).astype(jnp.bfloat16)
    grad_values = jnp.einsum(
        "kgts,tkgd->skd", probs, attended, preferred_element_type=jnp.float32
    ).astype(jnp.bfloat16)
    return (attended.reshape(tok_rows, QH * HD), grad_values.reshape(tok_rows, VH * HD))


def per_device(hidden_in, queries, keys, lengths, master, moment, second):
    tok_rows = hidden_in.shape[0]
    in_width = hidden_in.shape[1]
    kv_width = keys.shape[1]
    wide_count = lax.axis_size("wide")
    narrow_count = lax.axis_size("narrow")
    shard_rows = in_width // (wide_count * narrow_count)
    primary_rows = lax.all_gather(master.astype(jnp.bfloat16), "wide", axis=0, tiled=True)
    values = jnp.dot(
        hidden_in,
        lax.all_gather(primary_rows, "narrow", axis=0, tiled=True),
        preferred_element_type=jnp.float32,
    ).astype(jnp.bfloat16)
    attended, grad_values = attend_local(queries, keys, values, lengths[0])
    grad_hidden = lax.dot_general(
        grad_values,
        lax.all_gather(primary_rows, "narrow", axis=0, tiled=True),
        (((1,), (1,)), ((), ())),
        preferred_element_type=jnp.float32,
    )
    grad_hidden = grad_hidden.astype(jnp.bfloat16)
    partial_value = lax.dot_general(
        hidden_in, grad_values, (((0,), (0,)), ((), ())), preferred_element_type=jnp.float32
    ).astype(jnp.bfloat16)
    reduced = lax.psum_scatter(partial_value, "narrow", scatter_dimension=0, tiled=True).astype(
        jnp.float32
    )
    received = lax.all_to_all(
        reduced.astype(jnp.bfloat16), "wide", split_axis=0, concat_axis=0, tiled=True
    ).astype(reduced.dtype)
    summed = jnp.sum(received.reshape(wide_count, shard_rows, kv_width), axis=0)
    gradient = summed / jnp.float32(tok_rows * wide_count * narrow_count)
    moment_new = beta_one * moment + (1.0 - beta_one) * gradient
    second_new = beta_two * second + (1.0 - beta_two) * gradient * gradient
    moment_hat = moment_new / (1.0 - beta_one**10)
    second_hat = second_new / (1.0 - beta_two**10)
    master_new = master - learn_rate * (
        moment_hat / (jnp.sqrt(second_hat) + adam_eps) + decay_rate * master
    )
    return (attended, grad_hidden, master_new, moment_new, second_new)


def solution(mesh):
    in_specs = (
        P(("wide", "narrow"), None),
        P(("wide", "narrow"), None),
        P(("wide", "narrow"), None),
        P(("wide", "narrow"), None),
        P(("narrow", "wide"), None),
        P(("narrow", "wide"), None),
        P(("narrow", "wide"), None),
    )
    out_specs = (
        P(("wide", "narrow"), None),
        P(("wide", "narrow"), None),
        P(("narrow", "wide"), None),
        P(("narrow", "wide"), None),
        P(("narrow", "wide"), None),
    )
    return jax.shard_map(
        per_device, mesh=mesh, in_specs=in_specs, out_specs=out_specs, check_vma=False
    )
```

profile of v0, /device:TPU:1, one launch (start us, length us, event | category | flops | bytes accessed | tf_op | source)
XLA Modules:
  0.0 378.1 jit_solution(7162695005799933455)
XLA Ops:
  7.2 0.0 all-gather.2.cloned.1.call-start
  7.2 0.8 convert_element_type.39
  8.0 49.0 %all_gather.7 = bf16[256,512]{1,0:T(8,128)(2,1)} all-gather(bf16[8,512]{1,0:T(8,128)(2,1)S(1)} %convert_element_type.39), channel_id=1, replica_groups=mesh['wide'=32,'narrow'=16] {'wide'}, dimensions={0}, use_global_device_ids=true | all-gather | bytes 270336 | tf_op jit(solution)/shard_map/all_gather | solution.py:53
  57.1 0.0 reduce-scatter.2.cloned.1.call-start
  57.1 0.9 reshape.97
  58.1 1.5 copy.40
  59.6 0.2 reduce-window.8
  59.7 0.1 convert_reduce_fusion.1
  59.8 0.1 fusion.19
  59.9 2.3 fusion.26
  62.3 127.3 %all-gather.2.cloned.1.call-done = bf16[4096,512]{1,0:T(8,128)(2,1)} async-done(((bf16[256,512]{1,0:T(8,128)(2,1)}), bf16[4096,512]{1,0:T(8,128)(2,1)}) %all-gather.2.cloned.1.call-update) | async-done | bytes 4194320 | tf_op jit(solution)/shard_map/all_gather | solution.py:56
  189.5 2.9 convolution_convert_fusion.3
  192.5 0.1 copy.37
  192.6 2.2 convolution_convert_fusion.2
  194.8 0.0 copy-done.5
  194.8 0.5 fusion.3
  195.3 3.2 fusion.1
  198.5 152.9 %reduce-scatter.2.cloned.1.call-done = bf16[256,512]{0,1:T(8,128)(2,1)} async-done(((bf16[4096,512]{0,1:T(8,128)(2,1)}), bf16[256,512]{0,1:T(8,128)(2,1)}) %reduce-scatter.2.cloned.1.call-update) | async-done | bytes 262160 | tf_op jit(solution)/shard_map/reduce_scatter | solution.py:70
  351.4 1.8 copy.30
  353.2 6.3 %all-to-all-start = ((bf16[32,8,512]{2,1,0:T(8,128)(2,1)}), bf16[32,8,512]{2,1,0:T(8,128)(2,1)S(1)}, u32[]{:S(2)}, u32[]{:S(2)}) async-start(bf16[32,8,512]{2,1,0:T(8,128)(2,1)} %bitcast.15), calls=%async_computation.1 | async-start | bytes 524288 | tf_op jit(solution)/shard_map/all_to_all | solution.py:73
  359.5 1.3 copy.31
  360.8 4.7 %convolution_convert_fusion.1 = bf16[128,4096]{1,0:T(8,128)(2,1)} fusion(bf16[128,512]{0,1:T(8,128)(2,1)S(1)} %bitcast.45, bf16[4096,512]{1,0:T(8,128)(2,1)} %all-gather.2.cloned.1.call-done), kind=kOutput, calls=%fused_computation.3 | convolution fusion | flops 537395200 | bytes 5373952 | tf_op jit(solution)/shard_map/dot_general | solution.py:60
  365.5 5.1 %all-to-all-done = bf16[32,8,512]{2,1,0:T(8,128)(2,1)S(1)} async-done(((bf16[32,8,512]{2,1,0:T(8,128)(2,1)}), bf16[32,8,512]{2,1,0:T(8,128)(2,1)S(1)}, u32[]{:S(2)}, u32[]{:S(2)}) %all-to-all-start) | async-done | bytes 262176 | tf_op jit(solution)/shard_map/all_to_all | solution.py:73
  370.7 0.6 multiply_subtract_fusion
  (14 shorter events, 0.1 us)
Async XLA Ops:
  7.2 182.4 %copy-start = (bf16[128,4096]{1,0:T(8,128)(2,1)S(1)}, bf16[128,4096]{1,0:T(8,128)(2,1)}, u32[]{:S(2)}) copy-start(bf16[128,4096]{1,0:T(8,128)(2,1)} %param.7) | copy-start | bytes 3145732
  7.2 52.4 %copy-start.4 = (s32[1,4]{1,0:T(1,128)S(1)}, s32[1,4]{1,0:T(1,128)}, u32[]{:S(2)}) copy-start(s32[1,4]{1,0:T(1,128)} %param.10) | copy-start | bytes 52
  7.2 182.3 %all-gather.2.cloned.1.call-start = ((), (), s32[]{:S(2)}) async-start(), calls=%async_computation.2 | async-start | bytes 4456448 | tf_op jit(solution)/shard_map/all_gather | solution.py:56
  57.1 294.3 %reduce-scatter.2.cloned.1.call-start = ((), (), s32[]{:S(2)}) async-start(), calls=%async_computation.3 | async-start | bytes 4456448 | tf_op jit(solution)/shard_map/reduce_scatter | solution.py:70
  192.6 2.2 copy-start.5
  353.2 17.4 %all-to-all-start = ((bf16[32,8,512]{2,1,0:T(8,128)(2,1)}), bf16[32,8,512]{2,1,0:T(8,128)(2,1)S(1)}, u32[]{:S(2)}, u32[]{:S(2)}) async-start(bf16[32,8,512]{2,1,0:T(8,128)(2,1)} %bitcast.15), calls=%async_computation.1 | async-start | bytes 524288 | tf_op jit(solution)/shard_map/all_to_all | solution.py:73
  360.8 9.8 %copy-start.1 = (f32[8,512]{1,0:T(8,128)S(1)}, f32[8,512]{1,0:T(8,128)}, u32[]{:S(2)}) copy-start(f32[8,512]{1,0:T(8,128)} %param.11) | copy-start | bytes 49156
  360.8 9.8 %copy-start.2 = (f32[8,512]{1,0:T(8,128)S(1)}, f32[8,512]{1,0:T(8,128)}, u32[]{:S(2)}) copy-start(f32[8,512]{1,0:T(8,128)} %param.12) | copy-start | bytes 49156
  360.8 9.9 %copy-start.3 = (f32[8,512]{1,0:T(8,128)S(1)}, f32[8,512]{1,0:T(8,128)}, u32[]{:S(2)}) copy-start(f32[8,512]{1,0:T(8,128)} %param.13) | copy-start | bytes 49156
Sparse Core Ops, SparseCore 0:
  57.2 132.2 all-gather.1
  198.6 152.7 reduce-scatter.1
where the time goes:
time: 378 us
  waiting for transfers between devices  285 us (75%)
  blocking collectives  49 us (13%)
  matrix products  15.8 us (4%)
  between operations  14.2 us (4%)
  starting transfers between devices  6.37 us (2%)
  local copies, waits for them, and re-layouts  5.67 us (2%)
    reduce_scatter x1, waiting for transfers between devices, per_device(): lax.psum_scatter(partial_value, 'narrow', scatter_dimension=0, tiled=True)  153 us
    all_gather x1, waiting for transfers between devices, per_device(): lax.all_gather(primary_rows, 'narrow', axis=0, tiled=True)  127 us
    all_gather x1, blocking collectives, per_device(): lax.all_gather(master.astype(jnp.bfloat16), 'wide', axis=0, tiled=True)  49 us
  transfers between devices with their start and end apart: 3, of which 3 were waited for; matrix products, arithmetic and copies ran while one was open for 3% of the time, Pallas kernels for 0%

commit v1 on v0

v1 whole, which is shorter than its diff:
```python
import functools

import jax
import jax.numpy as jnp
import numpy as np
from jax import lax
from jax.experimental import pallas as pl
from jax.experimental.pallas import tpu as pltpu
from jax.sharding import Mesh
from jax.sharding import PartitionSpec as P

HD = 128
VH = 4
QH = 32
GROUPS = QH // VH

beta_one = 0.9
beta_two = 0.95
adam_eps = 1e-08
learn_rate = 0.001
decay_rate = 0.1

AXES = ("zl", "x", "c", "zh", "y")
SIZES = (4, 4, 2, 4, 4)
TOK_SPEC = P(AXES, None)
ROW_SPEC = P(("zh", "y", "zl", "x", "c"), None)
GROUP = ("x", "c")
DEPTH = ("zl", "zh")

F32 = jnp.float32
BF16 = jnp.bfloat16


def shuffle_matrix():
    source = np.arange(1024).reshape(4, 4, 8, 8).transpose(2, 1, 0, 3).reshape(-1)
    matrix = np.zeros((1024, 1024), np.float32)
    matrix[source, np.arange(1024)] = 1.0
    return matrix


def split_kernel(hidden_ref, shuffle_ref, out_ref):
    for y in range(4):
        parts = [hidden_ref[:, zh * 1024 + y * 256 : zh * 1024 + y * 256 + 256] for zh in range(4)]
        cols = jnp.concatenate(parts, axis=1)
        moved = jnp.dot(cols, shuffle_ref[...], preferred_element_type=F32).astype(BF16)
        for g in range(8):
            out_ref[g, :, y * 128 : (y + 1) * 128] = moved[:, g * 128 : (g + 1) * 128]


def join_kernel(blocks_ref, shuffle_ref, out_ref):
    for y in range(4):
        cols = jnp.concatenate([blocks_ref[g, :, y * 128 : (y + 1) * 128] for g in range(8)], axis=1)
        moved = lax.dot_general(
            cols, shuffle_ref[...], (((1,), (1,)), ((), ())), preferred_element_type=F32
        ).astype(BF16)
        for zh in range(4):
            at = zh * 1024 + y * 256
            out_ref[:, at : at + 256] = moved[:, zh * 256 : (zh + 1) * 256]


def probs_kernel(queries_ref, keys_ref, seg_row_ref, seg_col_ref, out_ref):
    tok = queries_ref.shape[0]
    rows = lax.broadcasted_iota(jnp.int32, (tok, tok), 0)
    cols = lax.broadcasted_iota(jnp.int32, (tok, tok), 1)
    allowed = (seg_col_ref[...] == seg_row_ref[...]) & (cols <= rows)
    scale = F32(1.0 / np.sqrt(HD))
    for j in range(VH):
        key = keys_ref[:, j * HD : (j + 1) * HD]
        for h in range(GROUPS):
            at = (j * GROUPS + h) * HD
            scores = lax.dot_general(
                queries_ref[:, at : at + HD], key, (((1,), (1,)), ((), ())), preferred_element_type=F32
            )
            scores = jnp.where(allowed, scores * scale, F32(-1000000000.0))
            expos = jnp.exp(scores - jnp.max(scores, axis=-1, keepdims=True))
            total = jnp.sum(expos, axis=-1, keepdims=True)
            out_ref[j, h * tok : (h + 1) * tok, :] = (expos / total).astype(BF16)


def attend_kernel(partial_ref, probs_ref, attended_ref, grad_ref):
    tok = partial_ref.shape[1]
    for j in range(VH):
        cols = slice(j * HD, (j + 1) * HD)
        total = partial_ref[0, :, cols].astype(F32)
        for g in range(1, 8):
            total = total + partial_ref[g, :, cols].astype(F32)
        value = total.astype(BF16)
        attended = jnp.dot(probs_ref[j], value, preferred_element_type=F32).astype(BF16)
        grad = lax.dot_general(
            probs_ref[j], attended, (((0,), (0,)), ((), ())), preferred_element_type=F32
        ).astype(BF16)
        for h in range(GROUPS):
            at = (j * GROUPS + h) * HD
            attended_ref[:, at : at + HD] = attended[h * tok : (h + 1) * tok]
        for g in range(8):
            grad_ref[g, :, cols] = grad


def call(kernel, out_shape, flops, nbytes):
    return pl.pallas_call(
        kernel,
        out_shape=out_shape,
        compiler_params=pltpu.CompilerParams(vmem_limit_bytes=48 * 1024 * 1024),
        cost_estimate=pl.CostEstimate(flops=flops, bytes_accessed=nbytes, transcendentals=0),
    )


def exchange(blocks, axes):
    return lax.all_to_all(blocks, axes, split_axis=0, concat_axis=0, tiled=True)


def per_device(hidden_in, queries, keys, lengths, master, moment, second):
    tok, width = hidden_in.shape
    kv = keys.shape[1]
    rows = master.shape[0]
    shuffle = jnp.asarray(shuffle_matrix(), BF16)

    blocks = call(
        split_kernel, jax.ShapeDtypeStruct((8, tok, width // 8), BF16), 2 * tok * width * 1024, 4 << 20
    )(hidden_in, shuffle)
    hidden = exchange(blocks, GROUP).reshape(8 * tok, width // 8)

    weight = master.astype(BF16)
    weight = exchange(jnp.broadcast_to(weight[None], (16, rows, kv)), DEPTH).reshape(16 * rows, kv)
    weight = exchange(jnp.broadcast_to(weight[None], (4, 16 * rows, kv)), "y").reshape(64 * rows, kv)

    ends = jnp.cumsum(lengths[0])
    seg = jnp.sum((jnp.arange(tok, dtype=jnp.int32)[:, None] >= ends[None, :]).astype(jnp.int32), axis=1)
    probs = call(
        probs_kernel, jax.ShapeDtypeStruct((VH, GROUPS * tok, tok), BF16), 4 * tok * tok * QH * HD, 8 << 20
    )(queries, keys, seg[None, :], seg[:, None])

    partial = jnp.dot(hidden, weight, preferred_element_type=F32).astype(BF16)
    partial = exchange(partial.reshape(8, tok, kv), GROUP)
    attended, grad = call(
        attend_kernel,
        (jax.ShapeDtypeStruct((tok, QH * HD), BF16), jax.ShapeDtypeStruct((8, tok, kv), BF16)),
        4 * tok * tok * QH * HD,
        4 << 20,
    )(partial, probs)
    grad = exchange(grad, GROUP).reshape(8 * tok, kv)

    part = lax.dot_general(hidden, grad, (((0,), (0,)), ((), ())), preferred_element_type=F32)
    part = exchange(part.astype(BF16).reshape(4, 16 * rows, kv), "y")
    part = jnp.sum(part.astype(F32), axis=0).astype(BF16)
    part = exchange(part.reshape(16, rows, kv), DEPTH)
    gradient = jnp.sum(part.astype(F32), axis=0) / F32(tok * 512)

    back = lax.dot_general(grad, weight, (((1,), (1,)), ((), ())), preferred_element_type=F32).astype(BF16)
    back = exchange(back.reshape(8, tok, width // 8), GROUP)
    grad_hidden = call(
        join_kernel, jax.ShapeDtypeStruct((tok, width), BF16), 2 * tok * width * 1024, 4 << 20
    )(back, shuffle)

    moment_new = beta_one * moment + (1.0 - beta_one) * gradient
    second_new = beta_two * second + (1.0 - beta_two) * gradient * gradient
    moment_hat = moment_new / (1.0 - beta_one**10)
    second_hat = second_new / (1.0 - beta_two**10)
    master_new = master - learn_rate * (
        moment_hat / (jnp.sqrt(second_hat) + adam_eps) + decay_rate * master
    )
    return (attended, grad_hidden, master_new, moment_new, second_new)


def solution(mesh):
    named = Mesh(mesh.devices.reshape(SIZES), AXES)
    return jax.shard_map(
        per_device,
        mesh=named,
        in_specs=(TOK_SPEC, TOK_SPEC, TOK_SPEC, TOK_SPEC, ROW_SPEC, ROW_SPEC, ROW_SPEC),
        out_specs=(TOK_SPEC, TOK_SPEC, ROW_SPEC, ROW_SPEC, ROW_SPEC),
        check_vma=False,
    )
```

time: 378 us -> 167 us (0.44)
  waiting for transfers between devices: 285 us -> 39.2 us
  blocking collectives: 49 us -> 80.9 us
  starting transfers between devices: 6.37 us -> 20.9 us
  between operations: 14.2 us -> 0.74 us
  Pallas kernels: 0 us -> 10.9 us
  matrix products: 15.8 us -> 6.56 us
    reduce_scatter x1 -> x0, waiting for transfers between devices: 153 us -> none  [per_device(): lax.psum_scatter(partial_value, 'narrow', scatter_dimension=0, tiled=True)]
    all_gather x1 -> x0, waiting for transfers between devices: 127 us -> none  [per_device(): lax.all_gather(primary_rows, 'narrow', axis=0, tiled=True)]
    all_to_all x0 -> x4, blocking collectives: none -> 80.9 us  [exchange(): return lax.all_to_all(blocks, axes, split_axis=0, concat_axis=0, tiled=True)]
    all_gather x1 -> x0, blocking collectives: 49 us -> none  [per_device(): lax.all_gather(master.astype(jnp.bfloat16), 'wide', axis=0, tiled=True)]
    all_to_all x1 -> x4, waiting for transfers between devices: 5.11 us -> 39.2 us  [exchange(): return lax.all_to_all(blocks, axes, split_axis=0, concat_axis=0, tiled=True)]
    all_to_all x1 -> x4, starting transfers between devices: 6.29 us -> 20.9 us  [exchange(): return lax.all_to_all(blocks, axes, split_axis=0, concat_axis=0, tiled=True)]
    pallas_call x0 -> x4, Pallas kernels: none -> 10.9 us  [the longest x1 3.81 us: per_device(): call(join_kernel, jax.ShapeDtypeStruct((tok, width), BF16), 2 * tok * wid...]
    dot_general x5 -> x3, matrix products: 13.4 us -> 6.56 us  [the longest x1 3.07 us: per_device(): lax.dot_general(grad, weight, (((1,), (1,)), ((), ())), preferred_element...]
  transfers between devices with their start and end apart: 3 -> 4, of which waited for: 3 -> 4; matrix products, arithmetic and copies ran while one was open for 3% -> 2% of each run, Pallas kernels for 0% -> 2%
where the time goes in v1:
time: 167 us; the launch traced here: 166 us
  blocking collectives  80.9 us (48%)
  waiting for transfers between devices  39.2 us (23%)
  starting transfers between devices  20.9 us (13%)
  Pallas kernels  10.9 us (7%)
  matrix products  6.56 us (4%)
  local copies, waits for them, and re-layouts  4.64 us (3%)
  other arithmetic  2.54 us (2%)
    all_to_all x4, blocking collectives, exchange(): return lax.all_to_all(blocks, axes, split_axis=0, concat_axis=0, tiled=True)  80.9 us
    all_to_all x4, waiting for transfers between devices, exchange(): return lax.all_to_all(blocks, axes, split_axis=0, concat_axis=0, tiled=True)  39.2 us
    all_to_all x4, starting transfers between devices, exchange(): return lax.all_to_all(blocks, axes, split_axis=0, concat_axis=0, tiled=True)  20.9 us
    pallas_call x1, Pallas kernels, per_device(): call(join_kernel, jax.ShapeDtypeStruct((tok, width), BF16), 2 * tok * wid...  3.81 us
    unnamed x22, local copies, waits for them, and re-layouts  3.67 us
  transfers between devices with their start and end apart: 4, of which 4 were waited for; matrix products, arithmetic and copies ran while one was open for 2% of the time, Pallas kernels for 2%

profile of v1, /device:TPU:1, one launch (start us, length us, event | category | flops | bytes accessed | tf_op | source)
XLA Modules:
  0.0 166.3 jit_solution(13326549195976401760)
XLA Ops:
  0.6 0.9 convert_element_type.20
  1.5 27.9 %all_to_all.40 = bf16[16,8,512]{2,1,0:T(8,128)(2,1)S(1)} all-to-all(bf16[16,8,512]{2,1,0:T(8,128)(2,1)S(1)} %broadcast_in_dim.10), channel_id=1, replica_groups=mesh['zl'=4,'x'=4,'c'=2,'zh'=4,'y'=4] {'zl','zh'}, dimensions={0} | all-to-all | bytes 262144 | tf_op jit(solution)/shard_map/all_to_all | solution.py:109
  29.5 0.8 broadcast_in_dim.23
  30.3 4.2 %all-to-all-start.2 = ((bf16[4,128,512]{2,1,0:T(8,128)(2,1)}), bf16[4,128,512]{2,1,0:T(8,128)(2,1)}, u32[]{:S(2)}, u32[]{:S(2)}) async-start(bf16[4,128,512]{2,1,0:T(8,128)(2,1)} %broadcast_in_dim.23), calls=%async_computation.2 | async-start | bytes 1048576 | tf_op jit(solution)/shard_map/all_to_all | solution.py:109
  34.5 1.2 copy-done.2
  35.7 1.3 shard_map.119
  37.0 4.5 %all-to-all-done.2 = bf16[4,128,512]{2,1,0:T(8,128)(2,1)} async-done(((bf16[4,128,512]{2,1,0:T(8,128)(2,1)}), bf16[4,128,512]{2,1,0:T(8,128)(2,1)}, u32[]{:S(2)}, u32[]{:S(2)}) %all-to-all-start.2) | async-done | bytes 524320 | tf_op jit(solution)/shard_map/all_to_all | solution.py:109
  41.5 23.7 %all_to_all.41 = bf16[8,128,512]{2,1,0:T(8,128)(2,1)S(1)} all-to-all(bf16[8,128,512]{2,1,0:T(8,128)(2,1)S(1)} %shard_map.119), channel_id=1, replica_groups=mesh['zl'=4,'x'=4,'c'=2,'zh'=4,'y'=4] {'x','c'}, dimensions={0} | all-to-all | bytes 2097152 | tf_op jit(solution)/shard_map/all_to_all | solution.py:109
  65.3 1.0 copy-done.4
  66.2 2.8 %convolution_convert_fusion.1 = bf16[1024,512]{1,0:T(8,128)(2,1)} fusion(bf16[1024,512]{1,0:T(8,128)(2,1)S(1)} %bitcast.24, bf16[512,512]{1,0:T(8,128)(2,1)} %bitcast.2), kind=kOutput, calls=%fused_computation.1 | convolution fusion | flops 537395200 | bytes 2621440 | tf_op jit(solution)/shard_map/dot_general | solution.py:133
  69.0 5.2 %all-to-all-start.3 = ((bf16[8,128,512]{2,1,0:T(8,128)(2,1)}), bf16[8,128,512]{2,1,0:T(8,128)(2,1)}, u32[]{:S(2)}, u32[]{:S(2)}) async-start(bf16[8,128,512]{2,1,0:T(8,128)(2,1)} %bitcast.3), calls=%async_computation.3 | async-start | bytes 2097152 | tf_op jit(solution)/shard_map/all_to_all | solution.py:109
  74.5 1.2 copy-done.1
  75.8 2.8 %shard_map.120.probs_ref = bf16[4,1024,128]{2,1,0:T(8,128)(2,1)S(1)} custom-call(bf16[128,4096]{1,0:T(8,128)(2,1)S(1)} %copy-done.1, bf16[128,512]{1,0:T(8,128)(2,1)S(1)} %copy-done.3, s32[1,128]{1,0:T(1,128)S(1)} %bitcast.23, s32[128,1]{1,0:T(8,128)S(1)} %copy.15.seg_col_ref), custom_call_target="tpu_custom_call" | custom-call | flops 268435456 | bytes 8388608 | tf_op jit(solution)/shard_map/pallas_call | solution.py:129
  78.6 10.8 %all-to-all-done.3.partial_ref = bf16[8,128,512]{2,1,0:T(8,128)(2,1)} async-done(((bf16[8,128,512]{2,1,0:T(8,128)(2,1)}), bf16[8,128,512]{2,1,0:T(8,128)(2,1)}, u32[]{:S(2)}, u32[]{:S(2)}) %all-to-all-start.3) | async-done | bytes 1048608 | tf_op jit(solution)/shard_map/all_to_all | solution.py:109
  89.4 3.1 %shard_map.121 = (bf16[128,4096]{1,0:T(8,128)(2,1)}, bf16[8,128,512]{2,1,0:T(8,128)(2,1)S(1)}) custom-call(bf16[8,128,512]{2,1,0:T(8,128)(2,1)} %all-to-all-done.3.partial_ref, bf16[4,1024,128]{2,1,0:T(8,128)(2,1)S(1)} %shard_map.120.probs_ref), custom_call_target="tpu_custom_call" | custom-call | flops 268435456 | bytes 4194304 | tf_op jit(solution)/shard_map/pallas_call | solution.py:135
  92.4 18.3 %all_to_all.42 = bf16[8,128,512]{2,1,0:T(8,128)(2,1)S(1)} all-to-all(bf16[8,128,512]{2,1,0:T(8,128)(2,1)S(1)} %get-tuple-element.8), channel_id=1, replica_groups=mesh['zl'=4,'x'=4,'c'=2,'zh'=4,'y'=4] {'x','c'}, dimensions={0} | all-to-all | bytes 2097152 | tf_op jit(solution)/shard_map/all_to_all | solution.py:109
  111.7 10.9 %all_to_all.43 = bf16[4,128,512]{2,1,0:T(8,128)(2,1)S(1)} all-to-all(bf16[4,128,512]{2,1,0:T(8,128)(2,1)S(1)} %bitcast.28), channel_id=1, replica_groups=mesh['zl'=4,'x'=4,'c'=2,'zh'=4,'y'=4] {'y'}, dimensions={0} | all-to-all | bytes 1048576 | tf_op jit(solution)/shard_map/all_to_all | solution.py:109
  122.6 0.7 reduce_sum.31
  123.3 4.7 %all-to-all-start.7 = ((bf16[16,8,512]{2,1,0:T(8,128)(2,1)}), bf16[16,8,512]{2,1,0:T(8,128)(2,1)S(1)}, u32[]{:S(2)}, u32[]{:S(2)}) async-start(bf16[16,8,512]{2,1,0:T(8,128)(2,1)} %bitcast.12), calls=%async_computation.7 | async-start | bytes 262144 | tf_op jit(solution)/shard_map/all_to_all | solution.py:109
  128.1 3.1 %convolution_convert_fusion = bf16[1024,512]{1,0:T(8,128)(2,1)} fusion(bf16[1024,512]{1,0:T(8,128)(2,1)} %bitcast.26, bf16[512,512]{1,0:T(8,128)(2,1)} %bitcast.2), kind=kOutput, calls=%fused_computation | convolution fusion | flops 537395200 | bytes 2621440 | tf_op jit(solution)/shard_map/dot_general | solution.py:149
  131.1 9.4 %all-to-all-done.7 = bf16[16,8,512]{2,1,0:T(8,128)(2,1)S(1)} async-done(((bf16[16,8,512]{2,1,0:T(8,128)(2,1)}), bf16[16,8,512]{2,1,0:T(8,128)(2,1)S(1)}, u32[]{:S(2)}, u32[]{:S(2)}) %all-to-all-start.7) | async-done | bytes 131104 | tf_op jit(solution)/shard_map/all_to_all | solution.py:109
  140.5 6.9 %all-to-all-start.5 = ((bf16[8,128,512]{2,1,0:T(8,128)(2,1)}), bf16[8,128,512]{2,1,0:T(8,128)(2,1)S(1)}, u32[]{:S(2)}, u32[]{:S(2)}) async-start(bf16[8,128,512]{2,1,0:T(8,128)(2,1)} %bitcast.25), calls=%async_computation.5 | async-start | bytes 2097152 | tf_op jit(solution)/shard_map/all_to_all | solution.py:109
  148.1 14.4 %all-to-all-done.5.blocks_ref = bf16[8,128,512]{2,1,0:T(8,128)(2,1)S(1)} async-done(((bf16[8,128,512]{2,1,0:T(8,128)(2,1)}), bf16[8,128,512]{2,1,0:T(8,128)(2,1)S(1)}, u32[]{:S(2)}, u32[]{:S(2)}) %all-to-all-start.5) | async-done | bytes 1048608 | tf_op jit(solution)/shard_map/all_to_all | solution.py:109
  162.5 3.8 %shard_map.122 = bf16[128,4096]{1,0:T(8,128)(2,1)} custom-call(bf16[8,128,512]{2,1,0:T(8,128)(2,1)S(1)} %all-to-all-done.5.blocks_ref, bf16[1024,1024]{1,0:T(8,128)(2,1)S(1)} %copy-done), custom_call_target="tpu_custom_call" | custom-call | flops 1073741824 | bytes 4194304 | tf_op jit(solution)/shard_map/pallas_call | solution.py:151
  (26 shorter events, 2.1 us)
Async XLA Ops:
  0.6 33.8 %copy-start = (bf16[1024,1024]{1,0:T(8,128)(2,1)S(1)}, bf16[1024,1024]{1,0:T(8,128)(2,1)}, u32[]{:S(2)}) copy-start(bf16[1024,1024]{1,0:T(8,128)(2,1)} %constant.35.clone.shuffle_ref) | copy-start | bytes 6291460
  30.3 11.2 %all-to-all-start.2 = ((bf16[4,128,512]{2,1,0:T(8,128)(2,1)}), bf16[4,128,512]{2,1,0:T(8,128)(2,1)}, u32[]{:S(2)}, u32[]{:S(2)}) async-start(bf16[4,128,512]{2,1,0:T(8,128)(2,1)} %broadcast_in_dim.23), calls=%async_computation.2 | async-start | bytes 1048576 | tf_op jit(solution)/shard_map/all_to_all | solution.py:109
  34.5 1.2 copy-start.2
  65.3 1.0 copy-start.4
  66.2 7.9 %copy-start.10 = (s32[1,4]{1,0:T(1,128)S(1)}, s32[1,4]{1,0:T(1,128)}, u32[]{:S(2)}) copy-start(s32[1,4]{1,0:T(1,128)} %param.11) | copy-start | bytes 52
  66.2 8.3 %copy-start.3 = (bf16[128,512]{1,0:T(8,128)(2,1)S(1)}, bf16[128,512]{1,0:T(8,128)(2,1)}, u32[]{:S(2)}) copy-start(bf16[128,512]{1,0:T(8,128)(2,1)} %keys_ref.1) | copy-start | bytes 393220
  69.0 20.4 %all-to-all-start.3 = ((bf16[8,128,512]{2,1,0:T(8,128)(2,1)}), bf16[8,128,512]{2,1,0:T(8,128)(2,1)}, u32[]{:S(2)}, u32[]{:S(2)}) async-start(bf16[8,128,512]{2,1,0:T(8,128)(2,1)} %bitcast.3), calls=%async_computation.3 | async-start | bytes 2097152 | tf_op jit(solution)/shard_map/all_to_all | solution.py:109
  74.5 1.2 copy-start.1
  89.4 21.4 %copy-start.5 = (bf16[8,128,512]{2,1,0:T(8,128)(2,1)S(1)}, bf16[8,128,512]{2,1,0:T(8,128)(2,1)}, u32[]{:S(2)}) copy-start(bf16[8,128,512]{2,1,0:T(8,128)(2,1)} %copy-done.4) | copy-start | bytes 3145732
  110.8 1.0 copy-start.6
  123.3 17.2 %all-to-all-start.7 = ((bf16[16,8,512]{2,1,0:T(8,128)(2,1)}), bf16[16,8,512]{2,1,0:T(8,128)(2,1)S(1)}, u32[]{:S(2)}, u32[]{:S(2)}) async-start(bf16[16,8,512]{2,1,0:T(8,128)(2,1)} %bitcast.12), calls=%async_computation.7 | async-start | bytes 262144 | tf_op jit(solution)/shard_map/all_to_all | solution.py:109
  128.0 19.4 %copy-start.7 = (f32[8,512]{1,0:T(8,128)S(1)}, f32[8,512]{1,0:T(8,128)}, u32[]{:S(2)}) copy-start(f32[8,512]{1,0:T(8,128)} %param.12) | copy-start | bytes 49156
  128.0 19.4 %copy-start.8 = (f32[8,512]{1,0:T(8,128)S(1)}, f32[8,512]{1,0:T(8,128)}, u32[]{:S(2)}) copy-start(f32[8,512]{1,0:T(8,128)} %param.13) | copy-start | bytes 49156
  128.1 19.4 %copy-start.9 = (f32[8,512]{1,0:T(8,128)S(1)}, f32[8,512]{1,0:T(8,128)}, u32[]{:S(2)}) copy-start(f32[8,512]{1,0:T(8,128)} %param.14) | copy-start | bytes 49156
  140.5 22.0 %all-to-all-start.5 = ((bf16[8,128,512]{2,1,0:T(8,128)(2,1)}), bf16[8,128,512]{2,1,0:T(8,128)(2,1)S(1)}, u32[]{:S(2)}, u32[]{:S(2)}) async-start(bf16[8,128,512]{2,1,0:T(8,128)(2,1)} %bitcast.25), calls=%async_computation.5 | async-start | bytes 2097152 | tf_op jit(solution)/shard_map/all_to_all | solution.py:109

commit v2 on v1

--- a/solution.py
+++ b/solution.py
@@ -1,5 +1,3 @@
-import functools
-
 import jax
 import jax.numpy as jnp
 import numpy as np
@@ -24,7 +22,6 @@
 SIZES = (4, 4, 2, 4, 4)
 TOK_SPEC = P(AXES, None)
 ROW_SPEC = P(("zh", "y", "zl", "x", "c"), None)
-GROUP = ("x", "c")
 DEPTH = ("zl", "zh")
 
 F32 = jnp.float32
@@ -32,26 +29,50 @@
 
 
 def shuffle_matrix():
-    source = np.arange(1024).reshape(4, 4, 8, 8).transpose(2, 1, 0, 3).reshape(-1)
+    source = np.arange(1024).reshape(4, 4, 4, 2, 8).transpose(3, 2, 1, 0, 4).reshape(-1)
     matrix = np.zeros((1024, 1024), np.float32)
     matrix[source, np.arange(1024)] = 1.0
     return matrix
 
 
-def split_kernel(hidden_ref, shuffle_ref, out_ref):
+def split_kernel(at_ref, hidden_ref, shuffle_ref, keep_ref, send_ref):
+    first = at_ref[1] == 0
     for y in range(4):
         parts = [hidden_ref[:, zh * 1024 + y * 256 : zh * 1024 + y * 256 + 256] for zh in range(4)]
         cols = jnp.concatenate(parts, axis=1)
         moved = jnp.dot(cols, shuffle_ref[...], preferred_element_type=F32).astype(BF16)
-        for g in range(8):
-            out_ref[g, :, y * 128 : (y + 1) * 128] = moved[:, g * 128 : (g + 1) * 128]
-
-
-def join_kernel(blocks_ref, shuffle_ref, out_ref):
+        low, high = moved[:, :512], moved[:, 512:]
+        keep, send = jnp.where(first, low, high), jnp.where(first, high, low)
+        for x in range(4):
+            keep_ref[x, :, y * 128 : (y + 1) * 128] = keep[:, x * 128 : (x + 1) * 128]
+            send_ref[x, :, y * 128 : (y + 1) * 128] = send[:, x * 128 : (x + 1) * 128]
+
+
+def deal_kernel(at_ref, own_ref, other_ref, *out_refs):
+    for d in range(4):
+        x = lax.rem(at_ref[0] + d, 4)
+        out_refs[d][0] = own_ref[x]
+        out_refs[d][1] = other_ref[x]
+
+
+def collect_kernel(at_ref, *refs):
+    in_refs, own_ref, other_ref = refs[:4], refs[4], refs[5]
+    for d in range(4):
+        x = lax.rem(at_ref[0] + 4 - d, 4)
+        own_ref[x] = in_refs[d][0]
+        other_ref[x] = in_refs[d][1]
+
+
+def join_kernel(at_ref, b0_ref, b1_ref, b2_ref, b3_ref, shuffle_ref, out_ref, cols_ref):
+    core = at_ref[1]
+    for d, ref in enumerate((b0_ref, b1_ref, b2_ref, b3_ref)):
+        x = lax.rem(at_ref[0] + 4 - d, 4)
+        cols_ref[core, x] = ref[0]
+        cols_ref[1 - core, x] = ref[1]
     for y in range(4):
-        cols = jnp.concatenate([blocks_ref[g, :, y * 128 : (y + 1) * 128] for g in range(8)], axis=1)
-        moved = lax.dot_general(
-            cols, shuffle_ref[...], (((1,), (1,)), ((), ())), preferred_element_type=F32
+        parts = [cols_ref[c, x, :, y * 128 : (y + 1) * 128] for c in range(2) for x in range(4)]
+        moved = jnp.dot(
+            jnp.concatenate(parts, axis=1), shuffle_ref[...], preferred_element_type=F32
         ).astype(BF16)
         for zh in range(4):
             at = zh * 1024 + y * 256
@@ -82,8 +103,8 @@
     for j in range(VH):
         cols = slice(j * HD, (j + 1) * HD)
         total = partial_ref[0, :, cols].astype(F32)
-        for g in range(1, 8):
-            total = total + partial_ref[g, :, cols].astype(F32)
+        for x in range(1, 4):
+            total = total + partial_ref[x, :, cols].astype(F32)
         value = total.astype(BF16)
         attended = jnp.dot(probs_ref[j], value, preferred_element_type=F32).astype(BF16)
         grad = lax.dot_general(
@@ -92,17 +113,32 @@
         for h in range(GROUPS):
             at = (j * GROUPS + h) * HD
             attended_ref[:, at : at + HD] = attended[h * tok : (h + 1) * tok]
-        for g in range(8):
-            grad_ref[g, :, cols] = grad
-
-
-def call(kernel, out_shape, flops, nbytes):
+        for x in range(4):
+            grad_ref[x, :, cols] = grad
+
+
+SMEM = pl.BlockSpec(memory_space=pltpu.SMEM)
+VMEM = pl.BlockSpec(memory_space=pltpu.VMEM)
+
+
+def call(kernel, out_shape, flops, nbytes, *args, scratch=()):
+    smem = [SMEM if a.dtype == jnp.int32 and a.ndim == 1 else VMEM for a in args]
     return pl.pallas_call(
         kernel,
         out_shape=out_shape,
+        in_specs=smem,
+        scratch_shapes=scratch,
         compiler_params=pltpu.CompilerParams(vmem_limit_bytes=48 * 1024 * 1024),
         cost_estimate=pl.CostEstimate(flops=flops, bytes_accessed=nbytes, transcendentals=0),
-    )
+    )(*args)
+
+
+def swap_core(array):
+    return lax.ppermute(array, "c", [(0, 1), (1, 0)])
+
+
+def along_x(array, step):
+    return lax.ppermute(array, "x", [(i, (i + step) % 4) for i in range(4)])
 
 
 def exchange(blocks, axes):
@@ -113,44 +149,76 @@
     tok, width = hidden_in.shape
     kv = keys.shape[1]
     rows = master.shape[0]
-    shuffle = jnp.asarray(shuffle_matrix(), BF16)
-
-    blocks = call(
-        split_kernel, jax.ShapeDtypeStruct((8, tok, width // 8), BF16), 2 * tok * width * 1024, 4 << 20
-    )(hidden_in, shuffle)
-    hidden = exchange(blocks, GROUP).reshape(8 * tok, width // 8)
+    feats = width // 8
+    at = jnp.stack([lax.axis_index("x"), lax.axis_index("c")]).astype(jnp.int32)
+    shuffle = shuffle_matrix()
+    back_shuffle = jnp.asarray(shuffle.T, BF16)
+    shuffle = jnp.asarray(shuffle, BF16)
+    half = jax.ShapeDtypeStruct((4, tok, feats), BF16)
+    pair = jax.ShapeDtypeStruct((2, tok, feats), BF16)
 
     weight = master.astype(BF16)
     weight = exchange(jnp.broadcast_to(weight[None], (16, rows, kv)), DEPTH).reshape(16 * rows, kv)
     weight = exchange(jnp.broadcast_to(weight[None], (4, 16 * rows, kv)), "y").reshape(64 * rows, kv)
 
+    keep, send = call(split_kernel, (half, half), 2 * tok * width * 1024, 4 << 20, at, hidden_in, shuffle)
+    dealt = call(deal_kernel, (pair,) * 4, 0, 2 << 20, at, keep, swap_core(send))
+    dealt = [dealt[0]] + [along_x(dealt[d], d) for d in range(1, 4)]
+    hidden_own, hidden_other = call(collect_kernel, (half, half), 0, 2 << 20, at, *dealt)
+    hidden_own = hidden_own.reshape(4 * tok, feats)
+    hidden_other = hidden_other.reshape(4 * tok, feats)
+
     ends = jnp.cumsum(lengths[0])
     seg = jnp.sum((jnp.arange(tok, dtype=jnp.int32)[:, None] >= ends[None, :]).astype(jnp.int32), axis=1)
     probs = call(
-        probs_kernel, jax.ShapeDtypeStruct((VH, GROUPS * tok, tok), BF16), 4 * tok * tok * QH * HD, 8 << 20
-    )(queries, keys, seg[None, :], seg[:, None])
-
-    partial = jnp.dot(hidden, weight, preferred_element_type=F32).astype(BF16)
-    partial = exchange(partial.reshape(8, tok, kv), GROUP)
+        probs_kernel,
+        jax.ShapeDtypeStruct((VH, GROUPS * tok, tok), BF16),
+        4 * tok * tok * QH * HD,
+        8 << 20,
+        queries,
+        keys,
+        seg[None, :],
+        seg[:, None],
+    )
+
+    sent = swap_core(jnp.dot(hidden_other, weight, preferred_element_type=F32).astype(BF16))
+    partial = jnp.dot(hidden_own, weight, preferred_element_type=F32) + sent.astype(F32)
+    partial = exchange(partial.astype(BF16).reshape(4, tok, kv), "x")
     attended, grad = call(
         attend_kernel,
-        (jax.ShapeDtypeStruct((tok, QH * HD), BF16), jax.ShapeDtypeStruct((8, tok, kv), BF16)),
+        (jax.ShapeDtypeStruct((tok, QH * HD), BF16), jax.ShapeDtypeStruct((4, tok, kv), BF16)),
         4 * tok * tok * QH * HD,
         4 << 20,
-    )(partial, probs)
-    grad = exchange(grad, GROUP).reshape(8 * tok, kv)
-
-    part = lax.dot_general(hidden, grad, (((0,), (0,)), ((), ())), preferred_element_type=F32)
+        partial,
+        probs,
+    )
+    grad_own = exchange(grad, "x").reshape(4 * tok, kv)
+    grad_other = swap_core(grad_own)
+
+    rowwise = (((0,), (0,)), ((), ()))
+    part = lax.dot_general(hidden_own, grad_own, rowwise, preferred_element_type=F32)
+    part = part + lax.dot_general(hidden_other, grad_other, rowwise, preferred_element_type=F32)
     part = exchange(part.astype(BF16).reshape(4, 16 * rows, kv), "y")
     part = jnp.sum(part.astype(F32), axis=0).astype(BF16)
     part = exchange(part.reshape(16, rows, kv), DEPTH)
     gradient = jnp.sum(part.astype(F32), axis=0) / F32(tok * 512)
 
-    back = lax.dot_general(grad, weight, (((1,), (1,)), ((), ())), preferred_element_type=F32).astype(BF16)
-    back = exchange(back.reshape(8, tok, width // 8), GROUP)
+    columnwise = (((1,), (1,)), ((), ()))
+    back_other = lax.dot_general(grad_other, weight, columnwise, preferred_element_type=F32).astype(BF16)
+    back_own = lax.dot_general(grad_own, weight, columnwise, preferred_element_type=F32).astype(BF16)
+    back_other = swap_core(back_other).reshape(4, tok, feats)
+    dealt = call(deal_kernel, (pair,) * 4, 0, 2 << 20, at, back_own.reshape(4, tok, feats), back_other)
+    dealt = [dealt[0]] + [along_x(dealt[d], d) for d in range(1, 4)]
     grad_hidden = call(
-        join_kernel, jax.ShapeDtypeStruct((tok, width), BF16), 2 * tok * width * 1024, 4 << 20
-    )(back, shuffle)
+        join_kernel,
+        jax.ShapeDtypeStruct((tok, width), BF16),
+        2 * tok * width * 1024,
+        4 << 20,
+        at,
+        *dealt,
+        back_shuffle,
+        scratch=[pltpu.VMEM((2, 4, tok, feats), BF16)],
+    )
 
     moment_new = beta_one * moment + (1.0 - beta_one) * gradient
     second_new = beta_two * second + (1.0 - beta_two) * gradient * gradient

time: 167 us -> 141 us (0.84)
  blocking collectives: 80.9 us -> 10.3 us
  starting transfers between devices: 20.9 us -> 68.6 us
  waiting for transfers between devices: 39.2 us -> 33.5 us
    all_to_all x4 -> x1, blocking collectives: 80.9 us -> 10.3 us  [exchange(): return lax.all_to_all(blocks, axes, split_axis=0, concat_axis=0, tiled=True)]
    ppermute x0 -> x10, starting transfers between devices: none -> 34.4 us  [the longest x6 19 us: along_x(): return lax.ppermute(array, 'x', [(i, (i + step) % 4) for i in range(4)])]
    all_to_all x4 -> x5, waiting for transfers between devices: 39.2 us -> 14.3 us  [exchange(): return lax.all_to_all(blocks, axes, split_axis=0, concat_axis=0, tiled=True)]
    ppermute x0 -> x10, waiting for transfers between devices: none -> 19.2 us  [the longest x6 16.2 us: along_x(): return lax.ppermute(array, 'x', [(i, (i + step) % 4) for i in range(4)])]
    all_to_all x4 -> x5, starting transfers between devices: 20.9 us -> 34.3 us  [exchange(): return lax.all_to_all(blocks, axes, split_axis=0, concat_axis=0, tiled=True)]
    unnamed x22 -> x20, local copies, waits for them, and re-layouts: 3.67 us -> 4.07 us
    dot_general x3 -> x6, matrix products: 6.56 us -> 6.19 us  [the longest x1 1.51 us: per_device(): lax.dot_general(grad_own, weight, columnwise, preferred_element_type=F32)]
    pallas_call x4 -> x7, Pallas kernels: 10.9 us -> 11.1 us  [call(): pl.pallas_call(kernel, out_shape=out_shape, in_specs=smem, scratch_shapes...]
  transfers between devices with their start and end apart: 4 -> 15, of which waited for: 4 -> 10; matrix products, arithmetic and copies ran while one was open for 2% -> 4% of each run, Pallas kernels for 2% -> 7%
where the time goes in v2:
time: 141 us; the launch traced here: 140 us
  starting transfers between devices  68.6 us (49%)
  waiting for transfers between devices  33.5 us (24%)
  Pallas kernels  11.1 us (8%)
  blocking collectives  10.3 us (7%)
  matrix products  6.19 us (4%)
  local copies, waits for them, and re-layouts  5.68 us (4%)
  other arithmetic  3.54 us (3%)
    all_to_all x5, starting transfers between devices, exchange(): return lax.all_to_all(blocks, axes, split_axis=0, concat_axis=0, tiled=True)  34.3 us
    ppermute x6, starting transfers between devices, along_x(): return lax.ppermute(array, 'x', [(i, (i + step) % 4) for i in range(4)])  19 us
    ppermute x6, waiting for transfers between devices, along_x(): return lax.ppermute(array, 'x', [(i, (i + step) % 4) for i in range(4)])  16.2 us
    ppermute x4, starting transfers between devices, swap_core(): return lax.ppermute(array, 'c', [(0, 1), (1, 0)])  15.4 us
    all_to_all x5, waiting for transfers between devices, exchange(): return lax.all_to_all(blocks, axes, split_axis=0, concat_axis=0, tiled=True)  14.3 us
    pallas_call x7, Pallas kernels, call(): pl.pallas_call(kernel, out_shape=out_shape, in_specs=smem, scratch_shapes...  11.1 us
    all_to_all x1, blocking collectives, exchange(): return lax.all_to_all(blocks, axes, split_axis=0, concat_axis=0, tiled=True)  10.3 us
    unnamed x20, local copies, waits for them, and re-layouts  4.07 us
  transfers between devices with their start and end apart: 15, of which 10 were waited for; matrix products, arithmetic and copies ran while one was open for 4% of the time, Pallas kernels for 7%

profile of v2, /device:TPU:1, one launch (start us, length us, event | category | flops | bytes accessed | tf_op | source)
XLA Modules:
  0.0 139.8 jit_solution(5869514634895129573)
XLA Ops:
  2.0 15.7 %all-to-all-start = ((bf16[16,8,512]{2,1,0:T(8,128)(2,1)}), bf16[16,8,512]{2,1,0:T(8,128)(2,1)S(1)}, u32[]{:S(2)}, u32[]{:S(2)}) async-start(bf16[16,8,512]{2,1,0:T(8,128)(2,1)} %broadcast_in_dim.10), calls=%async_computation | async-start | bytes 262144 | tf_op jit(solution)/shard_map/all_to_all | solution.py:145
  22.6 2.9 %collective-permute-start = (bf16[4,128,512]{2,1,0:T(8,128)(2,1)S(1)}, bf16[4,128,512]{2,1,0:T(8,128)(2,1)S(1)}, u32[]{:S(2)}, u32[]{:S(2)}) collective-permute-start(bf16[4,128,512]{2,1,0:T(8,128)(2,1)S(1)} %get-tuple-element.20), channel_id=1, source_target_pairs={{0,16},{16,0},{1,17},{17,1},{2,18},{18,2},{3,19},{19,3},{4,20},{20... | collective-permute-start | bytes 1572872 | tf_op jit(solution)/shard_map/ppermute | solution.py:137
  25.4 4.7 %all-to-all-done = bf16[16,8,512]{2,1,0:T(8,128)(2,1)S(1)} async-done(((bf16[16,8,512]{2,1,0:T(8,128)(2,1)}), bf16[16,8,512]{2,1,0:T(8,128)(2,1)S(1)}, u32[]{:S(2)}, u32[]{:S(2)}) %all-to-all-start) | async-done | bytes 131104 | tf_op jit(solution)/shard_map/all_to_all | solution.py:145
  31.0 4.2 %all-to-all-start.1 = ((bf16[4,128,512]{2,1,0:T(8,128)(2,1)}), bf16[4,128,512]{2,1,0:T(8,128)(2,1)S(1)}, u32[]{:S(2)}, u32[]{:S(2)}) async-start(bf16[4,128,512]{2,1,0:T(8,128)(2,1)} %broadcast_in_dim.23), calls=%async_computation.1 | async-start | bytes 1048576 | tf_op jit(solution)/shard_map/all_to_all | solution.py:145
  35.8 3.1 %collective-permute-start.1 = (bf16[2,128,512]{2,1,0:T(8,128)(2,1)S(1)}, bf16[2,128,512]{2,1,0:T(8,128)(2,1)S(1)}, u32[]{:S(2)}, u32[]{:S(2)}) collective-permute-start(bf16[2,128,512]{2,1,0:T(8,128)(2,1)S(1)} %get-tuple-element.22), channel_id=1, source_target_pairs={{0,32},{32,64},{64,96},{96,0},{1,33},{33,65},{65,97},{97,1},{2,34}... | collective-permute-start | bytes 786440 | tf_op jit(solution)/shard_map/ppermute | solution.py:141
  38.9 4.4 %collective-permute-start.2 = (bf16[2,128,512]{2,1,0:T(8,128)(2,1)S(1)}, bf16[2,128,512]{2,1,0:T(8,128)(2,1)S(1)}, u32[]{:S(2)}, u32[]{:S(2)}) collective-permute-start(bf16[2,128,512]{2,1,0:T(8,128)(2,1)S(1)} %get-tuple-element.23), channel_id=1, source_target_pairs={{0,64},{32,96},{64,0},{96,32},{1,65},{33,97},{65,1},{97,33},{2,66}... | collective-permute-start | bytes 786440 | tf_op jit(solution)/shard_map/ppermute | solution.py:141
  43.3 3.1 %collective-permute-start.3 = (bf16[2,128,512]{2,1,0:T(8,128)(2,1)S(1)}, bf16[2,128,512]{2,1,0:T(8,128)(2,1)S(1)}, u32[]{:S(2)}, u32[]{:S(2)}) collective-permute-start(bf16[2,128,512]{2,1,0:T(8,128)(2,1)S(1)} %get-tuple-element.24), channel_id=1, source_target_pairs={{0,96},{32,0},{64,32},{96,64},{1,97},{33,1},{65,33},{97,65},{2,98}... | collective-permute-start | bytes 786440 | tf_op jit(solution)/shard_map/ppermute | solution.py:141
  46.4 3.2 %collective-permute-done.2.refs_2_ = bf16[2,128,512]{2,1,0:T(8,128)(2,1)S(1)} collective-permute-done((bf16[2,128,512]{2,1,0:T(8,128)(2,1)S(1)}, bf16[2,128,512]{2,1,0:T(8,128)(2,1)S(1)}, u32[]{:S(2)}, u32[]{:S(2)}) %collective-permute-start.2) | collective-permute-done | bytes 262176 | tf_op jit(solution)/shard_map/ppermute | solution.py:141
  49.6 3.6 %collective-permute-done.3.refs_3_ = bf16[2,128,512]{2,1,0:T(8,128)(2,1)S(1)} collective-permute-done((bf16[2,128,512]{2,1,0:T(8,128)(2,1)S(1)}, bf16[2,128,512]{2,1,0:T(8,128)(2,1)S(1)}, u32[]{:S(2)}, u32[]{:S(2)}) %collective-permute-start.3) | collective-permute-done | bytes 262176 | tf_op jit(solution)/shard_map/ppermute | solution.py:141
  54.3 5.4 %collective-permute-start.4 = (bf16[512,512]{1,0:T(8,128)(2,1)S(1)}, bf16[512,512]{1,0:T(8,128)(2,1)S(1)}, u32[]{:S(2)}, u32[]{:S(2)}) collective-permute-start(bf16[512,512]{1,0:T(8,128)(2,1)S(1)} %convolution_convert_fusion.2), channel_id=1, source_target_pairs={{0,16},{16,0},{1,17},{17,1},{2,18},{18,2},{3,19},{19,3},{4,20},{20... | collective-permute-start | bytes 1572872 | tf_op jit(solution)/shard_map/ppermute | solution.py:137
  62.5 3.6 %all-to-all-start.2 = ((bf16[4,128,512]{2,1,0:T(8,128)(2,1)}), bf16[4,128,512]{2,1,0:T(8,128)(2,1)S(1)}, u32[]{:S(2)}, u32[]{:S(2)}) async-start(bf16[4,128,512]{2,1,0:T(8,128)(2,1)} %bitcast.6), calls=%async_computation.2 | async-start | bytes 1048576 | tf_op jit(solution)/shard_map/all_to_all | solution.py:145
  67.7 2.8 %shard_map.131.probs_ref = bf16[4,1024,128]{2,1,0:T(8,128)(2,1)S(1)} custom-call(bf16[128,4096]{1,0:T(8,128)(2,1)S(1)} %copy-done.1, bf16[128,512]{1,0:T(8,128)(2,1)S(1)} %copy-done.2, s32[1,128]{1,0:T(1,128)S(1)} %bitcast.40, s32[128,1]{1,0:T(8,128)S(1)} %copy.16.seg_col_ref), custom_call_target="tpu_custom_call" | custom-call | flops 268435456 | bytes 8388608 | tf_op jit(solution)/shard_map/pallas_call | solution.py:126
  70.5 4.5 %all-to-all-done.2.partial_ref = bf16[4,128,512]{2,1,0:T(8,128)(2,1)S(1)} async-done(((bf16[4,128,512]{2,1,0:T(8,128)(2,1)}), bf16[4,128,512]{2,1,0:T(8,128)(2,1)S(1)}, u32[]{:S(2)}, u32[]{:S(2)}) %all-to-all-start.2) | async-done | bytes 524320 | tf_op jit(solution)/shard_map/all_to_all | solution.py:145
  76.7 10.3 %all_to_all.30 = bf16[4,128,512]{2,1,0:T(8,128)(2,1)S(1)} all-to-all(bf16[4,128,512]{2,1,0:T(8,128)(2,1)S(1)} %get-tuple-element.28), channel_id=1, replica_groups=mesh['zl'=4,'x'=4,'c'=2,'zh'=4,'y'=4] {'x'}, dimensions={0} | all-to-all | bytes 1048576 | tf_op jit(solution)/shard_map/all_to_all | solution.py:145
  87.0 4.5 %collective-permute-start.5 = (bf16[512,512]{1,0:T(8,128)(2,1)S(1)}, bf16[512,512]{1,0:T(8,128)(2,1)S(1)}, u32[]{:S(2)}, u32[]{:S(2)}) collective-permute-start(bf16[512,512]{1,0:T(8,128)(2,1)S(1)} %bitcast.45), channel_id=1, source_target_pairs={{0,16},{16,0},{1,17},{17,1},{2,18},{18,2},{3,19},{19,3},{4,20},{20... | collective-permute-start | bytes 1572872 | tf_op jit(solution)/shard_map/ppermute | solution.py:137
  94.7 4.2 %all-to-all-start.4 = ((bf16[4,128,512]{2,1,0:T(8,128)(2,1)}), bf16[4,128,512]{2,1,0:T(8,128)(2,1)}, u32[]{:S(2)}, u32[]{:S(2)}) async-start(bf16[4,128,512]{2,1,0:T(8,128)(2,1)} %bitcast.15), calls=%async_computation.4 | async-start | bytes 1048576 | tf_op jit(solution)/shard_map/all_to_all | solution.py:145
  100.2 2.7 %collective-permute-start.6 = (bf16[512,512]{1,0:T(8,128)(2,1)}, bf16[512,512]{1,0:T(8,128)(2,1)S(1)}, u32[]{:S(2)}, u32[]{:S(2)}) collective-permute-start(bf16[512,512]{1,0:T(8,128)(2,1)} %convolution_convert_fusion), channel_id=1, source_target_pairs={{0,16},{16,0},{1,17},{17,1},{2,18},{18,2},{3,19},{19,3},{4,20},{20... | collective-permute-start | bytes 1572872 | tf_op jit(solution)/shard_map/ppermute | solution.py:137
  102.9 5.0 %all-to-all-done.4 = bf16[4,128,512]{2,1,0:T(8,128)(2,1)} async-done(((bf16[4,128,512]{2,1,0:T(8,128)(2,1)}), bf16[4,128,512]{2,1,0:T(8,128)(2,1)}, u32[]{:S(2)}, u32[]{:S(2)}) %all-to-all-start.4) | async-done | bytes 524320 | tf_op jit(solution)/shard_map/all_to_all | solution.py:145
  109.7 6.5 %all-to-all-start.5 = ((bf16[16,8,512]{2,1,0:T(8,128)(2,1)}), bf16[16,8,512]{2,1,0:T(8,128)(2,1)S(1)}, u32[]{:S(2)}, u32[]{:S(2)}) async-start(bf16[16,8,512]{2,1,0:T(8,128)(2,1)} %bitcast.16), calls=%async_computation.5 | async-start | bytes 262144 | tf_op jit(solution)/shard_map/all_to_all | solution.py:145
  120.6 3.7 %collective-permute-start.8 = (bf16[2,128,512]{2,1,0:T(8,128)(2,1)S(1)}, bf16[2,128,512]{2,1,0:T(8,128)(2,1)S(1)}, u32[]{:S(2)}, u32[]{:S(2)}) collective-permute-start(bf16[2,128,512]{2,1,0:T(8,128)(2,1)S(1)} %get-tuple-element.31), channel_id=1, source_target_pairs={{0,64},{32,96},{64,0},{96,32},{1,65},{33,97},{65,1},{97,33},{2,66}... | collective-permute-start | bytes 786440 | tf_op jit(solution)/shard_map/ppermute | solution.py:141
  124.3 2.5 %collective-permute-start.9 = (bf16[2,128,512]{2,1,0:T(8,128)(2,1)S(1)}, bf16[2,128,512]{2,1,0:T(8,128)(2,1)S(1)}, u32[]{:S(2)}, u32[]{:S(2)}) collective-permute-start(bf16[2,128,512]{2,1,0:T(8,128)(2,1)S(1)} %get-tuple-element.32), channel_id=1, source_target_pairs={{0,96},{32,0},{64,32},{96,64},{1,97},{33,1},{65,33},{97,65},{2,98}... | collective-permute-start | bytes 786440 | tf_op jit(solution)/shard_map/ppermute | solution.py:141
  128.1 4.4 %collective-permute-done.8.b2_ref = bf16[2,128,512]{2,1,0:T(8,128)(2,1)S(1)} collective-permute-done((bf16[2,128,512]{2,1,0:T(8,128)(2,1)S(1)}, bf16[2,128,512]{2,1,0:T(8,128)(2,1)S(1)}, u32[]{:S(2)}, u32[]{:S(2)}) %collective-permute-start.8) | collective-permute-done | bytes 262176 | tf_op jit(solution)/shard_map/ppermute | solution.py:141
  132.5 3.7 %collective-permute-done.9.b3_ref = bf16[2,128,512]{2,1,0:T(8,128)(2,1)S(1)} collective-permute-done((bf16[2,128,512]{2,1,0:T(8,128)(2,1)S(1)}, bf16[2,128,512]{2,1,0:T(8,128)(2,1)S(1)}, u32[]{:S(2)}, u32[]{:S(2)}) %collective-permute-start.9) | collective-permute-done | bytes 262176 | tf_op jit(solution)/shard_map/ppermute | solution.py:141
  136.2 2.9 %shard_map.134 = bf16[128,4096]{1,0:T(8,128)(2,1)} custom-call(s32[2]{0:T(128)S(1)} %pad_add_fusion.at_ref, bf16[2,128,512]{2,1,0:T(8,128)(2,1)S(1)} %get-tuple-element.29.b0_ref, bf16[2,128,512]{2,1,0:T(8,128)(2,1)S(1)} %collective-permute-done.7.b1_ref, bf16[2,128,512]{2,1,0:T(8,128)(2,1)S(1)} %collective-permute-done.8.b2_ref, ...), custom_call_target="tpu_custom_call" | custom-call | flops 1073741824 | bytes 4194304 | tf_op jit(solution)/shard_map/pallas_call | solution.py:126
  (50 shorter events, 27.3 us)
Async XLA Ops:
  2.0 28.1 %all-to-all-start = ((bf16[16,8,512]{2,1,0:T(8,128)(2,1)}), bf16[16,8,512]{2,1,0:T(8,128)(2,1)S(1)}, u32[]{:S(2)}, u32[]{:S(2)}) async-start(bf16[16,8,512]{2,1,0:T(8,128)(2,1)} %broadcast_in_dim.10), calls=%async_computation | async-start | bytes 262144 | tf_op jit(solution)/shard_map/all_to_all | solution.py:145
  19.1 1.6 %copy-start.4 = (bf16[1024,1024]{1,0:T(8,128)(2,1)S(1)}, bf16[1024,1024]{1,0:T(8,128)(2,1)}, u32[]{:S(2)}) copy-start(bf16[1024,1024]{1,0:T(8,128)(2,1)} %constant.50.clone.shuffle_ref) | copy-start | bytes 6291460
  22.6 12.6 %collective-permute-start = (bf16[4,128,512]{2,1,0:T(8,128)(2,1)S(1)}, bf16[4,128,512]{2,1,0:T(8,128)(2,1)S(1)}, u32[]{:S(2)}, u32[]{:S(2)}) collective-permute-start(bf16[4,128,512]{2,1,0:T(8,128)(2,1)S(1)} %get-tuple-element.20), channel_id=1, source_target_pairs={{0,16},{16,0},{1,17},{17,1},{2,18},{18,2},{3,19},{19,3},{4,20},{20... | collective-permute-start | bytes 1572872 | tf_op jit(solution)/shard_map/ppermute | solution.py:137
  31.0 22.8 %all-to-all-start.1 = ((bf16[4,128,512]{2,1,0:T(8,128)(2,1)}), bf16[4,128,512]{2,1,0:T(8,128)(2,1)S(1)}, u32[]{:S(2)}, u32[]{:S(2)}) async-start(bf16[4,128,512]{2,1,0:T(8,128)(2,1)} %broadcast_in_dim.23), calls=%async_computation.1 | async-start | bytes 1048576 | tf_op jit(solution)/shard_map/all_to_all | solution.py:145
  35.8 10.6 %collective-permute-start.1 = (bf16[2,128,512]{2,1,0:T(8,128)(2,1)S(1)}, bf16[2,128,512]{2,1,0:T(8,128)(2,1)S(1)}, u32[]{:S(2)}, u32[]{:S(2)}) collective-permute-start(bf16[2,128,512]{2,1,0:T(8,128)(2,1)S(1)} %get-tuple-element.22), channel_id=1, source_target_pairs={{0,32},{32,64},{64,96},{96,0},{1,33},{33,65},{65,97},{97,1},{2,34}... | collective-permute-start | bytes 786440 | tf_op jit(solution)/shard_map/ppermute | solution.py:141
  38.9 10.6 %collective-permute-start.2 = (bf16[2,128,512]{2,1,0:T(8,128)(2,1)S(1)}, bf16[2,128,512]{2,1,0:T(8,128)(2,1)S(1)}, u32[]{:S(2)}, u32[]{:S(2)}) collective-permute-start(bf16[2,128,512]{2,1,0:T(8,128)(2,1)S(1)} %get-tuple-element.23), channel_id=1, source_target_pairs={{0,64},{32,96},{64,0},{96,32},{1,65},{33,97},{65,1},{97,33},{2,66}... | collective-permute-start | bytes 786440 | tf_op jit(solution)/shard_map/ppermute | solution.py:141
  43.3 9.9 %collective-permute-start.3 = (bf16[2,128,512]{2,1,0:T(8,128)(2,1)S(1)}, bf16[2,128,512]{2,1,0:T(8,128)(2,1)S(1)}, u32[]{:S(2)}, u32[]{:S(2)}) collective-permute-start(bf16[2,128,512]{2,1,0:T(8,128)(2,1)S(1)} %get-tuple-element.24), channel_id=1, source_target_pairs={{0,96},{32,0},{64,32},{96,64},{1,97},{33,1},{65,33},{97,65},{2,98}... | collective-permute-start | bytes 786440 | tf_op jit(solution)/shard_map/ppermute | solution.py:141
  53.8 12.3 %copy-start.9 = (s32[1,4]{1,0:T(1,128)S(1)}, s32[1,4]{1,0:T(1,128)}, u32[]{:S(2)}) copy-start(s32[1,4]{1,0:T(1,128)} %param.12) | copy-start | bytes 52
  53.8 12.7 %copy-start.2 = (bf16[128,512]{1,0:T(8,128)(2,1)S(1)}, bf16[128,512]{1,0:T(8,128)(2,1)}, u32[]{:S(2)}) copy-start(bf16[128,512]{1,0:T(8,128)(2,1)} %keys_ref.1) | copy-start | bytes 393220
  54.3 7.0 %collective-permute-start.4 = (bf16[512,512]{1,0:T(8,128)(2,1)S(1)}, bf16[512,512]{1,0:T(8,128)(2,1)S(1)}, u32[]{:S(2)}, u32[]{:S(2)}) collective-permute-start(bf16[512,512]{1,0:T(8,128)(2,1)S(1)} %convolution_convert_fusion.2), channel_id=1, source_target_pairs={{0,16},{16,0},{1,17},{17,1},{2,18},{18,2},{3,19},{19,3},{4,20},{20... | collective-permute-start | bytes 1572872 | tf_op jit(solution)/shard_map/ppermute | solution.py:137
  62.5 12.5 %all-to-all-start.2 = ((bf16[4,128,512]{2,1,0:T(8,128)(2,1)}), bf16[4,128,512]{2,1,0:T(8,128)(2,1)S(1)}, u32[]{:S(2)}, u32[]{:S(2)}) async-start(bf16[4,128,512]{2,1,0:T(8,128)(2,1)} %bitcast.6), calls=%async_computation.2 | async-start | bytes 1048576 | tf_op jit(solution)/shard_map/all_to_all | solution.py:145
  66.5 1.2 copy-start.1
  87.0 7.7 %copy-start.5 = (bf16[4,128,512]{2,1,0:T(8,128)(2,1)}, bf16[4,128,512]{2,1,0:T(8,128)(2,1)S(1)}, u32[]{:S(2)}) copy-start(bf16[4,128,512]{2,1,0:T(8,128)(2,1)S(1)} %all_to_all.30) | copy-start | bytes 1572868
  87.0 6.0 %collective-permute-start.5 = (bf16[512,512]{1,0:T(8,128)(2,1)S(1)}, bf16[512,512]{1,0:T(8,128)(2,1)S(1)}, u32[]{:S(2)}, u32[]{:S(2)}) collective-permute-start(bf16[512,512]{1,0:T(8,128)(2,1)S(1)} %bitcast.45), channel_id=1, source_target_pairs={{0,16},{16,0},{1,17},{17,1},{2,18},{18,2},{3,19},{19,3},{4,20},{20... | collective-permute-start | bytes 1572872 | tf_op jit(solution)/shard_map/ppermute | solution.py:137
  94.7 13.2 %all-to-all-start.4 = ((bf16[4,128,512]{2,1,0:T(8,128)(2,1)}), bf16[4,128,512]{2,1,0:T(8,128)(2,1)}, u32[]{:S(2)}, u32[]{:S(2)}) async-start(bf16[4,128,512]{2,1,0:T(8,128)(2,1)} %bitcast.15), calls=%async_computation.4 | async-start | bytes 1048576 | tf_op jit(solution)/shard_map/all_to_all | solution.py:145
  100.2 36.0 %copy-start = (bf16[1024,1024]{1,0:T(8,128)(2,1)S(1)}, bf16[1024,1024]{1,0:T(8,128)(2,1)}, u32[]{:S(2)}) copy-start(bf16[1024,1024]{1,0:T(8,128)(2,1)} %constant.49.clone.shuffle_ref) | copy-start | bytes 6291460
  100.2 17.5 %collective-permute-start.6 = (bf16[512,512]{1,0:T(8,128)(2,1)}, bf16[512,512]{1,0:T(8,128)(2,1)S(1)}, u32[]{:S(2)}, u32[]{:S(2)}) collective-permute-start(bf16[512,512]{1,0:T(8,128)(2,1)} %convolution_convert_fusion), channel_id=1, source_target_pairs={{0,16},{16,0},{1,17},{17,1},{2,18},{18,2},{3,19},{19,3},{4,20},{20... | collective-permute-start | bytes 1572872 | tf_op jit(solution)/shard_map/ppermute | solution.py:137
  109.7 29.4 %all-to-all-start.5 = ((bf16[16,8,512]{2,1,0:T(8,128)(2,1)}), bf16[16,8,512]{2,1,0:T(8,128)(2,1)S(1)}, u32[]{:S(2)}, u32[]{:S(2)}) async-start(bf16[16,8,512]{2,1,0:T(8,128)(2,1)} %bitcast.16), calls=%async_computation.5 | async-start | bytes 262144 | tf_op jit(solution)/shard_map/all_to_all | solution.py:145
  118.4 9.7 %collective-permute-start.7 = (bf16[2,128,512]{2,1,0:T(8,128)(2,1)S(1)}, bf16[2,128,512]{2,1,0:T(8,128)(2,1)S(1)}, u32[]{:S(2)}, u32[]{:S(2)}) collective-permute-start(bf16[2,128,512]{2,1,0:T(8,128)(2,1)S(1)} %get-tuple-element.30), channel_id=1, source_target_pairs={{0,32},{32,64},{64,96},{96,0},{1,33},{33,65},{65,97},{97,1},{2,34}... | collective-permute-start | bytes 786440 | tf_op jit(solution)/shard_map/ppermute | solution.py:141
  120.6 11.9 %collective-permute-start.8 = (bf16[2,128,512]{2,1,0:T(8,128)(2,1)S(1)}, bf16[2,128,512]{2,1,0:T(8,128)(2,1)S(1)}, u32[]{:S(2)}, u32[]{:S(2)}) collective-permute-start(bf16[2,128,512]{2,1,0:T(8,128)(2,1)S(1)} %get-tuple-element.31), channel_id=1, source_target_pairs={{0,64},{32,96},{64,0},{96,32},{1,65},{33,97},{65,1},{97,33},{2,66}... | collective-permute-start | bytes 786440 | tf_op jit(solution)/shard_map/ppermute | solution.py:141
  124.3 11.9 %collective-permute-start.9 = (bf16[2,128,512]{2,1,0:T(8,128)(2,1)S(1)}, bf16[2,128,512]{2,1,0:T(8,128)(2,1)S(1)}, u32[]{:S(2)}, u32[]{:S(2)}) collective-permute-start(bf16[2,128,512]{2,1,0:T(8,128)(2,1)S(1)} %get-tuple-element.32), channel_id=1, source_target_pairs={{0,96},{32,0},{64,32},{96,64},{1,97},{33,1},{65,33},{97,65},{2,98}... | collective-permute-start | bytes 786440 | tf_op jit(solution)/shard_map/ppermute | solution.py:141
  136.1 3.0 %copy-start.6 = (f32[8,512]{1,0:T(8,128)S(1)}, f32[8,512]{1,0:T(8,128)}, u32[]{:S(2)}) copy-start(f32[8,512]{1,0:T(8,128)} %param.13) | copy-start | bytes 49156
  136.1 3.0 %copy-start.7 = (f32[8,512]{1,0:T(8,128)S(1)}, f32[8,512]{1,0:T(8,128)}, u32[]{:S(2)}) copy-start(f32[8,512]{1,0:T(8,128)} %param.14) | copy-start | bytes 49156
  136.1 3.0 %copy-start.8 = (f32[8,512]{1,0:T(8,128)S(1)}, f32[8,512]{1,0:T(8,128)}, u32[]{:S(2)}) copy-start(f32[8,512]{1,0:T(8,128)} %param.15) | copy-start | bytes 49156
  (1 other events, 1.2 us)

commit v3 on v1

v3 whole, which is shorter than its diff:
```python
import jax
import jax.numpy as jnp
import numpy as np
from jax import lax
from jax.experimental import pallas as pl
from jax.experimental.pallas import tpu as pltpu
from jax.sharding import Mesh
from jax.sharding import PartitionSpec as P

HD = 128
VH = 4
QH = 32
GROUPS = QH // VH

beta_one = 0.9
beta_two = 0.95
adam_eps = 1e-08
learn_rate = 0.001
decay_rate = 0.1

AXES = ("zl", "x", "c", "zh", "y")
SIZES = (4, 4, 2, 4, 4)
TOK_SPEC = P(AXES, None)
ROW_SPEC = P(("zh", "y", "zl", "x", "c"), None)
DEPTH = ("zl", "zh")
RING = 4

F32 = jnp.float32
BF16 = jnp.bfloat16


def order_matrix(core):
    to = lax.broadcasted_iota(jnp.int32, (1, 1024), 1)
    source = ((to >> 3) & 3) * 256 + ((to >> 5) & 3) * 64 + ((to >> 7) & 3) * 16 + (to & 7)
    source = source + ((to >> 9) ^ core) * 8
    hit = lax.broadcasted_iota(jnp.int32, (1024, 1024), 0) == source
    return jnp.where(hit, F32(1), F32(0)).astype(BF16)


WEIGHTY = 32 << 30


def spread_kernel(rows_ref, *refs):
    rows = rows_ref[...].astype(BF16)
    for i in range(refs[-1].shape[0]):
        refs[-1][i] = rows


def columns_of(y, zh):
    return pl.ds(pl.multiple_of(zh * 1024 + y * 256, 256), 256)


def deal_kernel(at_ref, hidden_ref, *out_refs):
    for d in range(RING):
        for zh in range(4):
            out_refs[d][:, zh * 256 : (zh + 1) * 256] = hidden_ref[:, columns_of(at_ref[0] ^ d, zh)]


def collect_kernel(at_ref, *refs):
    in_refs, own_ref, other_ref, matrix_ref = refs[:RING], refs[RING], refs[RING + 1], refs[RING + 2]
    matrix_ref[...] = order_matrix(at_ref[1])
    for d in range(RING):
        moved = jnp.dot(in_refs[d][...], matrix_ref[...], preferred_element_type=F32).astype(BF16)
        own_ref[at_ref[0] ^ d] = moved[:, :512]
        other_ref[at_ref[0] ^ d] = moved[:, 512:]


def turn_kernel(at_ref, own_ref, other_ref, out_ref):
    matrix = order_matrix(at_ref[1])
    contract = (((0,), (1,)), ((), ()))
    total = lax.dot_general(own_ref[...], matrix[:, :512], contract, preferred_element_type=F32)
    total = total + lax.dot_general(other_ref[...], matrix[:, 512:], contract, preferred_element_type=F32)
    out_ref[...] = total.astype(BF16)


def back_kernel(at_ref, grad_ref, weight_ref, *refs):
    out_refs, rows_ref = refs[:RING], refs[RING]
    tok = out_refs[0].shape[0]
    rows = jnp.dot(grad_ref[...], weight_ref[...], preferred_element_type=F32).astype(BF16)
    for y in range(RING):
        rows_ref[y] = rows[y * tok : (y + 1) * tok]
    for d in range(RING):
        out_refs[d][...] = rows_ref[at_ref[0] ^ d]


def join_kernel(at_ref, *refs):
    for d in range(RING):
        for zh in range(4):
            refs[RING][:, columns_of(at_ref[0] ^ d, zh)] = refs[d][:, zh * 256 : (zh + 1) * 256]


def sum_kernel(parts_ref, out_ref):
    total = parts_ref[0].astype(F32)
    for y in range(1, 4):
        total = total + parts_ref[y].astype(F32)
    total = total.astype(BF16)
    rows = out_ref.shape[1]
    for z in range(out_ref.shape[0]):
        out_ref[z] = total[z * rows : (z + 1) * rows]


def probs_kernel(queries_ref, keys_ref, seg_row_ref, seg_col_ref, out_ref):
    tok = queries_ref.shape[0]
    rows = lax.broadcasted_iota(jnp.int32, (tok, tok), 0)
    cols = lax.broadcasted_iota(jnp.int32, (tok, tok), 1)
    allowed = (seg_col_ref[...] == seg_row_ref[...]) & (cols <= rows)
    scale = F32(1.0 / np.sqrt(HD))
    for j in range(VH):
        key = keys_ref[:, j * HD : (j + 1) * HD]
        for h in range(GROUPS):
            at = (j * GROUPS + h) * HD
            scores = lax.dot_general(
                queries_ref[:, at : at + HD], key, (((1,), (1,)), ((), ())), preferred_element_type=F32
            )
            scores = jnp.where(allowed, scores * scale, F32(-1000000000.0))
            expos = jnp.exp(scores - jnp.max(scores, axis=-1, keepdims=True))
            total = jnp.sum(expos, axis=-1, keepdims=True)
            out_ref[j, h * tok : (h + 1) * tok, :] = (expos / total).astype(BF16)


def attend_kernel(partial_ref, probs_ref, attended_ref, grad_ref):
    tok = partial_ref.shape[1]
    for j in range(VH):
        cols = slice(j * HD, (j + 1) * HD)
        total = partial_ref[0, :, cols].astype(F32)
        for x in range(1, 4):
            total = total + partial_ref[x, :, cols].astype(F32)
        value = total.astype(BF16)
        attended = jnp.dot(probs_ref[j], value, preferred_element_type=F32).astype(BF16)
        grad = lax.dot_general(
            probs_ref[j], attended, (((0,), (0,)), ((), ())), preferred_element_type=F32
        ).astype(BF16)
        for h in range(GROUPS):
            at = (j * GROUPS + h) * HD
            attended_ref[:, at : at + HD] = attended[h * tok : (h + 1) * tok]
        for x in range(4):
            grad_ref[x, :, cols] = grad


SMEM = pl.BlockSpec(memory_space=pltpu.SMEM)
VMEM = pl.BlockSpec(memory_space=pltpu.VMEM)


def call(kernel, out_shape, flops, nbytes, *args, scratch=()):
    specs = [SMEM if a.dtype == jnp.int32 and a.ndim == 1 else VMEM for a in args]
    return pl.pallas_call(
        kernel,
        out_shape=out_shape,
        in_specs=specs,
        scratch_shapes=scratch,
        compiler_params=pltpu.CompilerParams(vmem_limit_bytes=24 * 1024 * 1024),
        cost_estimate=pl.CostEstimate(flops=flops, bytes_accessed=nbytes, transcendentals=0),
    )(*args)


def swap_core(array):
    return lax.ppermute(array, "c", [(0, 1), (1, 0)])


def along_y(blocks):
    moved = [lax.ppermute(blocks[d], "y", [(i, i ^ d) for i in range(RING)]) for d in range(1, RING)]
    return [blocks[0]] + moved


def exchange(blocks, axes):
    return lax.all_to_all(blocks, axes, split_axis=0, concat_axis=0, tiled=True)


def per_device(hidden_in, queries, keys, lengths, master, moment, second):
    tok, width = hidden_in.shape
    kv = keys.shape[1]
    rows = master.shape[0]
    feats = width // RING
    at = jnp.stack([lax.axis_index("y"), lax.axis_index("c")]).astype(jnp.int32)
    block = jax.ShapeDtypeStruct((tok, feats), BF16)
    half = jax.ShapeDtypeStruct((RING, tok, feats // 2), BF16)
    matrix = pltpu.VMEM((feats, feats), BF16)

    weight = call(spread_kernel, jax.ShapeDtypeStruct((16, rows, kv), BF16), 0, 1 << 17, master)
    weight = exchange(weight, DEPTH).reshape(16 * rows, kv)

    dealt = along_y(call(deal_kernel, (block,) * RING, 0, 2 << 20, at, hidden_in))
    hidden_own, hidden_other = call(
        collect_kernel, (half, half), WEIGHTY, 3 << 20, at, *dealt, scratch=[matrix]
    )

    weight = call(spread_kernel, jax.ShapeDtypeStruct((RING, 16 * rows, kv), BF16), 0, 1 << 19, weight)
    weight = exchange(weight, "x").reshape(RING * 16 * rows, kv)
    weight, hidden_own, hidden_other = lax.optimization_barrier((weight, hidden_own, hidden_other))
    weight_other = swap_core(weight)
    hidden_own = hidden_own.reshape(RING * tok, feats // 2)
    hidden_other = hidden_other.reshape(RING * tok, feats // 2)

    ends = jnp.cumsum(lengths[0])
    seg = jnp.sum((jnp.arange(tok, dtype=jnp.int32)[:, None] >= ends[None, :]).astype(jnp.int32), axis=1)
    probs = call(
        probs_kernel,
        jax.ShapeDtypeStruct((VH, GROUPS * tok, tok), BF16),
        4 * tok * tok * QH * HD,
        8 << 20,
        queries,
        keys,
        seg[None, :],
        seg[:, None],
    )

    partial = jnp.dot(hidden_own, weight, preferred_element_type=F32)
    partial = partial + jnp.dot(hidden_other, weight_other, preferred_element_type=F32)
    partial = exchange(partial.astype(BF16).reshape(RING, tok, kv), "y")
    attended, grad = call(
        attend_kernel,
        (jax.ShapeDtypeStruct((tok, QH * HD), BF16), jax.ShapeDtypeStruct((RING, tok, kv), BF16)),
        4 * tok * tok * QH * HD,
        4 << 20,
        partial,
        probs,
    )
    weight_cols = call(
        turn_kernel, jax.ShapeDtypeStruct((kv, feats), BF16), 2 * feats * feats * kv, 3 << 20, at, weight, weight_other
    )
    grad = exchange(grad, "y").reshape(RING * tok, kv)
    grad, weight_cols = lax.optimization_barrier((grad, weight_cols))

    rowwise = (((0,), (0,)), ((), ()))
    part = swap_core(
        lax.dot_general(hidden_other, grad, rowwise, preferred_element_type=F32).astype(BF16)
    ).astype(F32)
    part = part + lax.dot_general(hidden_own, grad, rowwise, preferred_element_type=F32)
    part = part.astype(BF16).reshape(RING, 16 * rows, kv)

    dealt = call(
        back_kernel,
        (block,) * RING,
        2 * RING * tok * feats * kv,
        3 << 20,
        at,
        grad,
        weight_cols,
        scratch=[pltpu.VMEM((RING, tok, feats), BF16)],
    )
    part, dealt = lax.optimization_barrier((part, dealt))
    dealt = along_y(dealt)
    grad_hidden = call(
        join_kernel, jax.ShapeDtypeStruct((tok, width), BF16), WEIGHTY, 2 << 20, at, *dealt
    )

    part = exchange(part, "x")
    part = call(sum_kernel, jax.ShapeDtypeStruct((16, rows, kv), BF16), 0, 1 << 20, part)
    part = exchange(part, DEPTH)
    gradient = jnp.sum(part.astype(F32), axis=0) / F32(tok * 512)

    moment_new = beta_one * moment + (1.0 - beta_one) * gradient
    second_new = beta_two * second + (1.0 - beta_two) * gradient * gradient
    moment_hat = moment_new / (1.0 - beta_one**10)
    second_hat = second_new / (1.0 - beta_two**10)
    master_new = master - learn_rate * (
        moment_hat / (jnp.sqrt(second_hat) + adam_eps) + decay_rate * master
    )
    return (attended, grad_hidden, master_new, moment_new, second_new)


def solution(mesh):
    named = Mesh(mesh.devices.reshape(SIZES), AXES)
    return jax.shard_map(
        per_device,
        mesh=named,
        in_specs=(TOK_SPEC, TOK_SPEC, TOK_SPEC, TOK_SPEC, ROW_SPEC, ROW_SPEC, ROW_SPEC),
        out_specs=(TOK_SPEC, TOK_SPEC, ROW_SPEC, ROW_SPEC, ROW_SPEC),
        check_vma=False,
    )
```

time: 167 us -> 126 us (0.75)
  the two profiles are of different devices: /device:TPU:1 before, /device:TPU:2 now
where the time goes in v3:
time: 126 us
  starting transfers between devices  69.2 us (55%)
  waiting for transfers between devices  33.9 us (27%)
  Pallas kernels  14.3 us (11%)
  matrix products  3.38 us (3%)
  local copies, waits for them, and re-layouts  2.76 us (2%)
    all_to_all x6, starting transfers between devices, exchange(): return lax.all_to_all(blocks, axes, split_axis=0, concat_axis=0, tiled=True)  44.4 us
    all_to_all x6, waiting for transfers between devices, exchange(): return lax.all_to_all(blocks, axes, split_axis=0, concat_axis=0, tiled=True)  27.2 us
    ppermute x6, starting transfers between devices, along_y(): lax.ppermute(blocks[d], 'y', [(i, i ^ d) for i in range(RING)])  20.8 us
    pallas_call x10, Pallas kernels, call(): pl.pallas_call(kernel, out_shape=out_shape, in_specs=specs, scratch_shape...  14.3 us
    ppermute x6, waiting for transfers between devices, along_y(): lax.ppermute(blocks[d], 'y', [(i, i ^ d) for i in range(RING)])  4.81 us
    ppermute x2, starting transfers between devices, swap_core(): return lax.ppermute(array, 'c', [(0, 1), (1, 0)])  3.97 us
    unnamed x32, local copies, waits for them, and re-layouts  2.64 us
  transfers between devices with their start and end apart: 14, of which 7 were waited for; matrix products, arithmetic and copies ran while one was open for 1% of the time, Pallas kernels for 9%

profile of v3, /device:TPU:2, one launch (start us, length us, event | category | flops | bytes accessed | tf_op | source)
XLA Modules:
  0.0 125.5 jit_solution(3169678178148230688)
XLA Ops:
  2.0 15.2 %all-to-all-start = ((bf16[16,8,512]{2,1,0:T(8,128)(2,1)}), bf16[16,8,512]{2,1,0:T(8,128)(2,1)S(1)}, u32[]{:S(2)}, u32[]{:S(2)}) async-start(bf16[16,8,512]{2,1,0:T(8,128)(2,1)} %shard_map.110), calls=%async_computation | async-start | bytes 262144 | tf_op jit(solution)/shard_map/all_to_all | solution.py:166
  19.2 3.5 %collective-permute-start = (bf16[128,1024]{1,0:T(8,128)(2,1)S(1)}, bf16[128,1024]{1,0:T(8,128)(2,1)S(1)}, u32[]{:S(2)}, u32[]{:S(2)}) collective-permute-start(bf16[128,1024]{1,0:T(8,128)(2,1)S(1)} %get-tuple-element.28), channel_id=1, source_target_pairs={{0,1},{1,0},{2,3},{3,2},{4,5},{5,4},{6,7},{7,6},{8,9},{9,8},{10,11... | collective-permute-start | bytes 786440 | tf_op jit(solution)/shard_map/ppermute | solution.py:161
  22.7 4.8 %collective-permute-start.1 = (bf16[128,1024]{1,0:T(8,128)(2,1)S(1)}, bf16[128,1024]{1,0:T(8,128)(2,1)S(1)}, u32[]{:S(2)}, u32[]{:S(2)}) collective-permute-start(bf16[128,1024]{1,0:T(8,128)(2,1)S(1)} %get-tuple-element.29), channel_id=1, source_target_pairs={{0,2},{1,3},{2,0},{3,1},{4,6},{5,7},{6,4},{7,5},{8,10},{9,11},{10,... | collective-permute-start | bytes 786440 | tf_op jit(solution)/shard_map/ppermute | solution.py:161
  27.5 2.1 %collective-permute-start.2 = (bf16[128,1024]{1,0:T(8,128)(2,1)S(1)}, bf16[128,1024]{1,0:T(8,128)(2,1)S(1)}, u32[]{:S(2)}, u32[]{:S(2)}) collective-permute-start(bf16[128,1024]{1,0:T(8,128)(2,1)S(1)} %get-tuple-element.30), channel_id=1, source_target_pairs={{0,3},{1,2},{2,1},{3,0},{4,7},{5,6},{6,5},{7,4},{8,11},{9,10},{10,... | collective-permute-start | bytes 786440 | tf_op jit(solution)/shard_map/ppermute | solution.py:161
  29.7 2.2 %all-to-all-done = bf16[16,8,512]{2,1,0:T(8,128)(2,1)S(1)} async-done(((bf16[16,8,512]{2,1,0:T(8,128)(2,1)}), bf16[16,8,512]{2,1,0:T(8,128)(2,1)S(1)}, u32[]{:S(2)}, u32[]{:S(2)}) %all-to-all-start) | async-done | bytes 131104 | tf_op jit(solution)/shard_map/all_to_all | solution.py:166
  32.6 4.8 %all-to-all-start.1 = ((bf16[4,128,512]{2,1,0:T(8,128)(2,1)}), bf16[4,128,512]{2,1,0:T(8,128)(2,1)S(1)}, u32[]{:S(2)}, u32[]{:S(2)}) async-start(bf16[4,128,512]{2,1,0:T(8,128)(2,1)} %shard_map.111), calls=%async_computation.1 | async-start | bytes 1048576 | tf_op jit(solution)/shard_map/all_to_all | solution.py:166
  37.5 4.8 %collective-permute-done.2.refs_3_ = bf16[128,1024]{1,0:T(8,128)(2,1)S(1)} collective-permute-done((bf16[128,1024]{1,0:T(8,128)(2,1)S(1)}, bf16[128,1024]{1,0:T(8,128)(2,1)S(1)}, u32[]{:S(2)}, u32[]{:S(2)}) %collective-permute-start.2) | collective-permute-done | bytes 262176 | tf_op jit(solution)/shard_map/ppermute | solution.py:161
  42.3 2.0 %shard_map.113 = (bf16[4,128,512]{2,1,0:T(8,128)(2,1)S(1)}, bf16[4,128,512]{2,1,0:T(8,128)(2,1)S(1)}) custom-call(s32[2]{0:T(128)S(1)} %pad_add_fusion.at_ref, bf16[128,1024]{1,0:T(8,128)(2,1)S(1)} %get-tuple-element.27.refs_0_, bf16[128,1024]{1,0:T(8,128)(2,1)S(1)} %collective-permute-done.refs_1_, bf16[128,1024]{1,0:T(8,128)(2,1)S(1)} %collective-permute-done.1.refs_2_, ...), custom_call_target="tpu_custom_call" | custom-call | flops 34359738368 | bytes 3145728 | tf_op jit(solution)/shard_map/pallas_call | solution.py:146
  44.3 1.9 %collective-permute-start.3 = (bf16[512,512]{1,0:T(8,128)(2,1)S(1)}, bf16[512,512]{1,0:T(8,128)(2,1)S(1)}, u32[]{:S(2)}, u32[]{:S(2)}) collective-permute-start(bf16[512,512]{1,0:T(8,128)(2,1)S(1)} %bitcast.21), channel_id=1, source_target_pairs={{0,16},{16,0},{1,17},{17,1},{2,18},{18,2},{3,19},{19,3},{4,20},{20... | collective-permute-start | bytes 1572872 | tf_op jit(solution)/shard_map/ppermute | solution.py:157
  49.4 4.4 %all-to-all-start.2 = ((bf16[4,128,512]{2,1,0:T(8,128)(2,1)}), bf16[4,128,512]{2,1,0:T(8,128)(2,1)S(1)}, u32[]{:S(2)}, u32[]{:S(2)}) async-start(bf16[4,128,512]{2,1,0:T(8,128)(2,1)} %bitcast.6), calls=%async_computation.2 | async-start | bytes 1048576 | tf_op jit(solution)/shard_map/all_to_all | solution.py:166
  54.8 2.8 %shard_map.114.probs_ref = bf16[4,1024,128]{2,1,0:T(8,128)(2,1)S(1)} custom-call(bf16[128,4096]{1,0:T(8,128)(2,1)S(1)} %copy-done, bf16[128,512]{1,0:T(8,128)(2,1)S(1)} %copy-done.8, s32[1,128]{1,0:T(1,128)S(1)} %bitcast.33, s32[128,1]{1,0:T(8,128)S(1)} %copy.13.seg_col_ref), custom_call_target="tpu_custom_call" | custom-call | flops 268435456 | bytes 8388608 | tf_op jit(solution)/shard_map/pallas_call | solution.py:146
  57.6 5.9 %all-to-all-done.2.partial_ref = bf16[4,128,512]{2,1,0:T(8,128)(2,1)S(1)} async-done(((bf16[4,128,512]{2,1,0:T(8,128)(2,1)}), bf16[4,128,512]{2,1,0:T(8,128)(2,1)S(1)}, u32[]{:S(2)}, u32[]{:S(2)}) %all-to-all-start.2) | async-done | bytes 524320 | tf_op jit(solution)/shard_map/all_to_all | solution.py:166
  63.5 1.8 %shard_map.115 = (bf16[128,4096]{1,0:T(8,128)(2,1)}, bf16[4,128,512]{2,1,0:T(8,128)(2,1)}) custom-call(bf16[4,128,512]{2,1,0:T(8,128)(2,1)S(1)} %all-to-all-done.2.partial_ref, bf16[4,1024,128]{2,1,0:T(8,128)(2,1)S(1)} %shard_map.114.probs_ref), custom_call_target="tpu_custom_call" | custom-call | flops 268435456 | bytes 4194304 | tf_op jit(solution)/shard_map/pallas_call | solution.py:146
  65.4 3.6 %all-to-all-start.3 = ((bf16[4,128,512]{2,1,0:T(8,128)(2,1)}), bf16[4,128,512]{2,1,0:T(8,128)(2,1)S(1)}, u32[]{:S(2)}, u32[]{:S(2)}) async-start(bf16[4,128,512]{2,1,0:T(8,128)(2,1)} %get-tuple-element.37), calls=%async_computation.3 | async-start | bytes 1048576 | tf_op jit(solution)/shard_map/all_to_all | solution.py:166
  69.0 1.8 %shard_map.116.weight_ref = bf16[512,1024]{1,0:T(8,128)(2,1)S(1)} custom-call(s32[2]{0:T(128)S(1)} %pad_add_fusion.at_ref, bf16[512,512]{1,0:T(8,128)(2,1)S(1)} %bitcast.23, bf16[512,512]{1,0:T(8,128)(2,1)S(1)} %copy-done.5), custom_call_target="tpu_custom_call" | custom-call | flops 1073741824 | bytes 3145728 | tf_op jit(solution)/shard_map/pallas_call | solution.py:146
  70.8 7.0 %all-to-all-done.3 = bf16[4,128,512]{2,1,0:T(8,128)(2,1)S(1)} async-done(((bf16[4,128,512]{2,1,0:T(8,128)(2,1)}), bf16[4,128,512]{2,1,0:T(8,128)(2,1)S(1)}, u32[]{:S(2)}, u32[]{:S(2)}) %all-to-all-start.3) | async-done | bytes 524320 | tf_op jit(solution)/shard_map/all_to_all | solution.py:166
  78.3 2.1 %collective-permute-start.4 = (bf16[512,512]{1,0:T(8,128)(2,1)S(1)}, bf16[512,512]{1,0:T(8,128)(2,1)S(1)}, u32[]{:S(2)}, u32[]{:S(2)}) collective-permute-start(bf16[512,512]{1,0:T(8,128)(2,1)S(1)} %convolution_convert_fusion), channel_id=1, source_target_pairs={{0,16},{16,0},{1,17},{17,1},{2,18},{18,2},{3,19},{19,3},{4,20},{20... | collective-permute-start | bytes 1572872 | tf_op jit(solution)/shard_map/ppermute | solution.py:157
  83.5 4.9 %all-to-all-start.4 = ((bf16[4,128,512]{2,1,0:T(8,128)(2,1)}), bf16[4,128,512]{2,1,0:T(8,128)(2,1)S(1)}, u32[]{:S(2)}, u32[]{:S(2)}) async-start(bf16[4,128,512]{2,1,0:T(8,128)(2,1)} %bitcast.12), calls=%async_computation.4 | async-start | bytes 1048576 | tf_op jit(solution)/shard_map/all_to_all | solution.py:166
  88.4 2.5 %collective-permute-start.5 = (bf16[128,1024]{1,0:T(8,128)(2,1)S(1)}, bf16[128,1024]{1,0:T(8,128)(2,1)S(1)}, u32[]{:S(2)}, u32[]{:S(2)}) collective-permute-start(bf16[128,1024]{1,0:T(8,128)(2,1)S(1)} %get-tuple-element.45), channel_id=1, source_target_pairs={{0,1},{1,0},{2,3},{3,2},{4,5},{5,4},{6,7},{7,6},{8,9},{9,8},{10,11... | collective-permute-start | bytes 786440 | tf_op jit(solution)/shard_map/ppermute | solution.py:161
  90.9 4.0 %collective-permute-start.6 = (bf16[128,1024]{1,0:T(8,128)(2,1)S(1)}, bf16[128,1024]{1,0:T(8,128)(2,1)S(1)}, u32[]{:S(2)}, u32[]{:S(2)}) collective-permute-start(bf16[128,1024]{1,0:T(8,128)(2,1)S(1)} %get-tuple-element.46), channel_id=1, source_target_pairs={{0,2},{1,3},{2,0},{3,1},{4,6},{5,7},{6,4},{7,5},{8,10},{9,11},{10,... | collective-permute-start | bytes 786440 | tf_op jit(solution)/shard_map/ppermute | solution.py:161
  94.9 4.0 %collective-permute-start.7 = (bf16[128,1024]{1,0:T(8,128)(2,1)S(1)}, bf16[128,1024]{1,0:T(8,128)(2,1)S(1)}, u32[]{:S(2)}, u32[]{:S(2)}) collective-permute-start(bf16[128,1024]{1,0:T(8,128)(2,1)S(1)} %get-tuple-element.47), channel_id=1, source_target_pairs={{0,3},{1,2},{2,1},{3,0},{4,7},{5,6},{6,5},{7,4},{8,11},{9,10},{10,... | collective-permute-start | bytes 786440 | tf_op jit(solution)/shard_map/ppermute | solution.py:161
  99.6 11.5 %all-to-all-start.5 = ((bf16[16,8,512]{2,1,0:T(8,128)(2,1)}), bf16[16,8,512]{2,1,0:T(8,128)(2,1)S(1)}, u32[]{:S(2)}, u32[]{:S(2)}) async-start(bf16[16,8,512]{2,1,0:T(8,128)(2,1)} %shard_map.119), calls=%async_computation.5 | async-start | bytes 262144 | tf_op jit(solution)/shard_map/all_to_all | solution.py:166
  111.1 1.7 %shard_map.118 = bf16[128,4096]{1,0:T(8,128)(2,1)} custom-call(s32[2]{0:T(128)S(1)} %pad_add_fusion.at_ref, bf16[128,1024]{1,0:T(8,128)(2,1)S(1)} %copy-done.12, bf16[128,1024]{1,0:T(8,128)(2,1)S(1)} %collective-permute-done.5.refs_1_, bf16[128,1024]{1,0:T(8,128)(2,1)S(1)} %collective-permute-done.6.refs_2_, bf16[128,1024]{1,0:T(8,128)(2,1)S(1)} %collective-permute-done.7.refs_3_), custom_call_target="tpu_custom_call" | custom-call | flops 34359738368 | bytes 2097152 | tf_op jit(solution)/shard_map/pallas_call | solution.py:146
  112.8 12.1 %all-to-all-done.5 = bf16[16,8,512]{2,1,0:T(8,128)(2,1)S(1)} async-done(((bf16[16,8,512]{2,1,0:T(8,128)(2,1)}), bf16[16,8,512]{2,1,0:T(8,128)(2,1)S(1)}, u32[]{:S(2)}, u32[]{:S(2)}) %all-to-all-start.5) | async-done | bytes 131104 | tf_op jit(solution)/shard_map/all_to_all | solution.py:166
  (56 shorter events, 13.3 us)
Async XLA Ops:
  2.0 29.8 %all-to-all-start = ((bf16[16,8,512]{2,1,0:T(8,128)(2,1)}), bf16[16,8,512]{2,1,0:T(8,128)(2,1)S(1)}, u32[]{:S(2)}, u32[]{:S(2)}) async-start(bf16[16,8,512]{2,1,0:T(8,128)(2,1)} %shard_map.110), calls=%async_computation | async-start | bytes 262144 | tf_op jit(solution)/shard_map/all_to_all | solution.py:166
  19.2 18.3 %collective-permute-start = (bf16[128,1024]{1,0:T(8,128)(2,1)S(1)}, bf16[128,1024]{1,0:T(8,128)(2,1)S(1)}, u32[]{:S(2)}, u32[]{:S(2)}) collective-permute-start(bf16[128,1024]{1,0:T(8,128)(2,1)S(1)} %get-tuple-element.28), channel_id=1, source_target_pairs={{0,1},{1,0},{2,3},{3,2},{4,5},{5,4},{6,7},{7,6},{8,9},{9,8},{10,11... | collective-permute-start | bytes 786440 | tf_op jit(solution)/shard_map/ppermute | solution.py:161
  22.7 14.8 %collective-permute-start.1 = (bf16[128,1024]{1,0:T(8,128)(2,1)S(1)}, bf16[128,1024]{1,0:T(8,128)(2,1)S(1)}, u32[]{:S(2)}, u32[]{:S(2)}) collective-permute-start(bf16[128,1024]{1,0:T(8,128)(2,1)S(1)} %get-tuple-element.29), channel_id=1, source_target_pairs={{0,2},{1,3},{2,0},{3,1},{4,6},{5,7},{6,4},{7,5},{8,10},{9,11},{10,... | collective-permute-start | bytes 786440 | tf_op jit(solution)/shard_map/ppermute | solution.py:161
  27.5 14.7 %collective-permute-start.2 = (bf16[128,1024]{1,0:T(8,128)(2,1)S(1)}, bf16[128,1024]{1,0:T(8,128)(2,1)S(1)}, u32[]{:S(2)}, u32[]{:S(2)}) collective-permute-start(bf16[128,1024]{1,0:T(8,128)(2,1)S(1)} %get-tuple-element.30), channel_id=1, source_target_pairs={{0,3},{1,2},{2,1},{3,0},{4,7},{5,6},{6,5},{7,4},{8,11},{9,10},{10,... | collective-permute-start | bytes 786440 | tf_op jit(solution)/shard_map/ppermute | solution.py:161
  32.6 11.7 %all-to-all-start.1 = ((bf16[4,128,512]{2,1,0:T(8,128)(2,1)}), bf16[4,128,512]{2,1,0:T(8,128)(2,1)S(1)}, u32[]{:S(2)}, u32[]{:S(2)}) async-start(bf16[4,128,512]{2,1,0:T(8,128)(2,1)} %shard_map.111), calls=%async_computation.1 | async-start | bytes 1048576 | tf_op jit(solution)/shard_map/all_to_all | solution.py:166
  44.3 3.8 %copy-start.2 = (bf16[4,128,512]{2,1,0:T(8,128)(2,1)}, bf16[4,128,512]{2,1,0:T(8,128)(2,1)S(1)}, u32[]{:S(2)}) copy-start(bf16[4,128,512]{2,1,0:T(8,128)(2,1)S(1)} %get-tuple-element.35) | copy-start | bytes 1572868
  44.3 3.8 %collective-permute-start.3 = (bf16[512,512]{1,0:T(8,128)(2,1)S(1)}, bf16[512,512]{1,0:T(8,128)(2,1)S(1)}, u32[]{:S(2)}, u32[]{:S(2)}) collective-permute-start(bf16[512,512]{1,0:T(8,128)(2,1)S(1)} %bitcast.21), channel_id=1, source_target_pairs={{0,16},{16,0},{1,17},{17,1},{2,18},{18,2},{3,19},{19,3},{4,20},{20... | collective-permute-start | bytes 1572872 | tf_op jit(solution)/shard_map/ppermute | solution.py:157
  48.1 6.7 %copy-start.8 = (bf16[128,512]{1,0:T(8,128)(2,1)S(1)}, bf16[128,512]{1,0:T(8,128)(2,1)}, u32[]{:S(2)}) copy-start(bf16[128,512]{1,0:T(8,128)(2,1)} %keys_ref.1) | copy-start | bytes 393220
  49.4 5.4 %copy-start = (bf16[128,4096]{1,0:T(8,128)(2,1)S(1)}, bf16[128,4096]{1,0:T(8,128)(2,1)}, u32[]{:S(2)}) copy-start(bf16[128,4096]{1,0:T(8,128)(2,1)} %queries_ref.1) | copy-start | bytes 3145732
  49.4 14.2 %all-to-all-start.2 = ((bf16[4,128,512]{2,1,0:T(8,128)(2,1)}), bf16[4,128,512]{2,1,0:T(8,128)(2,1)S(1)}, u32[]{:S(2)}, u32[]{:S(2)}) async-start(bf16[4,128,512]{2,1,0:T(8,128)(2,1)} %bitcast.6), calls=%async_computation.2 | async-start | bytes 1048576 | tf_op jit(solution)/shard_map/all_to_all | solution.py:166
  65.4 3.6 %copy-start.5 = (bf16[512,512]{1,0:T(8,128)(2,1)S(1)}, bf16[512,512]{1,0:T(8,128)(2,1)}, u32[]{:S(2)}) copy-start(bf16[512,512]{1,0:T(8,128)(2,1)} %copy-done.4) | copy-start | bytes 1572868
  65.4 12.5 %all-to-all-start.3 = ((bf16[4,128,512]{2,1,0:T(8,128)(2,1)}), bf16[4,128,512]{2,1,0:T(8,128)(2,1)S(1)}, u32[]{:S(2)}, u32[]{:S(2)}) async-start(bf16[4,128,512]{2,1,0:T(8,128)(2,1)} %get-tuple-element.37), calls=%async_computation.3 | async-start | bytes 1048576 | tf_op jit(solution)/shard_map/all_to_all | solution.py:166
  69.0 8.9 %copy-start.3 = (bf16[4,128,512]{2,1,0:T(8,128)(2,1)S(1)}, bf16[4,128,512]{2,1,0:T(8,128)(2,1)}, u32[]{:S(2)}) copy-start(bf16[4,128,512]{2,1,0:T(8,128)(2,1)} %copy-done.2) | copy-start | bytes 1572868
  78.3 3.9 %copy-start.7 = (bf16[4,128,512]{2,1,0:T(8,128)(2,1)S(1)}, bf16[4,128,512]{2,1,0:T(8,128)(2,1)}, u32[]{:S(2)}) copy-start(bf16[4,128,512]{2,1,0:T(8,128)(2,1)} %copy-done.6) | copy-start | bytes 1572868
  78.3 3.9 %collective-permute-start.4 = (bf16[512,512]{1,0:T(8,128)(2,1)S(1)}, bf16[512,512]{1,0:T(8,128)(2,1)S(1)}, u32[]{:S(2)}, u32[]{:S(2)}) collective-permute-start(bf16[512,512]{1,0:T(8,128)(2,1)S(1)} %convolution_convert_fusion), channel_id=1, source_target_pairs={{0,16},{16,0},{1,17},{17,1},{2,18},{18,2},{3,19},{19,3},{4,20},{20... | collective-permute-start | bytes 1572872 | tf_op jit(solution)/shard_map/ppermute | solution.py:157
  83.5 15.3 %all-to-all-start.4 = ((bf16[4,128,512]{2,1,0:T(8,128)(2,1)}), bf16[4,128,512]{2,1,0:T(8,128)(2,1)S(1)}, u32[]{:S(2)}, u32[]{:S(2)}) async-start(bf16[4,128,512]{2,1,0:T(8,128)(2,1)} %bitcast.12), calls=%async_computation.4 | async-start | bytes 1048576 | tf_op jit(solution)/shard_map/all_to_all | solution.py:166
  88.4 22.6 %collective-permute-start.5 = (bf16[128,1024]{1,0:T(8,128)(2,1)S(1)}, bf16[128,1024]{1,0:T(8,128)(2,1)S(1)}, u32[]{:S(2)}, u32[]{:S(2)}) collective-permute-start(bf16[128,1024]{1,0:T(8,128)(2,1)S(1)} %get-tuple-element.45), channel_id=1, source_target_pairs={{0,1},{1,0},{2,3},{3,2},{4,5},{5,4},{6,7},{7,6},{8,9},{9,8},{10,11... | collective-permute-start | bytes 786440 | tf_op jit(solution)/shard_map/ppermute | solution.py:161
  90.9 20.2 %collective-permute-start.6 = (bf16[128,1024]{1,0:T(8,128)(2,1)S(1)}, bf16[128,1024]{1,0:T(8,128)(2,1)S(1)}, u32[]{:S(2)}, u32[]{:S(2)}) collective-permute-start(bf16[128,1024]{1,0:T(8,128)(2,1)S(1)} %get-tuple-element.46), channel_id=1, source_target_pairs={{0,2},{1,3},{2,0},{3,1},{4,6},{5,7},{6,4},{7,5},{8,10},{9,11},{10,... | collective-permute-start | bytes 786440 | tf_op jit(solution)/shard_map/ppermute | solution.py:161
  94.9 16.2 %collective-permute-start.7 = (bf16[128,1024]{1,0:T(8,128)(2,1)S(1)}, bf16[128,1024]{1,0:T(8,128)(2,1)S(1)}, u32[]{:S(2)}, u32[]{:S(2)}) collective-permute-start(bf16[128,1024]{1,0:T(8,128)(2,1)S(1)} %get-tuple-element.47), channel_id=1, source_target_pairs={{0,3},{1,2},{2,1},{3,0},{4,7},{5,6},{6,5},{7,4},{8,11},{9,10},{10,... | collective-permute-start | bytes 786440 | tf_op jit(solution)/shard_map/ppermute | solution.py:161
  99.6 11.5 %copy-start.12 = (bf16[128,1024]{1,0:T(8,128)(2,1)S(1)}, bf16[128,1024]{1,0:T(8,128)(2,1)}, u32[]{:S(2)}) copy-start(bf16[128,1024]{1,0:T(8,128)(2,1)} %copy-done.11) | copy-start | bytes 786436
  99.6 25.2 %all-to-all-start.5 = ((bf16[16,8,512]{2,1,0:T(8,128)(2,1)}), bf16[16,8,512]{2,1,0:T(8,128)(2,1)S(1)}, u32[]{:S(2)}, u32[]{:S(2)}) async-start(bf16[16,8,512]{2,1,0:T(8,128)(2,1)} %shard_map.119), calls=%async_computation.5 | async-start | bytes 262144 | tf_op jit(solution)/shard_map/all_to_all | solution.py:166
  112.7 12.1 %copy-start.10 = (f32[8,512]{1,0:T(8,128)S(1)}, f32[8,512]{1,0:T(8,128)}, u32[]{:S(2)}) copy-start(f32[8,512]{1,0:T(8,128)} %rows_ref.1) | copy-start | bytes 49156
  112.7 12.1 %copy-start.13 = (f32[8,512]{1,0:T(8,128)S(1)}, f32[8,512]{1,0:T(8,128)}, u32[]{:S(2)}) copy-start(f32[8,512]{1,0:T(8,128)} %param.12) | copy-start | bytes 49156
  112.7 12.1 %copy-start.14 = (f32[8,512]{1,0:T(8,128)S(1)}, f32[8,512]{1,0:T(8,128)}, u32[]{:S(2)}) copy-start(f32[8,512]{1,0:T(8,128)} %param.13) | copy-start | bytes 49156
  (6 other events, 8.0 us)

commit v4 on v3

--- a/solution.py
+++ b/solution.py
@@ -83,10 +83,47 @@
         out_refs[d][...] = rows_ref[at_ref[0] ^ d]
 
 
-def join_kernel(at_ref, *refs):
-    for d in range(RING):
+def join_kernel(steps, at_ref, *refs):
+    out_ref, sem_ref = refs[-2], refs[-1]
+    copies = []
+    for i, d in enumerate(steps):
         for zh in range(4):
-            refs[RING][:, columns_of(at_ref[0] ^ d, zh)] = refs[d][:, zh * 256 : (zh + 1) * 256]
+            copies.append(
+                pltpu.make_async_copy(
+                    refs[i].at[:, zh * 256 : (zh + 1) * 256],
+                    out_ref.at[:, columns_of(at_ref[0] ^ d, zh)],
+                    sem_ref.at[i * 4 + zh],
+                )
+            )
+    for copy in copies:
+        copy.start()
+    for copy in copies:
+        copy.wait()
+
+
+def join(steps, at, blocks, shape, flops, into=()):
+    def kernel(at_ref, *refs):
+        join_kernel(steps, at_ref, *refs[: len(steps)], refs[-2], refs[-1])
+
+    return pl.pallas_call(
+        kernel,
+        out_shape=shape,
+        in_specs=[SMEM] + [VMEM] * len(steps) + [ANY] * len(into),
+        out_specs=ANY,
+        scratch_shapes=[pltpu.SemaphoreType.DMA((4 * len(steps),))],
+        input_output_aliases={1 + len(steps): 0} if into else {},
+        compiler_params=pltpu.CompilerParams(vmem_limit_bytes=24 * 1024 * 1024),
+        cost_estimate=pl.CostEstimate(flops=flops, bytes_accessed=1 << 20, transcendentals=0),
+    )(at, *blocks, *into)
+
+
+def values_kernel(own_ref, other_ref, weight_ref, weight_other_ref, out_ref):
+    tok = out_ref.shape[1]
+    for y in range(RING):
+        rows = slice(y * tok, (y + 1) * tok)
+        total = jnp.dot(own_ref[rows], weight_ref[...], preferred_element_type=F32)
+        total = total + jnp.dot(other_ref[rows], weight_other_ref[...], preferred_element_type=F32)
+        out_ref[y] = total.astype(BF16)
 
 
 def sum_kernel(parts_ref, out_ref):
@@ -139,6 +176,7 @@
 
 SMEM = pl.BlockSpec(memory_space=pltpu.SMEM)
 VMEM = pl.BlockSpec(memory_space=pltpu.VMEM)
+ANY = pl.BlockSpec(memory_space=pl.ANY)
 
 
 def call(kernel, out_shape, flops, nbytes, *args, scratch=()):
@@ -157,9 +195,8 @@
     return lax.ppermute(array, "c", [(0, 1), (1, 0)])
 
 
-def along_y(blocks):
-    moved = [lax.ppermute(blocks[d], "y", [(i, i ^ d) for i in range(RING)]) for d in range(1, RING)]
-    return [blocks[0]] + moved
+def along_y(block, d):
+    return lax.ppermute(block, "y", [(i, i ^ d) for i in range(RING)])
 
 
 def exchange(blocks, axes):
@@ -179,7 +216,8 @@
     weight = call(spread_kernel, jax.ShapeDtypeStruct((16, rows, kv), BF16), 0, 1 << 17, master)
     weight = exchange(weight, DEPTH).reshape(16 * rows, kv)
 
-    dealt = along_y(call(deal_kernel, (block,) * RING, 0, 2 << 20, at, hidden_in))
+    dealt = call(deal_kernel, (block,) * RING, 0, 2 << 20, at, hidden_in)
+    dealt = [dealt[0]] + [along_y(dealt[d], d) for d in range(1, RING)]
     hidden_own, hidden_other = call(
         collect_kernel, (half, half), WEIGHTY, 3 << 20, at, *dealt, scratch=[matrix]
     )
@@ -204,9 +242,17 @@
         seg[:, None],
     )
 
-    partial = jnp.dot(hidden_own, weight, preferred_element_type=F32)
-    partial = partial + jnp.dot(hidden_other, weight_other, preferred_element_type=F32)
-    partial = exchange(partial.astype(BF16).reshape(RING, tok, kv), "y")
+    partial = call(
+        values_kernel,
+        jax.ShapeDtypeStruct((RING, tok, kv), BF16),
+        2 * RING * tok * feats * kv,
+        3 << 20,
+        hidden_own,
+        hidden_other,
+        weight,
+        weight_other,
+    )
+    partial = exchange(partial, "y")
     attended, grad = call(
         attend_kernel,
         (jax.ShapeDtypeStruct((tok, QH * HD), BF16), jax.ShapeDtypeStruct((RING, tok, kv), BF16)),
@@ -239,14 +285,15 @@
         scratch=[pltpu.VMEM((RING, tok, feats), BF16)],
     )
     part, dealt = lax.optimization_barrier((part, dealt))
-    dealt = along_y(dealt)
-    grad_hidden = call(
-        join_kernel, jax.ShapeDtypeStruct((tok, width), BF16), WEIGHTY, 2 << 20, at, *dealt
-    )
+    near = [dealt[0], along_y(dealt[2], 2), along_y(dealt[1], 1)]
+    whole = jax.ShapeDtypeStruct((tok, width), BF16)
+    grad_hidden = join((0, 2, 1), at, near, whole, WEIGHTY)
 
     part = exchange(part, "x")
     part = call(sum_kernel, jax.ShapeDtypeStruct((16, rows, kv), BF16), 0, 1 << 20, part)
+    part, last = lax.optimization_barrier((part, dealt[3]))
     part = exchange(part, DEPTH)
+    grad_hidden = join((3,), at, [along_y(last, 3)], whole, 0, [grad_hidden])
     gradient = jnp.sum(part.astype(F32), axis=0) / F32(tok * 512)
 
     moment_new = beta_one * moment + (1.0 - beta_one) * gradient

time: 126 us -> 126 us (level)
  the two profiles are of different devices: /device:TPU:2 before, /device:TPU:32 now
where the time goes in v4:
time: 126 us
  starting transfers between devices  65.5 us (52%)
  waiting for transfers between devices  35.9 us (28%)
  Pallas kernels  16.9 us (13%)
  local copies, waits for them, and re-layouts  3.57 us (3%)
  matrix products  1.73 us (1%)
    all_to_all x6, starting transfers between devices, exchange(): return lax.all_to_all(blocks, axes, split_axis=0, concat_axis=0, tiled=True)  42.2 us
    all_to_all x6, waiting for transfers between devices, exchange(): return lax.all_to_all(blocks, axes, split_axis=0, concat_axis=0, tiled=True)  23.7 us
    ppermute x6, starting transfers between devices, along_y(): return lax.ppermute(block, 'y', [(i, i ^ d) for i in range(RING)])  19.3 us
    pallas_call x10, Pallas kernels, call(): pl.pallas_call(kernel, out_shape=out_shape, in_specs=specs, scratch_shape...  14.2 us
    ppermute x6, waiting for transfers between devices, along_y(): return lax.ppermute(block, 'y', [(i, i ^ d) for i in range(RING)])  9.85 us
    ppermute x2, starting transfers between devices, swap_core(): return lax.ppermute(array, 'c', [(0, 1), (1, 0)])  3.96 us
    unnamed x32, local copies, waits for them, and re-layouts  3.45 us
    pallas_call x2, Pallas kernels, join(): pl.pallas_call(kernel, out_shape=shape, in_specs=[SMEM] + [VMEM] * len(st...  2.79 us
  transfers between devices with their start and end apart: 14, of which 10 were waited for; matrix products, arithmetic and copies ran while one was open for 0% of the time, Pallas kernels for 10%

profile of v4, /device:TPU:32, one launch (start us, length us, event | category | flops | bytes accessed | tf_op | source)
XLA Modules:
  0.0 125.6 jit_solution(7948381341409297891)
XLA Ops:
  2.0 15.2 %all-to-all-start = ((bf16[16,8,512]{2,1,0:T(8,128)(2,1)}), bf16[16,8,512]{2,1,0:T(8,128)(2,1)S(1)}, u32[]{:S(2)}, u32[]{:S(2)}) async-start(bf16[16,8,512]{2,1,0:T(8,128)(2,1)} %shard_map.110), calls=%async_computation | async-start | bytes 262144 | tf_op jit(solution)/shard_map/all_to_all | solution.py:203
  19.2 3.5 %collective-permute-start = (bf16[128,1024]{1,0:T(8,128)(2,1)S(1)}, bf16[128,1024]{1,0:T(8,128)(2,1)S(1)}, u32[]{:S(2)}, u32[]{:S(2)}) collective-permute-start(bf16[128,1024]{1,0:T(8,128)(2,1)S(1)} %get-tuple-element.30), channel_id=1, source_target_pairs={{0,1},{1,0},{2,3},{3,2},{4,5},{5,4},{6,7},{7,6},{8,9},{9,8},{10,11... | collective-permute-start | bytes 786440 | tf_op jit(solution)/shard_map/ppermute | solution.py:199
  22.7 4.8 %collective-permute-start.1 = (bf16[128,1024]{1,0:T(8,128)(2,1)S(1)}, bf16[128,1024]{1,0:T(8,128)(2,1)S(1)}, u32[]{:S(2)}, u32[]{:S(2)}) collective-permute-start(bf16[128,1024]{1,0:T(8,128)(2,1)S(1)} %get-tuple-element.31), channel_id=1, source_target_pairs={{0,2},{1,3},{2,0},{3,1},{4,6},{5,7},{6,4},{7,5},{8,10},{9,11},{10,... | collective-permute-start | bytes 786440 | tf_op jit(solution)/shard_map/ppermute | solution.py:199
  27.5 2.1 %collective-permute-start.2 = (bf16[128,1024]{1,0:T(8,128)(2,1)S(1)}, bf16[128,1024]{1,0:T(8,128)(2,1)S(1)}, u32[]{:S(2)}, u32[]{:S(2)}) collective-permute-start(bf16[128,1024]{1,0:T(8,128)(2,1)S(1)} %get-tuple-element.32), channel_id=1, source_target_pairs={{0,3},{1,2},{2,1},{3,0},{4,7},{5,6},{6,5},{7,4},{8,11},{9,10},{10,... | collective-permute-start | bytes 786440 | tf_op jit(solution)/shard_map/ppermute | solution.py:199
  29.7 2.3 %all-to-all-done = bf16[16,8,512]{2,1,0:T(8,128)(2,1)S(1)} async-done(((bf16[16,8,512]{2,1,0:T(8,128)(2,1)}), bf16[16,8,512]{2,1,0:T(8,128)(2,1)S(1)}, u32[]{:S(2)}, u32[]{:S(2)}) %all-to-all-start) | async-done | bytes 131104 | tf_op jit(solution)/shard_map/all_to_all | solution.py:203
  32.8 4.3 %all-to-all-start.1 = ((bf16[4,128,512]{2,1,0:T(8,128)(2,1)}), bf16[4,128,512]{2,1,0:T(8,128)(2,1)S(1)}, u32[]{:S(2)}, u32[]{:S(2)}) async-start(bf16[4,128,512]{2,1,0:T(8,128)(2,1)} %shard_map.111), calls=%async_computation.1 | async-start | bytes 1048576 | tf_op jit(solution)/shard_map/all_to_all | solution.py:203
  37.1 4.7 %collective-permute-done.2.refs_3_ = bf16[128,1024]{1,0:T(8,128)(2,1)S(1)} collective-permute-done((bf16[128,1024]{1,0:T(8,128)(2,1)S(1)}, bf16[128,1024]{1,0:T(8,128)(2,1)S(1)}, u32[]{:S(2)}, u32[]{:S(2)}) %collective-permute-start.2) | collective-permute-done | bytes 262176 | tf_op jit(solution)/shard_map/ppermute | solution.py:199
  41.9 2.0 %shard_map.113 = (bf16[4,128,512]{2,1,0:T(8,128)(2,1)S(1)}, bf16[4,128,512]{2,1,0:T(8,128)(2,1)S(1)}) custom-call(s32[2]{0:T(128)S(1)} %pad_add_fusion.at_ref, bf16[128,1024]{1,0:T(8,128)(2,1)S(1)} %get-tuple-element.29.refs_0_, bf16[128,1024]{1,0:T(8,128)(2,1)S(1)} %collective-permute-done.refs_1_, bf16[128,1024]{1,0:T(8,128)(2,1)S(1)} %collective-permute-done.1.refs_2_, ...), custom_call_target="tpu_custom_call" | custom-call | flops 34359738368 | bytes 3145728 | tf_op jit(solution)/shard_map/pallas_call | solution.py:184
  45.2 1.9 %collective-permute-start.3 = (bf16[512,512]{1,0:T(8,128)(2,1)S(1)}, bf16[512,512]{1,0:T(8,128)(2,1)S(1)}, u32[]{:S(2)}, u32[]{:S(2)}) collective-permute-start(bf16[512,512]{1,0:T(8,128)(2,1)S(1)} %bitcast.16), channel_id=1, source_target_pairs={{0,16},{16,0},{1,17},{17,1},{2,18},{18,2},{3,19},{19,3},{4,20},{20... | collective-permute-start | bytes 1572872 | tf_op jit(solution)/shard_map/ppermute | solution.py:195
  47.1 1.9 %collective-permute-done.3.weight_other_ref.other_ref = bf16[512,512]{1,0:T(8,128)(2,1)S(1)} collective-permute-done((bf16[512,512]{1,0:T(8,128)(2,1)S(1)}, bf16[512,512]{1,0:T(8,128)(2,1)S(1)}, u32[]{:S(2)}, u32[]{:S(2)}) %collective-permute-start.3) | collective-permute-done | bytes 524320 | tf_op jit(solution)/shard_map/ppermute | solution.py:195
  51.3 4.6 %all-to-all-start.2 = ((bf16[4,128,512]{2,1,0:T(8,128)(2,1)}), bf16[4,128,512]{2,1,0:T(8,128)(2,1)S(1)}, u32[]{:S(2)}, u32[]{:S(2)}) async-start(bf16[4,128,512]{2,1,0:T(8,128)(2,1)} %shard_map.114), calls=%async_computation.2 | async-start | bytes 1048576 | tf_op jit(solution)/shard_map/all_to_all | solution.py:203
  57.0 2.8 %shard_map.115.probs_ref = bf16[4,1024,128]{2,1,0:T(8,128)(2,1)S(1)} custom-call(bf16[128,4096]{1,0:T(8,128)(2,1)S(1)} %copy-done, bf16[128,512]{1,0:T(8,128)(2,1)S(1)} %copy-done.8, s32[1,128]{1,0:T(1,128)S(1)} %bitcast.28, s32[128,1]{1,0:T(8,128)S(1)} %copy.14.seg_col_ref), custom_call_target="tpu_custom_call" | custom-call | flops 268435456 | bytes 8388608 | tf_op jit(solution)/shard_map/pallas_call | solution.py:184
  59.8 5.9 %all-to-all-done.2.partial_ref = bf16[4,128,512]{2,1,0:T(8,128)(2,1)S(1)} async-done(((bf16[4,128,512]{2,1,0:T(8,128)(2,1)}), bf16[4,128,512]{2,1,0:T(8,128)(2,1)S(1)}, u32[]{:S(2)}, u32[]{:S(2)}) %all-to-all-start.2) | async-done | bytes 524320 | tf_op jit(solution)/shard_map/all_to_all | solution.py:203
  67.5 3.6 %all-to-all-start.3 = ((bf16[4,128,512]{2,1,0:T(8,128)(2,1)}), bf16[4,128,512]{2,1,0:T(8,128)(2,1)S(1)}, u32[]{:S(2)}, u32[]{:S(2)}) async-start(bf16[4,128,512]{2,1,0:T(8,128)(2,1)} %get-tuple-element.39), calls=%async_computation.3 | async-start | bytes 1048576 | tf_op jit(solution)/shard_map/all_to_all | solution.py:203
  73.0 7.0 %all-to-all-done.3 = bf16[4,128,512]{2,1,0:T(8,128)(2,1)S(1)} async-done(((bf16[4,128,512]{2,1,0:T(8,128)(2,1)}), bf16[4,128,512]{2,1,0:T(8,128)(2,1)S(1)}, u32[]{:S(2)}, u32[]{:S(2)}) %all-to-all-start.3) | async-done | bytes 524320 | tf_op jit(solution)/shard_map/all_to_all | solution.py:203
  80.5 2.1 %collective-permute-start.4 = (bf16[512,512]{1,0:T(8,128)(2,1)S(1)}, bf16[512,512]{1,0:T(8,128)(2,1)S(1)}, u32[]{:S(2)}, u32[]{:S(2)}) collective-permute-start(bf16[512,512]{1,0:T(8,128)(2,1)S(1)} %convolution_convert_fusion), channel_id=1, source_target_pairs={{0,16},{16,0},{1,17},{17,1},{2,18},{18,2},{3,19},{19,3},{4,20},{20... | collective-permute-start | bytes 1572872 | tf_op jit(solution)/shard_map/ppermute | solution.py:195
  85.7 3.5 %all-to-all-start.4 = ((bf16[4,128,512]{2,1,0:T(8,128)(2,1)}), bf16[4,128,512]{2,1,0:T(8,128)(2,1)S(1)}, u32[]{:S(2)}, u32[]{:S(2)}) async-start(bf16[4,128,512]{2,1,0:T(8,128)(2,1)} %bitcast.11), calls=%async_computation.4 | async-start | bytes 1048576 | tf_op jit(solution)/shard_map/all_to_all | solution.py:203
  89.2 2.5 %collective-permute-start.6 = (bf16[128,1024]{1,0:T(8,128)(2,1)S(1)}, bf16[128,1024]{1,0:T(8,128)(2,1)S(1)}, u32[]{:S(2)}, u32[]{:S(2)}) collective-permute-start(bf16[128,1024]{1,0:T(8,128)(2,1)S(1)} %get-tuple-element.50), channel_id=1, source_target_pairs={{0,2},{1,3},{2,0},{3,1},{4,6},{5,7},{6,4},{7,5},{8,10},{9,11},{10,... | collective-permute-start | bytes 786440 | tf_op jit(solution)/shard_map/ppermute | solution.py:199
  91.7 3.4 %collective-permute-start.7 = (bf16[128,1024]{1,0:T(8,128)(2,1)S(1)}, bf16[128,1024]{1,0:T(8,128)(2,1)S(1)}, u32[]{:S(2)}, u32[]{:S(2)}) collective-permute-start(bf16[128,1024]{1,0:T(8,128)(2,1)S(1)} %get-tuple-element.51), channel_id=1, source_target_pairs={{0,1},{1,0},{2,3},{3,2},{4,5},{5,4},{6,7},{7,6},{8,9},{9,8},{10,11... | collective-permute-start | bytes 786440 | tf_op jit(solution)/shard_map/ppermute | solution.py:199
  95.0 4.2 %all-to-all-done.4.parts_ref = bf16[4,128,512]{2,1,0:T(8,128)(2,1)S(1)} async-done(((bf16[4,128,512]{2,1,0:T(8,128)(2,1)}), bf16[4,128,512]{2,1,0:T(8,128)(2,1)S(1)}, u32[]{:S(2)}, u32[]{:S(2)}) %all-to-all-start.4) | async-done | bytes 524320 | tf_op jit(solution)/shard_map/all_to_all | solution.py:203
  99.9 11.0 %all-to-all-start.5 = ((bf16[16,8,512]{2,1,0:T(8,128)(2,1)}), bf16[16,8,512]{2,1,0:T(8,128)(2,1)S(1)}, u32[]{:S(2)}, u32[]{:S(2)}) async-start(bf16[16,8,512]{2,1,0:T(8,128)(2,1)} %shard_map.119), calls=%async_computation.5 | async-start | bytes 262144 | tf_op jit(solution)/shard_map/all_to_all | solution.py:203
  110.9 3.1 %collective-permute-start.5 = (bf16[128,1024]{1,0:T(8,128)(2,1)S(1)}, bf16[128,1024]{1,0:T(8,128)(2,1)S(1)}, u32[]{:S(2)}, u32[]{:S(2)}) collective-permute-start(bf16[128,1024]{1,0:T(8,128)(2,1)S(1)} %get-tuple-element.48), channel_id=1, source_target_pairs={{0,3},{1,2},{2,1},{3,0},{4,7},{5,6},{6,5},{7,4},{8,11},{9,10},{10,... | collective-permute-start | bytes 786440 | tf_op jit(solution)/shard_map/ppermute | solution.py:199
  115.5 5.1 %collective-permute-done.5.refs_0_ = bf16[128,1024]{1,0:T(8,128)(2,1)S(1)} collective-permute-done((bf16[128,1024]{1,0:T(8,128)(2,1)S(1)}, bf16[128,1024]{1,0:T(8,128)(2,1)S(1)}, u32[]{:S(2)}, u32[]{:S(2)}) %collective-permute-start.5) | collective-permute-done | bytes 262176 | tf_op jit(solution)/shard_map/ppermute | solution.py:199
  122.0 2.9 %all-to-all-done.5 = bf16[16,8,512]{2,1,0:T(8,128)(2,1)S(1)} async-done(((bf16[16,8,512]{2,1,0:T(8,128)(2,1)}), bf16[16,8,512]{2,1,0:T(8,128)(2,1)S(1)}, u32[]{:S(2)}, u32[]{:S(2)}) %all-to-all-start.5) | async-done | bytes 131104 | tf_op jit(solution)/shard_map/all_to_all | solution.py:203
  (56 shorter events, 20.4 us)
Async XLA Ops:
  2.0 30.0 %all-to-all-start = ((bf16[16,8,512]{2,1,0:T(8,128)(2,1)}), bf16[16,8,512]{2,1,0:T(8,128)(2,1)S(1)}, u32[]{:S(2)}, u32[]{:S(2)}) async-start(bf16[16,8,512]{2,1,0:T(8,128)(2,1)} %shard_map.110), calls=%async_computation | async-start | bytes 262144 | tf_op jit(solution)/shard_map/all_to_all | solution.py:203
  19.2 17.9 %collective-permute-start = (bf16[128,1024]{1,0:T(8,128)(2,1)S(1)}, bf16[128,1024]{1,0:T(8,128)(2,1)S(1)}, u32[]{:S(2)}, u32[]{:S(2)}) collective-permute-start(bf16[128,1024]{1,0:T(8,128)(2,1)S(1)} %get-tuple-element.30), channel_id=1, source_target_pairs={{0,1},{1,0},{2,3},{3,2},{4,5},{5,4},{6,7},{7,6},{8,9},{9,8},{10,11... | collective-permute-start | bytes 786440 | tf_op jit(solution)/shard_map/ppermute | solution.py:199
  22.7 14.4 %collective-permute-start.1 = (bf16[128,1024]{1,0:T(8,128)(2,1)S(1)}, bf16[128,1024]{1,0:T(8,128)(2,1)S(1)}, u32[]{:S(2)}, u32[]{:S(2)}) collective-permute-start(bf16[128,1024]{1,0:T(8,128)(2,1)S(1)} %get-tuple-element.31), channel_id=1, source_target_pairs={{0,2},{1,3},{2,0},{3,1},{4,6},{5,7},{6,4},{7,5},{8,10},{9,11},{10,... | collective-permute-start | bytes 786440 | tf_op jit(solution)/shard_map/ppermute | solution.py:199
  27.5 14.3 %collective-permute-start.2 = (bf16[128,1024]{1,0:T(8,128)(2,1)S(1)}, bf16[128,1024]{1,0:T(8,128)(2,1)S(1)}, u32[]{:S(2)}, u32[]{:S(2)}) collective-permute-start(bf16[128,1024]{1,0:T(8,128)(2,1)S(1)} %get-tuple-element.32), channel_id=1, source_target_pairs={{0,3},{1,2},{2,1},{3,0},{4,7},{5,6},{6,5},{7,4},{8,11},{9,10},{10,... | collective-permute-start | bytes 786440 | tf_op jit(solution)/shard_map/ppermute | solution.py:199
  32.8 12.4 %all-to-all-start.1 = ((bf16[4,128,512]{2,1,0:T(8,128)(2,1)}), bf16[4,128,512]{2,1,0:T(8,128)(2,1)S(1)}, u32[]{:S(2)}, u32[]{:S(2)}) async-start(bf16[4,128,512]{2,1,0:T(8,128)(2,1)} %shard_map.111), calls=%async_computation.1 | async-start | bytes 1048576 | tf_op jit(solution)/shard_map/all_to_all | solution.py:203
  43.8 6.7 %copy-start.2 = (bf16[4,128,512]{2,1,0:T(8,128)(2,1)}, bf16[4,128,512]{2,1,0:T(8,128)(2,1)S(1)}, u32[]{:S(2)}) copy-start(bf16[4,128,512]{2,1,0:T(8,128)(2,1)S(1)} %get-tuple-element.35) | copy-start | bytes 1572868
  43.9 6.7 %copy-start.4 = (bf16[4,128,512]{2,1,0:T(8,128)(2,1)}, bf16[4,128,512]{2,1,0:T(8,128)(2,1)S(1)}, u32[]{:S(2)}) copy-start(bf16[4,128,512]{2,1,0:T(8,128)(2,1)S(1)} %get-tuple-element.36) | copy-start | bytes 1572868
  45.2 3.8 %collective-permute-start.3 = (bf16[512,512]{1,0:T(8,128)(2,1)S(1)}, bf16[512,512]{1,0:T(8,128)(2,1)S(1)}, u32[]{:S(2)}, u32[]{:S(2)}) collective-permute-start(bf16[512,512]{1,0:T(8,128)(2,1)S(1)} %bitcast.16), channel_id=1, source_target_pairs={{0,16},{16,0},{1,17},{17,1},{2,18},{18,2},{3,19},{19,3},{4,20},{20... | collective-permute-start | bytes 1572872 | tf_op jit(solution)/shard_map/ppermute | solution.py:195
  49.0 8.0 %copy-start.8 = (bf16[128,512]{1,0:T(8,128)(2,1)S(1)}, bf16[128,512]{1,0:T(8,128)(2,1)}, u32[]{:S(2)}) copy-start(bf16[128,512]{1,0:T(8,128)(2,1)} %keys_ref.1) | copy-start | bytes 393220
  51.3 5.6 %copy-start = (bf16[128,4096]{1,0:T(8,128)(2,1)S(1)}, bf16[128,4096]{1,0:T(8,128)(2,1)}, u32[]{:S(2)}) copy-start(bf16[128,4096]{1,0:T(8,128)(2,1)} %queries_ref.1) | copy-start | bytes 3145732
  51.3 14.4 %all-to-all-start.2 = ((bf16[4,128,512]{2,1,0:T(8,128)(2,1)}), bf16[4,128,512]{2,1,0:T(8,128)(2,1)S(1)}, u32[]{:S(2)}, u32[]{:S(2)}) async-start(bf16[4,128,512]{2,1,0:T(8,128)(2,1)} %shard_map.114), calls=%async_computation.2 | async-start | bytes 1048576 | tf_op jit(solution)/shard_map/all_to_all | solution.py:203
  67.5 3.6 %copy-start.7 = (bf16[512,512]{1,0:T(8,128)(2,1)S(1)}, bf16[512,512]{1,0:T(8,128)(2,1)}, u32[]{:S(2)}) copy-start(bf16[512,512]{1,0:T(8,128)(2,1)} %copy-done.6) | copy-start | bytes 1572868
  67.5 12.5 %all-to-all-start.3 = ((bf16[4,128,512]{2,1,0:T(8,128)(2,1)}), bf16[4,128,512]{2,1,0:T(8,128)(2,1)S(1)}, u32[]{:S(2)}, u32[]{:S(2)}) async-start(bf16[4,128,512]{2,1,0:T(8,128)(2,1)} %get-tuple-element.39), calls=%async_computation.3 | async-start | bytes 1048576 | tf_op jit(solution)/shard_map/all_to_all | solution.py:203
  71.2 8.9 %copy-start.5 = (bf16[4,128,512]{2,1,0:T(8,128)(2,1)S(1)}, bf16[4,128,512]{2,1,0:T(8,128)(2,1)}, u32[]{:S(2)}) copy-start(bf16[4,128,512]{2,1,0:T(8,128)(2,1)} %copy-done.4) | copy-start | bytes 1572868
  80.5 3.9 %copy-start.3 = (bf16[4,128,512]{2,1,0:T(8,128)(2,1)S(1)}, bf16[4,128,512]{2,1,0:T(8,128)(2,1)}, u32[]{:S(2)}) copy-start(bf16[4,128,512]{2,1,0:T(8,128)(2,1)} %copy-done.2) | copy-start | bytes 1572868
  80.5 3.9 %collective-permute-start.4 = (bf16[512,512]{1,0:T(8,128)(2,1)S(1)}, bf16[512,512]{1,0:T(8,128)(2,1)S(1)}, u32[]{:S(2)}, u32[]{:S(2)}) collective-permute-start(bf16[512,512]{1,0:T(8,128)(2,1)S(1)} %convolution_convert_fusion), channel_id=1, source_target_pairs={{0,16},{16,0},{1,17},{17,1},{2,18},{18,2},{3,19},{19,3},{4,20},{20... | collective-permute-start | bytes 1572872 | tf_op jit(solution)/shard_map/ppermute | solution.py:195
  85.7 13.5 %all-to-all-start.4 = ((bf16[4,128,512]{2,1,0:T(8,128)(2,1)}), bf16[4,128,512]{2,1,0:T(8,128)(2,1)S(1)}, u32[]{:S(2)}, u32[]{:S(2)}) async-start(bf16[4,128,512]{2,1,0:T(8,128)(2,1)} %bitcast.11), calls=%async_computation.4 | async-start | bytes 1048576 | tf_op jit(solution)/shard_map/all_to_all | solution.py:203
  89.2 24.8 %collective-permute-start.6 = (bf16[128,1024]{1,0:T(8,128)(2,1)S(1)}, bf16[128,1024]{1,0:T(8,128)(2,1)S(1)}, u32[]{:S(2)}, u32[]{:S(2)}) collective-permute-start(bf16[128,1024]{1,0:T(8,128)(2,1)S(1)} %get-tuple-element.50), channel_id=1, source_target_pairs={{0,2},{1,3},{2,0},{3,1},{4,6},{5,7},{6,4},{7,5},{8,10},{9,11},{10,... | collective-permute-start | bytes 786440 | tf_op jit(solution)/shard_map/ppermute | solution.py:199
  91.7 22.3 %collective-permute-start.7 = (bf16[128,1024]{1,0:T(8,128)(2,1)S(1)}, bf16[128,1024]{1,0:T(8,128)(2,1)S(1)}, u32[]{:S(2)}, u32[]{:S(2)}) collective-permute-start(bf16[128,1024]{1,0:T(8,128)(2,1)S(1)} %get-tuple-element.51), channel_id=1, source_target_pairs={{0,1},{1,0},{2,3},{3,2},{4,5},{5,4},{6,7},{7,6},{8,9},{9,8},{10,11... | collective-permute-start | bytes 786440 | tf_op jit(solution)/shard_map/ppermute | solution.py:199
  99.9 14.1 %copy-start.12 = (bf16[128,1024]{1,0:T(8,128)(2,1)S(1)}, bf16[128,1024]{1,0:T(8,128)(2,1)}, u32[]{:S(2)}) copy-start(bf16[128,1024]{1,0:T(8,128)(2,1)} %copy-done.11) | copy-start | bytes 786436
  99.9 24.9 %all-to-all-start.5 = ((bf16[16,8,512]{2,1,0:T(8,128)(2,1)}), bf16[16,8,512]{2,1,0:T(8,128)(2,1)S(1)}, u32[]{:S(2)}, u32[]{:S(2)}) async-start(bf16[16,8,512]{2,1,0:T(8,128)(2,1)} %shard_map.119), calls=%async_computation.5 | async-start | bytes 262144 | tf_op jit(solution)/shard_map/all_to_all | solution.py:203
  110.9 9.7 %collective-permute-start.5 = (bf16[128,1024]{1,0:T(8,128)(2,1)S(1)}, bf16[128,1024]{1,0:T(8,128)(2,1)S(1)}, u32[]{:S(2)}, u32[]{:S(2)}) collective-permute-start(bf16[128,1024]{1,0:T(8,128)(2,1)S(1)} %get-tuple-element.48), channel_id=1, source_target_pairs={{0,3},{1,2},{2,1},{3,0},{4,7},{5,6},{6,5},{7,4},{8,11},{9,10},{10,... | collective-permute-start | bytes 786440 | tf_op jit(solution)/shard_map/ppermute | solution.py:199
  121.9 3.0 %copy-start.10 = (f32[8,512]{1,0:T(8,128)S(1)}, f32[8,512]{1,0:T(8,128)}, u32[]{:S(2)}) copy-start(f32[8,512]{1,0:T(8,128)} %rows_ref.1) | copy-start | bytes 49156
  122.0 2.9 %copy-start.13 = (f32[8,512]{1,0:T(8,128)S(1)}, f32[8,512]{1,0:T(8,128)}, u32[]{:S(2)}) copy-start(f32[8,512]{1,0:T(8,128)} %param.12) | copy-start | bytes 49156
  (6 other events, 8.2 us)

commit v5 on v3

--- a/solution.py
+++ b/solution.py
@@ -22,8 +22,10 @@
 SIZES = (4, 4, 2, 4, 4)
 TOK_SPEC = P(AXES, None)
 ROW_SPEC = P(("zh", "y", "zl", "x", "c"), None)
-DEPTH = ("zl", "zh")
+DEPTH = 16
 RING = 4
+GATHER_FIRST = 3
+REDUCE_FIRST = 6
 
 F32 = jnp.float32
 BF16 = jnp.bfloat16
@@ -31,7 +33,8 @@
 
 def order_matrix(core):
     to = lax.broadcasted_iota(jnp.int32, (1, 1024), 1)
-    source = ((to >> 3) & 3) * 256 + ((to >> 5) & 3) * 64 + ((to >> 7) & 3) * 16 + (to & 7)
+    z = ((to >> 3) & 15) ^ GATHER_FIRST
+    source = (z & 3) * 256 + (z >> 2) * 64 + ((to >> 7) & 3) * 16 + (to & 7)
     source = source + ((to >> 9) ^ core) * 8
     hit = lax.broadcasted_iota(jnp.int32, (1024, 1024), 0) == source
     return jnp.where(hit, F32(1), F32(0)).astype(BF16)
@@ -40,20 +43,43 @@
 WEIGHTY = 32 << 30
 
 
-def spread_kernel(rows_ref, *refs):
-    rows = rows_ref[...].astype(BF16)
-    for i in range(refs[-1].shape[0]):
-        refs[-1][i] = rows
+def run_copies(sem_ref, pairs):
+    copies = [pltpu.make_async_copy(a, b, sem_ref.at[i]) for i, (a, b) in enumerate(pairs)]
+    for copy in copies:
+        copy.start()
+    for copy in copies:
+        copy.wait()
+
+
+def master_kernel(master_ref, out_ref, rows_ref, sem_ref):
+    run_copies(sem_ref, [(master_ref, rows_ref)])
+    weight = rows_ref[...].astype(BF16)
+    for z in range(DEPTH):
+        out_ref[z] = weight
+
+
+def spread_kernel(rows_ref, out_ref, sem_ref):
+    run_copies(sem_ref, [(rows_ref, out_ref.at[i]) for i in range(RING)])
 
 
 def columns_of(y, zh):
     return pl.ds(pl.multiple_of(zh * 1024 + y * 256, 256), 256)
 
 
-def deal_kernel(at_ref, hidden_ref, *out_refs):
-    for d in range(RING):
-        for zh in range(4):
-            out_refs[d][:, zh * 256 : (zh + 1) * 256] = hidden_ref[:, columns_of(at_ref[0] ^ d, zh)]
+def block_columns(at_ref, blocks, whole_ref):
+    return [
+        (blocks[d].at[:, zh * 256 : (zh + 1) * 256], whole_ref.at[:, columns_of(at_ref[0] ^ d, zh)])
+        for d in range(RING)
+        for zh in range(4)
+    ]
+
+
+def deal_kernel(at_ref, hidden_ref, *refs):
+    run_copies(refs[RING], [(b, a) for a, b in block_columns(at_ref, refs[:RING], hidden_ref)])
+
+
+def join_kernel(at_ref, *refs):
+    run_copies(refs[RING + 1], block_columns(at_ref, refs[:RING], refs[RING]))
 
 
 def collect_kernel(at_ref, *refs):
@@ -83,10 +109,31 @@
         out_refs[d][...] = rows_ref[at_ref[0] ^ d]
 
 
-def join_kernel(at_ref, *refs):
-    for d in range(RING):
-        for zh in range(4):
-            refs[RING][:, columns_of(at_ref[0] ^ d, zh)] = refs[d][:, zh * 256 : (zh + 1) * 256]
+def values_kernel(own_ref, other_ref, weight_ref, weight_other_ref, out_ref, rows_ref, sem_ref):
+    tok = out_ref.shape[1]
+    copies = []
+    for y in range(RING):
+        rows = slice(y * tok, (y + 1) * tok)
+        total = jnp.dot(own_ref[rows], weight_ref[...], preferred_element_type=F32)
+        total = total + jnp.dot(other_ref[rows], weight_other_ref[...], preferred_element_type=F32)
+        rows_ref[y] = total.astype(BF16)
+        copies.append(pltpu.make_async_copy(rows_ref.at[y], out_ref.at[y], sem_ref.at[y]))
+        copies[-1].start()
+    for copy in copies:
+        copy.wait()
+
+
+def fold_kernel(own_ref, grad_ref, sent_ref, out_ref, rows_ref, sem_ref):
+    copies = []
+    step = out_ref.shape[1]
+    for x in range(RING):
+        at = slice(x * step, (x + 1) * step)
+        part = lax.dot_general(own_ref[:, at], grad_ref[...], (((0,), (0,)), ((), ())), preferred_element_type=F32)
+        rows_ref[x] = (part + sent_ref[at].astype(F32)).astype(BF16)
+        copies.append(pltpu.make_async_copy(rows_ref.at[x], out_ref.at[x], sem_ref.at[x]))
+        copies[-1].start()
+    for copy in copies:
+        copy.wait()
 
 
 def sum_kernel(parts_ref, out_ref):
@@ -96,7 +143,7 @@
     total = total.astype(BF16)
     rows = out_ref.shape[1]
     for z in range(out_ref.shape[0]):
-        out_ref[z] = total[z * rows : (z + 1) * rows]
+        out_ref[z ^ GATHER_FIRST ^ REDUCE_FIRST] = total[z * rows : (z + 1) * rows]
 
 
 def probs_kernel(queries_ref, keys_ref, seg_row_ref, seg_col_ref, out_ref):
@@ -118,35 +165,51 @@
             out_ref[j, h * tok : (h + 1) * tok, :] = (expos / total).astype(BF16)
 
 
-def attend_kernel(partial_ref, probs_ref, attended_ref, grad_ref):
+def attend_kernel(partial_ref, probs_ref, attended_ref, grad_ref, rows_ref, sum_ref, sem_ref):
     tok = partial_ref.shape[1]
+    wide = GROUPS * HD
+    copies = []
     for j in range(VH):
         cols = slice(j * HD, (j + 1) * HD)
         total = partial_ref[0, :, cols].astype(F32)
-        for x in range(1, 4):
-            total = total + partial_ref[x, :, cols].astype(F32)
+        for y in range(1, RING):
+            total = total + partial_ref[y, :, cols].astype(F32)
         value = total.astype(BF16)
         attended = jnp.dot(probs_ref[j], value, preferred_element_type=F32).astype(BF16)
-        grad = lax.dot_general(
+        for h in range(GROUPS):
+            rows_ref[j, :, h * HD : (h + 1) * HD] = attended[h * tok : (h + 1) * tok]
+        copies.append(
+            pltpu.make_async_copy(rows_ref.at[j], attended_ref.at[:, j * wide : (j + 1) * wide], sem_ref.at[j])
+        )
+        copies[-1].start()
+        sum_ref[:, cols] = lax.dot_general(
             probs_ref[j], attended, (((0,), (0,)), ((), ())), preferred_element_type=F32
         ).astype(BF16)
-        for h in range(GROUPS):
-            at = (j * GROUPS + h) * HD
-            attended_ref[:, at : at + HD] = attended[h * tok : (h + 1) * tok]
-        for x in range(4):
-            grad_ref[x, :, cols] = grad
+    for y in range(RING):
+        copies.append(pltpu.make_async_copy(sum_ref, grad_ref.at[y], sem_ref.at[VH + y]))
+        copies[-1].start()
+    for copy in copies:
+        copy.wait()
 
 
 SMEM = pl.BlockSpec(memory_space=pltpu.SMEM)
 VMEM = pl.BlockSpec(memory_space=pltpu.VMEM)
-
-
-def call(kernel, out_shape, flops, nbytes, *args, scratch=()):
+HBM = pl.BlockSpec(memory_space=pltpu.HBM)
+
+
+def copies(n):
+    return pltpu.SemaphoreType.DMA((n,))
+
+
+def call(kernel, out_shape, flops, nbytes, *args, scratch=(), out=VMEM, hbm=()):
     specs = [SMEM if a.dtype == jnp.int32 and a.ndim == 1 else VMEM for a in args]
+    specs = [HBM if i in hbm else spec for i, spec in enumerate(specs)]
+    args = [pltpu.with_memory_space_constraint(a, pltpu.HBM) if i in hbm else a for i, a in enumerate(args)]
     return pl.pallas_call(
         kernel,
         out_shape=out_shape,
         in_specs=specs,
+        out_specs=(out,) * len(out_shape) if isinstance(out_shape, tuple) else out,
         scratch_shapes=scratch,
         compiler_params=pltpu.CompilerParams(vmem_limit_bytes=24 * 1024 * 1024),
         cost_estimate=pl.CostEstimate(flops=flops, bytes_accessed=nbytes, transcendentals=0),
@@ -157,13 +220,18 @@
     return lax.ppermute(array, "c", [(0, 1), (1, 0)])
 
 
-def along_y(blocks):
-    moved = [lax.ppermute(blocks[d], "y", [(i, i ^ d) for i in range(RING)]) for d in range(1, RING)]
-    return [blocks[0]] + moved
+def along_y(block, d):
+    return lax.ppermute(block, "y", [(i, i ^ d) for i in range(RING)])
 
 
 def exchange(blocks, axes):
     return lax.all_to_all(blocks, axes, split_axis=0, concat_axis=0, tiled=True)
+
+
+def exchange_z(blocks, first):
+    ids = np.arange(np.prod(SIZES)).reshape(SIZES).transpose(1, 2, 4, 0, 3).reshape(-1, DEPTH)
+    groups = ids[:, np.arange(DEPTH) ^ first].tolist()
+    return lax.all_to_all(blocks, AXES, split_axis=0, concat_axis=0, axis_index_groups=groups, tiled=True)
 
 
 def per_device(hidden_in, queries, keys, lengths, master, moment, second):
@@ -176,16 +244,35 @@
     half = jax.ShapeDtypeStruct((RING, tok, feats // 2), BF16)
     matrix = pltpu.VMEM((feats, feats), BF16)
 
-    weight = call(spread_kernel, jax.ShapeDtypeStruct((16, rows, kv), BF16), 0, 1 << 17, master)
-    weight = exchange(weight, DEPTH).reshape(16 * rows, kv)
-
-    dealt = along_y(call(deal_kernel, (block,) * RING, 0, 2 << 20, at, hidden_in))
+    weight = call(
+        master_kernel,
+        jax.ShapeDtypeStruct((DEPTH, rows, kv), BF16),
+        0,
+        1 << 17,
+        master,
+        scratch=[pltpu.VMEM((rows, kv), F32), copies(1)],
+        hbm=(0,),
+    )
+    weight = exchange_z(weight, GATHER_FIRST).reshape(DEPTH * rows, kv)
+
+    dealt = call(
+        deal_kernel, (block,) * RING, 0, 2 << 20, at, hidden_in, scratch=[copies(4 * RING)], hbm=(1,)
+    )
+    dealt = [dealt[0]] + [along_y(dealt[d], d) for d in range(1, RING)]
     hidden_own, hidden_other = call(
         collect_kernel, (half, half), WEIGHTY, 3 << 20, at, *dealt, scratch=[matrix]
     )
 
-    weight = call(spread_kernel, jax.ShapeDtypeStruct((RING, 16 * rows, kv), BF16), 0, 1 << 19, weight)
-    weight = exchange(weight, "x").reshape(RING * 16 * rows, kv)
+    weight = call(
+        spread_kernel,
+        jax.ShapeDtypeStruct((RING, DEPTH * rows, kv), BF16),
+        0,
+        1 << 19,
+        weight,
+        scratch=[copies(RING)],
+        out=HBM,
+    )
+    weight = exchange(weight, "x").reshape(RING * DEPTH * rows, kv)
     weight, hidden_own, hidden_other = lax.optimization_barrier((weight, hidden_own, hidden_other))
     weight_other = swap_core(weight)
     hidden_own = hidden_own.reshape(RING * tok, feats // 2)
@@ -204,9 +291,19 @@
         seg[:, None],
     )
 
-    partial = jnp.dot(hidden_own, weight, preferred_element_type=F32)
-    partial = partial + jnp.dot(hidden_other, weight_other, preferred_element_type=F32)
-    partial = exchange(partial.astype(BF16).reshape(RING, tok, kv), "y")
+    partial = call(
+        values_kernel,
+        jax.ShapeDtypeStruct((RING, tok, kv), BF16),
+        2 * RING * tok * feats * kv,
+        3 << 20,
+        hidden_own,
+        hidden_other,
+        weight,
+        weight_other,
+        scratch=[pltpu.VMEM((RING, tok, kv), BF16), copies(RING)],
+        out=HBM,
+    )
+    partial = exchange(partial, "y")
     attended, grad = call(
         attend_kernel,
         (jax.ShapeDtypeStruct((tok, QH * HD), BF16), jax.ShapeDtypeStruct((RING, tok, kv), BF16)),
@@ -214,6 +311,8 @@
         4 << 20,
         partial,
         probs,
+        scratch=[pltpu.VMEM((VH, tok, GROUPS * HD), BF16), pltpu.VMEM((tok, kv), BF16), copies(VH + RING)],
+        out=HBM,
     )
     weight_cols = call(
         turn_kernel, jax.ShapeDtypeStruct((kv, feats), BF16), 2 * feats * feats * kv, 3 << 20, at, weight, weight_other
@@ -222,11 +321,18 @@
     grad, weight_cols = lax.optimization_barrier((grad, weight_cols))
 
     rowwise = (((0,), (0,)), ((), ()))
-    part = swap_core(
-        lax.dot_general(hidden_other, grad, rowwise, preferred_element_type=F32).astype(BF16)
-    ).astype(F32)
-    part = part + lax.dot_general(hidden_own, grad, rowwise, preferred_element_type=F32)
-    part = part.astype(BF16).reshape(RING, 16 * rows, kv)
+    sent = lax.dot_general(hidden_other, grad, rowwise, preferred_element_type=F32).astype(BF16)
+    part = call(
+        fold_kernel,
+        jax.ShapeDtypeStruct((RING, DEPTH * rows, kv), BF16),
+        2 * RING * tok * feats * kv // 2,
+        2 << 20,
+        hidden_own,
+        grad,
+        swap_core(sent),
+        scratch=[pltpu.VMEM((RING, DEPTH * rows, kv), BF16), copies(RING)],
+        out=HBM,
+    )
 
     dealt = call(
         back_kernel,
@@ -239,14 +345,21 @@
         scratch=[pltpu.VMEM((RING, tok, feats), BF16)],
     )
     part, dealt = lax.optimization_barrier((part, dealt))
-    dealt = along_y(dealt)
+    dealt = [dealt[0]] + [along_y(dealt[d], d) for d in range(1, RING)]
     grad_hidden = call(
-        join_kernel, jax.ShapeDtypeStruct((tok, width), BF16), WEIGHTY, 2 << 20, at, *dealt
+        join_kernel,
+        jax.ShapeDtypeStruct((tok, width), BF16),
+        WEIGHTY,
+        2 << 20,
+        at,
+        *dealt,
+        scratch=[copies(4 * RING)],
+        out=HBM,
     )
 
     part = exchange(part, "x")
-    part = call(sum_kernel, jax.ShapeDtypeStruct((16, rows, kv), BF16), 0, 1 << 20, part)
-    part = exchange(part, DEPTH)
+    part = call(sum_kernel, jax.ShapeDtypeStruct((DEPTH, rows, kv), BF16), 0, 1 << 20, part)
+    part = exchange_z(part, REDUCE_FIRST)
     gradient = jnp.sum(part.astype(F32), axis=0) / F32(tok * 512)
 
     moment_new = beta_one * moment + (1.0 - beta_one) * gradient

time: 126 us -> 119 us (0.944)
  waiting for transfers between devices: 33.9 us -> 24 us
  Pallas kernels: 14.3 us -> 18.6 us
  matrix products: 3.38 us -> 0.46 us
    all_to_all x0 -> x2, starting transfers between devices: none -> 27.8 us  [exchange_z(): lax.all_to_all(blocks, AXES, split_axis=0, concat_axis=0, axis_index_grou...]
    all_to_all x6 -> x4, starting transfers between devices: 44.4 us -> 16.9 us  [exchange(): return lax.all_to_all(blocks, axes, split_axis=0, concat_axis=0, tiled=True)]
    all_to_all x6 -> x4, waiting for transfers between devices: 27.2 us -> 11.3 us  [exchange(): return lax.all_to_all(blocks, axes, split_axis=0, concat_axis=0, tiled=True)]
    pallas_call x10 -> x12, Pallas kernels: 14.3 us -> 18.6 us  [call(): pl.pallas_call(kernel, out_shape=out_shape, in_specs=specs, out_specs=(ou...]
    all_to_all x0 -> x2, waiting for transfers between devices: none -> 3.75 us  [exchange_z(): lax.all_to_all(blocks, AXES, split_axis=0, concat_axis=0, axis_index_grou...]
    dot_general x3 -> x0, matrix products: 2.92 us -> none  [the longest x1 1.25 us: per_device(): lax.dot_general(hidden_own, grad, rowwise, preferred_element_type=F32)]
    ppermute x6, waiting for transfers between devices: 4.81 us -> 6.51 us  [along_y(): return lax.ppermute(block, 'y', [(i, i ^ d) for i in range(RING)])]
    unnamed x32 -> x26, local copies, waits for them, and re-layouts: 2.64 us -> 3.68 us
  transfers between devices with their start and end apart: 14 -> 14, of which waited for: 7 -> 7; matrix products, arithmetic and copies ran while one was open for 1% -> 0% of each run, Pallas kernels for 9% -> 11%
where the time goes in v5:
time: 119 us; the launch traced here: 118 us
  starting transfers between devices  69.4 us (58%)
  waiting for transfers between devices  24 us (20%)
  Pallas kernels  18.6 us (16%)
  local copies, waits for them, and re-layouts  3.8 us (3%)
    all_to_all x2, starting transfers between devices, exchange_z(): lax.all_to_all(blocks, AXES, split_axis=0, concat_axis=0, axis_index_grou...  27.8 us
    ppermute x6, starting transfers between devices, along_y(): return lax.ppermute(block, 'y', [(i, i ^ d) for i in range(RING)])  20.8 us
    pallas_call x12, Pallas kernels, call(): pl.pallas_call(kernel, out_shape=out_shape, in_specs=specs, out_specs=(ou...  18.6 us
    all_to_all x4, starting transfers between devices, exchange(): return lax.all_to_all(blocks, axes, split_axis=0, concat_axis=0, tiled=True)  16.9 us
    all_to_all x4, waiting for transfers between devices, exchange(): return lax.all_to_all(blocks, axes, split_axis=0, concat_axis=0, tiled=True)  11.3 us
    ppermute x6, waiting for transfers between devices, along_y(): return lax.ppermute(block, 'y', [(i, i ^ d) for i in range(RING)])  6.51 us
    ppermute x2, starting transfers between devices, swap_core(): return lax.ppermute(array, 'c', [(0, 1), (1, 0)])  3.84 us
    all_to_all x2, waiting for transfers between devices, exchange_z(): lax.all_to_all(blocks, AXES, split_axis=0, concat_axis=0, axis_index_grou...  3.75 us
  transfers between devices with their start and end apart: 14, of which 7 were waited for; matrix products, arithmetic and copies ran while one was open for 0% of the time, Pallas kernels for 11%

profile of v5, /device:TPU:2, one launch (start us, length us, event | category | flops | bytes accessed | tf_op | source)
XLA Modules:
  0.0 118.3 jit_solution(6056588300027520620)
XLA Ops:
  2.0 15.7 %all-to-all-start = ((bf16[16,8,512]{2,1,0:T(8,128)(2,1)}), bf16[16,8,512]{2,1,0:T(8,128)(2,1)S(1)}, u32[]{:S(2)}, u32[]{:S(2)}) async-start(bf16[16,8,512]{2,1,0:T(8,128)(2,1)} %shard_map.110), calls=%async_computation | async-start | bytes 262144 | tf_op jit(solution)/shard_map/all_to_all | solution.py:234
  17.8 1.9 %shard_map.112 = (bf16[128,1024]{1,0:T(8,128)(2,1)S(1)}, bf16[128,1024]{1,0:T(8,128)(2,1)S(1)}, bf16[128,1024]{1,0:T(8,128)(2,1)S(1)}, bf16[128,1024]{1,0:T(8,128)(2,1)S(1)}) custom-call(s32[2]{0:T(128)S(1)} %pad_add_fusion.at_ref, bf16[128,4096]{1,0:T(8,128)(2,1)} %hidden_ref.1), custom_call_target="tpu_custom_call" | custom-call | bytes 2097152 | tf_op jit(solution)/shard_map/pallas_call | solution.py:208
  19.7 3.5 %collective-permute-start = (bf16[128,1024]{1,0:T(8,128)(2,1)S(1)}, bf16[128,1024]{1,0:T(8,128)(2,1)S(1)}, u32[]{:S(2)}, u32[]{:S(2)}) collective-permute-start(bf16[128,1024]{1,0:T(8,128)(2,1)S(1)} %get-tuple-element.28), channel_id=1, source_target_pairs={{0,1},{1,0},{2,3},{3,2},{4,5},{5,4},{6,7},{7,6},{8,9},{9,8},{10,11... | collective-permute-start | bytes 786440 | tf_op jit(solution)/shard_map/ppermute | solution.py:224
  23.2 4.8 %collective-permute-start.1 = (bf16[128,1024]{1,0:T(8,128)(2,1)S(1)}, bf16[128,1024]{1,0:T(8,128)(2,1)S(1)}, u32[]{:S(2)}, u32[]{:S(2)}) collective-permute-start(bf16[128,1024]{1,0:T(8,128)(2,1)S(1)} %get-tuple-element.29), channel_id=1, source_target_pairs={{0,2},{1,3},{2,0},{3,1},{4,6},{5,7},{6,4},{7,5},{8,10},{9,11},{10,... | collective-permute-start | bytes 786440 | tf_op jit(solution)/shard_map/ppermute | solution.py:224
  28.0 2.1 %collective-permute-start.2 = (bf16[128,1024]{1,0:T(8,128)(2,1)S(1)}, bf16[128,1024]{1,0:T(8,128)(2,1)S(1)}, u32[]{:S(2)}, u32[]{:S(2)}) collective-permute-start(bf16[128,1024]{1,0:T(8,128)(2,1)S(1)} %get-tuple-element.30), channel_id=1, source_target_pairs={{0,3},{1,2},{2,1},{3,0},{4,7},{5,6},{6,5},{7,4},{8,11},{9,10},{10,... | collective-permute-start | bytes 786440 | tf_op jit(solution)/shard_map/ppermute | solution.py:224
  31.0 4.8 %all-to-all-start.1 = ((bf16[4,128,512]{2,1,0:T(8,128)(2,1)}), bf16[4,128,512]{2,1,0:T(8,128)(2,1)S(1)}, u32[]{:S(2)}, u32[]{:S(2)}) async-start(bf16[4,128,512]{2,1,0:T(8,128)(2,1)} %shard_map.111), calls=%async_computation.1 | async-start | bytes 1048576 | tf_op jit(solution)/shard_map/all_to_all | solution.py:228
  37.3 5.1 %collective-permute-done.2.refs_3_ = bf16[128,1024]{1,0:T(8,128)(2,1)S(1)} collective-permute-done((bf16[128,1024]{1,0:T(8,128)(2,1)S(1)}, bf16[128,1024]{1,0:T(8,128)(2,1)S(1)}, u32[]{:S(2)}, u32[]{:S(2)}) %collective-permute-start.2) | collective-permute-done | bytes 262176 | tf_op jit(solution)/shard_map/ppermute | solution.py:224
  42.4 2.0 %shard_map.113 = (bf16[4,128,512]{2,1,0:T(8,128)(2,1)S(1)}, bf16[4,128,512]{2,1,0:T(8,128)(2,1)S(1)}) custom-call(s32[2]{0:T(128)S(1)} %pad_add_fusion.at_ref, bf16[128,1024]{1,0:T(8,128)(2,1)S(1)} %get-tuple-element.27.refs_0_, bf16[128,1024]{1,0:T(8,128)(2,1)S(1)} %collective-permute-done.refs_1_, bf16[128,1024]{1,0:T(8,128)(2,1)S(1)} %collective-permute-done.1.refs_2_, ...), custom_call_target="tpu_custom_call" | custom-call | flops 34359738368 | bytes 3145728 | tf_op jit(solution)/shard_map/pallas_call | solution.py:208
  44.4 1.9 %collective-permute-start.3 = (bf16[512,512]{1,0:T(8,128)(2,1)S(1)}, bf16[512,512]{1,0:T(8,128)(2,1)S(1)}, u32[]{:S(2)}, u32[]{:S(2)}) collective-permute-start(bf16[512,512]{1,0:T(8,128)(2,1)S(1)} %bitcast.13), channel_id=1, source_target_pairs={{0,16},{16,0},{1,17},{17,1},{2,18},{18,2},{3,19},{19,3},{4,20},{20... | collective-permute-start | bytes 1572872 | tf_op jit(solution)/shard_map/ppermute | solution.py:220
  46.3 1.9 %collective-permute-done.3.weight_other_ref.other_ref = bf16[512,512]{1,0:T(8,128)(2,1)S(1)} collective-permute-done((bf16[512,512]{1,0:T(8,128)(2,1)S(1)}, bf16[512,512]{1,0:T(8,128)(2,1)S(1)}, u32[]{:S(2)}, u32[]{:S(2)}) %collective-permute-start.3) | collective-permute-done | bytes 524320 | tf_op jit(solution)/shard_map/ppermute | solution.py:220
  49.6 3.6 %all-to-all-start.2 = ((bf16[4,128,512]{2,1,0:T(8,128)(2,1)}), bf16[4,128,512]{2,1,0:T(8,128)(2,1)S(1)}, u32[]{:S(2)}, u32[]{:S(2)}) async-start(bf16[4,128,512]{2,1,0:T(8,128)(2,1)} %shard_map.114), calls=%async_computation.2 | async-start | bytes 1048576 | tf_op jit(solution)/shard_map/all_to_all | solution.py:228
  55.5 2.8 %shard_map.115.probs_ref = bf16[4,1024,128]{2,1,0:T(8,128)(2,1)S(1)} custom-call(bf16[128,4096]{1,0:T(8,128)(2,1)S(1)} %copy-done, bf16[128,512]{1,0:T(8,128)(2,1)S(1)} %copy-done.4, s32[1,128]{1,0:T(1,128)S(1)} %bitcast.25, s32[128,1]{1,0:T(8,128)S(1)} %copy.13.seg_col_ref), custom_call_target="tpu_custom_call" | custom-call | flops 268435456 | bytes 8388608 | tf_op jit(solution)/shard_map/pallas_call | solution.py:208
  58.3 5.0 %all-to-all-done.2.partial_ref = bf16[4,128,512]{2,1,0:T(8,128)(2,1)S(1)} async-done(((bf16[4,128,512]{2,1,0:T(8,128)(2,1)}), bf16[4,128,512]{2,1,0:T(8,128)(2,1)S(1)}, u32[]{:S(2)}, u32[]{:S(2)}) %all-to-all-start.2) | async-done | bytes 524320 | tf_op jit(solution)/shard_map/all_to_all | solution.py:228
  65.7 3.6 %all-to-all-start.3 = ((bf16[4,128,512]{2,1,0:T(8,128)(2,1)}), bf16[4,128,512]{2,1,0:T(8,128)(2,1)S(1)}, u32[]{:S(2)}, u32[]{:S(2)}) async-start(bf16[4,128,512]{2,1,0:T(8,128)(2,1)} %copy-done.3), calls=%async_computation.3 | async-start | bytes 1048576 | tf_op jit(solution)/shard_map/all_to_all | solution.py:228
  69.3 1.8 %shard_map.117.weight_ref = bf16[512,1024]{1,0:T(8,128)(2,1)S(1)} custom-call(s32[2]{0:T(128)S(1)} %pad_add_fusion.at_ref, bf16[512,512]{1,0:T(8,128)(2,1)S(1)} %bitcast.15, bf16[512,512]{1,0:T(8,128)(2,1)S(1)} %copy-done.2), custom_call_target="tpu_custom_call" | custom-call | flops 1073741824 | bytes 3145728 | tf_op jit(solution)/shard_map/pallas_call | solution.py:208
  72.1 6.4 %all-to-all-done.3 = bf16[4,128,512]{2,1,0:T(8,128)(2,1)S(1)} async-done(((bf16[4,128,512]{2,1,0:T(8,128)(2,1)}), bf16[4,128,512]{2,1,0:T(8,128)(2,1)S(1)}, u32[]{:S(2)}, u32[]{:S(2)}) %all-to-all-start.3) | async-done | bytes 524320 | tf_op jit(solution)/shard_map/all_to_all | solution.py:228
  79.0 1.9 %collective-permute-start.4 = (bf16[512,512]{1,0:T(8,128)(2,1)S(1)}, bf16[512,512]{1,0:T(8,128)(2,1)S(1)}, u32[]{:S(2)}, u32[]{:S(2)}) collective-permute-start(bf16[512,512]{1,0:T(8,128)(2,1)S(1)} %convolution_convert_fusion), channel_id=1, source_target_pairs={{0,16},{16,0},{1,17},{17,1},{2,18},{18,2},{3,19},{19,3},{4,20},{20... | collective-permute-start | bytes 1572872 | tf_op jit(solution)/shard_map/ppermute | solution.py:220
  84.0 4.8 %all-to-all-start.4 = ((bf16[4,128,512]{2,1,0:T(8,128)(2,1)}), bf16[4,128,512]{2,1,0:T(8,128)(2,1)S(1)}, u32[]{:S(2)}, u32[]{:S(2)}) async-start(bf16[4,128,512]{2,1,0:T(8,128)(2,1)} %shard_map.118), calls=%async_computation.4 | async-start | bytes 1048576 | tf_op jit(solution)/shard_map/all_to_all | solution.py:228
  88.8 2.5 %collective-permute-start.5 = (bf16[128,1024]{1,0:T(8,128)(2,1)S(1)}, bf16[128,1024]{1,0:T(8,128)(2,1)S(1)}, u32[]{:S(2)}, u32[]{:S(2)}) collective-permute-start(bf16[128,1024]{1,0:T(8,128)(2,1)S(1)} %get-tuple-element.45), channel_id=1, source_target_pairs={{0,1},{1,0},{2,3},{3,2},{4,5},{5,4},{6,7},{7,6},{8,9},{9,8},{10,11... | collective-permute-start | bytes 786440 | tf_op jit(solution)/shard_map/ppermute | solution.py:224
  91.3 4.0 %collective-permute-start.6 = (bf16[128,1024]{1,0:T(8,128)(2,1)S(1)}, bf16[128,1024]{1,0:T(8,128)(2,1)S(1)}, u32[]{:S(2)}, u32[]{:S(2)}) collective-permute-start(bf16[128,1024]{1,0:T(8,128)(2,1)S(1)} %get-tuple-element.46), channel_id=1, source_target_pairs={{0,2},{1,3},{2,0},{3,1},{4,6},{5,7},{6,4},{7,5},{8,10},{9,11},{10,... | collective-permute-start | bytes 786440 | tf_op jit(solution)/shard_map/ppermute | solution.py:224
  95.2 4.0 %collective-permute-start.7 = (bf16[128,1024]{1,0:T(8,128)(2,1)S(1)}, bf16[128,1024]{1,0:T(8,128)(2,1)S(1)}, u32[]{:S(2)}, u32[]{:S(2)}) collective-permute-start(bf16[128,1024]{1,0:T(8,128)(2,1)S(1)} %get-tuple-element.47), channel_id=1, source_target_pairs={{0,3},{1,2},{2,1},{3,0},{4,7},{5,6},{6,5},{7,4},{8,11},{9,10},{10,... | collective-permute-start | bytes 786440 | tf_op jit(solution)/shard_map/ppermute | solution.py:224
  100.0 12.2 %all-to-all-start.5 = ((bf16[16,8,512]{2,1,0:T(8,128)(2,1)}), bf16[16,8,512]{2,1,0:T(8,128)(2,1)S(1)}, u32[]{:S(2)}, u32[]{:S(2)}) async-start(bf16[16,8,512]{2,1,0:T(8,128)(2,1)} %shard_map.121), calls=%async_computation.5 | async-start | bytes 262144 | tf_op jit(solution)/shard_map/all_to_all | solution.py:234
  112.2 1.6 %shard_map.120 = bf16[128,4096]{1,0:T(8,128)(2,1)} custom-call(s32[2]{0:T(128)S(1)} %pad_add_fusion.at_ref, bf16[128,1024]{1,0:T(8,128)(2,1)S(1)} %copy-done.8, bf16[128,1024]{1,0:T(8,128)(2,1)S(1)} %collective-permute-done.5.refs_1_, bf16[128,1024]{1,0:T(8,128)(2,1)S(1)} %collective-permute-done.6.refs_2_, bf16[128,1024]{1,0:T(8,128)(2,1)S(1)} %collective-permute-done.7.refs_3_), custom_call_target="tpu_custom_call" | custom-call | flops 34359738368 | bytes 2097152 | tf_op jit(solution)/shard_map/pallas_call | solution.py:208
  113.8 3.7 %all-to-all-done.5 = bf16[16,8,512]{2,1,0:T(8,128)(2,1)S(1)} async-done(((bf16[16,8,512]{2,1,0:T(8,128)(2,1)}), bf16[16,8,512]{2,1,0:T(8,128)(2,1)S(1)}, u32[]{:S(2)}, u32[]{:S(2)}) %all-to-all-start.5) | async-done | bytes 131104 | tf_op jit(solution)/shard_map/all_to_all | solution.py:234
  (49 shorter events, 15.6 us)
Async XLA Ops:
  2.0 28.1 %all-to-all-start = ((bf16[16,8,512]{2,1,0:T(8,128)(2,1)}), bf16[16,8,512]{2,1,0:T(8,128)(2,1)S(1)}, u32[]{:S(2)}, u32[]{:S(2)}) async-start(bf16[16,8,512]{2,1,0:T(8,128)(2,1)} %shard_map.110), calls=%async_computation | async-start | bytes 262144 | tf_op jit(solution)/shard_map/all_to_all | solution.py:234
  19.7 16.1 %collective-permute-start = (bf16[128,1024]{1,0:T(8,128)(2,1)S(1)}, bf16[128,1024]{1,0:T(8,128)(2,1)S(1)}, u32[]{:S(2)}, u32[]{:S(2)}) collective-permute-start(bf16[128,1024]{1,0:T(8,128)(2,1)S(1)} %get-tuple-element.28), channel_id=1, source_target_pairs={{0,1},{1,0},{2,3},{3,2},{4,5},{5,4},{6,7},{7,6},{8,9},{9,8},{10,11... | collective-permute-start | bytes 786440 | tf_op jit(solution)/shard_map/ppermute | solution.py:224
  23.2 14.1 %collective-permute-start.1 = (bf16[128,1024]{1,0:T(8,128)(2,1)S(1)}, bf16[128,1024]{1,0:T(8,128)(2,1)S(1)}, u32[]{:S(2)}, u32[]{:S(2)}) collective-permute-start(bf16[128,1024]{1,0:T(8,128)(2,1)S(1)} %get-tuple-element.29), channel_id=1, source_target_pairs={{0,2},{1,3},{2,0},{3,1},{4,6},{5,7},{6,4},{7,5},{8,10},{9,11},{10,... | collective-permute-start | bytes 786440 | tf_op jit(solution)/shard_map/ppermute | solution.py:224
  28.0 14.3 %collective-permute-start.2 = (bf16[128,1024]{1,0:T(8,128)(2,1)S(1)}, bf16[128,1024]{1,0:T(8,128)(2,1)S(1)}, u32[]{:S(2)}, u32[]{:S(2)}) collective-permute-start(bf16[128,1024]{1,0:T(8,128)(2,1)S(1)} %get-tuple-element.30), channel_id=1, source_target_pairs={{0,3},{1,2},{2,1},{3,0},{4,7},{5,6},{6,5},{7,4},{8,11},{9,10},{10,... | collective-permute-start | bytes 786440 | tf_op jit(solution)/shard_map/ppermute | solution.py:224
  31.0 13.4 %all-to-all-start.1 = ((bf16[4,128,512]{2,1,0:T(8,128)(2,1)}), bf16[4,128,512]{2,1,0:T(8,128)(2,1)S(1)}, u32[]{:S(2)}, u32[]{:S(2)}) async-start(bf16[4,128,512]{2,1,0:T(8,128)(2,1)} %shard_map.111), calls=%async_computation.1 | async-start | bytes 1048576 | tf_op jit(solution)/shard_map/all_to_all | solution.py:228
  44.4 3.8 %collective-permute-start.3 = (bf16[512,512]{1,0:T(8,128)(2,1)S(1)}, bf16[512,512]{1,0:T(8,128)(2,1)S(1)}, u32[]{:S(2)}, u32[]{:S(2)}) collective-permute-start(bf16[512,512]{1,0:T(8,128)(2,1)S(1)} %bitcast.13), channel_id=1, source_target_pairs={{0,16},{16,0},{1,17},{17,1},{2,18},{18,2},{3,19},{19,3},{4,20},{20... | collective-permute-start | bytes 1572872 | tf_op jit(solution)/shard_map/ppermute | solution.py:220
  48.2 1.4 %copy-start.1 = (bf16[512,512]{1,0:T(8,128)(2,1)}, bf16[512,512]{1,0:T(8,128)(2,1)S(1)}, u32[]{:S(2)}) copy-start(bf16[512,512]{1,0:T(8,128)(2,1)S(1)} %collective-permute-done.3.weight_other_ref.other_ref) | copy-start | bytes 1572868
  49.6 4.7 %copy-start.4 = (bf16[128,512]{1,0:T(8,128)(2,1)S(1)}, bf16[128,512]{1,0:T(8,128)(2,1)}, u32[]{:S(2)}) copy-start(bf16[128,512]{1,0:T(8,128)(2,1)} %keys_ref.1) | copy-start | bytes 393220
  49.6 13.7 %all-to-all-start.2 = ((bf16[4,128,512]{2,1,0:T(8,128)(2,1)}), bf16[4,128,512]{2,1,0:T(8,128)(2,1)S(1)}, u32[]{:S(2)}, u32[]{:S(2)}) async-start(bf16[4,128,512]{2,1,0:T(8,128)(2,1)} %shard_map.114), calls=%async_computation.2 | async-start | bytes 1048576 | tf_op jit(solution)/shard_map/all_to_all | solution.py:228
  54.3 1.2 %copy-start = (bf16[128,4096]{1,0:T(8,128)(2,1)S(1)}, bf16[128,4096]{1,0:T(8,128)(2,1)}, u32[]{:S(2)}) copy-start(bf16[128,4096]{1,0:T(8,128)(2,1)} %queries_ref.1) | copy-start | bytes 3145732
  65.7 3.6 %copy-start.2 = (bf16[512,512]{1,0:T(8,128)(2,1)S(1)}, bf16[512,512]{1,0:T(8,128)(2,1)}, u32[]{:S(2)}) copy-start(bf16[512,512]{1,0:T(8,128)(2,1)} %copy-done.1) | copy-start | bytes 1572868
  65.7 12.8 %all-to-all-start.3 = ((bf16[4,128,512]{2,1,0:T(8,128)(2,1)}), bf16[4,128,512]{2,1,0:T(8,128)(2,1)S(1)}, u32[]{:S(2)}, u32[]{:S(2)}) async-start(bf16[4,128,512]{2,1,0:T(8,128)(2,1)} %copy-done.3), calls=%async_computation.3 | async-start | bytes 1048576 | tf_op jit(solution)/shard_map/all_to_all | solution.py:228
  78.5 2.4 %copy-start.6 = (bf16[512,1024]{1,0:T(8,128)(2,1)S(1)}, bf16[512,1024]{1,0:T(8,128)(2,1)}, u32[]{:S(2)}) copy-start(bf16[512,1024]{1,0:T(8,128)(2,1)} %copy-done.5) | copy-start | bytes 3145732
  79.0 3.8 %collective-permute-start.4 = (bf16[512,512]{1,0:T(8,128)(2,1)S(1)}, bf16[512,512]{1,0:T(8,128)(2,1)S(1)}, u32[]{:S(2)}, u32[]{:S(2)}) collective-permute-start(bf16[512,512]{1,0:T(8,128)(2,1)S(1)} %convolution_convert_fusion), channel_id=1, source_target_pairs={{0,16},{16,0},{1,17},{17,1},{2,18},{18,2},{3,19},{19,3},{4,20},{20... | collective-permute-start | bytes 1572872 | tf_op jit(solution)/shard_map/ppermute | solution.py:220
  82.2 1.7 %copy-start.7 = (bf16[128,1024]{1,0:T(8,128)(2,1)}, bf16[128,1024]{1,0:T(8,128)(2,1)S(1)}, u32[]{:S(2)}) copy-start(bf16[128,1024]{1,0:T(8,128)(2,1)S(1)} %get-tuple-element.44.refs_0_) | copy-start | bytes 786436
  84.0 15.3 %all-to-all-start.4 = ((bf16[4,128,512]{2,1,0:T(8,128)(2,1)}), bf16[4,128,512]{2,1,0:T(8,128)(2,1)S(1)}, u32[]{:S(2)}, u32[]{:S(2)}) async-start(bf16[4,128,512]{2,1,0:T(8,128)(2,1)} %shard_map.118), calls=%async_computation.4 | async-start | bytes 1048576 | tf_op jit(solution)/shard_map/all_to_all | solution.py:228
  88.8 23.3 %collective-permute-start.5 = (bf16[128,1024]{1,0:T(8,128)(2,1)S(1)}, bf16[128,1024]{1,0:T(8,128)(2,1)S(1)}, u32[]{:S(2)}, u32[]{:S(2)}) collective-permute-start(bf16[128,1024]{1,0:T(8,128)(2,1)S(1)} %get-tuple-element.45), channel_id=1, source_target_pairs={{0,1},{1,0},{2,3},{3,2},{4,5},{5,4},{6,7},{7,6},{8,9},{9,8},{10,11... | collective-permute-start | bytes 786440 | tf_op jit(solution)/shard_map/ppermute | solution.py:224
  91.3 20.9 %collective-permute-start.6 = (bf16[128,1024]{1,0:T(8,128)(2,1)S(1)}, bf16[128,1024]{1,0:T(8,128)(2,1)S(1)}, u32[]{:S(2)}, u32[]{:S(2)}) collective-permute-start(bf16[128,1024]{1,0:T(8,128)(2,1)S(1)} %get-tuple-element.46), channel_id=1, source_target_pairs={{0,2},{1,3},{2,0},{3,1},{4,6},{5,7},{6,4},{7,5},{8,10},{9,11},{10,... | collective-permute-start | bytes 786440 | tf_op jit(solution)/shard_map/ppermute | solution.py:224
  95.2 16.9 %collective-permute-start.7 = (bf16[128,1024]{1,0:T(8,128)(2,1)S(1)}, bf16[128,1024]{1,0:T(8,128)(2,1)S(1)}, u32[]{:S(2)}, u32[]{:S(2)}) collective-permute-start(bf16[128,1024]{1,0:T(8,128)(2,1)S(1)} %get-tuple-element.47), channel_id=1, source_target_pairs={{0,3},{1,2},{2,1},{3,0},{4,7},{5,6},{6,5},{7,4},{8,11},{9,10},{10,... | collective-permute-start | bytes 786440 | tf_op jit(solution)/shard_map/ppermute | solution.py:224
  100.0 12.2 %copy-start.8 = (bf16[128,1024]{1,0:T(8,128)(2,1)S(1)}, bf16[128,1024]{1,0:T(8,128)(2,1)}, u32[]{:S(2)}) copy-start(bf16[128,1024]{1,0:T(8,128)(2,1)} %copy-done.7) | copy-start | bytes 786436
  100.0 17.6 %all-to-all-start.5 = ((bf16[16,8,512]{2,1,0:T(8,128)(2,1)}), bf16[16,8,512]{2,1,0:T(8,128)(2,1)S(1)}, u32[]{:S(2)}, u32[]{:S(2)}) async-start(bf16[16,8,512]{2,1,0:T(8,128)(2,1)} %shard_map.121), calls=%async_computation.5 | async-start | bytes 262144 | tf_op jit(solution)/shard_map/all_to_all | solution.py:234
  113.8 3.8 %copy-start.9 = (f32[8,512]{1,0:T(8,128)S(1)}, f32[8,512]{1,0:T(8,128)}, u32[]{:S(2)}) copy-start(f32[8,512]{1,0:T(8,128)} %master_ref.1) | copy-start | bytes 49156
  113.8 3.8 %copy-start.10 = (f32[8,512]{1,0:T(8,128)S(1)}, f32[8,512]{1,0:T(8,128)}, u32[]{:S(2)}) copy-start(f32[8,512]{1,0:T(8,128)} %param.12) | copy-start | bytes 49156
  113.8 3.8 %copy-start.11 = (f32[8,512]{1,0:T(8,128)S(1)}, f32[8,512]{1,0:T(8,128)}, u32[]{:S(2)}) copy-start(f32[8,512]{1,0:T(8,128)} %param.13) | copy-start | bytes 49156
  (3 other events, 2.4 us)

commit v6 on v5

v6 whole, which is shorter than its diff:
```python
import jax
import jax.numpy as jnp
import numpy as np
from jax import lax
from jax.experimental import pallas as pl
from jax.experimental.pallas import tpu as pltpu
from jax.sharding import Mesh
from jax.sharding import PartitionSpec as P

HD = 128
VH = 4
QH = 32
GROUPS = QH // VH

beta_one = 0.9
beta_two = 0.95
adam_eps = 1e-08
learn_rate = 0.001
decay_rate = 0.1

AXES = ("zl", "x", "c", "zh", "yh", "yl")
SIZES = (4, 4, 2, 4, 2, 2)
TOK_SPEC = P(AXES, None)
ROW_SPEC = P(("zh", "yh", "yl", "zl", "x", "c"), None)
DEPTH = 16
PLANE = ("x", "yh")
GATHER_FIRST = 3
REDUCE_FIRST = 6

F32 = jnp.float32
BF16 = jnp.bfloat16


def order_matrix(core):
    to = lax.broadcasted_iota(jnp.int32, (1, 1024), 1)
    z = ((to >> 3) & 15) ^ GATHER_FIRST
    source = (z & 3) * 256 + (z >> 2) * 64 + ((to >> 7) & 3) * 16 + (to & 7)
    source = source + ((to >> 9) ^ core) * 8
    hit = lax.broadcasted_iota(jnp.int32, (1024, 1024), 0) == source
    return jnp.where(hit, F32(1), F32(0)).astype(BF16)


def return_matrix(core):
    to = lax.broadcasted_iota(jnp.int32, (1, 1024), 1)
    z = (((to >> 6) & 3) * 4 + (to >> 8)) ^ GATHER_FIRST
    source = z * 8 + ((to >> 4) & 3) * 128 + (to & 7)
    source = source + (((to >> 3) & 1) ^ core) * 512
    hit = lax.broadcasted_iota(jnp.int32, (1024, 1024), 0) == source
    return jnp.where(hit, F32(1), F32(0)).astype(BF16)


WEIGHTY = 32 << 30


def run_copies(sem_ref, pairs):
    copies = [pltpu.make_async_copy(a, b, sem_ref.at[i]) for i, (a, b) in enumerate(pairs)]
    for copy in copies:
        copy.start()
    for copy in copies:
        copy.wait()


def master_kernel(master_ref, out_ref, rows_ref, sem_ref):
    run_copies(sem_ref, [(master_ref, rows_ref)])
    weight = rows_ref[...].astype(BF16)
    for z in range(DEPTH):
        out_ref[z] = weight


def spread_kernel(rows_ref, out_ref, sem_ref):
    run_copies(sem_ref, [(rows_ref, out_ref.at[i]) for i in range(out_ref.shape[0])])


def block_columns(yl, block_ref, whole_ref):
    pairs = []
    for yh in range(2):
        for zh in range(4):
            at = pl.ds(pl.multiple_of(zh * 1024 + yh * 512 + yl * 256, 256), 256)
            pairs.append((block_ref.at[:, yh * 1024 + zh * 256 : yh * 1024 + zh * 256 + 256], whole_ref.at[:, at]))
    return pairs


def deal_kernel(at_ref, hidden_ref, keep_ref, send_ref, sem_ref):
    yl = at_ref[0]
    pairs = block_columns(yl, keep_ref, hidden_ref) + block_columns(1 - yl, send_ref, hidden_ref)
    run_copies(sem_ref, [(b, a) for a, b in pairs])


def join_kernel(at_ref, keep_ref, got_ref, out_ref, sem_ref):
    yl = at_ref[0]
    run_copies(sem_ref, block_columns(yl, keep_ref, out_ref) + block_columns(1 - yl, got_ref, out_ref))


def collect_kernel(at_ref, block_ref, own_ref, other_ref, matrix_ref):
    matrix_ref[...] = order_matrix(at_ref[1])
    for yh in range(2):
        moved = jnp.dot(
            block_ref[:, yh * 1024 : yh * 1024 + 1024], matrix_ref[...], preferred_element_type=F32
        ).astype(BF16)
        for x in range(4):
            to = slice((x * 2 + yh) * 128, (x * 2 + yh) * 128 + 128)
            own_ref[:, to] = moved[:, x * 128 : x * 128 + 128]
            other_ref[:, to] = moved[:, 512 + x * 128 : 640 + x * 128]


def first_kernel(near_ref, far_ref, weight_ref, near_out_ref, far_out_ref):
    near_out_ref[...] = jnp.dot(near_ref[...], weight_ref[...], preferred_element_type=F32)
    far_out_ref[...] = jnp.dot(far_ref[...], weight_ref[...], preferred_element_type=F32)


def second_kernel(rows_ref, weight_ref, first_ref, out_ref):
    total = first_ref[...] + jnp.dot(rows_ref[...], weight_ref[...], preferred_element_type=F32)
    out_ref[...] = total.astype(out_ref.dtype)


def flip_kernel(near_own_ref, near_other_ref, far_own_ref, far_other_ref, own_ref, other_ref):
    tok = near_own_ref.shape[0]
    own_ref[:, :tok] = near_own_ref[...].T
    own_ref[:, tok:] = far_own_ref[...].T
    other_ref[:, :tok] = near_other_ref[...].T
    other_ref[:, tok:] = far_other_ref[...].T


def part_kernel(hidden_ref, near_ref, far_ref, out_ref):
    grad = jnp.concatenate([near_ref[...], far_ref[...]], axis=0)
    out_ref[...] = jnp.dot(hidden_ref[...], grad, preferred_element_type=F32).astype(BF16)


def fold_kernel(hidden_ref, near_ref, far_ref, sent_ref, out_ref, rows_ref, sem_ref):
    grad = jnp.concatenate([near_ref[...], far_ref[...]], axis=0)
    step = out_ref.shape[1]
    copies = []
    for i in range(out_ref.shape[0]):
        at = slice(i * step, (i + 1) * step)
        part = jnp.dot(hidden_ref[at], grad, preferred_element_type=F32)
        rows_ref[i] = (part + sent_ref[at].astype(F32)).astype(BF16)
        copies.append(pltpu.make_async_copy(rows_ref.at[i], out_ref.at[i], sem_ref.at[i]))
        copies[-1].start()
    for copy in copies:
        copy.wait()


def back_kernel(at_ref, near_ref, far_ref, own_ref, other_ref, keep_ref, send_ref, cols_ref, matrix_ref):
    tok = near_ref.shape[0]
    matrix_ref[...] = return_matrix(at_ref[1])
    grad = jnp.concatenate([near_ref[...], far_ref[...]], axis=0)
    for c, weight_ref in enumerate((own_ref, other_ref)):
        rows = lax.dot_general(
            grad, weight_ref[...], (((1,), (1,)), ((), ())), preferred_element_type=F32
        ).astype(BF16)
        for x in range(4):
            for yh in range(2):
                at = (x * 2 + yh) * 128
                cols_ref[yh, :, c * 512 + x * 128 : c * 512 + x * 128 + 128] = rows[:, at : at + 128]
    for yh in range(2):
        moved = jnp.dot(cols_ref[yh], matrix_ref[...], preferred_element_type=F32).astype(BF16)
        keep_ref[:, yh * 1024 : yh * 1024 + 1024] = moved[:tok]
        send_ref[:, yh * 1024 : yh * 1024 + 1024] = moved[tok:]


def sum_kernel(parts_ref, out_ref):
    total = parts_ref[0].astype(F32)
    for i in range(1, parts_ref.shape[0]):
        total = total + parts_ref[i].astype(F32)
    total = total.astype(BF16)
    rows = out_ref.shape[1]
    for z in range(out_ref.shape[0]):
        out_ref[z ^ GATHER_FIRST ^ REDUCE_FIRST] = total[z * rows : (z + 1) * rows]


def probs_kernel(queries_ref, keys_ref, seg_row_ref, seg_col_ref, out_ref):
    tok = queries_ref.shape[0]
    rows = lax.broadcasted_iota(jnp.int32, (tok, tok), 0)
    cols = lax.broadcasted_iota(jnp.int32, (tok, tok), 1)
    allowed = (seg_col_ref[...] == seg_row_ref[...]) & (cols <= rows)
    scale = F32(1.0 / np.sqrt(HD))
    for j in range(VH):
        key = keys_ref[:, j * HD : (j + 1) * HD]
        for h in range(GROUPS):
            at = (j * GROUPS + h) * HD
            scores = lax.dot_general(
                queries_ref[:, at : at + HD], key, (((1,), (1,)), ((), ())), preferred_element_type=F32
            )
            scores = jnp.where(allowed, scores * scale, F32(-1000000000.0))
            expos = jnp.exp(scores - jnp.max(scores, axis=-1, keepdims=True))
            total = jnp.sum(expos, axis=-1, keepdims=True)
            out_ref[j, h * tok : (h + 1) * tok, :] = (expos / total).astype(BF16)


def attend_kernel(near_ref, sent_ref, probs_ref, attended_ref, grad_ref, rows_ref, sem_ref):
    tok = near_ref.shape[0]
    wide = GROUPS * HD
    copies = []
    for j in range(VH):
        cols = slice(j * HD, (j + 1) * HD)
        value = (near_ref[:, cols] + sent_ref[:, cols].astype(F32)).astype(BF16)
        attended = jnp.dot(probs_ref[j], value, preferred_element_type=F32).astype(BF16)
        for h in range(GROUPS):
            rows_ref[j, :, h * HD : (h + 1) * HD] = attended[h * tok : (h + 1) * tok]
        copies.append(
            pltpu.make_async_copy(rows_ref.at[j], attended_ref.at[:, j * wide : (j + 1) * wide], sem_ref.at[j])
        )
        copies[-1].start()
        grad_ref[:, cols] = lax.dot_general(
            probs_ref[j], attended, (((0,), (0,)), ((), ())), preferred_element_type=F32
        ).astype(BF16)
    for copy in copies:
        copy.wait()


SMEM = pl.BlockSpec(memory_space=pltpu.SMEM)
VMEM = pl.BlockSpec(memory_space=pltpu.VMEM)
HBM = pl.BlockSpec(memory_space=pltpu.HBM)


def copies(n):
    return pltpu.SemaphoreType.DMA((n,))


def call(kernel, out_shape, flops, nbytes, *args, scratch=(), out=None, hbm=()):
    specs = [SMEM if a.dtype == jnp.int32 and a.ndim == 1 else VMEM for a in args]
    specs = [HBM if i in hbm else spec for i, spec in enumerate(specs)]
    if out is None:
        out = (VMEM,) * len(out_shape) if isinstance(out_shape, tuple) else VMEM
    if out is HBM:
        out_shape = pltpu.HBM(out_shape.shape, out_shape.dtype)
    args = [pltpu.with_memory_space_constraint(a, pltpu.HBM) if i in hbm else a for i, a in enumerate(args)]
    return pl.pallas_call(
        kernel,
        out_shape=out_shape,
        in_specs=specs,
        out_specs=out,
        scratch_shapes=scratch,
        compiler_params=pltpu.CompilerParams(vmem_limit_bytes=24 * 1024 * 1024),
        cost_estimate=pl.CostEstimate(flops=flops, bytes_accessed=nbytes, transcendentals=0),
    )(*args)


def swap_core(array):
    return lax.ppermute(array, "c", [(0, 1), (1, 0)])


def swap_pair(array):
    return lax.ppermute(array, "yl", [(0, 1), (1, 0)])


def exchange(blocks, axes):
    return lax.all_to_all(blocks, axes, split_axis=0, concat_axis=0, tiled=True)


def exchange_z(blocks, first):
    ids = np.arange(np.prod(SIZES)).reshape(SIZES).transpose(1, 2, 4, 5, 0, 3).reshape(-1, DEPTH)
    groups = ids[:, np.arange(DEPTH) ^ first].tolist()
    return lax.all_to_all(blocks, AXES, split_axis=0, concat_axis=0, axis_index_groups=groups, tiled=True)


def per_device(hidden_in, queries, keys, lengths, master, moment, second):
    tok, width = hidden_in.shape
    kv = keys.shape[1]
    rows = master.shape[0]
    feats = width // 4
    peers = 8
    at = jnp.stack([lax.axis_index("yl"), lax.axis_index("c")]).astype(jnp.int32)
    block = jax.ShapeDtypeStruct((tok, 2 * feats), BF16)
    half = jax.ShapeDtypeStruct((tok, feats), BF16)
    value = jax.ShapeDtypeStruct((tok, kv), BF16)
    total = jax.ShapeDtypeStruct((tok, kv), F32)
    matrix = pltpu.VMEM((1024, 1024), BF16)

    weight = call(
        master_kernel,
        jax.ShapeDtypeStruct((DEPTH, rows, kv), BF16),
        0,
        1 << 17,
        master,
        scratch=[pltpu.VMEM((rows, kv), F32), copies(1)],
        hbm=(0,),
    )
    weight = exchange_z(weight, GATHER_FIRST).reshape(DEPTH * rows, kv)

    keep, send = call(
        deal_kernel, (block, block), 0, 2 << 20, at, hidden_in, scratch=[copies(16)], hbm=(1,)
    )
    got = swap_pair(send)

    weight = call(
        spread_kernel,
        jax.ShapeDtypeStruct((peers, DEPTH * rows, kv), BF16),
        0,
        1 << 20,
        weight,
        scratch=[copies(peers)],
        out=HBM,
    )
    weight, keep, keys = lax.optimization_barrier((weight, keep, keys))
    weight = exchange(weight, PLANE).reshape(peers * DEPTH * rows, kv)

    def collect(array):
        return call(collect_kernel, (half, half), WEIGHTY, 3 << 20, at, array, scratch=[matrix])

    near_own, near_other = collect(keep)
    far_own, far_other = collect(got)

    ends = jnp.cumsum(lengths[0])
    seg = jnp.sum((jnp.arange(tok, dtype=jnp.int32)[:, None] >= ends[None, :]).astype(jnp.int32), axis=1)
    probs = call(
        probs_kernel,
        jax.ShapeDtypeStruct((VH, GROUPS * tok, tok), BF16),
        4 * tok * tok * QH * HD,
        8 << 20,
        queries,
        keys,
        seg[None, :],
        seg[:, None],
    )
    flipped = jax.ShapeDtypeStruct((feats, 2 * tok), BF16)
    columns_own, columns_other = call(
        flip_kernel, (flipped, flipped), 0, 2 << 20, near_own, near_other, far_own, far_other
    )

    weight, near_own, near_other, far_own, far_other, columns_own, columns_other, probs = lax.optimization_barrier(
        (weight, near_own, near_other, far_own, far_other, columns_own, columns_other, probs)
    )
    weight_other = swap_core(weight)

    flops = 2 * tok * feats * kv
    near, far = call(first_kernel, (total, total), 2 * flops, 2 << 20, near_own, far_own, weight)
    far = call(second_kernel, value, flops, 2 << 20, far_other, weight_other, far)
    sent = swap_pair(far)
    near = call(second_kernel, total, flops, 2 << 20, near_other, weight_other, near)
    attended, grad = call(
        attend_kernel,
        (jax.ShapeDtypeStruct((tok, QH * HD), BF16), value),
        4 * tok * tok * QH * HD,
        4 << 20,
        near,
        sent,
        probs,
        scratch=[pltpu.VMEM((VH, tok, GROUPS * HD), BF16), copies(VH)],
        out=(HBM, VMEM),
    )
    grad_far = swap_pair(grad)

    part = call(
        part_kernel,
        jax.ShapeDtypeStruct((feats, kv), BF16),
        2 * flops,
        2 << 20,
        columns_other,
        grad,
        grad_far,
    )
    part = call(
        fold_kernel,
        jax.ShapeDtypeStruct((peers, DEPTH * rows, kv), BF16),
        2 * flops,
        2 << 20,
        columns_own,
        grad,
        grad_far,
        swap_core(part),
        scratch=[pltpu.VMEM((peers, DEPTH * rows, kv), BF16), copies(peers)],
        out=HBM,
    )
    part, grad, grad_far = lax.optimization_barrier((part, grad, grad_far))

    keep, send = call(
        back_kernel,
        (block, block),
        8 * tok * feats * kv,
        4 << 20,
        at,
        grad,
        grad_far,
        weight,
        weight_other,
        scratch=[pltpu.VMEM((2, 2 * tok, 1024), BF16), matrix],
    )
    grad_hidden = call(
        join_kernel,
        jax.ShapeDtypeStruct((tok, width), BF16),
        WEIGHTY,
        2 << 20,
        at,
        keep,
        swap_pair(send),
        scratch=[copies(16)],
        out=HBM,
    )

    part = exchange(part, PLANE)
    part = call(sum_kernel, jax.ShapeDtypeStruct((DEPTH, rows, kv), BF16), 0, 1 << 20, part)
    part = exchange_z(part, REDUCE_FIRST)
    gradient = jnp.sum(part.astype(F32), axis=0) / F32(tok * 512)

    moment_new = beta_one * moment + (1.0 - beta_one) * gradient
    second_new = beta_two * second + (1.0 - beta_two) * gradient * gradient
    moment_hat = moment_new / (1.0 - beta_one**10)
    second_hat = second_new / (1.0 - beta_two**10)
    master_new = master - learn_rate * (
        moment_hat / (jnp.sqrt(second_hat) + adam_eps) + decay_rate * master
    )
    return (attended, grad_hidden, master_new, moment_new, second_new)


def solution(mesh):
    named = Mesh(mesh.devices.reshape(SIZES), AXES)
    return jax.shard_map(
        per_device,
        mesh=named,
        in_specs=(TOK_SPEC, TOK_SPEC, TOK_SPEC, TOK_SPEC, ROW_SPEC, ROW_SPEC, ROW_SPEC),
        out_specs=(TOK_SPEC, TOK_SPEC, ROW_SPEC, ROW_SPEC, ROW_SPEC),
        check_vma=False,
    )
```

time: 119 us -> 123 us (1.034)
  the two profiles are of different devices: /device:TPU:2 before, /device:TPU:1 now
where the time goes in v6:
time: 123 us; the launch traced here: 120 us
  starting transfers between devices  59.5 us (48%)
  waiting for transfers between devices  30.8 us (25%)
  Pallas kernels  22 us (18%)
  local copies, waits for them, and re-layouts  6.03 us (5%)
    all_to_all x2, starting transfers between devices, exchange_z(): lax.all_to_all(blocks, AXES, split_axis=0, concat_axis=0, axis_index_grou...  30.4 us
    pallas_call x16, Pallas kernels, call(): pl.pallas_call(kernel, out_shape=out_shape, in_specs=specs, out_specs=out...  22 us
    all_to_all x2, waiting for transfers between devices, exchange(): return lax.all_to_all(blocks, axes, split_axis=0, concat_axis=0, tiled=True)  13.5 us
    ppermute x4, starting transfers between devices, swap_pair(): return lax.ppermute(array, 'yl', [(0, 1), (1, 0)])  10.4 us
    all_to_all x2, starting transfers between devices, exchange(): return lax.all_to_all(blocks, axes, split_axis=0, concat_axis=0, tiled=True)  10.2 us
    ppermute x2, starting transfers between devices, swap_core(): return lax.ppermute(array, 'c', [(0, 1), (1, 0)])  8.53 us
    ppermute x4, waiting for transfers between devices, swap_pair(): return lax.ppermute(array, 'yl', [(0, 1), (1, 0)])  8.19 us
    all_to_all x2, waiting for transfers between devices, exchange_z(): lax.all_to_all(blocks, AXES, split_axis=0, concat_axis=0, axis_index_grou...  6.78 us
  transfers between devices with their start and end apart: 10, of which 7 were waited for; matrix products, arithmetic and copies ran while one was open for 0% of the time, Pallas kernels for 14%

profile of v6, /device:TPU:1, one launch (start us, length us, event | category | flops | bytes accessed | tf_op | source)
XLA Modules:
  0.0 120.3 jit_solution(15569444439293643193)
XLA Ops:
  2.0 15.9 %all-to-all-start = ((bf16[16,8,512]{2,1,0:T(8,128)(2,1)}), bf16[16,8,512]{2,1,0:T(8,128)(2,1)S(1)}, u32[]{:S(2)}, u32[]{:S(2)}) async-start(bf16[16,8,512]{2,1,0:T(8,128)(2,1)} %shard_map.110), calls=%async_computation | async-start | bytes 262144 | tf_op jit(solution)/shard_map/all_to_all | solution.py:254
  18.1 2.7 %shard_map.112 = (bf16[128,2048]{1,0:T(8,128)(2,1)S(1)}, bf16[128,2048]{1,0:T(8,128)(2,1)}) custom-call(s32[2]{0:T(128)S(1)} %pad_add_fusion.at_ref, bf16[128,4096]{1,0:T(8,128)(2,1)} %hidden_ref.1), custom_call_target="tpu_custom_call" | custom-call | bytes 2097152 | tf_op jit(solution)/shard_map/pallas_call | solution.py:228
  20.8 3.2 %collective-permute-start = (bf16[128,2048]{1,0:T(8,128)(2,1)}, bf16[128,2048]{1,0:T(8,128)(2,1)}, u32[]{:S(2)}, u32[]{:S(2)}) collective-permute-start(bf16[128,2048]{1,0:T(8,128)(2,1)} %get-tuple-element.38), channel_id=1, source_target_pairs={{0,1},{1,0},{2,3},{3,2},{4,5},{5,4},{6,7},{7,6},{8,9},{9,8},{10,11... | collective-permute-start | bytes 1572872 | tf_op jit(solution)/shard_map/ppermute | solution.py:244
  24.4 3.2 %all-to-all-done = bf16[16,8,512]{2,1,0:T(8,128)(2,1)S(1)} async-done(((bf16[16,8,512]{2,1,0:T(8,128)(2,1)}), bf16[16,8,512]{2,1,0:T(8,128)(2,1)S(1)}, u32[]{:S(2)}, u32[]{:S(2)}) %all-to-all-start) | async-done | bytes 131104 | tf_op jit(solution)/shard_map/all_to_all | solution.py:254
  28.7 6.7 %all-to-all-start.1 = ((bf16[8,128,512]{2,1,0:T(8,128)(2,1)}), bf16[8,128,512]{2,1,0:T(8,128)(2,1)S(1)}, u32[]{:S(2)}, u32[]{:S(2)}) async-start(bf16[8,128,512]{2,1,0:T(8,128)(2,1)} %shard_map.111), calls=%async_computation.1 | async-start | bytes 2097152 | tf_op jit(solution)/shard_map/all_to_all | solution.py:248
  35.3 1.6 %shard_map.113 = (bf16[128,1024]{1,0:T(8,128)(2,1)S(1)}, bf16[128,1024]{1,0:T(8,128)(2,1)S(1)}) custom-call(s32[2]{0:T(128)S(1)} %pad_add_fusion.at_ref, bf16[128,2048]{1,0:T(8,128)(2,1)S(1)} %get-tuple-element.35.block_ref), custom_call_target="tpu_custom_call" | custom-call | flops 34359738368 | bytes 3145728 | tf_op jit(solution)/shard_map/pallas_call | solution.py:228
  36.9 2.8 %shard_map.116.probs_ref = bf16[4,1024,128]{2,1,0:T(8,128)(2,1)S(1)} custom-call(bf16[128,4096]{1,0:T(8,128)(2,1)S(1)} %copy-done, bf16[128,512]{1,0:T(8,128)(2,1)S(1)} %copy-done.11, s32[1,128]{1,0:T(1,128)S(1)} %bitcast.13, s32[128,1]{1,0:T(8,128)S(1)} %copy.13.seg_col_ref), custom_call_target="tpu_custom_call" | custom-call | flops 268435456 | bytes 8388608 | tf_op jit(solution)/shard_map/pallas_call | solution.py:228
  39.7 2.1 %shard_map.114 = (bf16[128,1024]{1,0:T(8,128)(2,1)S(1)}, bf16[128,1024]{1,0:T(8,128)(2,1)S(1)}) custom-call(s32[2]{0:T(128)S(1)} %pad_add_fusion.at_ref, bf16[128,2048]{1,0:T(8,128)(2,1)} %collective-permute-done.block_ref), custom_call_target="tpu_custom_call" | custom-call | flops 34359738368 | bytes 3145728 | tf_op jit(solution)/shard_map/pallas_call | solution.py:228
  44.9 4.6 %all-to-all-done.1 = bf16[8,128,512]{2,1,0:T(8,128)(2,1)S(1)} async-done(((bf16[8,128,512]{2,1,0:T(8,128)(2,1)}), bf16[8,128,512]{2,1,0:T(8,128)(2,1)S(1)}, u32[]{:S(2)}, u32[]{:S(2)}) %all-to-all-start.1) | async-done | bytes 1048608 | tf_op jit(solution)/shard_map/all_to_all | solution.py:248
  49.4 4.9 %collective-permute-start.1 = (bf16[1024,512]{1,0:T(8,128)(2,1)S(1)}, bf16[1024,512]{1,0:T(8,128)(2,1)S(1)}, u32[]{:S(2)}, u32[]{:S(2)}) collective-permute-start(bf16[1024,512]{1,0:T(8,128)(2,1)S(1)} %bitcast.8), channel_id=1, source_target_pairs={{0,16},{16,0},{1,17},{17,1},{2,18},{18,2},{3,19},{19,3},{4,20},{20... | collective-permute-start | bytes 3145736 | tf_op jit(solution)/shard_map/ppermute | solution.py:240
  57.6 2.3 %collective-permute-start.2 = (bf16[128,512]{1,0:T(8,128)(2,1)S(1)}, bf16[128,512]{1,0:T(8,128)(2,1)S(1)}, u32[]{:S(2)}, u32[]{:S(2)}) collective-permute-start(bf16[128,512]{1,0:T(8,128)(2,1)S(1)} %shard_map.119), channel_id=1, source_target_pairs={{0,1},{1,0},{2,3},{3,2},{4,5},{5,4},{6,7},{7,6},{8,9},{9,8},{10,11... | collective-permute-start | bytes 393224 | tf_op jit(solution)/shard_map/ppermute | solution.py:244
  60.2 4.4 %collective-permute-done.2.sent_ref = bf16[128,512]{1,0:T(8,128)(2,1)S(1)} collective-permute-done((bf16[128,512]{1,0:T(8,128)(2,1)S(1)}, bf16[128,512]{1,0:T(8,128)(2,1)S(1)}, u32[]{:S(2)}, u32[]{:S(2)}) %collective-permute-start.2) | collective-permute-done | bytes 131104 | tf_op jit(solution)/shard_map/ppermute | solution.py:244
  64.6 1.4 %shard_map.120 = (bf16[128,4096]{1,0:T(8,128)(2,1)}, bf16[128,512]{1,0:T(8,128)(2,1)S(1)}) custom-call(f32[128,512]{1,0:T(8,128)S(1)} %shard_map.118.near_ref, bf16[128,512]{1,0:T(8,128)(2,1)S(1)} %collective-permute-done.2.sent_ref, bf16[4,1024,128]{2,1,0:T(8,128)(2,1)S(1)} %shard_map.116.probs_ref), custom_call_target="tpu_custom_call" | custom-call | flops 268435456 | bytes 4194304 | tf_op jit(solution)/shard_map/pallas_call | solution.py:228
  66.0 2.4 %collective-permute-start.3 = (bf16[128,512]{1,0:T(8,128)(2,1)S(1)}, bf16[128,512]{1,0:T(8,128)(2,1)S(1)}, u32[]{:S(2)}, u32[]{:S(2)}) collective-permute-start(bf16[128,512]{1,0:T(8,128)(2,1)S(1)} %get-tuple-element.56.near_ref), channel_id=1, source_target_pairs={{0,1},{1,0},{2,3},{3,2},{4,5},{5,4},{6,7},{7,6},{8,9},{9,8},{10,11... | collective-permute-start | bytes 393224 | tf_op jit(solution)/shard_map/ppermute | solution.py:244
  68.5 3.8 %collective-permute-done.3.far_ref = bf16[128,512]{1,0:T(8,128)(2,1)S(1)} collective-permute-done((bf16[128,512]{1,0:T(8,128)(2,1)S(1)}, bf16[128,512]{1,0:T(8,128)(2,1)S(1)}, u32[]{:S(2)}, u32[]{:S(2)}) %collective-permute-start.3) | collective-permute-done | bytes 131104 | tf_op jit(solution)/shard_map/ppermute | solution.py:244
  72.7 3.6 %collective-permute-start.4 = (bf16[1024,512]{1,0:T(8,128)(2,1)S(1)}, bf16[1024,512]{1,0:T(8,128)(2,1)S(1)}, u32[]{:S(2)}, u32[]{:S(2)}) collective-permute-start(bf16[1024,512]{1,0:T(8,128)(2,1)S(1)} %shard_map.121), channel_id=1, source_target_pairs={{0,16},{16,0},{1,17},{17,1},{2,18},{18,2},{3,19},{19,3},{4,20},{20... | collective-permute-start | bytes 3145736 | tf_op jit(solution)/shard_map/ppermute | solution.py:240
  76.3 2.3 %collective-permute-done.4.sent_ref = bf16[1024,512]{1,0:T(8,128)(2,1)S(1)} collective-permute-done((bf16[1024,512]{1,0:T(8,128)(2,1)S(1)}, bf16[1024,512]{1,0:T(8,128)(2,1)S(1)}, u32[]{:S(2)}, u32[]{:S(2)}) %collective-permute-start.4) | collective-permute-done | bytes 1048608 | tf_op jit(solution)/shard_map/ppermute | solution.py:240
  79.8 3.6 %all-to-all-start.2 = ((bf16[8,128,512]{2,1,0:T(8,128)(2,1)}), bf16[8,128,512]{2,1,0:T(8,128)(2,1)S(1)}, u32[]{:S(2)}, u32[]{:S(2)}) async-start(bf16[8,128,512]{2,1,0:T(8,128)(2,1)} %shard_map.122), calls=%async_computation.2 | async-start | bytes 2097152 | tf_op jit(solution)/shard_map/all_to_all | solution.py:248
  83.4 3.5 %shard_map.123 = (bf16[128,2048]{1,0:T(8,128)(2,1)S(1)}, bf16[128,2048]{1,0:T(8,128)(2,1)}) custom-call(s32[2]{0:T(128)S(1)} %pad_add_fusion.at_ref, bf16[128,512]{1,0:T(8,128)(2,1)S(1)} %get-tuple-element.56.near_ref, bf16[128,512]{1,0:T(8,128)(2,1)S(1)} %collective-permute-done.3.far_ref, bf16[1024,512]{1,0:T(8,128)(2,1)S(1)} %bitcast.10, ...), custom_call_target="tpu_custom_call" | custom-call | flops 536870912 | bytes 4194304 | tf_op jit(solution)/shard_map/pallas_call | solution.py:228
  87.7 2.4 %collective-permute-start.5 = (bf16[128,2048]{1,0:T(8,128)(2,1)}, bf16[128,2048]{1,0:T(8,128)(2,1)S(1)}, u32[]{:S(2)}, u32[]{:S(2)}) collective-permute-start(bf16[128,2048]{1,0:T(8,128)(2,1)} %get-tuple-element.59), channel_id=1, source_target_pairs={{0,1},{1,0},{2,3},{3,2},{4,5},{5,4},{6,7},{7,6},{8,9},{9,8},{10,11... | collective-permute-start | bytes 1572872 | tf_op jit(solution)/shard_map/ppermute | solution.py:244
  90.2 9.0 %all-to-all-done.2.parts_ref = bf16[8,128,512]{2,1,0:T(8,128)(2,1)S(1)} async-done(((bf16[8,128,512]{2,1,0:T(8,128)(2,1)}), bf16[8,128,512]{2,1,0:T(8,128)(2,1)S(1)}, u32[]{:S(2)}, u32[]{:S(2)}) %all-to-all-start.2) | async-done | bytes 1048608 | tf_op jit(solution)/shard_map/all_to_all | solution.py:248
  99.9 14.4 %all-to-all-start.3 = ((bf16[16,8,512]{2,1,0:T(8,128)(2,1)}), bf16[16,8,512]{2,1,0:T(8,128)(2,1)S(1)}, u32[]{:S(2)}, u32[]{:S(2)}) async-start(bf16[16,8,512]{2,1,0:T(8,128)(2,1)} %shard_map.125), calls=%async_computation.3 | async-start | bytes 262144 | tf_op jit(solution)/shard_map/all_to_all | solution.py:254
  114.4 1.6 %shard_map.124 = bf16[128,4096]{1,0:T(8,128)(2,1)} custom-call(s32[2]{0:T(128)S(1)} %pad_add_fusion.at_ref, bf16[128,2048]{1,0:T(8,128)(2,1)S(1)} %copy-done.13, bf16[128,2048]{1,0:T(8,128)(2,1)S(1)} %collective-permute-done.5.got_ref), custom_call_target="tpu_custom_call" | custom-call | flops 34359738368 | bytes 2097152 | tf_op jit(solution)/shard_map/pallas_call | solution.py:228
  116.1 3.6 %all-to-all-done.3 = bf16[16,8,512]{2,1,0:T(8,128)(2,1)S(1)} async-done(((bf16[16,8,512]{2,1,0:T(8,128)(2,1)}), bf16[16,8,512]{2,1,0:T(8,128)(2,1)S(1)}, u32[]{:S(2)}, u32[]{:S(2)}) %all-to-all-start.3) | async-done | bytes 131104 | tf_op jit(solution)/shard_map/all_to_all | solution.py:254
  (54 shorter events, 13.3 us)
Async XLA Ops:
  2.0 25.6 %all-to-all-start = ((bf16[16,8,512]{2,1,0:T(8,128)(2,1)}), bf16[16,8,512]{2,1,0:T(8,128)(2,1)S(1)}, u32[]{:S(2)}, u32[]{:S(2)}) async-start(bf16[16,8,512]{2,1,0:T(8,128)(2,1)} %shard_map.110), calls=%async_computation | async-start | bytes 262144 | tf_op jit(solution)/shard_map/all_to_all | solution.py:254
  20.8 3.2 %copy-start.17 = (s32[1,4]{1,0:T(1,128)S(1)}, s32[1,4]{1,0:T(1,128)}, u32[]{:S(2)}) copy-start(s32[1,4]{1,0:T(1,128)} %param.10) | copy-start | bytes 52
  20.8 18.9 %collective-permute-start = (bf16[128,2048]{1,0:T(8,128)(2,1)}, bf16[128,2048]{1,0:T(8,128)(2,1)}, u32[]{:S(2)}, u32[]{:S(2)}) collective-permute-start(bf16[128,2048]{1,0:T(8,128)(2,1)} %get-tuple-element.38), channel_id=1, source_target_pairs={{0,1},{1,0},{2,3},{3,2},{4,5},{5,4},{6,7},{7,6},{8,9},{9,8},{10,11... | collective-permute-start | bytes 1572872 | tf_op jit(solution)/shard_map/ppermute | solution.py:244
  28.7 20.8 %all-to-all-start.1 = ((bf16[8,128,512]{2,1,0:T(8,128)(2,1)}), bf16[8,128,512]{2,1,0:T(8,128)(2,1)S(1)}, u32[]{:S(2)}, u32[]{:S(2)}) async-start(bf16[8,128,512]{2,1,0:T(8,128)(2,1)} %shard_map.111), calls=%async_computation.1 | async-start | bytes 2097152 | tf_op jit(solution)/shard_map/all_to_all | solution.py:248
  35.3 1.6 %copy-start = (bf16[128,4096]{1,0:T(8,128)(2,1)S(1)}, bf16[128,4096]{1,0:T(8,128)(2,1)}, u32[]{:S(2)}) copy-start(bf16[128,4096]{1,0:T(8,128)(2,1)} %queries_ref.1) | copy-start | bytes 3145732
  35.3 1.6 %copy-start.11 = (bf16[128,512]{1,0:T(8,128)(2,1)S(1)}, bf16[128,512]{1,0:T(8,128)(2,1)}, u32[]{:S(2)}) copy-start(bf16[128,512]{1,0:T(8,128)(2,1)} %keys_ref) | copy-start | bytes 393220
  36.9 4.9 %copy-start.1 = (bf16[128,1024]{1,0:T(8,128)(2,1)}, bf16[128,1024]{1,0:T(8,128)(2,1)S(1)}, u32[]{:S(2)}) copy-start(bf16[128,1024]{1,0:T(8,128)(2,1)S(1)} %get-tuple-element.46.near_own_ref.near_ref) | copy-start | bytes 786436
  43.2 0.8 copy-start.7
  49.4 7.3 %collective-permute-start.1 = (bf16[1024,512]{1,0:T(8,128)(2,1)S(1)}, bf16[1024,512]{1,0:T(8,128)(2,1)S(1)}, u32[]{:S(2)}, u32[]{:S(2)}) collective-permute-start(bf16[1024,512]{1,0:T(8,128)(2,1)S(1)} %bitcast.8), channel_id=1, source_target_pairs={{0,16},{16,0},{1,17},{17,1},{2,18},{18,2},{3,19},{19,3},{4,20},{20... | collective-permute-start | bytes 3145736 | tf_op jit(solution)/shard_map/ppermute | solution.py:240
  54.4 1.0 copy-start.2
  55.3 0.9 copy-start.6
  56.3 0.9 copy-start.4
  57.6 7.0 %collective-permute-start.2 = (bf16[128,512]{1,0:T(8,128)(2,1)S(1)}, bf16[128,512]{1,0:T(8,128)(2,1)S(1)}, u32[]{:S(2)}, u32[]{:S(2)}) collective-permute-start(bf16[128,512]{1,0:T(8,128)(2,1)S(1)} %shard_map.119), channel_id=1, source_target_pairs={{0,1},{1,0},{2,3},{3,2},{4,5},{5,4},{6,7},{7,6},{8,9},{9,8},{10,11... | collective-permute-start | bytes 393224 | tf_op jit(solution)/shard_map/ppermute | solution.py:244
  60.2 12.1 %copy-start.8 = (bf16[1024,256]{1,0:T(8,128)(2,1)S(1)}, bf16[1024,256]{1,0:T(8,128)(2,1)}, u32[]{:S(2)}) copy-start(bf16[1024,256]{1,0:T(8,128)(2,1)} %copy-done.7) | copy-start | bytes 1572868
  66.0 12.6 %copy-start.10 = (bf16[1024,256]{1,0:T(8,128)(2,1)S(1)}, bf16[1024,256]{1,0:T(8,128)(2,1)}, u32[]{:S(2)}) copy-start(bf16[1024,256]{1,0:T(8,128)(2,1)} %copy-done.9) | copy-start | bytes 1572868
  66.0 6.3 %collective-permute-start.3 = (bf16[128,512]{1,0:T(8,128)(2,1)S(1)}, bf16[128,512]{1,0:T(8,128)(2,1)S(1)}, u32[]{:S(2)}, u32[]{:S(2)}) collective-permute-start(bf16[128,512]{1,0:T(8,128)(2,1)S(1)} %get-tuple-element.56.near_ref), channel_id=1, source_target_pairs={{0,1},{1,0},{2,3},{3,2},{4,5},{5,4},{6,7},{7,6},{8,9},{9,8},{10,11... | collective-permute-start | bytes 393224 | tf_op jit(solution)/shard_map/ppermute | solution.py:244
  72.7 5.9 %collective-permute-start.4 = (bf16[1024,512]{1,0:T(8,128)(2,1)S(1)}, bf16[1024,512]{1,0:T(8,128)(2,1)S(1)}, u32[]{:S(2)}, u32[]{:S(2)}) collective-permute-start(bf16[1024,512]{1,0:T(8,128)(2,1)S(1)} %shard_map.121), channel_id=1, source_target_pairs={{0,16},{16,0},{1,17},{17,1},{2,18},{18,2},{3,19},{19,3},{4,20},{20... | collective-permute-start | bytes 3145736 | tf_op jit(solution)/shard_map/ppermute | solution.py:240
  79.8 19.3 %all-to-all-start.2 = ((bf16[8,128,512]{2,1,0:T(8,128)(2,1)}), bf16[8,128,512]{2,1,0:T(8,128)(2,1)S(1)}, u32[]{:S(2)}, u32[]{:S(2)}) async-start(bf16[8,128,512]{2,1,0:T(8,128)(2,1)} %shard_map.122), calls=%async_computation.2 | async-start | bytes 2097152 | tf_op jit(solution)/shard_map/all_to_all | solution.py:248
  87.7 26.6 %copy-start.13 = (bf16[128,2048]{1,0:T(8,128)(2,1)S(1)}, bf16[128,2048]{1,0:T(8,128)(2,1)}, u32[]{:S(2)}) copy-start(bf16[128,2048]{1,0:T(8,128)(2,1)} %copy-done.12) | copy-start | bytes 1572868
  87.7 26.6 %collective-permute-start.5 = (bf16[128,2048]{1,0:T(8,128)(2,1)}, bf16[128,2048]{1,0:T(8,128)(2,1)S(1)}, u32[]{:S(2)}, u32[]{:S(2)}) collective-permute-start(bf16[128,2048]{1,0:T(8,128)(2,1)} %get-tuple-element.59), channel_id=1, source_target_pairs={{0,1},{1,0},{2,3},{3,2},{4,5},{5,4},{6,7},{7,6},{8,9},{9,8},{10,11... | collective-permute-start | bytes 1572872 | tf_op jit(solution)/shard_map/ppermute | solution.py:244
  99.9 19.7 %all-to-all-start.3 = ((bf16[16,8,512]{2,1,0:T(8,128)(2,1)}), bf16[16,8,512]{2,1,0:T(8,128)(2,1)S(1)}, u32[]{:S(2)}, u32[]{:S(2)}) async-start(bf16[16,8,512]{2,1,0:T(8,128)(2,1)} %shard_map.125), calls=%async_computation.3 | async-start | bytes 262144 | tf_op jit(solution)/shard_map/all_to_all | solution.py:254
  116.0 3.6 %copy-start.14 = (f32[8,512]{1,0:T(8,128)S(1)}, f32[8,512]{1,0:T(8,128)}, u32[]{:S(2)}) copy-start(f32[8,512]{1,0:T(8,128)} %master_ref.1) | copy-start | bytes 49156
  116.0 3.6 %copy-start.15 = (f32[8,512]{1,0:T(8,128)S(1)}, f32[8,512]{1,0:T(8,128)}, u32[]{:S(2)}) copy-start(f32[8,512]{1,0:T(8,128)} %param.12) | copy-start | bytes 49156
  116.0 3.6 %copy-start.16 = (f32[8,512]{1,0:T(8,128)S(1)}, f32[8,512]{1,0:T(8,128)}, u32[]{:S(2)}) copy-start(f32[8,512]{1,0:T(8,128)} %param.13) | copy-start | bytes 49156
  (4 other events, 3.0 us)

commit v7 on v6

v7 whole, which is shorter than its diff:
```python
import jax
import jax.numpy as jnp
import numpy as np
from jax import lax
from jax.experimental import pallas as pl
from jax.experimental.pallas import tpu as pltpu
from jax.sharding import Mesh
from jax.sharding import PartitionSpec as P

HD = 128
VH = 4
QH = 32
GROUPS = QH // VH

beta_one = 0.9
beta_two = 0.95
adam_eps = 1e-08
learn_rate = 0.001
decay_rate = 0.1

AXES = ("zlh", "zll", "x", "c", "zh", "y")
SIZES = (2, 2, 4, 2, 4, 4)
TOK_SPEC = P(AXES, None)
ROW_SPEC = P(("zh", "y", "zlh", "zll", "x", "c"), None)
DEPTH = 8
PLANE = 16
GATHER_FIRST = 3
REDUCE_FIRST = 2

F32 = jnp.float32
BF16 = jnp.bfloat16


def order_matrix(zll, core):
    to = lax.broadcasted_iota(jnp.int32, (1, 1024), 1)
    z = ((to >> 3) & 7) ^ GATHER_FIRST
    source = (z & 3) * 256 + (z >> 2) * 128 + ((to >> 6) & 3) * 16 + (to & 7)
    source = source + ((to >> 9) ^ zll) * 64 + (((to >> 8) & 1) ^ core) * 8
    hit = lax.broadcasted_iota(jnp.int32, (1024, 1024), 0) == source
    return jnp.where(hit, F32(1), F32(0)).astype(BF16)


def return_matrix(zll, core):
    to = lax.broadcasted_iota(jnp.int32, (1, 1024), 1)
    z = (((to >> 7) & 1) * 4 + (to >> 8)) ^ GATHER_FIRST
    source = z * 8 + ((to >> 4) & 3) * 64 + (to & 7)
    source = source + (((to >> 6) & 1) ^ zll) * 512 + (((to >> 3) & 1) ^ core) * 256
    hit = lax.broadcasted_iota(jnp.int32, (1024, 1024), 0) == source
    return jnp.where(hit, F32(1), F32(0)).astype(BF16)


WEIGHTY = 32 << 30


def run_copies(sem_ref, pairs):
    copies = [pltpu.make_async_copy(a, b, sem_ref.at[i]) for i, (a, b) in enumerate(pairs)]
    for copy in copies:
        copy.start()
    for copy in copies:
        copy.wait()


def master_kernel(master_ref, out_ref, rows_ref, sem_ref):
    run_copies(sem_ref, [(master_ref, rows_ref)])
    weight = rows_ref[...].astype(BF16)
    for z in range(DEPTH):
        out_ref[z] = weight


def spread_kernel(rows_ref, out_ref, sem_ref):
    run_copies(sem_ref, [(rows_ref, out_ref.at[i]) for i in range(out_ref.shape[0])])


def whole_columns(whole_ref, cols_ref):
    tok = whole_ref.shape[0]
    return [
        (
            whole_ref.at[:, zh * 1024 + y * 256 : zh * 1024 + y * 256 + 256],
            cols_ref.at[y * tok : (y + 1) * tok, zh * 256 : (zh + 1) * 256],
        )
        for y in range(4)
        for zh in range(4)
    ]


def split_kernel(at_ref, hidden_ref, own_ref, other_ref, send_ref, cols_ref, matrix_ref, sem_ref):
    tok = own_ref.shape[0]
    half = own_ref.shape[1]
    copies = [pltpu.make_async_copy(a, b, sem_ref.at[i]) for i, (a, b) in enumerate(whole_columns(hidden_ref, cols_ref))]
    for copy in copies:
        copy.start()
    matrix_ref[...] = order_matrix(at_ref[0], at_ref[1])
    for copy in copies:
        copy.wait()
    moved = jnp.dot(cols_ref[...], matrix_ref[...], preferred_element_type=F32).astype(BF16)
    for y in range(4):
        rows = slice(y * tok, (y + 1) * tok)
        to = slice(y * 256, (y + 1) * 256)
        own_ref[:, to] = moved[rows, :256]
        other_ref[:, to] = moved[rows, 256:512]
        send_ref[:, to] = moved[rows, 512:768]
        send_ref[:, half + y * 256 : half + (y + 1) * 256] = moved[rows, 768:]


def join_kernel(at_ref, keep_ref, got_ref, out_ref, cols_ref, moved_ref, matrix_ref, sem_ref):
    tok = keep_ref.shape[0]
    half = keep_ref.shape[1] // 2
    matrix_ref[...] = return_matrix(at_ref[0], at_ref[1])
    for y in range(4):
        for t, ref in enumerate((keep_ref, got_ref)):
            for c in range(2):
                to = (t * 2 + c) * 256
                cols_ref[y * tok : (y + 1) * tok, to : to + 256] = ref[:, c * half + y * 256 : c * half + y * 256 + 256]
    moved_ref[...] = jnp.dot(cols_ref[...], matrix_ref[...], preferred_element_type=F32).astype(BF16)
    run_copies(sem_ref, [(b, a) for a, b in whole_columns(out_ref, moved_ref)])


def first_kernel(near_ref, far_ref, weight_ref, near_out_ref, far_out_ref):
    half = near_ref.shape[1]
    near_out_ref[...] = jnp.dot(near_ref[...], weight_ref[...], preferred_element_type=F32)
    far_out_ref[...] = jnp.dot(far_ref[:, :half], weight_ref[...], preferred_element_type=F32)


def second_kernel(rows_ref, weight_ref, first_ref, out_ref):
    rows = rows_ref[:, rows_ref.shape[1] - weight_ref.shape[0] :]
    total = first_ref[...] + jnp.dot(rows, weight_ref[...], preferred_element_type=F32)
    out_ref[...] = total.astype(out_ref.dtype)


def flip_kernel(near_own_ref, near_other_ref, far_ref, own_ref, other_ref):
    tok, half = near_own_ref.shape
    own_ref[:, :tok] = near_own_ref[...].T
    own_ref[:, tok:] = far_ref[:, :half].T
    other_ref[:, :tok] = near_other_ref[...].T
    other_ref[:, tok:] = far_ref[:, half:].T


def part_kernel(hidden_ref, near_ref, far_ref, out_ref):
    grad = jnp.concatenate([near_ref[...], far_ref[...]], axis=0)
    out_ref[...] = jnp.dot(hidden_ref[...], grad, preferred_element_type=F32).astype(BF16)


def fold_kernel(hidden_ref, near_ref, far_ref, sent_ref, out_ref, rows_ref, sem_ref):
    grad = jnp.concatenate([near_ref[...], far_ref[...]], axis=0)
    step = out_ref.shape[1]
    copies = []
    for i in range(out_ref.shape[0]):
        at = slice(i * step, (i + 1) * step)
        part = jnp.dot(hidden_ref[at], grad, preferred_element_type=F32)
        rows_ref[i] = (part + sent_ref[at].astype(F32)).astype(BF16)
        copies.append(pltpu.make_async_copy(rows_ref.at[i], out_ref.at[i], sem_ref.at[i]))
        copies[-1].start()
    for copy in copies:
        copy.wait()


def back_kernel(near_ref, far_ref, own_ref, other_ref, keep_ref, send_ref):
    tok = near_ref.shape[0]
    half = own_ref.shape[0]
    grad = jnp.concatenate([near_ref[...], far_ref[...]], axis=0)
    for c, weight_ref in enumerate((own_ref, other_ref)):
        rows = lax.dot_general(
            grad, weight_ref[...], (((1,), (1,)), ((), ())), preferred_element_type=F32
        ).astype(BF16)
        keep_ref[:, c * half : (c + 1) * half] = rows[:tok]
        send_ref[:, c * half : (c + 1) * half] = rows[tok:]


def sum_kernel(parts_ref, out_ref):
    total = parts_ref[0].astype(F32)
    for i in range(1, parts_ref.shape[0]):
        total = total + parts_ref[i].astype(F32)
    total = total.astype(BF16)
    rows = out_ref.shape[1]
    for z in range(out_ref.shape[0]):
        out_ref[z ^ GATHER_FIRST ^ REDUCE_FIRST] = total[z * rows : (z + 1) * rows]


def probs_kernel(queries_ref, keys_ref, seg_row_ref, seg_col_ref, out_ref):
    tok = queries_ref.shape[0]
    rows = lax.broadcasted_iota(jnp.int32, (tok, tok), 0)
    cols = lax.broadcasted_iota(jnp.int32, (tok, tok), 1)
    allowed = (seg_col_ref[...] == seg_row_ref[...]) & (cols <= rows)
    scale = F32(1.0 / np.sqrt(HD))
    for j in range(VH):
        key = keys_ref[:, j * HD : (j + 1) * HD]
        for h in range(GROUPS):
            at = (j * GROUPS + h) * HD
            scores = lax.dot_general(
                queries_ref[:, at : at + HD], key, (((1,), (1,)), ((), ())), preferred_element_type=F32
            )
            scores = jnp.where(allowed, scores * scale, F32(-1000000000.0))
            expos = jnp.exp(scores - jnp.max(scores, axis=-1, keepdims=True))
            total = jnp.sum(expos, axis=-1, keepdims=True)
            out_ref[j, h * tok : (h + 1) * tok, :] = (expos / total).astype(BF16)


def attend_kernel(near_ref, sent_ref, probs_ref, attended_ref, grad_ref, rows_ref, sem_ref):
    tok = near_ref.shape[0]
    wide = GROUPS * HD
    copies = []
    for j in range(VH):
        cols = slice(j * HD, (j + 1) * HD)
        value = (near_ref[:, cols] + sent_ref[:, cols].astype(F32)).astype(BF16)
        attended = jnp.dot(probs_ref[j], value, preferred_element_type=F32).astype(BF16)
        for h in range(GROUPS):
            rows_ref[j, :, h * HD : (h + 1) * HD] = attended[h * tok : (h + 1) * tok]
        copies.append(
            pltpu.make_async_copy(rows_ref.at[j], attended_ref.at[:, j * wide : (j + 1) * wide], sem_ref.at[j])
        )
        copies[-1].start()
        grad_ref[:, cols] = lax.dot_general(
            probs_ref[j], attended, (((0,), (0,)), ((), ())), preferred_element_type=F32
        ).astype(BF16)
    for copy in copies:
        copy.wait()


SMEM = pl.BlockSpec(memory_space=pltpu.SMEM)
VMEM = pl.BlockSpec(memory_space=pltpu.VMEM)
HBM = pl.BlockSpec(memory_space=pltpu.HBM)


def copies(n):
    return pltpu.SemaphoreType.DMA((n,))


def call(kernel, out_shape, flops, nbytes, *args, scratch=(), out=None, hbm=(), late=()):
    specs = [SMEM if a.dtype == jnp.int32 and a.ndim == 1 else VMEM for a in args]
    specs = [HBM if i in hbm else spec for i, spec in enumerate(specs)]
    if out is None:
        out = (VMEM,) * len(out_shape) if isinstance(out_shape, tuple) else VMEM
    if out is HBM:
        out_shape = pltpu.HBM(out_shape.shape, out_shape.dtype)
    if late:
        out_shape = tuple(pltpu.HBM(o.shape, o.dtype) if i in late else o for i, o in enumerate(out_shape))
    args = [pltpu.with_memory_space_constraint(a, pltpu.HBM) if i in hbm else a for i, a in enumerate(args)]
    return pl.pallas_call(
        kernel,
        out_shape=out_shape,
        in_specs=specs,
        out_specs=out,
        scratch_shapes=scratch,
        compiler_params=pltpu.CompilerParams(vmem_limit_bytes=24 * 1024 * 1024),
        cost_estimate=pl.CostEstimate(flops=flops, bytes_accessed=nbytes, transcendentals=0),
    )(*args)


def swap_core(array):
    return lax.ppermute(array, "c", [(0, 1), (1, 0)])


def swap_pair(array):
    return lax.ppermute(array, "zll", [(0, 1), (1, 0)])


def exchange(blocks, members, first):
    ids = np.arange(np.prod(SIZES)).reshape(SIZES)
    last = [AXES.index(a) for a in members]
    ids = ids.transpose([i for i in range(len(SIZES)) if i not in last] + last).reshape(-1, blocks.shape[0])
    groups = ids[:, np.arange(blocks.shape[0]) ^ first].tolist()
    return lax.all_to_all(blocks, AXES, split_axis=0, concat_axis=0, axis_index_groups=groups, tiled=True)


def exchange_z(blocks, first):
    return exchange(blocks, ("zlh", "zh"), first)


def exchange_plane(blocks):
    return exchange(blocks, ("y", "x"), 0)


def per_device(hidden_in, queries, keys, lengths, master, moment, second):
    tok, width = hidden_in.shape
    kv = keys.shape[1]
    rows = master.shape[0]
    feats = width // 4
    at = jnp.stack([lax.axis_index("zll"), lax.axis_index("c")]).astype(jnp.int32)
    block = jax.ShapeDtypeStruct((tok, 2 * feats), BF16)
    half = jax.ShapeDtypeStruct((tok, feats), BF16)
    value = jax.ShapeDtypeStruct((tok, kv), BF16)
    total = jax.ShapeDtypeStruct((tok, kv), F32)
    matrix = pltpu.VMEM((1024, 1024), BF16)
    cols = pltpu.VMEM((4 * tok, 1024), BF16)

    weight = call(
        master_kernel,
        jax.ShapeDtypeStruct((DEPTH, rows, kv), BF16),
        0,
        1 << 17,
        master,
        scratch=[pltpu.VMEM((rows, kv), F32), copies(1)],
        hbm=(0,),
    )
    weight, hidden_in = lax.optimization_barrier((weight, hidden_in))
    weight = exchange_z(weight, GATHER_FIRST).reshape(DEPTH * rows, kv)

    near_own, near_other, send = call(
        split_kernel,
        (half, half, block),
        8 * tok * 1024 * 1024,
        2 << 20,
        at,
        hidden_in,
        scratch=[cols, matrix, copies(16)],
        hbm=(1,),
        late=(0, 1),
    )
    far = swap_pair(send)

    weight = call(
        spread_kernel,
        jax.ShapeDtypeStruct((PLANE, DEPTH * rows, kv), BF16),
        0,
        1 << 20,
        weight,
        scratch=[copies(PLANE)],
        out=HBM,
    )
    weight, keys = lax.optimization_barrier((weight, keys))
    weight = exchange_plane(weight).reshape(PLANE * DEPTH * rows, kv)

    ends = jnp.cumsum(lengths[0])
    seg = jnp.sum((jnp.arange(tok, dtype=jnp.int32)[:, None] >= ends[None, :]).astype(jnp.int32), axis=1)
    (probs,) = call(
        probs_kernel,
        (jax.ShapeDtypeStruct((VH, GROUPS * tok, tok), BF16),),
        4 * tok * tok * QH * HD,
        8 << 20,
        queries,
        keys,
        seg[None, :],
        seg[:, None],
        late=(0,),
    )
    flipped = jax.ShapeDtypeStruct((feats, 2 * tok), BF16)
    columns_own, columns_other = call(
        flip_kernel, (flipped, flipped), WEIGHTY // 6, 2 << 20, near_own, near_other, far, late=(0, 1)
    )
    weight, near_own, near_other, far, columns_own, columns_other, probs = lax.optimization_barrier(
        (weight, near_own, near_other, far, columns_own, columns_other, probs)
    )
    weight_other = swap_core(weight)

    flops = 2 * tok * feats * kv
    near, far_values = call(first_kernel, (total, total), 2 * flops, 2 << 20, near_own, far, weight)
    sent = swap_pair(call(second_kernel, value, flops, 2 << 20, far, weight_other, far_values))
    near = call(second_kernel, total, flops, 2 << 20, near_other, weight_other, near)
    attended, grad = call(
        attend_kernel,
        (jax.ShapeDtypeStruct((tok, QH * HD), BF16), value),
        4 * tok * tok * QH * HD,
        4 << 20,
        near,
        sent,
        probs,
        scratch=[pltpu.VMEM((VH, tok, GROUPS * HD), BF16), copies(VH)],
        out=(HBM, VMEM),
    )
    grad_far = swap_pair(grad)

    part = call(
        part_kernel,
        jax.ShapeDtypeStruct((feats, kv), BF16),
        2 * flops,
        2 << 20,
        columns_other,
        grad,
        grad_far,
    )
    part = call(
        fold_kernel,
        jax.ShapeDtypeStruct((PLANE, DEPTH * rows, kv), BF16),
        2 * flops,
        2 << 20,
        columns_own,
        grad,
        grad_far,
        swap_core(part),
        scratch=[pltpu.VMEM((PLANE, DEPTH * rows, kv), BF16), copies(PLANE)],
        out=HBM,
    )
    part, grad, grad_far = lax.optimization_barrier((part, grad, grad_far))

    keep, send = call(
        back_kernel, (block, block), 8 * tok * feats * kv, 4 << 20, grad, grad_far, weight, weight_other, late=(0,)
    )
    grad_hidden = call(
        join_kernel,
        jax.ShapeDtypeStruct((tok, width), BF16),
        WEIGHTY,
        2 << 20,
        at,
        keep,
        swap_pair(send),
        scratch=[cols, cols, matrix, copies(16)],
        out=HBM,
    )

    part = exchange_plane(part)
    part = call(sum_kernel, jax.ShapeDtypeStruct((DEPTH, rows, kv), BF16), 0, 1 << 20, part)
    part = exchange_z(part, REDUCE_FIRST)
    gradient = jnp.sum(part.astype(F32), axis=0) / F32(tok * 512)

    moment_new = beta_one * moment + (1.0 - beta_one) * gradient
    second_new = beta_two * second + (1.0 - beta_two) * gradient * gradient
    moment_hat = moment_new / (1.0 - beta_one**10)
    second_hat = second_new / (1.0 - beta_two**10)
    master_new = master - learn_rate * (
        moment_hat / (jnp.sqrt(second_hat) + adam_eps) + decay_rate * master
    )
    return (attended, grad_hidden, master_new, moment_new, second_new)


def solution(mesh):
    named = Mesh(mesh.devices.reshape(SIZES), AXES)
    return jax.shard_map(
        per_device,
        mesh=named,
        in_specs=(TOK_SPEC, TOK_SPEC, TOK_SPEC, TOK_SPEC, ROW_SPEC, ROW_SPEC, ROW_SPEC),
        out_specs=(TOK_SPEC, TOK_SPEC, ROW_SPEC, ROW_SPEC, ROW_SPEC),
        check_vma=False,
    )
```

time: 123 us -> 117 us (0.951); the launches traced: 120 us -> 116 us
  local copies, waits for them, and re-layouts: 6.03 us -> 1.34 us
  waiting for transfers between devices: 30.8 us -> 33.4 us
    unnamed x36 -> x24, local copies, waits for them, and re-layouts: 5.91 us -> 1.23 us
    all_to_all x4, starting transfers between devices: 40.6 us -> 37.9 us  [exchange(): lax.all_to_all(blocks, AXES, split_axis=0, concat_axis=0, axis_index_grou...]
    all_to_all x4, waiting for transfers between devices: 20.3 us -> 22.5 us  [exchange(): lax.all_to_all(blocks, AXES, split_axis=0, concat_axis=0, axis_index_grou...]
    ppermute x2, waiting for transfers between devices: 2.27 us -> 4.08 us  [swap_core(): return lax.ppermute(array, 'c', [(0, 1), (1, 0)])]
    ppermute x4, waiting for transfers between devices: 8.19 us -> 6.81 us  [swap_pair(): return lax.ppermute(array, 'zll', [(0, 1), (1, 0)])]
    ppermute x2, starting transfers between devices: 8.53 us -> 9.77 us  [swap_core(): return lax.ppermute(array, 'c', [(0, 1), (1, 0)])]
    pallas_call x16 -> x14, Pallas kernels: 22 us -> 21.3 us  [call(): pl.pallas_call(kernel, out_shape=out_shape, in_specs=specs, out_specs=out...]
  transfers between devices with their start and end apart: 10 -> 10, of which waited for: 7 -> 8; matrix products, arithmetic and copies ran while one was open for 0% -> 0% of each run, Pallas kernels for 14% -> 14%
where the time goes in v7:
time: 117 us; the launch traced here: 116 us
  starting transfers between devices  58.5 us (50%)
  waiting for transfers between devices  33.4 us (29%)
  Pallas kernels  21.3 us (18%)
  local copies, waits for them, and re-layouts  1.34 us (1%)
    all_to_all x4, starting transfers between devices, exchange(): lax.all_to_all(blocks, AXES, split_axis=0, concat_axis=0, axis_index_grou...  37.9 us
    all_to_all x4, waiting for transfers between devices, exchange(): lax.all_to_all(blocks, AXES, split_axis=0, concat_axis=0, axis_index_grou...  22.5 us
    pallas_call x14, Pallas kernels, call(): pl.pallas_call(kernel, out_shape=out_shape, in_specs=specs, out_specs=out...  21.3 us
    ppermute x4, starting transfers between devices, swap_pair(): return lax.ppermute(array, 'zll', [(0, 1), (1, 0)])  10.8 us
    ppermute x2, starting transfers between devices, swap_core(): return lax.ppermute(array, 'c', [(0, 1), (1, 0)])  9.77 us
    ppermute x4, waiting for transfers between devices, swap_pair(): return lax.ppermute(array, 'zll', [(0, 1), (1, 0)])  6.81 us
    ppermute x2, waiting for transfers between devices, swap_core(): return lax.ppermute(array, 'c', [(0, 1), (1, 0)])  4.08 us
  transfers between devices with their start and end apart: 10, of which 8 were waited for; matrix products, arithmetic and copies ran while one was open for 0% of the time, Pallas kernels for 14%

profile of v7, /device:TPU:1, one launch (start us, length us, event | category | flops | bytes accessed | tf_op | source)
XLA Modules:
  0.0 116.3 jit_solution(7810215601003752067)
XLA Ops:
  0.6 1.4 %shard_map.110 = bf16[8,8,512]{2,1,0:T(8,128)(2,1)} custom-call(f32[8,512]{1,0:T(8,128)} %master_ref.1), custom_call_target="tpu_custom_call" | custom-call | bytes 131072 | tf_op jit(solution)/shard_map/pallas_call | solution.py:238
  2.0 15.9 %all-to-all-start = ((bf16[8,8,512]{2,1,0:T(8,128)(2,1)}), bf16[8,8,512]{2,1,0:T(8,128)(2,1)S(1)}, u32[]{:S(2)}, u32[]{:S(2)}) async-start(bf16[8,8,512]{2,1,0:T(8,128)(2,1)} %shard_map.110), calls=%async_computation | async-start | bytes 131072 | tf_op jit(solution)/shard_map/all_to_all | solution.py:262
  18.0 4.0 %shard_map.112 = (bf16[128,1024]{1,0:T(8,128)(2,1)}, bf16[128,1024]{1,0:T(8,128)(2,1)}, bf16[128,2048]{1,0:T(8,128)(2,1)}) custom-call(s32[2]{0:T(128)S(1)} %pad_add_fusion.at_ref, bf16[128,4096]{1,0:T(8,128)(2,1)} %hidden_ref), custom_call_target="tpu_custom_call" | custom-call | flops 1073741824 | bytes 2097152 | tf_op jit(solution)/shard_map/pallas_call | solution.py:238
  22.0 2.6 %collective-permute-start = (bf16[128,2048]{1,0:T(8,128)(2,1)}, bf16[128,2048]{1,0:T(8,128)(2,1)S(1)}, u32[]{:S(2)}, u32[]{:S(2)}) collective-permute-start(bf16[128,2048]{1,0:T(8,128)(2,1)} %get-tuple-element.35), channel_id=1, source_target_pairs={{0,128},{128,0},{1,129},{129,1},{2,130},{130,2},{3,131},{131,3},{4... | collective-permute-start | bytes 1572872 | tf_op jit(solution)/shard_map/ppermute | solution.py:254
  26.6 6.9 %all-to-all-start.1 = ((bf16[16,64,512]{2,1,0:T(8,128)(2,1)}), bf16[16,64,512]{2,1,0:T(8,128)(2,1)S(1)}, u32[]{:S(2)}, u32[]{:S(2)}) async-start(bf16[16,64,512]{2,1,0:T(8,128)(2,1)} %shard_map.111), calls=%async_computation.1 | async-start | bytes 2097152 | tf_op jit(solution)/shard_map/all_to_all | solution.py:262
  34.6 3.8 %shard_map.114.probs_ref = bf16[4,1024,128]{2,1,0:T(8,128)(2,1)} custom-call(bf16[128,4096]{1,0:T(8,128)(2,1)S(1)} %copy-done.1, bf16[128,512]{1,0:T(8,128)(2,1)S(1)} %copy-done.6, s32[1,128]{1,0:T(1,128)S(1)} %bitcast.13, s32[128,1]{1,0:T(8,128)S(1)} %copy.13.seg_col_ref), custom_call_target="tpu_custom_call" | custom-call | flops 268435456 | bytes 8388608 | tf_op jit(solution)/shard_map/pallas_call | solution.py:238
  38.3 1.2 %shard_map.113 = (bf16[1024,256]{1,0:T(8,128)(2,1)}, bf16[1024,256]{1,0:T(8,128)(2,1)}) custom-call(bf16[128,1024]{1,0:T(8,128)(2,1)S(1)} %copy-done.5, bf16[128,1024]{1,0:T(8,128)(2,1)S(1)} %copy-done.4, bf16[128,2048]{1,0:T(8,128)(2,1)S(1)} %collective-permute-done.far_ref.rows_ref), custom_call_target="tpu_custom_call" | custom-call | flops 5726623232 | bytes 2097152 | tf_op jit(solution)/shard_map/pallas_call | solution.py:238
  39.5 8.9 %all-to-all-done.1 = bf16[16,64,512]{2,1,0:T(8,128)(2,1)S(1)} async-done(((bf16[16,64,512]{2,1,0:T(8,128)(2,1)}), bf16[16,64,512]{2,1,0:T(8,128)(2,1)S(1)}, u32[]{:S(2)}, u32[]{:S(2)}) %all-to-all-start.1) | async-done | bytes 1048608 | tf_op jit(solution)/shard_map/all_to_all | solution.py:262
  48.4 5.5 %collective-permute-start.1 = (bf16[1024,512]{1,0:T(8,128)(2,1)S(1)}, bf16[1024,512]{1,0:T(8,128)(2,1)S(1)}, u32[]{:S(2)}, u32[]{:S(2)}) collective-permute-start(bf16[1024,512]{1,0:T(8,128)(2,1)S(1)} %bitcast.8), channel_id=1, source_target_pairs={{0,16},{16,0},{1,17},{17,1},{2,18},{18,2},{3,19},{19,3},{4,20},{20... | collective-permute-start | bytes 3145736 | tf_op jit(solution)/shard_map/ppermute | solution.py:250
  54.3 1.8 %collective-permute-done.1.weight_ref.other_ref = bf16[1024,512]{1,0:T(8,128)(2,1)S(1)} collective-permute-done((bf16[1024,512]{1,0:T(8,128)(2,1)S(1)}, bf16[1024,512]{1,0:T(8,128)(2,1)S(1)}, u32[]{:S(2)}, u32[]{:S(2)}) %collective-permute-start.1) | collective-permute-done | bytes 1048608 | tf_op jit(solution)/shard_map/ppermute | solution.py:250
  56.5 2.7 %collective-permute-start.2 = (bf16[128,512]{1,0:T(8,128)(2,1)S(1)}, bf16[128,512]{1,0:T(8,128)(2,1)S(1)}, u32[]{:S(2)}, u32[]{:S(2)}) collective-permute-start(bf16[128,512]{1,0:T(8,128)(2,1)S(1)} %shard_map.117), channel_id=1, source_target_pairs={{0,128},{128,0},{1,129},{129,1},{2,130},{130,2},{3,131},{131,3},{4... | collective-permute-start | bytes 393224 | tf_op jit(solution)/shard_map/ppermute | solution.py:254
  59.5 3.7 %collective-permute-done.2.sent_ref = bf16[128,512]{1,0:T(8,128)(2,1)S(1)} collective-permute-done((bf16[128,512]{1,0:T(8,128)(2,1)S(1)}, bf16[128,512]{1,0:T(8,128)(2,1)S(1)}, u32[]{:S(2)}, u32[]{:S(2)}) %collective-permute-start.2) | collective-permute-done | bytes 131104 | tf_op jit(solution)/shard_map/ppermute | solution.py:254
  63.2 1.4 %shard_map.118 = (bf16[128,4096]{1,0:T(8,128)(2,1)}, bf16[128,512]{1,0:T(8,128)(2,1)S(1)}) custom-call(f32[128,512]{1,0:T(8,128)S(1)} %shard_map.116.near_ref, bf16[128,512]{1,0:T(8,128)(2,1)S(1)} %collective-permute-done.2.sent_ref, bf16[4,1024,128]{2,1,0:T(8,128)(2,1)S(1)} %copy-done), custom_call_target="tpu_custom_call" | custom-call | flops 268435456 | bytes 4194304 | tf_op jit(solution)/shard_map/pallas_call | solution.py:238
  64.7 2.7 %collective-permute-start.3 = (bf16[128,512]{1,0:T(8,128)(2,1)S(1)}, bf16[128,512]{1,0:T(8,128)(2,1)S(1)}, u32[]{:S(2)}, u32[]{:S(2)}) collective-permute-start(bf16[128,512]{1,0:T(8,128)(2,1)S(1)} %get-tuple-element.50.near_ref), channel_id=1, source_target_pairs={{0,128},{128,0},{1,129},{129,1},{2,130},{130,2},{3,131},{131,3},{4... | collective-permute-start | bytes 393224 | tf_op jit(solution)/shard_map/ppermute | solution.py:254
  67.4 3.1 %collective-permute-done.3.far_ref = bf16[128,512]{1,0:T(8,128)(2,1)S(1)} collective-permute-done((bf16[128,512]{1,0:T(8,128)(2,1)S(1)}, bf16[128,512]{1,0:T(8,128)(2,1)S(1)}, u32[]{:S(2)}, u32[]{:S(2)}) %collective-permute-start.3) | collective-permute-done | bytes 131104 | tf_op jit(solution)/shard_map/ppermute | solution.py:254
  71.0 4.3 %collective-permute-start.4 = (bf16[1024,512]{1,0:T(8,128)(2,1)S(1)}, bf16[1024,512]{1,0:T(8,128)(2,1)S(1)}, u32[]{:S(2)}, u32[]{:S(2)}) collective-permute-start(bf16[1024,512]{1,0:T(8,128)(2,1)S(1)} %shard_map.119), channel_id=1, source_target_pairs={{0,16},{16,0},{1,17},{17,1},{2,18},{18,2},{3,19},{19,3},{4,20},{20... | collective-permute-start | bytes 3145736 | tf_op jit(solution)/shard_map/ppermute | solution.py:250
  75.2 2.3 %collective-permute-done.4.sent_ref = bf16[1024,512]{1,0:T(8,128)(2,1)S(1)} collective-permute-done((bf16[1024,512]{1,0:T(8,128)(2,1)S(1)}, bf16[1024,512]{1,0:T(8,128)(2,1)S(1)}, u32[]{:S(2)}, u32[]{:S(2)}) %collective-permute-start.4) | collective-permute-done | bytes 1048608 | tf_op jit(solution)/shard_map/ppermute | solution.py:250
  77.5 1.6 %shard_map.120 = bf16[16,64,512]{2,1,0:T(8,128)(2,1)} custom-call(bf16[1024,256]{1,0:T(8,128)(2,1)S(1)} %copy-done.3, bf16[128,512]{1,0:T(8,128)(2,1)S(1)} %get-tuple-element.50.near_ref, bf16[128,512]{1,0:T(8,128)(2,1)S(1)} %collective-permute-done.3.far_ref, bf16[1024,512]{1,0:T(8,128)(2,1)S(1)} %collective-permute-done.4.sent_ref), custom_call_target="tpu_custom_call" | custom-call | flops 268435456 | bytes 2097152 | tf_op jit(solution)/shard_map/pallas_call | solution.py:238
  79.1 3.7 %all-to-all-start.2 = ((bf16[16,64,512]{2,1,0:T(8,128)(2,1)}), bf16[16,64,512]{2,1,0:T(8,128)(2,1)S(1)}, u32[]{:S(2)}, u32[]{:S(2)}) async-start(bf16[16,64,512]{2,1,0:T(8,128)(2,1)} %shard_map.120), calls=%async_computation.2 | async-start | bytes 2097152 | tf_op jit(solution)/shard_map/all_to_all | solution.py:262
  82.8 1.7 %shard_map.121 = (bf16[128,2048]{1,0:T(8,128)(2,1)}, bf16[128,2048]{1,0:T(8,128)(2,1)}) custom-call(bf16[128,512]{1,0:T(8,128)(2,1)S(1)} %get-tuple-element.50.near_ref, bf16[128,512]{1,0:T(8,128)(2,1)S(1)} %collective-permute-done.3.far_ref, bf16[1024,512]{1,0:T(8,128)(2,1)S(1)} %bitcast.10, bf16[1024,512]{1,0:T(8,128)(2,1)S(1)} %collective-permute-done.1.weight_ref.other_ref), custom_call_target="tpu_custom_call" | custom-call | flops 536870912 | bytes 4194304 | tf_op jit(solution)/shard_map/pallas_call | solution.py:238
  84.5 2.7 %collective-permute-start.5 = (bf16[128,2048]{1,0:T(8,128)(2,1)}, bf16[128,2048]{1,0:T(8,128)(2,1)S(1)}, u32[]{:S(2)}, u32[]{:S(2)}) collective-permute-start(bf16[128,2048]{1,0:T(8,128)(2,1)} %get-tuple-element.53), channel_id=1, source_target_pairs={{0,128},{128,0},{1,129},{129,1},{2,130},{130,2},{3,131},{131,3},{4... | collective-permute-start | bytes 1572872 | tf_op jit(solution)/shard_map/ppermute | solution.py:254
  87.2 12.6 %all-to-all-done.2.parts_ref = bf16[16,64,512]{2,1,0:T(8,128)(2,1)S(1)} async-done(((bf16[16,64,512]{2,1,0:T(8,128)(2,1)}), bf16[16,64,512]{2,1,0:T(8,128)(2,1)S(1)}, u32[]{:S(2)}, u32[]{:S(2)}) %all-to-all-start.2) | async-done | bytes 1048608 | tf_op jit(solution)/shard_map/all_to_all | solution.py:262
  100.6 11.5 %all-to-all-start.3 = ((bf16[8,8,512]{2,1,0:T(8,128)(2,1)}), bf16[8,8,512]{2,1,0:T(8,128)(2,1)S(1)}, u32[]{:S(2)}, u32[]{:S(2)}) async-start(bf16[8,8,512]{2,1,0:T(8,128)(2,1)} %shard_map.123), calls=%async_computation.3 | async-start | bytes 131072 | tf_op jit(solution)/shard_map/all_to_all | solution.py:262
  112.0 2.9 %shard_map.122 = bf16[128,4096]{1,0:T(8,128)(2,1)} custom-call(s32[2]{0:T(128)S(1)} %pad_add_fusion.at_ref, bf16[128,2048]{1,0:T(8,128)(2,1)S(1)} %copy-done.7, bf16[128,2048]{1,0:T(8,128)(2,1)S(1)} %collective-permute-done.5.got_ref), custom_call_target="tpu_custom_call" | custom-call | flops 34359738368 | bytes 2097152 | tf_op jit(solution)/shard_map/pallas_call | solution.py:238
  (40 shorter events, 6.7 us)
Async XLA Ops:
  2.0 23.5 %all-to-all-start = ((bf16[8,8,512]{2,1,0:T(8,128)(2,1)}), bf16[8,8,512]{2,1,0:T(8,128)(2,1)S(1)}, u32[]{:S(2)}, u32[]{:S(2)}) async-start(bf16[8,8,512]{2,1,0:T(8,128)(2,1)} %shard_map.110), calls=%async_computation | async-start | bytes 131072 | tf_op jit(solution)/shard_map/all_to_all | solution.py:262
  22.0 16.3 %collective-permute-start = (bf16[128,2048]{1,0:T(8,128)(2,1)}, bf16[128,2048]{1,0:T(8,128)(2,1)S(1)}, u32[]{:S(2)}, u32[]{:S(2)}) collective-permute-start(bf16[128,2048]{1,0:T(8,128)(2,1)} %get-tuple-element.35), channel_id=1, source_target_pairs={{0,128},{128,0},{1,129},{129,1},{2,130},{130,2},{3,131},{131,3},{4... | collective-permute-start | bytes 1572872 | tf_op jit(solution)/shard_map/ppermute | solution.py:254
  26.6 8.0 %copy-start.1 = (bf16[128,4096]{1,0:T(8,128)(2,1)S(1)}, bf16[128,4096]{1,0:T(8,128)(2,1)}, u32[]{:S(2)}) copy-start(bf16[128,4096]{1,0:T(8,128)(2,1)} %queries_ref.1) | copy-start | bytes 3145732
  26.6 8.0 %copy-start.6 = (bf16[128,512]{1,0:T(8,128)(2,1)S(1)}, bf16[128,512]{1,0:T(8,128)(2,1)}, u32[]{:S(2)}) copy-start(bf16[128,512]{1,0:T(8,128)(2,1)} %keys_ref) | copy-start | bytes 393220
  26.6 21.8 %all-to-all-start.1 = ((bf16[16,64,512]{2,1,0:T(8,128)(2,1)}), bf16[16,64,512]{2,1,0:T(8,128)(2,1)S(1)}, u32[]{:S(2)}, u32[]{:S(2)}) async-start(bf16[16,64,512]{2,1,0:T(8,128)(2,1)} %shard_map.111), calls=%async_computation.1 | async-start | bytes 2097152 | tf_op jit(solution)/shard_map/all_to_all | solution.py:262
  33.5 0.7 copy-start.11
  34.5 3.8 %copy-start.4 = (bf16[128,1024]{1,0:T(8,128)(2,1)S(1)}, bf16[128,1024]{1,0:T(8,128)(2,1)}, u32[]{:S(2)}) copy-start(bf16[128,1024]{1,0:T(8,128)(2,1)} %get-tuple-element.39.near_other_ref.rows_ref) | copy-start | bytes 786436
  34.5 3.8 %copy-start.5 = (bf16[128,1024]{1,0:T(8,128)(2,1)S(1)}, bf16[128,1024]{1,0:T(8,128)(2,1)}, u32[]{:S(2)}) copy-start(bf16[128,1024]{1,0:T(8,128)(2,1)} %get-tuple-element.41.near_own_ref.near_ref) | copy-start | bytes 786436
  48.4 7.8 %collective-permute-start.1 = (bf16[1024,512]{1,0:T(8,128)(2,1)S(1)}, bf16[1024,512]{1,0:T(8,128)(2,1)S(1)}, u32[]{:S(2)}, u32[]{:S(2)}) collective-permute-start(bf16[1024,512]{1,0:T(8,128)(2,1)S(1)} %bitcast.8), channel_id=1, source_target_pairs={{0,16},{16,0},{1,17},{17,1},{2,18},{18,2},{3,19},{19,3},{4,20},{20... | collective-permute-start | bytes 3145736 | tf_op jit(solution)/shard_map/ppermute | solution.py:250
  56.5 6.7 %copy-start = (bf16[4,1024,128]{2,1,0:T(8,128)(2,1)S(1)}, bf16[4,1024,128]{2,1,0:T(8,128)(2,1)}, u32[]{:S(2)}) copy-start(bf16[4,1024,128]{2,1,0:T(8,128)(2,1)} %shard_map.114.probs_ref) | copy-start | bytes 3145732
  56.5 6.7 %collective-permute-start.2 = (bf16[128,512]{1,0:T(8,128)(2,1)S(1)}, bf16[128,512]{1,0:T(8,128)(2,1)S(1)}, u32[]{:S(2)}, u32[]{:S(2)}) collective-permute-start(bf16[128,512]{1,0:T(8,128)(2,1)S(1)} %shard_map.117), channel_id=1, source_target_pairs={{0,128},{128,0},{1,129},{129,1},{2,130},{130,2},{3,131},{131,3},{4... | collective-permute-start | bytes 393224 | tf_op jit(solution)/shard_map/ppermute | solution.py:254
  59.5 11.0 %copy-start.2 = (bf16[1024,256]{1,0:T(8,128)(2,1)S(1)}, bf16[1024,256]{1,0:T(8,128)(2,1)}, u32[]{:S(2)}) copy-start(bf16[1024,256]{1,0:T(8,128)(2,1)} %get-tuple-element.49.hidden_ref) | copy-start | bytes 1572868
  64.7 12.8 %copy-start.3 = (bf16[1024,256]{1,0:T(8,128)(2,1)S(1)}, bf16[1024,256]{1,0:T(8,128)(2,1)}, u32[]{:S(2)}) copy-start(bf16[1024,256]{1,0:T(8,128)(2,1)} %get-tuple-element.47.hidden_ref) | copy-start | bytes 1572868
  64.7 5.8 %collective-permute-start.3 = (bf16[128,512]{1,0:T(8,128)(2,1)S(1)}, bf16[128,512]{1,0:T(8,128)(2,1)S(1)}, u32[]{:S(2)}, u32[]{:S(2)}) collective-permute-start(bf16[128,512]{1,0:T(8,128)(2,1)S(1)} %get-tuple-element.50.near_ref), channel_id=1, source_target_pairs={{0,128},{128,0},{1,129},{129,1},{2,130},{130,2},{3,131},{131,3},{4... | collective-permute-start | bytes 393224 | tf_op jit(solution)/shard_map/ppermute | solution.py:254
  71.0 6.5 %collective-permute-start.4 = (bf16[1024,512]{1,0:T(8,128)(2,1)S(1)}, bf16[1024,512]{1,0:T(8,128)(2,1)S(1)}, u32[]{:S(2)}, u32[]{:S(2)}) collective-permute-start(bf16[1024,512]{1,0:T(8,128)(2,1)S(1)} %shard_map.119), channel_id=1, source_target_pairs={{0,16},{16,0},{1,17},{17,1},{2,18},{18,2},{3,19},{19,3},{4,20},{20... | collective-permute-start | bytes 3145736 | tf_op jit(solution)/shard_map/ppermute | solution.py:250
  79.1 20.7 %all-to-all-start.2 = ((bf16[16,64,512]{2,1,0:T(8,128)(2,1)}), bf16[16,64,512]{2,1,0:T(8,128)(2,1)S(1)}, u32[]{:S(2)}, u32[]{:S(2)}) async-start(bf16[16,64,512]{2,1,0:T(8,128)(2,1)} %shard_map.120), calls=%async_computation.2 | async-start | bytes 2097152 | tf_op jit(solution)/shard_map/all_to_all | solution.py:262
  84.5 27.6 %copy-start.7 = (bf16[128,2048]{1,0:T(8,128)(2,1)S(1)}, bf16[128,2048]{1,0:T(8,128)(2,1)}, u32[]{:S(2)}) copy-start(bf16[128,2048]{1,0:T(8,128)(2,1)} %get-tuple-element.52.keep_ref) | copy-start | bytes 1572868
  84.5 27.5 %collective-permute-start.5 = (bf16[128,2048]{1,0:T(8,128)(2,1)}, bf16[128,2048]{1,0:T(8,128)(2,1)S(1)}, u32[]{:S(2)}, u32[]{:S(2)}) collective-permute-start(bf16[128,2048]{1,0:T(8,128)(2,1)} %get-tuple-element.53), channel_id=1, source_target_pairs={{0,128},{128,0},{1,129},{129,1},{2,130},{130,2},{3,131},{131,3},{4... | collective-permute-start | bytes 1572872 | tf_op jit(solution)/shard_map/ppermute | solution.py:254
  100.6 14.6 %all-to-all-start.3 = ((bf16[8,8,512]{2,1,0:T(8,128)(2,1)}), bf16[8,8,512]{2,1,0:T(8,128)(2,1)S(1)}, u32[]{:S(2)}, u32[]{:S(2)}) async-start(bf16[8,8,512]{2,1,0:T(8,128)(2,1)} %shard_map.123), calls=%async_computation.3 | async-start | bytes 131072 | tf_op jit(solution)/shard_map/all_to_all | solution.py:262
  115.0 0.7 copy-start.8
  115.0 0.7 copy-start.9
  115.0 0.7 copy-start.10

commit v8 on v7

--- a/solution.py
+++ b/solution.py
@@ -144,11 +144,15 @@
     grad = jnp.concatenate([near_ref[...], far_ref[...]], axis=0)
     step = out_ref.shape[1]
     copies = []
-    for i in range(out_ref.shape[0]):
-        at = slice(i * step, (i + 1) * step)
+    blocks = 4
+    for i in range(0, out_ref.shape[0], blocks):
+        at = slice(i * step, (i + blocks) * step)
         part = jnp.dot(hidden_ref[at], grad, preferred_element_type=F32)
-        rows_ref[i] = (part + sent_ref[at].astype(F32)).astype(BF16)
-        copies.append(pltpu.make_async_copy(rows_ref.at[i], out_ref.at[i], sem_ref.at[i]))
+        part = (part + sent_ref[at].astype(F32)).astype(BF16)
+        for j in range(blocks):
+            rows_ref[i + j] = part[j * step : (j + 1) * step]
+        to = pl.ds(i, blocks)
+        copies.append(pltpu.make_async_copy(rows_ref.at[to], out_ref.at[to], sem_ref.at[i // blocks]))
         copies[-1].start()
     for copy in copies:
         copy.wait()
@@ -193,6 +197,13 @@
             expos = jnp.exp(scores - jnp.max(scores, axis=-1, keepdims=True))
             total = jnp.sum(expos, axis=-1, keepdims=True)
             out_ref[j, h * tok : (h + 1) * tok, :] = (expos / total).astype(BF16)
+
+
+def states_kernel(moment_ref, second_ref, master_ref, moment_out_ref, second_out_ref, master_out_ref, decay_ref):
+    moment_out_ref[...] = beta_one * moment_ref[...]
+    second_out_ref[...] = beta_two * second_ref[...]
+    master_out_ref[...] = master_ref[...]
+    decay_ref[...] = decay_rate * master_ref[...]
 
 
 def attend_kernel(near_ref, sent_ref, probs_ref, attended_ref, grad_ref, rows_ref, sem_ref):
@@ -377,18 +388,17 @@
         grad,
         grad_far,
         swap_core(part),
-        scratch=[pltpu.VMEM((PLANE, DEPTH * rows, kv), BF16), copies(PLANE)],
+        scratch=[pltpu.VMEM((PLANE, DEPTH * rows, kv), BF16), copies(PLANE // 4)],
         out=HBM,
     )
-    part, grad, grad_far = lax.optimization_barrier((part, grad, grad_far))
-
     keep, send = call(
         back_kernel, (block, block), 8 * tok * feats * kv, 4 << 20, grad, grad_far, weight, weight_other, late=(0,)
     )
+    part, keep, send = lax.optimization_barrier((part, keep, send))
     grad_hidden = call(
         join_kernel,
         jax.ShapeDtypeStruct((tok, width), BF16),
-        WEIGHTY,
+        8 * tok * 1024 * 1024,
         2 << 20,
         at,
         keep,
@@ -399,15 +409,21 @@
 
     part = exchange_plane(part)
     part = call(sum_kernel, jax.ShapeDtypeStruct((DEPTH, rows, kv), BF16), 0, 1 << 20, part)
+    part, grad_hidden, moment, second, master = lax.optimization_barrier(
+        (part, grad_hidden, moment, second, master)
+    )
     part = exchange_z(part, REDUCE_FIRST)
+    moment, second, master, decay = call(
+        states_kernel, (jax.ShapeDtypeStruct(master.shape, F32),) * 4, 0, 1 << 17, moment, second, master
+    )
     gradient = jnp.sum(part.astype(F32), axis=0) / F32(tok * 512)
 
-    moment_new = beta_one * moment + (1.0 - beta_one) * gradient
-    second_new = beta_two * second + (1.0 - beta_two) * gradient * gradient
+    moment_new = moment + (1.0 - beta_one) * gradient
+    second_new = second + (1.0 - beta_two) * gradient * gradient
     moment_hat = moment_new / (1.0 - beta_one**10)
     second_hat = second_new / (1.0 - beta_two**10)
     master_new = master - learn_rate * (
-        moment_hat / (jnp.sqrt(second_hat) + adam_eps) + decay_rate * master
+        moment_hat / (jnp.sqrt(second_hat) + adam_eps) + decay
     )
     return (attended, grad_hidden, master_new, moment_new, second_new)
 

time: 117 us -> 118 us (level)
  waiting for transfers between devices: 33.4 us -> 34.6 us
    ppermute x4, waiting for transfers between devices: 6.81 us -> 19.3 us  [swap_pair(): return lax.ppermute(array, 'zll', [(0, 1), (1, 0)])]
    all_to_all x4, waiting for transfers between devices: 22.5 us -> 12.8 us  [exchange(): lax.all_to_all(blocks, AXES, split_axis=0, concat_axis=0, axis_index_grou...]
    ppermute x2, waiting for transfers between devices: 4.08 us -> 2.57 us  [swap_core(): return lax.ppermute(array, 'c', [(0, 1), (1, 0)])]
    pallas_call x14 -> x15, Pallas kernels: 21.3 us -> 20.7 us  [call(): pl.pallas_call(kernel, out_shape=out_shape, in_specs=specs, out_specs=out...]
  transfers between devices with their start and end apart: 10 -> 10, of which waited for: 8 -> 8; matrix products, arithmetic and copies ran while one was open for 0% -> 0% of each run, Pallas kernels for 14% -> 13%
where the time goes in v8:
time: 118 us; the launch traced here: 117 us
  starting transfers between devices  58.6 us (50%)
  waiting for transfers between devices  34.6 us (29%)
  Pallas kernels  20.7 us (18%)
    all_to_all x4, starting transfers between devices, exchange(): lax.all_to_all(blocks, AXES, split_axis=0, concat_axis=0, axis_index_grou...  38.2 us
    pallas_call x15, Pallas kernels, call(): pl.pallas_call(kernel, out_shape=out_shape, in_specs=specs, out_specs=out...  20.7 us
    ppermute x4, waiting for transfers between devices, swap_pair(): return lax.ppermute(array, 'zll', [(0, 1), (1, 0)])  19.3 us
    all_to_all x4, waiting for transfers between devices, exchange(): lax.all_to_all(blocks, AXES, split_axis=0, concat_axis=0, axis_index_grou...  12.8 us
    ppermute x4, starting transfers between devices, swap_pair(): return lax.ppermute(array, 'zll', [(0, 1), (1, 0)])  10.5 us
    ppermute x2, starting transfers between devices, swap_core(): return lax.ppermute(array, 'c', [(0, 1), (1, 0)])  9.91 us
    ppermute x2, waiting for transfers between devices, swap_core(): return lax.ppermute(array, 'c', [(0, 1), (1, 0)])  2.57 us
  transfers between devices with their start and end apart: 10, of which 8 were waited for; matrix products, arithmetic and copies ran while one was open for 0% of the time, Pallas kernels for 13%

profile of v8, /device:TPU:1, one launch (start us, length us, event | category | flops | bytes accessed | tf_op | source)
XLA Modules:
  0.0 116.7 jit_solution(9587402916819832035)
XLA Ops:
  0.6 1.4 %shard_map.110 = bf16[8,8,512]{2,1,0:T(8,128)(2,1)} custom-call(f32[8,512]{1,0:T(8,128)} %master_ref.2), custom_call_target="tpu_custom_call" | custom-call | bytes 131072 | tf_op jit(solution)/shard_map/pallas_call | solution.py:249
  2.0 15.9 %all-to-all-start = ((bf16[8,8,512]{2,1,0:T(8,128)(2,1)}), bf16[8,8,512]{2,1,0:T(8,128)(2,1)S(1)}, u32[]{:S(2)}, u32[]{:S(2)}) async-start(bf16[8,8,512]{2,1,0:T(8,128)(2,1)} %shard_map.110), calls=%async_computation | async-start | bytes 131072 | tf_op jit(solution)/shard_map/all_to_all | solution.py:273
  18.0 4.0 %shard_map.112 = (bf16[128,1024]{1,0:T(8,128)(2,1)}, bf16[128,1024]{1,0:T(8,128)(2,1)}, bf16[128,2048]{1,0:T(8,128)(2,1)}) custom-call(s32[2]{0:T(128)S(1)} %pad_add_fusion.at_ref, bf16[128,4096]{1,0:T(8,128)(2,1)} %hidden_ref), custom_call_target="tpu_custom_call" | custom-call | flops 1073741824 | bytes 2097152 | tf_op jit(solution)/shard_map/pallas_call | solution.py:249
  22.0 2.6 %collective-permute-start = (bf16[128,2048]{1,0:T(8,128)(2,1)}, bf16[128,2048]{1,0:T(8,128)(2,1)S(1)}, u32[]{:S(2)}, u32[]{:S(2)}) collective-permute-start(bf16[128,2048]{1,0:T(8,128)(2,1)} %get-tuple-element.44), channel_id=1, source_target_pairs={{0,128},{128,0},{1,129},{129,1},{2,130},{130,2},{3,131},{131,3},{4... | collective-permute-start | bytes 1572872 | tf_op jit(solution)/shard_map/ppermute | solution.py:265
  26.6 6.9 %all-to-all-start.1 = ((bf16[16,64,512]{2,1,0:T(8,128)(2,1)}), bf16[16,64,512]{2,1,0:T(8,128)(2,1)S(1)}, u32[]{:S(2)}, u32[]{:S(2)}) async-start(bf16[16,64,512]{2,1,0:T(8,128)(2,1)} %shard_map.111), calls=%async_computation.1 | async-start | bytes 2097152 | tf_op jit(solution)/shard_map/all_to_all | solution.py:273
  34.6 3.8 %shard_map.114.probs_ref = bf16[4,1024,128]{2,1,0:T(8,128)(2,1)} custom-call(bf16[128,4096]{1,0:T(8,128)(2,1)S(1)} %copy-done.1, bf16[128,512]{1,0:T(8,128)(2,1)S(1)} %copy-done.6, s32[1,128]{1,0:T(1,128)S(1)} %bitcast.13, s32[128,1]{1,0:T(8,128)S(1)} %copy.13.seg_col_ref), custom_call_target="tpu_custom_call" | custom-call | flops 268435456 | bytes 8388608 | tf_op jit(solution)/shard_map/pallas_call | solution.py:249
  38.3 1.2 %shard_map.113 = (bf16[1024,256]{1,0:T(8,128)(2,1)}, bf16[1024,256]{1,0:T(8,128)(2,1)}) custom-call(bf16[128,1024]{1,0:T(8,128)(2,1)S(1)} %copy-done.5, bf16[128,1024]{1,0:T(8,128)(2,1)S(1)} %copy-done.4, bf16[128,2048]{1,0:T(8,128)(2,1)S(1)} %collective-permute-done.far_ref.rows_ref), custom_call_target="tpu_custom_call" | custom-call | flops 5726623232 | bytes 2097152 | tf_op jit(solution)/shard_map/pallas_call | solution.py:249
  39.5 8.8 %all-to-all-done.1 = bf16[16,64,512]{2,1,0:T(8,128)(2,1)S(1)} async-done(((bf16[16,64,512]{2,1,0:T(8,128)(2,1)}), bf16[16,64,512]{2,1,0:T(8,128)(2,1)S(1)}, u32[]{:S(2)}, u32[]{:S(2)}) %all-to-all-start.1) | async-done | bytes 1048608 | tf_op jit(solution)/shard_map/all_to_all | solution.py:273
  48.4 5.5 %collective-permute-start.1 = (bf16[1024,512]{1,0:T(8,128)(2,1)S(1)}, bf16[1024,512]{1,0:T(8,128)(2,1)S(1)}, u32[]{:S(2)}, u32[]{:S(2)}) collective-permute-start(bf16[1024,512]{1,0:T(8,128)(2,1)S(1)} %bitcast.8), channel_id=1, source_target_pairs={{0,16},{16,0},{1,17},{17,1},{2,18},{18,2},{3,19},{19,3},{4,20},{20... | collective-permute-start | bytes 3145736 | tf_op jit(solution)/shard_map/ppermute | solution.py:261
  54.3 1.8 %collective-permute-done.1.weight_ref.other_ref = bf16[1024,512]{1,0:T(8,128)(2,1)S(1)} collective-permute-done((bf16[1024,512]{1,0:T(8,128)(2,1)S(1)}, bf16[1024,512]{1,0:T(8,128)(2,1)S(1)}, u32[]{:S(2)}, u32[]{:S(2)}) %collective-permute-start.1) | collective-permute-done | bytes 1048608 | tf_op jit(solution)/shard_map/ppermute | solution.py:261
  56.5 2.7 %collective-permute-start.2 = (bf16[128,512]{1,0:T(8,128)(2,1)S(1)}, bf16[128,512]{1,0:T(8,128)(2,1)S(1)}, u32[]{:S(2)}, u32[]{:S(2)}) collective-permute-start(bf16[128,512]{1,0:T(8,128)(2,1)S(1)} %shard_map.117), channel_id=1, source_target_pairs={{0,128},{128,0},{1,129},{129,1},{2,130},{130,2},{3,131},{131,3},{4... | collective-permute-start | bytes 393224 | tf_op jit(solution)/shard_map/ppermute | solution.py:265
  59.5 3.7 %collective-permute-done.2.sent_ref = bf16[128,512]{1,0:T(8,128)(2,1)S(1)} collective-permute-done((bf16[128,512]{1,0:T(8,128)(2,1)S(1)}, bf16[128,512]{1,0:T(8,128)(2,1)S(1)}, u32[]{:S(2)}, u32[]{:S(2)}) %collective-permute-start.2) | collective-permute-done | bytes 131104 | tf_op jit(solution)/shard_map/ppermute | solution.py:265
  63.2 1.4 %shard_map.118 = (bf16[128,4096]{1,0:T(8,128)(2,1)}, bf16[128,512]{1,0:T(8,128)(2,1)S(1)}) custom-call(f32[128,512]{1,0:T(8,128)S(1)} %shard_map.116.near_ref, bf16[128,512]{1,0:T(8,128)(2,1)S(1)} %collective-permute-done.2.sent_ref, bf16[4,1024,128]{2,1,0:T(8,128)(2,1)S(1)} %copy-done), custom_call_target="tpu_custom_call" | custom-call | flops 268435456 | bytes 4194304 | tf_op jit(solution)/shard_map/pallas_call | solution.py:249
  64.7 2.6 %collective-permute-start.3 = (bf16[128,512]{1,0:T(8,128)(2,1)S(1)}, bf16[128,512]{1,0:T(8,128)(2,1)S(1)}, u32[]{:S(2)}, u32[]{:S(2)}) collective-permute-start(bf16[128,512]{1,0:T(8,128)(2,1)S(1)} %get-tuple-element.57.near_ref), channel_id=1, source_target_pairs={{0,128},{128,0},{1,129},{129,1},{2,130},{130,2},{3,131},{131,3},{4... | collective-permute-start | bytes 393224 | tf_op jit(solution)/shard_map/ppermute | solution.py:265
  67.2 3.1 %collective-permute-done.3.far_ref = bf16[128,512]{1,0:T(8,128)(2,1)S(1)} collective-permute-done((bf16[128,512]{1,0:T(8,128)(2,1)S(1)}, bf16[128,512]{1,0:T(8,128)(2,1)S(1)}, u32[]{:S(2)}, u32[]{:S(2)}) %collective-permute-start.3) | collective-permute-done | bytes 131104 | tf_op jit(solution)/shard_map/ppermute | solution.py:265
  70.8 4.4 %collective-permute-start.4 = (bf16[1024,512]{1,0:T(8,128)(2,1)S(1)}, bf16[1024,512]{1,0:T(8,128)(2,1)S(1)}, u32[]{:S(2)}, u32[]{:S(2)}) collective-permute-start(bf16[1024,512]{1,0:T(8,128)(2,1)S(1)} %shard_map.119), channel_id=1, source_target_pairs={{0,16},{16,0},{1,17},{17,1},{2,18},{18,2},{3,19},{19,3},{4,20},{20... | collective-permute-start | bytes 3145736 | tf_op jit(solution)/shard_map/ppermute | solution.py:261
  75.2 1.5 %shard_map.121 = (bf16[128,2048]{1,0:T(8,128)(2,1)}, bf16[128,2048]{1,0:T(8,128)(2,1)S(1)}) custom-call(bf16[128,512]{1,0:T(8,128)(2,1)S(1)} %get-tuple-element.57.near_ref, bf16[128,512]{1,0:T(8,128)(2,1)S(1)} %collective-permute-done.3.far_ref, bf16[1024,512]{1,0:T(8,128)(2,1)S(1)} %bitcast.10, ...), custom_call_target="tpu_custom_call" | custom-call | flops 536870912 | bytes 4194304 | tf_op jit(solution)/shard_map/pallas_call | solution.py:249
  77.5 1.3 %shard_map.120 = bf16[16,64,512]{2,1,0:T(8,128)(2,1)} custom-call(bf16[1024,256]{1,0:T(8,128)(2,1)S(1)} %copy-done.3, bf16[128,512]{1,0:T(8,128)(2,1)S(1)} %get-tuple-element.57.near_ref, bf16[128,512]{1,0:T(8,128)(2,1)S(1)} %collective-permute-done.3.far_ref, bf16[1024,512]{1,0:T(8,128)(2,1)S(1)} %collective-permute-done.4.sent_ref), custom_call_target="tpu_custom_call" | custom-call | flops 268435456 | bytes 2097152 | tf_op jit(solution)/shard_map/pallas_call | solution.py:249
  78.8 3.8 %all-to-all-start.2 = ((bf16[16,64,512]{2,1,0:T(8,128)(2,1)}), bf16[16,64,512]{2,1,0:T(8,128)(2,1)S(1)}, u32[]{:S(2)}, u32[]{:S(2)}) async-start(bf16[16,64,512]{2,1,0:T(8,128)(2,1)} %shard_map.120), calls=%async_computation.2 | async-start | bytes 2097152 | tf_op jit(solution)/shard_map/all_to_all | solution.py:273
  82.6 2.6 %collective-permute-start.5 = (bf16[128,2048]{1,0:T(8,128)(2,1)S(1)}, bf16[128,2048]{1,0:T(8,128)(2,1)S(1)}, u32[]{:S(2)}, u32[]{:S(2)}) collective-permute-start(bf16[128,2048]{1,0:T(8,128)(2,1)S(1)} %get-tuple-element.63), channel_id=1, source_target_pairs={{0,128},{128,0},{1,129},{129,1},{2,130},{130,2},{3,131},{131,3},{4... | collective-permute-start | bytes 1572872 | tf_op jit(solution)/shard_map/ppermute | solution.py:265
  85.2 12.4 %collective-permute-done.5.got_ref = bf16[128,2048]{1,0:T(8,128)(2,1)S(1)} collective-permute-done((bf16[128,2048]{1,0:T(8,128)(2,1)S(1)}, bf16[128,2048]{1,0:T(8,128)(2,1)S(1)}, u32[]{:S(2)}, u32[]{:S(2)}) %collective-permute-start.5) | collective-permute-done | bytes 524320 | tf_op jit(solution)/shard_map/ppermute | solution.py:265
  97.6 2.9 %shard_map.123 = bf16[128,4096]{1,0:T(8,128)(2,1)} custom-call(s32[2]{0:T(128)S(1)} %pad_add_fusion.at_ref, bf16[128,2048]{1,0:T(8,128)(2,1)S(1)} %copy-done.10, bf16[128,2048]{1,0:T(8,128)(2,1)S(1)} %collective-permute-done.5.got_ref), custom_call_target="tpu_custom_call" | custom-call | flops 1073741824 | bytes 2097152 | tf_op jit(solution)/shard_map/pallas_call | solution.py:249
  101.3 11.6 %all-to-all-start.3 = ((bf16[8,8,512]{2,1,0:T(8,128)(2,1)}), bf16[8,8,512]{2,1,0:T(8,128)(2,1)S(1)}, u32[]{:S(2)}, u32[]{:S(2)}) async-start(bf16[8,8,512]{2,1,0:T(8,128)(2,1)} %shard_map.122), calls=%async_computation.3 | async-start | bytes 131072 | tf_op jit(solution)/shard_map/all_to_all | solution.py:273
  112.9 3.1 %all-to-all-done.3 = bf16[8,8,512]{2,1,0:T(8,128)(2,1)S(1)} async-done(((bf16[8,8,512]{2,1,0:T(8,128)(2,1)}), bf16[8,8,512]{2,1,0:T(8,128)(2,1)S(1)}, u32[]{:S(2)}, u32[]{:S(2)}) %all-to-all-start.3) | async-done | bytes 65568 | tf_op jit(solution)/shard_map/all_to_all | solution.py:273
  (41 shorter events, 6.7 us)
Async XLA Ops:
  2.0 23.5 %all-to-all-start = ((bf16[8,8,512]{2,1,0:T(8,128)(2,1)}), bf16[8,8,512]{2,1,0:T(8,128)(2,1)S(1)}, u32[]{:S(2)}, u32[]{:S(2)}) async-start(bf16[8,8,512]{2,1,0:T(8,128)(2,1)} %shard_map.110), calls=%async_computation | async-start | bytes 131072 | tf_op jit(solution)/shard_map/all_to_all | solution.py:273
  22.0 16.3 %collective-permute-start = (bf16[128,2048]{1,0:T(8,128)(2,1)}, bf16[128,2048]{1,0:T(8,128)(2,1)S(1)}, u32[]{:S(2)}, u32[]{:S(2)}) collective-permute-start(bf16[128,2048]{1,0:T(8,128)(2,1)} %get-tuple-element.44), channel_id=1, source_target_pairs={{0,128},{128,0},{1,129},{129,1},{2,130},{130,2},{3,131},{131,3},{4... | collective-permute-start | bytes 1572872 | tf_op jit(solution)/shard_map/ppermute | solution.py:265
  26.6 8.0 %copy-start.1 = (bf16[128,4096]{1,0:T(8,128)(2,1)S(1)}, bf16[128,4096]{1,0:T(8,128)(2,1)}, u32[]{:S(2)}) copy-start(bf16[128,4096]{1,0:T(8,128)(2,1)} %queries_ref.1) | copy-start | bytes 3145732
  26.6 8.0 %copy-start.6 = (bf16[128,512]{1,0:T(8,128)(2,1)S(1)}, bf16[128,512]{1,0:T(8,128)(2,1)}, u32[]{:S(2)}) copy-start(bf16[128,512]{1,0:T(8,128)(2,1)} %keys_ref) | copy-start | bytes 393220
  26.6 21.8 %all-to-all-start.1 = ((bf16[16,64,512]{2,1,0:T(8,128)(2,1)}), bf16[16,64,512]{2,1,0:T(8,128)(2,1)S(1)}, u32[]{:S(2)}, u32[]{:S(2)}) async-start(bf16[16,64,512]{2,1,0:T(8,128)(2,1)} %shard_map.111), calls=%async_computation.1 | async-start | bytes 2097152 | tf_op jit(solution)/shard_map/all_to_all | solution.py:273
  33.5 0.7 copy-start.11
  34.5 3.8 %copy-start.4 = (bf16[128,1024]{1,0:T(8,128)(2,1)S(1)}, bf16[128,1024]{1,0:T(8,128)(2,1)}, u32[]{:S(2)}) copy-start(bf16[128,1024]{1,0:T(8,128)(2,1)} %get-tuple-element.48.near_other_ref.rows_ref) | copy-start | bytes 786436
  34.5 3.8 %copy-start.5 = (bf16[128,1024]{1,0:T(8,128)(2,1)S(1)}, bf16[128,1024]{1,0:T(8,128)(2,1)}, u32[]{:S(2)}) copy-start(bf16[128,1024]{1,0:T(8,128)(2,1)} %get-tuple-element.50.near_own_ref.near_ref) | copy-start | bytes 786436
  48.4 7.8 %collective-permute-start.1 = (bf16[1024,512]{1,0:T(8,128)(2,1)S(1)}, bf16[1024,512]{1,0:T(8,128)(2,1)S(1)}, u32[]{:S(2)}, u32[]{:S(2)}) collective-permute-start(bf16[1024,512]{1,0:T(8,128)(2,1)S(1)} %bitcast.8), channel_id=1, source_target_pairs={{0,16},{16,0},{1,17},{17,1},{2,18},{18,2},{3,19},{19,3},{4,20},{20... | collective-permute-start | bytes 3145736 | tf_op jit(solution)/shard_map/ppermute | solution.py:261
  56.5 6.7 %copy-start = (bf16[4,1024,128]{2,1,0:T(8,128)(2,1)S(1)}, bf16[4,1024,128]{2,1,0:T(8,128)(2,1)}, u32[]{:S(2)}) copy-start(bf16[4,1024,128]{2,1,0:T(8,128)(2,1)} %shard_map.114.probs_ref) | copy-start | bytes 3145732
  56.5 6.7 %collective-permute-start.2 = (bf16[128,512]{1,0:T(8,128)(2,1)S(1)}, bf16[128,512]{1,0:T(8,128)(2,1)S(1)}, u32[]{:S(2)}, u32[]{:S(2)}) collective-permute-start(bf16[128,512]{1,0:T(8,128)(2,1)S(1)} %shard_map.117), channel_id=1, source_target_pairs={{0,128},{128,0},{1,129},{129,1},{2,130},{130,2},{3,131},{131,3},{4... | collective-permute-start | bytes 393224 | tf_op jit(solution)/shard_map/ppermute | solution.py:265
  59.5 10.8 %copy-start.2 = (bf16[1024,256]{1,0:T(8,128)(2,1)S(1)}, bf16[1024,256]{1,0:T(8,128)(2,1)}, u32[]{:S(2)}) copy-start(bf16[1024,256]{1,0:T(8,128)(2,1)} %get-tuple-element.58.hidden_ref) | copy-start | bytes 1572868
  64.7 5.7 %collective-permute-start.3 = (bf16[128,512]{1,0:T(8,128)(2,1)S(1)}, bf16[128,512]{1,0:T(8,128)(2,1)S(1)}, u32[]{:S(2)}, u32[]{:S(2)}) collective-permute-start(bf16[128,512]{1,0:T(8,128)(2,1)S(1)} %get-tuple-element.57.near_ref), channel_id=1, source_target_pairs={{0,128},{128,0},{1,129},{129,1},{2,130},{130,2},{3,131},{131,3},{4... | collective-permute-start | bytes 393224 | tf_op jit(solution)/shard_map/ppermute | solution.py:265
  70.8 6.7 %copy-start.3 = (bf16[1024,256]{1,0:T(8,128)(2,1)S(1)}, bf16[1024,256]{1,0:T(8,128)(2,1)}, u32[]{:S(2)}) copy-start(bf16[1024,256]{1,0:T(8,128)(2,1)} %get-tuple-element.56.hidden_ref) | copy-start | bytes 1572868
  70.8 6.7 %collective-permute-start.4 = (bf16[1024,512]{1,0:T(8,128)(2,1)S(1)}, bf16[1024,512]{1,0:T(8,128)(2,1)S(1)}, u32[]{:S(2)}, u32[]{:S(2)}) collective-permute-start(bf16[1024,512]{1,0:T(8,128)(2,1)S(1)} %shard_map.119), channel_id=1, source_target_pairs={{0,16},{16,0},{1,17},{17,1},{2,18},{18,2},{3,19},{19,3},{4,20},{20... | collective-permute-start | bytes 3145736 | tf_op jit(solution)/shard_map/ppermute | solution.py:261
  78.8 18.9 %copy-start.10 = (bf16[128,2048]{1,0:T(8,128)(2,1)S(1)}, bf16[128,2048]{1,0:T(8,128)(2,1)}, u32[]{:S(2)}) copy-start(bf16[128,2048]{1,0:T(8,128)(2,1)} %get-tuple-element.62.keep_ref) | copy-start | bytes 1572868
  78.8 21.8 %all-to-all-start.2 = ((bf16[16,64,512]{2,1,0:T(8,128)(2,1)}), bf16[16,64,512]{2,1,0:T(8,128)(2,1)S(1)}, u32[]{:S(2)}, u32[]{:S(2)}) async-start(bf16[16,64,512]{2,1,0:T(8,128)(2,1)} %shard_map.120), calls=%async_computation.2 | async-start | bytes 2097152 | tf_op jit(solution)/shard_map/all_to_all | solution.py:273
  82.6 15.0 %collective-permute-start.5 = (bf16[128,2048]{1,0:T(8,128)(2,1)S(1)}, bf16[128,2048]{1,0:T(8,128)(2,1)S(1)}, u32[]{:S(2)}, u32[]{:S(2)}) collective-permute-start(bf16[128,2048]{1,0:T(8,128)(2,1)S(1)} %get-tuple-element.63), channel_id=1, source_target_pairs={{0,128},{128,0},{1,129},{129,1},{2,130},{130,2},{3,131},{131,3},{4... | collective-permute-start | bytes 1572872 | tf_op jit(solution)/shard_map/ppermute | solution.py:265
  101.3 11.6 %copy-start.7 = (f32[8,512]{1,0:T(8,128)S(1)}, f32[8,512]{1,0:T(8,128)}, u32[]{:S(2)}) copy-start(f32[8,512]{1,0:T(8,128)} %master_ref.2) | copy-start | bytes 49156
  101.3 11.6 %copy-start.8 = (f32[8,512]{1,0:T(8,128)S(1)}, f32[8,512]{1,0:T(8,128)}, u32[]{:S(2)}) copy-start(f32[8,512]{1,0:T(8,128)} %moment_ref) | copy-start | bytes 49156
  101.3 11.6 %copy-start.9 = (f32[8,512]{1,0:T(8,128)S(1)}, f32[8,512]{1,0:T(8,128)}, u32[]{:S(2)}) copy-start(f32[8,512]{1,0:T(8,128)} %second_ref) | copy-start | bytes 49156
  101.3 14.7 %all-to-all-start.3 = ((bf16[8,8,512]{2,1,0:T(8,128)(2,1)}), bf16[8,8,512]{2,1,0:T(8,128)(2,1)S(1)}, u32[]{:S(2)}, u32[]{:S(2)}) async-start(bf16[8,8,512]{2,1,0:T(8,128)(2,1)} %shard_map.122), calls=%async_computation.3 | async-start | bytes 131072 | tf_op jit(solution)/shard_map/all_to_all | solution.py:273

commit v9 on v8

--- a/solution.py
+++ b/solution.py
@@ -24,7 +24,7 @@
 ROW_SPEC = P(("zh", "y", "zlh", "zll", "x", "c"), None)
 DEPTH = 8
 PLANE = 16
-GATHER_FIRST = 3
+GATHER_FIRST = 6
 REDUCE_FIRST = 2
 
 F32 = jnp.float32
@@ -180,7 +180,7 @@
         out_ref[z ^ GATHER_FIRST ^ REDUCE_FIRST] = total[z * rows : (z + 1) * rows]
 
 
-def probs_kernel(queries_ref, keys_ref, seg_row_ref, seg_col_ref, out_ref):
+def probs_kernel(queries_ref, keys_ref, seg_row_ref, seg_col_ref, out_ref, turned_ref):
     tok = queries_ref.shape[0]
     rows = lax.broadcasted_iota(jnp.int32, (tok, tok), 0)
     cols = lax.broadcasted_iota(jnp.int32, (tok, tok), 1)
@@ -196,7 +196,9 @@
             scores = jnp.where(allowed, scores * scale, F32(-1000000000.0))
             expos = jnp.exp(scores - jnp.max(scores, axis=-1, keepdims=True))
             total = jnp.sum(expos, axis=-1, keepdims=True)
-            out_ref[j, h * tok : (h + 1) * tok, :] = (expos / total).astype(BF16)
+            probs = (expos / total).astype(BF16)
+            out_ref[j, h * tok : (h + 1) * tok, :] = probs
+            turned_ref[j, :, h * tok : (h + 1) * tok] = probs.T
 
 
 def states_kernel(moment_ref, second_ref, master_ref, moment_out_ref, second_out_ref, master_out_ref, decay_ref):
@@ -206,7 +208,7 @@
     decay_ref[...] = decay_rate * master_ref[...]
 
 
-def attend_kernel(near_ref, sent_ref, probs_ref, attended_ref, grad_ref, rows_ref, sem_ref):
+def attend_kernel(near_ref, sent_ref, probs_ref, turned_ref, attended_ref, grad_ref, rows_ref, sem_ref):
     tok = near_ref.shape[0]
     wide = GROUPS * HD
     copies = []
@@ -220,9 +222,7 @@
             pltpu.make_async_copy(rows_ref.at[j], attended_ref.at[:, j * wide : (j + 1) * wide], sem_ref.at[j])
         )
         copies[-1].start()
-        grad_ref[:, cols] = lax.dot_general(
-            probs_ref[j], attended, (((0,), (0,)), ((), ())), preferred_element_type=F32
-        ).astype(BF16)
+        grad_ref[:, cols] = jnp.dot(turned_ref[j], attended, preferred_element_type=F32).astype(BF16)
     for copy in copies:
         copy.wait()
 
@@ -333,23 +333,26 @@
 
     ends = jnp.cumsum(lengths[0])
     seg = jnp.sum((jnp.arange(tok, dtype=jnp.int32)[:, None] >= ends[None, :]).astype(jnp.int32), axis=1)
-    (probs,) = call(
+    probs, turned = call(
         probs_kernel,
-        (jax.ShapeDtypeStruct((VH, GROUPS * tok, tok), BF16),),
+        (
+            jax.ShapeDtypeStruct((VH, GROUPS * tok, tok), BF16),
+            jax.ShapeDtypeStruct((VH, tok, GROUPS * tok), BF16),
+        ),
         4 * tok * tok * QH * HD,
         8 << 20,
         queries,
         keys,
         seg[None, :],
         seg[:, None],
-        late=(0,),
+        late=(0, 1),
     )
     flipped = jax.ShapeDtypeStruct((feats, 2 * tok), BF16)
     columns_own, columns_other = call(
         flip_kernel, (flipped, flipped), WEIGHTY // 6, 2 << 20, near_own, near_other, far, late=(0, 1)
     )
-    weight, near_own, near_other, far, columns_own, columns_other, probs = lax.optimization_barrier(
-        (weight, near_own, near_other, far, columns_own, columns_other, probs)
+    weight, near_own, near_other, far, columns_own, columns_other, probs, turned = lax.optimization_barrier(
+        (weight, near_own, near_other, far, columns_own, columns_other, probs, turned)
     )
     weight_other = swap_core(weight)
 
@@ -365,6 +368,7 @@
         near,
         sent,
         probs,
+        turned,
         scratch=[pltpu.VMEM((VH, tok, GROUPS * HD), BF16), copies(VH)],
         out=(HBM, VMEM),
     )
@@ -394,11 +398,16 @@
     keep, send = call(
         back_kernel, (block, block), 8 * tok * feats * kv, 4 << 20, grad, grad_far, weight, weight_other, late=(0,)
     )
-    part, keep, send = lax.optimization_barrier((part, keep, send))
+    part, keep, send, moment, second, master = lax.optimization_barrier(
+        (part, keep, send, moment, second, master)
+    )
+    moment, second, master, decay = call(
+        states_kernel, (jax.ShapeDtypeStruct(master.shape, F32),) * 4, 0, 1 << 17, moment, second, master
+    )
     grad_hidden = call(
         join_kernel,
         jax.ShapeDtypeStruct((tok, width), BF16),
-        8 * tok * 1024 * 1024,
+        WEIGHTY,
         2 << 20,
         at,
         keep,
@@ -409,13 +418,7 @@
 
     part = exchange_plane(part)
     part = call(sum_kernel, jax.ShapeDtypeStruct((DEPTH, rows, kv), BF16), 0, 1 << 20, part)
-    part, grad_hidden, moment, second, master = lax.optimization_barrier(
-        (part, grad_hidden, moment, second, master)
-    )
     part = exchange_z(part, REDUCE_FIRST)
-    moment, second, master, decay = call(
-        states_kernel, (jax.ShapeDtypeStruct(master.shape, F32),) * 4, 0, 1 << 17, moment, second, master
-    )
     gradient = jnp.sum(part.astype(F32), axis=0) / F32(tok * 512)
 
     moment_new = moment + (1.0 - beta_one) * gradient

time: 118 us -> 116 us (0.983)
  waiting for transfers between devices: 34.6 us -> 31.8 us
    ppermute x4, waiting for transfers between devices: 19.3 us -> 6.7 us  [swap_pair(): return lax.ppermute(array, 'zll', [(0, 1), (1, 0)])]
    all_to_all x4, waiting for transfers between devices: 12.8 us -> 22.5 us  [exchange(): lax.all_to_all(blocks, AXES, split_axis=0, concat_axis=0, axis_index_grou...]
  transfers between devices with their start and end apart: 10 -> 10, of which waited for: 8 -> 6; matrix products, arithmetic and copies ran while one was open for 0% -> 0% of each run, Pallas kernels for 13% -> 15%
where the time goes in v9:
time: 116 us; the launch traced here: 115 us
  starting transfers between devices  59 us (51%)
  waiting for transfers between devices  31.8 us (27%)
  Pallas kernels  21.8 us (19%)
    all_to_all x4, starting transfers between devices, exchange(): lax.all_to_all(blocks, AXES, split_axis=0, concat_axis=0, axis_index_grou...  39 us
    all_to_all x4, waiting for transfers between devices, exchange(): lax.all_to_all(blocks, AXES, split_axis=0, concat_axis=0, axis_index_grou...  22.5 us
    pallas_call x15, Pallas kernels, call(): pl.pallas_call(kernel, out_shape=out_shape, in_specs=specs, out_specs=out...  21.8 us
    ppermute x4, starting transfers between devices, swap_pair(): return lax.ppermute(array, 'zll', [(0, 1), (1, 0)])  10.7 us
    ppermute x2, starting transfers between devices, swap_core(): return lax.ppermute(array, 'c', [(0, 1), (1, 0)])  9.31 us
    ppermute x4, waiting for transfers between devices, swap_pair(): return lax.ppermute(array, 'zll', [(0, 1), (1, 0)])  6.7 us
    ppermute x2, waiting for transfers between devices, swap_core(): return lax.ppermute(array, 'c', [(0, 1), (1, 0)])  2.55 us
  transfers between devices with their start and end apart: 10, of which 6 were waited for; matrix products, arithmetic and copies ran while one was open for 0% of the time, Pallas kernels for 15%

profile of v9, /device:TPU:1, one launch (start us, length us, event | category | flops | bytes accessed | tf_op | source)
XLA Modules:
  0.0 115.3 jit_solution(17745134397795593981)
XLA Ops:
  0.6 1.4 %shard_map.110 = bf16[8,8,512]{2,1,0:T(8,128)(2,1)} custom-call(f32[8,512]{1,0:T(8,128)} %master_ref.2), custom_call_target="tpu_custom_call" | custom-call | bytes 131072 | tf_op jit(solution)/shard_map/pallas_call | solution.py:249
  2.0 16.9 %all-to-all-start = ((bf16[8,8,512]{2,1,0:T(8,128)(2,1)}), bf16[8,8,512]{2,1,0:T(8,128)(2,1)S(1)}, u32[]{:S(2)}, u32[]{:S(2)}) async-start(bf16[8,8,512]{2,1,0:T(8,128)(2,1)} %shard_map.110), calls=%async_computation | async-start | bytes 131072 | tf_op jit(solution)/shard_map/all_to_all | solution.py:273
  18.9 4.0 %shard_map.112 = (bf16[128,1024]{1,0:T(8,128)(2,1)}, bf16[128,1024]{1,0:T(8,128)(2,1)}, bf16[128,2048]{1,0:T(8,128)(2,1)}) custom-call(s32[2]{0:T(128)S(1)} %pad_add_fusion.at_ref, bf16[128,4096]{1,0:T(8,128)(2,1)} %hidden_ref), custom_call_target="tpu_custom_call" | custom-call | flops 1073741824 | bytes 2097152 | tf_op jit(solution)/shard_map/pallas_call | solution.py:249
  22.9 2.6 %collective-permute-start = (bf16[128,2048]{1,0:T(8,128)(2,1)}, bf16[128,2048]{1,0:T(8,128)(2,1)S(1)}, u32[]{:S(2)}, u32[]{:S(2)}) collective-permute-start(bf16[128,2048]{1,0:T(8,128)(2,1)} %get-tuple-element.45), channel_id=1, source_target_pairs={{0,128},{128,0},{1,129},{129,1},{2,130},{130,2},{3,131},{131,3},{4... | collective-permute-start | bytes 1572872 | tf_op jit(solution)/shard_map/ppermute | solution.py:265
  25.6 1.1 shard_map.111
  26.7 6.9 %all-to-all-start.1 = ((bf16[16,64,512]{2,1,0:T(8,128)(2,1)}), bf16[16,64,512]{2,1,0:T(8,128)(2,1)S(1)}, u32[]{:S(2)}, u32[]{:S(2)}) async-start(bf16[16,64,512]{2,1,0:T(8,128)(2,1)} %shard_map.111), calls=%async_computation.1 | async-start | bytes 2097152 | tf_op jit(solution)/shard_map/all_to_all | solution.py:273
  34.7 4.8 %shard_map.114 = (bf16[4,1024,128]{2,1,0:T(8,128)(2,1)}, bf16[4,128,1024]{2,1,0:T(8,128)(2,1)}) custom-call(bf16[128,4096]{1,0:T(8,128)(2,1)S(1)} %copy-done, bf16[128,512]{1,0:T(8,128)(2,1)S(1)} %copy-done.7, s32[1,128]{1,0:T(1,128)S(1)} %bitcast.13, s32[128,1]{1,0:T(8,128)S(1)} %copy.13.seg_col_ref), custom_call_target="tpu_custom_call" | custom-call | flops 268435456 | bytes 8388608 | tf_op jit(solution)/shard_map/pallas_call | solution.py:249
  39.5 1.2 %shard_map.113 = (bf16[1024,256]{1,0:T(8,128)(2,1)}, bf16[1024,256]{1,0:T(8,128)(2,1)}) custom-call(bf16[128,1024]{1,0:T(8,128)(2,1)S(1)} %copy-done.6, bf16[128,1024]{1,0:T(8,128)(2,1)S(1)} %copy-done.5, bf16[128,2048]{1,0:T(8,128)(2,1)S(1)} %collective-permute-done.far_ref.rows_ref), custom_call_target="tpu_custom_call" | custom-call | flops 5726623232 | bytes 2097152 | tf_op jit(solution)/shard_map/pallas_call | solution.py:249
  40.7 8.2 %all-to-all-done.1 = bf16[16,64,512]{2,1,0:T(8,128)(2,1)S(1)} async-done(((bf16[16,64,512]{2,1,0:T(8,128)(2,1)}), bf16[16,64,512]{2,1,0:T(8,128)(2,1)S(1)}, u32[]{:S(2)}, u32[]{:S(2)}) %all-to-all-start.1) | async-done | bytes 1048608 | tf_op jit(solution)/shard_map/all_to_all | solution.py:273
  48.9 4.9 %collective-permute-start.1 = (bf16[1024,512]{1,0:T(8,128)(2,1)S(1)}, bf16[1024,512]{1,0:T(8,128)(2,1)S(1)}, u32[]{:S(2)}, u32[]{:S(2)}) collective-permute-start(bf16[1024,512]{1,0:T(8,128)(2,1)S(1)} %bitcast.8), channel_id=1, source_target_pairs={{0,16},{16,0},{1,17},{17,1},{2,18},{18,2},{3,19},{19,3},{4,20},{20... | collective-permute-start | bytes 3145736 | tf_op jit(solution)/shard_map/ppermute | solution.py:261
  54.3 1.8 %collective-permute-done.1.weight_ref.other_ref = bf16[1024,512]{1,0:T(8,128)(2,1)S(1)} collective-permute-done((bf16[1024,512]{1,0:T(8,128)(2,1)S(1)}, bf16[1024,512]{1,0:T(8,128)(2,1)S(1)}, u32[]{:S(2)}, u32[]{:S(2)}) %collective-permute-start.1) | collective-permute-done | bytes 1048608 | tf_op jit(solution)/shard_map/ppermute | solution.py:261
  56.4 2.8 %collective-permute-start.2 = (bf16[128,512]{1,0:T(8,128)(2,1)S(1)}, bf16[128,512]{1,0:T(8,128)(2,1)S(1)}, u32[]{:S(2)}, u32[]{:S(2)}) collective-permute-start(bf16[128,512]{1,0:T(8,128)(2,1)S(1)} %shard_map.117), channel_id=1, source_target_pairs={{0,128},{128,0},{1,129},{129,1},{2,130},{130,2},{3,131},{131,3},{4... | collective-permute-start | bytes 393224 | tf_op jit(solution)/shard_map/ppermute | solution.py:265
  59.5 3.6 %collective-permute-done.2.sent_ref = bf16[128,512]{1,0:T(8,128)(2,1)S(1)} collective-permute-done((bf16[128,512]{1,0:T(8,128)(2,1)S(1)}, bf16[128,512]{1,0:T(8,128)(2,1)S(1)}, u32[]{:S(2)}, u32[]{:S(2)}) %collective-permute-start.2) | collective-permute-done | bytes 131104 | tf_op jit(solution)/shard_map/ppermute | solution.py:265
  63.2 1.4 %shard_map.118 = (bf16[128,4096]{1,0:T(8,128)(2,1)}, bf16[128,512]{1,0:T(8,128)(2,1)S(1)}) custom-call(f32[128,512]{1,0:T(8,128)S(1)} %shard_map.116.near_ref, bf16[128,512]{1,0:T(8,128)(2,1)S(1)} %collective-permute-done.2.sent_ref, bf16[4,1024,128]{2,1,0:T(8,128)(2,1)S(1)} %copy-done.1, bf16[4,128,1024]{2,1,0:T(8,128)(2,1)S(1)} %copy-done.2), custom_call_target="tpu_custom_call" | custom-call | flops 268435456 | bytes 4194304 | tf_op jit(solution)/shard_map/pallas_call | solution.py:249
  64.6 2.6 %collective-permute-start.3 = (bf16[128,512]{1,0:T(8,128)(2,1)S(1)}, bf16[128,512]{1,0:T(8,128)(2,1)S(1)}, u32[]{:S(2)}, u32[]{:S(2)}) collective-permute-start(bf16[128,512]{1,0:T(8,128)(2,1)S(1)} %get-tuple-element.61.near_ref), channel_id=1, source_target_pairs={{0,128},{128,0},{1,129},{129,1},{2,130},{130,2},{3,131},{131,3},{4... | collective-permute-start | bytes 393224 | tf_op jit(solution)/shard_map/ppermute | solution.py:265
  67.2 3.1 %collective-permute-done.3.far_ref = bf16[128,512]{1,0:T(8,128)(2,1)S(1)} collective-permute-done((bf16[128,512]{1,0:T(8,128)(2,1)S(1)}, bf16[128,512]{1,0:T(8,128)(2,1)S(1)}, u32[]{:S(2)}, u32[]{:S(2)}) %collective-permute-start.3) | collective-permute-done | bytes 131104 | tf_op jit(solution)/shard_map/ppermute | solution.py:265
  70.8 4.4 %collective-permute-start.4 = (bf16[1024,512]{1,0:T(8,128)(2,1)S(1)}, bf16[1024,512]{1,0:T(8,128)(2,1)S(1)}, u32[]{:S(2)}, u32[]{:S(2)}) collective-permute-start(bf16[1024,512]{1,0:T(8,128)(2,1)S(1)} %shard_map.119), channel_id=1, source_target_pairs={{0,16},{16,0},{1,17},{17,1},{2,18},{18,2},{3,19},{19,3},{4,20},{20... | collective-permute-start | bytes 3145736 | tf_op jit(solution)/shard_map/ppermute | solution.py:261
  75.2 1.5 %shard_map.121 = (bf16[128,2048]{1,0:T(8,128)(2,1)}, bf16[128,2048]{1,0:T(8,128)(2,1)S(1)}) custom-call(bf16[128,512]{1,0:T(8,128)(2,1)S(1)} %get-tuple-element.61.near_ref, bf16[128,512]{1,0:T(8,128)(2,1)S(1)} %collective-permute-done.3.far_ref, bf16[1024,512]{1,0:T(8,128)(2,1)S(1)} %bitcast.10, ...), custom_call_target="tpu_custom_call" | custom-call | flops 536870912 | bytes 4194304 | tf_op jit(solution)/shard_map/pallas_call | solution.py:249
  77.4 1.2 %shard_map.120 = bf16[16,64,512]{2,1,0:T(8,128)(2,1)} custom-call(bf16[1024,256]{1,0:T(8,128)(2,1)S(1)} %copy-done.4, bf16[128,512]{1,0:T(8,128)(2,1)S(1)} %get-tuple-element.61.near_ref, bf16[128,512]{1,0:T(8,128)(2,1)S(1)} %collective-permute-done.3.far_ref, bf16[1024,512]{1,0:T(8,128)(2,1)S(1)} %collective-permute-done.4.sent_ref), custom_call_target="tpu_custom_call" | custom-call | flops 268435456 | bytes 2097152 | tf_op jit(solution)/shard_map/pallas_call | solution.py:249
  78.7 3.8 %all-to-all-start.2 = ((bf16[16,64,512]{2,1,0:T(8,128)(2,1)}), bf16[16,64,512]{2,1,0:T(8,128)(2,1)S(1)}, u32[]{:S(2)}, u32[]{:S(2)}) async-start(bf16[16,64,512]{2,1,0:T(8,128)(2,1)} %shard_map.120), calls=%async_computation.2 | async-start | bytes 2097152 | tf_op jit(solution)/shard_map/all_to_all | solution.py:273
  82.5 2.6 %collective-permute-start.5 = (bf16[128,2048]{1,0:T(8,128)(2,1)S(1)}, bf16[128,2048]{1,0:T(8,128)(2,1)S(1)}, u32[]{:S(2)}, u32[]{:S(2)}) collective-permute-start(bf16[128,2048]{1,0:T(8,128)(2,1)S(1)} %get-tuple-element.66), channel_id=1, source_target_pairs={{0,128},{128,0},{1,129},{129,1},{2,130},{130,2},{3,131},{131,3},{4... | collective-permute-start | bytes 1572872 | tf_op jit(solution)/shard_map/ppermute | solution.py:265
  85.2 14.3 %all-to-all-done.2.parts_ref = bf16[16,64,512]{2,1,0:T(8,128)(2,1)S(1)} async-done(((bf16[16,64,512]{2,1,0:T(8,128)(2,1)}), bf16[16,64,512]{2,1,0:T(8,128)(2,1)S(1)}, u32[]{:S(2)}, u32[]{:S(2)}) %all-to-all-start.2) | async-done | bytes 1048608 | tf_op jit(solution)/shard_map/all_to_all | solution.py:273
  100.3 11.5 %all-to-all-start.3 = ((bf16[8,8,512]{2,1,0:T(8,128)(2,1)}), bf16[8,8,512]{2,1,0:T(8,128)(2,1)S(1)}, u32[]{:S(2)}, u32[]{:S(2)}) async-start(bf16[8,8,512]{2,1,0:T(8,128)(2,1)} %shard_map.124), calls=%async_computation.3 | async-start | bytes 131072 | tf_op jit(solution)/shard_map/all_to_all | solution.py:273
  111.7 2.9 %shard_map.122 = bf16[128,4096]{1,0:T(8,128)(2,1)} custom-call(s32[2]{0:T(128)S(1)} %pad_add_fusion.at_ref, bf16[128,2048]{1,0:T(8,128)(2,1)S(1)} %copy-done.11, bf16[128,2048]{1,0:T(8,128)(2,1)S(1)} %collective-permute-done.5.got_ref), custom_call_target="tpu_custom_call" | custom-call | flops 34359738368 | bytes 2097152 | tf_op jit(solution)/shard_map/pallas_call | solution.py:249
  (43 shorter events, 4.9 us)
Async XLA Ops:
  2.0 23.6 %all-to-all-start = ((bf16[8,8,512]{2,1,0:T(8,128)(2,1)}), bf16[8,8,512]{2,1,0:T(8,128)(2,1)S(1)}, u32[]{:S(2)}, u32[]{:S(2)}) async-start(bf16[8,8,512]{2,1,0:T(8,128)(2,1)} %shard_map.110), calls=%async_computation | async-start | bytes 131072 | tf_op jit(solution)/shard_map/all_to_all | solution.py:273
  22.9 16.6 %collective-permute-start = (bf16[128,2048]{1,0:T(8,128)(2,1)}, bf16[128,2048]{1,0:T(8,128)(2,1)S(1)}, u32[]{:S(2)}, u32[]{:S(2)}) collective-permute-start(bf16[128,2048]{1,0:T(8,128)(2,1)} %get-tuple-element.45), channel_id=1, source_target_pairs={{0,128},{128,0},{1,129},{129,1},{2,130},{130,2},{3,131},{131,3},{4... | collective-permute-start | bytes 1572872 | tf_op jit(solution)/shard_map/ppermute | solution.py:265
  26.7 8.0 %copy-start = (bf16[128,4096]{1,0:T(8,128)(2,1)S(1)}, bf16[128,4096]{1,0:T(8,128)(2,1)}, u32[]{:S(2)}) copy-start(bf16[128,4096]{1,0:T(8,128)(2,1)} %queries_ref.1) | copy-start | bytes 3145732
  26.7 8.0 %copy-start.7 = (bf16[128,512]{1,0:T(8,128)(2,1)S(1)}, bf16[128,512]{1,0:T(8,128)(2,1)}, u32[]{:S(2)}) copy-start(bf16[128,512]{1,0:T(8,128)(2,1)} %keys_ref) | copy-start | bytes 393220
  26.7 22.2 %all-to-all-start.1 = ((bf16[16,64,512]{2,1,0:T(8,128)(2,1)}), bf16[16,64,512]{2,1,0:T(8,128)(2,1)S(1)}, u32[]{:S(2)}, u32[]{:S(2)}) async-start(bf16[16,64,512]{2,1,0:T(8,128)(2,1)} %shard_map.111), calls=%async_computation.1 | async-start | bytes 2097152 | tf_op jit(solution)/shard_map/all_to_all | solution.py:273
  33.6 0.7 copy-start.12
  34.7 4.8 %copy-start.5 = (bf16[128,1024]{1,0:T(8,128)(2,1)S(1)}, bf16[128,1024]{1,0:T(8,128)(2,1)}, u32[]{:S(2)}) copy-start(bf16[128,1024]{1,0:T(8,128)(2,1)} %get-tuple-element.51.near_other_ref.rows_ref) | copy-start | bytes 786436
  34.7 4.8 %copy-start.6 = (bf16[128,1024]{1,0:T(8,128)(2,1)S(1)}, bf16[128,1024]{1,0:T(8,128)(2,1)}, u32[]{:S(2)}) copy-start(bf16[128,1024]{1,0:T(8,128)(2,1)} %get-tuple-element.53.near_own_ref.near_ref) | copy-start | bytes 786436
  48.9 7.2 %collective-permute-start.1 = (bf16[1024,512]{1,0:T(8,128)(2,1)S(1)}, bf16[1024,512]{1,0:T(8,128)(2,1)S(1)}, u32[]{:S(2)}, u32[]{:S(2)}) collective-permute-start(bf16[1024,512]{1,0:T(8,128)(2,1)S(1)} %bitcast.8), channel_id=1, source_target_pairs={{0,16},{16,0},{1,17},{17,1},{2,18},{18,2},{3,19},{19,3},{4,20},{20... | collective-permute-start | bytes 3145736 | tf_op jit(solution)/shard_map/ppermute | solution.py:261
  56.1 7.1 %copy-start.2 = (bf16[4,128,1024]{2,1,0:T(8,128)(2,1)S(1)}, bf16[4,128,1024]{2,1,0:T(8,128)(2,1)}, u32[]{:S(2)}) copy-start(bf16[4,128,1024]{2,1,0:T(8,128)(2,1)} %get-tuple-element.58.turned_ref) | copy-start | bytes 3145732
  56.4 6.7 %copy-start.1 = (bf16[4,1024,128]{2,1,0:T(8,128)(2,1)S(1)}, bf16[4,1024,128]{2,1,0:T(8,128)(2,1)}, u32[]{:S(2)}) copy-start(bf16[4,1024,128]{2,1,0:T(8,128)(2,1)} %get-tuple-element.57.probs_ref) | copy-start | bytes 3145732
  56.4 6.7 %collective-permute-start.2 = (bf16[128,512]{1,0:T(8,128)(2,1)S(1)}, bf16[128,512]{1,0:T(8,128)(2,1)S(1)}, u32[]{:S(2)}, u32[]{:S(2)}) collective-permute-start(bf16[128,512]{1,0:T(8,128)(2,1)S(1)} %shard_map.117), channel_id=1, source_target_pairs={{0,128},{128,0},{1,129},{129,1},{2,130},{130,2},{3,131},{131,3},{4... | collective-permute-start | bytes 393224 | tf_op jit(solution)/shard_map/ppermute | solution.py:265
  59.5 10.8 %copy-start.3 = (bf16[1024,256]{1,0:T(8,128)(2,1)S(1)}, bf16[1024,256]{1,0:T(8,128)(2,1)}, u32[]{:S(2)}) copy-start(bf16[1024,256]{1,0:T(8,128)(2,1)} %get-tuple-element.62.hidden_ref) | copy-start | bytes 1572868
  64.6 5.7 %collective-permute-start.3 = (bf16[128,512]{1,0:T(8,128)(2,1)S(1)}, bf16[128,512]{1,0:T(8,128)(2,1)S(1)}, u32[]{:S(2)}, u32[]{:S(2)}) collective-permute-start(bf16[128,512]{1,0:T(8,128)(2,1)S(1)} %get-tuple-element.61.near_ref), channel_id=1, source_target_pairs={{0,128},{128,0},{1,129},{129,1},{2,130},{130,2},{3,131},{131,3},{4... | collective-permute-start | bytes 393224 | tf_op jit(solution)/shard_map/ppermute | solution.py:265
  70.8 6.7 %copy-start.4 = (bf16[1024,256]{1,0:T(8,128)(2,1)S(1)}, bf16[1024,256]{1,0:T(8,128)(2,1)}, u32[]{:S(2)}) copy-start(bf16[1024,256]{1,0:T(8,128)(2,1)} %get-tuple-element.60.hidden_ref) | copy-start | bytes 1572868
  70.8 6.7 %collective-permute-start.4 = (bf16[1024,512]{1,0:T(8,128)(2,1)S(1)}, bf16[1024,512]{1,0:T(8,128)(2,1)S(1)}, u32[]{:S(2)}, u32[]{:S(2)}) collective-permute-start(bf16[1024,512]{1,0:T(8,128)(2,1)S(1)} %shard_map.119), channel_id=1, source_target_pairs={{0,16},{16,0},{1,17},{17,1},{2,18},{18,2},{3,19},{19,3},{4,20},{20... | collective-permute-start | bytes 3145736 | tf_op jit(solution)/shard_map/ppermute | solution.py:261
  78.7 6.5 %copy-start.8 = (f32[8,512]{1,0:T(8,128)S(1)}, f32[8,512]{1,0:T(8,128)}, u32[]{:S(2)}) copy-start(f32[8,512]{1,0:T(8,128)} %master_ref.2) | copy-start | bytes 49156
  78.7 6.5 %copy-start.9 = (f32[8,512]{1,0:T(8,128)S(1)}, f32[8,512]{1,0:T(8,128)}, u32[]{:S(2)}) copy-start(f32[8,512]{1,0:T(8,128)} %moment_ref) | copy-start | bytes 49156
  78.7 6.5 %copy-start.10 = (f32[8,512]{1,0:T(8,128)S(1)}, f32[8,512]{1,0:T(8,128)}, u32[]{:S(2)}) copy-start(f32[8,512]{1,0:T(8,128)} %second_ref) | copy-start | bytes 49156
  78.7 20.8 %all-to-all-start.2 = ((bf16[16,64,512]{2,1,0:T(8,128)(2,1)}), bf16[16,64,512]{2,1,0:T(8,128)(2,1)S(1)}, u32[]{:S(2)}, u32[]{:S(2)}) async-start(bf16[16,64,512]{2,1,0:T(8,128)(2,1)} %shard_map.120), calls=%async_computation.2 | async-start | bytes 2097152 | tf_op jit(solution)/shard_map/all_to_all | solution.py:273
  82.5 29.2 %collective-permute-start.5 = (bf16[128,2048]{1,0:T(8,128)(2,1)S(1)}, bf16[128,2048]{1,0:T(8,128)(2,1)S(1)}, u32[]{:S(2)}, u32[]{:S(2)}) collective-permute-start(bf16[128,2048]{1,0:T(8,128)(2,1)S(1)} %get-tuple-element.66), channel_id=1, source_target_pairs={{0,128},{128,0},{1,129},{129,1},{2,130},{130,2},{3,131},{131,3},{4... | collective-permute-start | bytes 1572872 | tf_op jit(solution)/shard_map/ppermute | solution.py:265
  85.2 26.5 %copy-start.11 = (bf16[128,2048]{1,0:T(8,128)(2,1)S(1)}, bf16[128,2048]{1,0:T(8,128)(2,1)}, u32[]{:S(2)}) copy-start(bf16[128,2048]{1,0:T(8,128)(2,1)} %get-tuple-element.65.keep_ref) | copy-start | bytes 1572868
  100.3 14.4 %all-to-all-start.3 = ((bf16[8,8,512]{2,1,0:T(8,128)(2,1)}), bf16[8,8,512]{2,1,0:T(8,128)(2,1)S(1)}, u32[]{:S(2)}, u32[]{:S(2)}) async-start(bf16[8,8,512]{2,1,0:T(8,128)(2,1)} %shard_map.124), calls=%async_computation.3 | async-start | bytes 131072 | tf_op jit(solution)/shard_map/all_to_all | solution.py:273

commit v10 on v9

--- a/solution.py
+++ b/solution.py
@@ -1,3 +1,5 @@
+import functools
+
 import jax
 import jax.numpy as jnp
 import numpy as np
@@ -32,11 +34,11 @@
 
 
 def order_matrix(zll, core):
-    to = lax.broadcasted_iota(jnp.int32, (1, 1024), 1)
+    to = lax.broadcasted_iota(jnp.int32, (1, 512), 1)
     z = ((to >> 3) & 7) ^ GATHER_FIRST
     source = (z & 3) * 256 + (z >> 2) * 128 + ((to >> 6) & 3) * 16 + (to & 7)
-    source = source + ((to >> 9) ^ zll) * 64 + (((to >> 8) & 1) ^ core) * 8
-    hit = lax.broadcasted_iota(jnp.int32, (1024, 1024), 0) == source
+    source = source + zll * 64 + ((to >> 8) ^ core) * 8
+    hit = lax.broadcasted_iota(jnp.int32, (1024, 512), 0) == source
     return jnp.where(hit, F32(1), F32(0)).astype(BF16)
 
 
@@ -83,23 +85,22 @@
     ]
 
 
-def split_kernel(at_ref, hidden_ref, own_ref, other_ref, send_ref, cols_ref, matrix_ref, sem_ref):
-    tok = own_ref.shape[0]
-    half = own_ref.shape[1]
+def split_kernel(far, at_ref, hidden_ref, *refs):
+    out_refs, (cols_ref, matrix_ref, sem_ref) = refs[:-3], refs[-3:]
+    tok = hidden_ref.shape[0]
+    half = hidden_ref.shape[1] // 4
     copies = [pltpu.make_async_copy(a, b, sem_ref.at[i]) for i, (a, b) in enumerate(whole_columns(hidden_ref, cols_ref))]
     for copy in copies:
         copy.start()
-    matrix_ref[...] = order_matrix(at_ref[0], at_ref[1])
-    for copy in copies:
-        copy.wait()
-    moved = jnp.dot(cols_ref[...], matrix_ref[...], preferred_element_type=F32).astype(BF16)
+    matrix_ref[...] = order_matrix(at_ref[0] ^ far, at_ref[1])
     for y in range(4):
         rows = slice(y * tok, (y + 1) * tok)
-        to = slice(y * 256, (y + 1) * 256)
-        own_ref[:, to] = moved[rows, :256]
-        other_ref[:, to] = moved[rows, 256:512]
-        send_ref[:, to] = moved[rows, 512:768]
-        send_ref[:, half + y * 256 : half + (y + 1) * 256] = moved[rows, 768:]
+        for copy in copies[y * 4 : y * 4 + 4]:
+            copy.wait()
+        moved = jnp.dot(cols_ref[rows], matrix_ref[...], preferred_element_type=F32).astype(BF16)
+        for c in range(2):
+            at = (c * half if far else 0) + y * 256
+            out_refs[0 if far else c][:, at : at + 256] = moved[:, c * 256 : (c + 1) * 256]
 
 
 def join_kernel(at_ref, keep_ref, got_ref, out_ref, cols_ref, moved_ref, matrix_ref, sem_ref):
@@ -236,7 +237,8 @@
     return pltpu.SemaphoreType.DMA((n,))
 
 
-def call(kernel, out_shape, flops, nbytes, *args, scratch=(), out=None, hbm=(), late=()):
+def call(kernel, out_shape, flops, nbytes, *more, args=(), scratch=(), out=None, hbm=(), late=()):
+    args = (*args, *more)
     specs = [SMEM if a.dtype == jnp.int32 and a.ndim == 1 else VMEM for a in args]
     specs = [HBM if i in hbm else spec for i, spec in enumerate(specs)]
     if out is None:
@@ -306,17 +308,14 @@
     weight, hidden_in = lax.optimization_barrier((weight, hidden_in))
     weight = exchange_z(weight, GATHER_FIRST).reshape(DEPTH * rows, kv)
 
-    near_own, near_other, send = call(
-        split_kernel,
-        (half, half, block),
-        8 * tok * 1024 * 1024,
-        2 << 20,
-        at,
-        hidden_in,
-        scratch=[cols, matrix, copies(16)],
+    split = functools.partial(
+        call,
+        flops=4 * tok * 1024 * 1024,
+        nbytes=2 << 20,
+        scratch=[cols, pltpu.VMEM((1024, 512), BF16), copies(16)],
         hbm=(1,),
-        late=(0, 1),
-    )
+    )
+    (send,) = split(functools.partial(split_kernel, 1), (block,), args=(at, hidden_in))
     far = swap_pair(send)
 
     weight = call(
@@ -328,8 +327,10 @@
         scratch=[copies(PLANE)],
         out=HBM,
     )
-    weight, keys = lax.optimization_barrier((weight, keys))
+    weight, keys, hidden_in = lax.optimization_barrier((weight, keys, hidden_in))
     weight = exchange_plane(weight).reshape(PLANE * DEPTH * rows, kv)
+
+    near_own, near_other = split(functools.partial(split_kernel, 0), (half, half), args=(at, hidden_in), late=(0, 1))
 
     ends = jnp.cumsum(lengths[0])
     seg = jnp.sum((jnp.arange(tok, dtype=jnp.int32)[:, None] >= ends[None, :]).astype(jnp.int32), axis=1)

time: 116 us -> 116 us (level)
  waiting for transfers between devices: 31.8 us -> 26.3 us
  Pallas kernels: 21.8 us -> 24.3 us
  local copies, waits for them, and re-layouts: 0.83 us -> 2.72 us
    all_to_all x4, waiting for transfers between devices: 22.5 us -> 17 us  [exchange(): lax.all_to_all(blocks, AXES, split_axis=0, concat_axis=0, axis_index_grou...]
    pallas_call x15 -> x16, Pallas kernels: 21.8 us -> 24.3 us  [call(): pl.pallas_call(kernel, out_shape=out_shape, in_specs=specs, out_specs=out...]
    unnamed x26 -> x30, local copies, waits for them, and re-layouts: 0.71 us -> 2.6 us
  transfers between devices with their start and end apart: 10 -> 10, of which waited for: 6 -> 6; matrix products, arithmetic and copies ran while one was open for 0% -> 0% of each run, Pallas kernels for 15% -> 17%
where the time goes in v10:
time: 116 us; the launch traced here: 114 us
  starting transfers between devices  59 us (51%)
  waiting for transfers between devices  26.3 us (23%)
  Pallas kernels  24.3 us (21%)
  local copies, waits for them, and re-layouts  2.72 us (2%)
    all_to_all x4, starting transfers between devices, exchange(): lax.all_to_all(blocks, AXES, split_axis=0, concat_axis=0, axis_index_grou...  39 us
    pallas_call x16, Pallas kernels, call(): pl.pallas_call(kernel, out_shape=out_shape, in_specs=specs, out_specs=out...  24.3 us
    all_to_all x4, waiting for transfers between devices, exchange(): lax.all_to_all(blocks, AXES, split_axis=0, concat_axis=0, axis_index_grou...  17 us
    ppermute x4, starting transfers between devices, swap_pair(): return lax.ppermute(array, 'zll', [(0, 1), (1, 0)])  10.7 us
    ppermute x2, starting transfers between devices, swap_core(): return lax.ppermute(array, 'c', [(0, 1), (1, 0)])  9.31 us
    ppermute x4, waiting for transfers between devices, swap_pair(): return lax.ppermute(array, 'zll', [(0, 1), (1, 0)])  6.7 us
    unnamed x30, local copies, waits for them, and re-layouts  2.6 us
    ppermute x2, waiting for transfers between devices, swap_core(): return lax.ppermute(array, 'c', [(0, 1), (1, 0)])  2.53 us
  transfers between devices with their start and end apart: 10, of which 6 were waited for; matrix products, arithmetic and copies ran while one was open for 0% of the time, Pallas kernels for 17%

profile of v10, /device:TPU:1, one launch (start us, length us, event | category | flops | bytes accessed | tf_op | source)
XLA Modules:
  0.0 114.2 jit_solution(14914582427079648970)
XLA Ops:
  0.6 1.4 %shard_map.110 = bf16[8,8,512]{2,1,0:T(8,128)(2,1)} custom-call(f32[8,512]{1,0:T(8,128)} %master_ref.2), custom_call_target="tpu_custom_call" | custom-call | bytes 131072 | tf_op jit(solution)/shard_map/pallas_call | solution.py:251
  2.0 16.9 %all-to-all-start = ((bf16[8,8,512]{2,1,0:T(8,128)(2,1)}), bf16[8,8,512]{2,1,0:T(8,128)(2,1)S(1)}, u32[]{:S(2)}, u32[]{:S(2)}) async-start(bf16[8,8,512]{2,1,0:T(8,128)(2,1)} %shard_map.110), calls=%async_computation | async-start | bytes 131072 | tf_op jit(solution)/shard_map/all_to_all | solution.py:275
  18.9 2.9 %shard_map.113 = bf16[128,2048]{1,0:T(8,128)(2,1)S(1)} custom-call(s32[2]{0:T(128)S(1)} %pad_add_fusion.at_ref, bf16[128,4096]{1,0:T(8,128)(2,1)} %hidden_ref.1), custom_call_target="tpu_custom_call" | custom-call | flops 536870912 | bytes 2097152 | tf_op jit(solution)/shard_map/pallas_call | solution.py:251
  21.8 2.6 %collective-permute-start = (bf16[128,2048]{1,0:T(8,128)(2,1)S(1)}, bf16[128,2048]{1,0:T(8,128)(2,1)S(1)}, u32[]{:S(2)}, u32[]{:S(2)}) collective-permute-start(bf16[128,2048]{1,0:T(8,128)(2,1)S(1)} %shard_map.113), channel_id=1, source_target_pairs={{0,128},{128,0},{1,129},{129,1},{2,130},{130,2},{3,131},{131,3},{4... | collective-permute-start | bytes 1572872 | tf_op jit(solution)/shard_map/ppermute | solution.py:267
  25.6 6.9 %all-to-all-start.1 = ((bf16[16,64,512]{2,1,0:T(8,128)(2,1)}), bf16[16,64,512]{2,1,0:T(8,128)(2,1)S(1)}, u32[]{:S(2)}, u32[]{:S(2)}) async-start(bf16[16,64,512]{2,1,0:T(8,128)(2,1)} %shard_map.111), calls=%async_computation.1 | async-start | bytes 2097152 | tf_op jit(solution)/shard_map/all_to_all | solution.py:275
  33.6 4.8 %shard_map.115 = (bf16[4,1024,128]{2,1,0:T(8,128)(2,1)}, bf16[4,128,1024]{2,1,0:T(8,128)(2,1)}) custom-call(bf16[128,4096]{1,0:T(8,128)(2,1)S(1)} %copy-done, bf16[128,512]{1,0:T(8,128)(2,1)S(1)} %copy-done.9, s32[1,128]{1,0:T(1,128)S(1)} %bitcast.13, s32[128,1]{1,0:T(8,128)S(1)} %copy.13.seg_col_ref), custom_call_target="tpu_custom_call" | custom-call | flops 268435456 | bytes 8388608 | tf_op jit(solution)/shard_map/pallas_call | solution.py:251
  38.3 3.7 %shard_map.112 = (bf16[128,1024]{1,0:T(8,128)(2,1)}, bf16[128,1024]{1,0:T(8,128)(2,1)}) custom-call(s32[2]{0:T(128)S(1)} %pad_add_fusion.at_ref, bf16[128,4096]{1,0:T(8,128)(2,1)} %hidden_ref.1), custom_call_target="tpu_custom_call" | custom-call | flops 536870912 | bytes 2097152 | tf_op jit(solution)/shard_map/pallas_call | solution.py:251
  43.9 1.2 %shard_map.114 = (bf16[1024,256]{1,0:T(8,128)(2,1)}, bf16[1024,256]{1,0:T(8,128)(2,1)}) custom-call(bf16[128,1024]{1,0:T(8,128)(2,1)S(1)} %copy-done.7, bf16[128,1024]{1,0:T(8,128)(2,1)S(1)} %copy-done.5, bf16[128,2048]{1,0:T(8,128)(2,1)S(1)} %collective-permute-done.far_ref.rows_ref), custom_call_target="tpu_custom_call" | custom-call | flops 5726623232 | bytes 2097152 | tf_op jit(solution)/shard_map/pallas_call | solution.py:251
  45.1 2.7 %all-to-all-done.1 = bf16[16,64,512]{2,1,0:T(8,128)(2,1)S(1)} async-done(((bf16[16,64,512]{2,1,0:T(8,128)(2,1)}), bf16[16,64,512]{2,1,0:T(8,128)(2,1)S(1)}, u32[]{:S(2)}, u32[]{:S(2)}) %all-to-all-start.1) | async-done | bytes 1048608 | tf_op jit(solution)/shard_map/all_to_all | solution.py:275
  47.8 4.9 %collective-permute-start.1 = (bf16[1024,512]{1,0:T(8,128)(2,1)S(1)}, bf16[1024,512]{1,0:T(8,128)(2,1)S(1)}, u32[]{:S(2)}, u32[]{:S(2)}) collective-permute-start(bf16[1024,512]{1,0:T(8,128)(2,1)S(1)} %bitcast.8), channel_id=1, source_target_pairs={{0,16},{16,0},{1,17},{17,1},{2,18},{18,2},{3,19},{19,3},{4,20},{20... | collective-permute-start | bytes 3145736 | tf_op jit(solution)/shard_map/ppermute | solution.py:263
  53.2 1.8 %collective-permute-done.1.weight_ref.other_ref = bf16[1024,512]{1,0:T(8,128)(2,1)S(1)} collective-permute-done((bf16[1024,512]{1,0:T(8,128)(2,1)S(1)}, bf16[1024,512]{1,0:T(8,128)(2,1)S(1)}, u32[]{:S(2)}, u32[]{:S(2)}) %collective-permute-start.1) | collective-permute-done | bytes 1048608 | tf_op jit(solution)/shard_map/ppermute | solution.py:263
  55.3 2.8 %collective-permute-start.2 = (bf16[128,512]{1,0:T(8,128)(2,1)S(1)}, bf16[128,512]{1,0:T(8,128)(2,1)S(1)}, u32[]{:S(2)}, u32[]{:S(2)}) collective-permute-start(bf16[128,512]{1,0:T(8,128)(2,1)S(1)} %shard_map.118), channel_id=1, source_target_pairs={{0,128},{128,0},{1,129},{129,1},{2,130},{130,2},{3,131},{131,3},{4... | collective-permute-start | bytes 393224 | tf_op jit(solution)/shard_map/ppermute | solution.py:267
  58.4 3.6 %collective-permute-done.2.sent_ref = bf16[128,512]{1,0:T(8,128)(2,1)S(1)} collective-permute-done((bf16[128,512]{1,0:T(8,128)(2,1)S(1)}, bf16[128,512]{1,0:T(8,128)(2,1)S(1)}, u32[]{:S(2)}, u32[]{:S(2)}) %collective-permute-start.2) | collective-permute-done | bytes 131104 | tf_op jit(solution)/shard_map/ppermute | solution.py:267
  62.0 1.4 %shard_map.119 = (bf16[128,4096]{1,0:T(8,128)(2,1)}, bf16[128,512]{1,0:T(8,128)(2,1)S(1)}) custom-call(f32[128,512]{1,0:T(8,128)S(1)} %shard_map.117.near_ref, bf16[128,512]{1,0:T(8,128)(2,1)S(1)} %collective-permute-done.2.sent_ref, bf16[4,1024,128]{2,1,0:T(8,128)(2,1)S(1)} %copy-done.1, bf16[4,128,1024]{2,1,0:T(8,128)(2,1)S(1)} %copy-done.2), custom_call_target="tpu_custom_call" | custom-call | flops 268435456 | bytes 4194304 | tf_op jit(solution)/shard_map/pallas_call | solution.py:251
  63.5 2.6 %collective-permute-start.3 = (bf16[128,512]{1,0:T(8,128)(2,1)S(1)}, bf16[128,512]{1,0:T(8,128)(2,1)S(1)}, u32[]{:S(2)}, u32[]{:S(2)}) collective-permute-start(bf16[128,512]{1,0:T(8,128)(2,1)S(1)} %get-tuple-element.61.near_ref), channel_id=1, source_target_pairs={{0,128},{128,0},{1,129},{129,1},{2,130},{130,2},{3,131},{131,3},{4... | collective-permute-start | bytes 393224 | tf_op jit(solution)/shard_map/ppermute | solution.py:267
  66.1 3.1 %collective-permute-done.3.far_ref = bf16[128,512]{1,0:T(8,128)(2,1)S(1)} collective-permute-done((bf16[128,512]{1,0:T(8,128)(2,1)S(1)}, bf16[128,512]{1,0:T(8,128)(2,1)S(1)}, u32[]{:S(2)}, u32[]{:S(2)}) %collective-permute-start.3) | collective-permute-done | bytes 131104 | tf_op jit(solution)/shard_map/ppermute | solution.py:267
  69.6 4.4 %collective-permute-start.4 = (bf16[1024,512]{1,0:T(8,128)(2,1)S(1)}, bf16[1024,512]{1,0:T(8,128)(2,1)S(1)}, u32[]{:S(2)}, u32[]{:S(2)}) collective-permute-start(bf16[1024,512]{1,0:T(8,128)(2,1)S(1)} %shard_map.120), channel_id=1, source_target_pairs={{0,16},{16,0},{1,17},{17,1},{2,18},{18,2},{3,19},{19,3},{4,20},{20... | collective-permute-start | bytes 3145736 | tf_op jit(solution)/shard_map/ppermute | solution.py:263
  74.0 1.5 %shard_map.122 = (bf16[128,2048]{1,0:T(8,128)(2,1)}, bf16[128,2048]{1,0:T(8,128)(2,1)S(1)}) custom-call(bf16[128,512]{1,0:T(8,128)(2,1)S(1)} %get-tuple-element.61.near_ref, bf16[128,512]{1,0:T(8,128)(2,1)S(1)} %collective-permute-done.3.far_ref, bf16[1024,512]{1,0:T(8,128)(2,1)S(1)} %bitcast.10, ...), custom_call_target="tpu_custom_call" | custom-call | flops 536870912 | bytes 4194304 | tf_op jit(solution)/shard_map/pallas_call | solution.py:251
  76.3 1.2 %shard_map.121 = bf16[16,64,512]{2,1,0:T(8,128)(2,1)} custom-call(bf16[1024,256]{1,0:T(8,128)(2,1)S(1)} %copy-done.4, bf16[128,512]{1,0:T(8,128)(2,1)S(1)} %get-tuple-element.61.near_ref, bf16[128,512]{1,0:T(8,128)(2,1)S(1)} %collective-permute-done.3.far_ref, bf16[1024,512]{1,0:T(8,128)(2,1)S(1)} %collective-permute-done.4.sent_ref), custom_call_target="tpu_custom_call" | custom-call | flops 268435456 | bytes 2097152 | tf_op jit(solution)/shard_map/pallas_call | solution.py:251
  77.6 3.8 %all-to-all-start.2 = ((bf16[16,64,512]{2,1,0:T(8,128)(2,1)}), bf16[16,64,512]{2,1,0:T(8,128)(2,1)S(1)}, u32[]{:S(2)}, u32[]{:S(2)}) async-start(bf16[16,64,512]{2,1,0:T(8,128)(2,1)} %shard_map.121), calls=%async_computation.2 | async-start | bytes 2097152 | tf_op jit(solution)/shard_map/all_to_all | solution.py:275
  81.4 2.6 %collective-permute-start.5 = (bf16[128,2048]{1,0:T(8,128)(2,1)S(1)}, bf16[128,2048]{1,0:T(8,128)(2,1)S(1)}, u32[]{:S(2)}, u32[]{:S(2)}) collective-permute-start(bf16[128,2048]{1,0:T(8,128)(2,1)S(1)} %get-tuple-element.66), channel_id=1, source_target_pairs={{0,128},{128,0},{1,129},{129,1},{2,130},{130,2},{3,131},{131,3},{4... | collective-permute-start | bytes 1572872 | tf_op jit(solution)/shard_map/ppermute | solution.py:267
  84.1 14.3 %all-to-all-done.2.parts_ref = bf16[16,64,512]{2,1,0:T(8,128)(2,1)S(1)} async-done(((bf16[16,64,512]{2,1,0:T(8,128)(2,1)}), bf16[16,64,512]{2,1,0:T(8,128)(2,1)S(1)}, u32[]{:S(2)}, u32[]{:S(2)}) %all-to-all-start.2) | async-done | bytes 1048608 | tf_op jit(solution)/shard_map/all_to_all | solution.py:275
  99.2 11.5 %all-to-all-start.3 = ((bf16[8,8,512]{2,1,0:T(8,128)(2,1)}), bf16[8,8,512]{2,1,0:T(8,128)(2,1)S(1)}, u32[]{:S(2)}, u32[]{:S(2)}) async-start(bf16[8,8,512]{2,1,0:T(8,128)(2,1)} %shard_map.125), calls=%async_computation.3 | async-start | bytes 131072 | tf_op jit(solution)/shard_map/all_to_all | solution.py:275
  110.7 2.9 %shard_map.123 = bf16[128,4096]{1,0:T(8,128)(2,1)} custom-call(s32[2]{0:T(128)S(1)} %pad_add_fusion.at_ref, bf16[128,2048]{1,0:T(8,128)(2,1)S(1)} %copy-done.13, bf16[128,2048]{1,0:T(8,128)(2,1)S(1)} %collective-permute-done.5.got_ref), custom_call_target="tpu_custom_call" | custom-call | flops 34359738368 | bytes 2097152 | tf_op jit(solution)/shard_map/pallas_call | solution.py:251
  (48 shorter events, 7.8 us)
Async XLA Ops:
  2.0 22.5 %all-to-all-start = ((bf16[8,8,512]{2,1,0:T(8,128)(2,1)}), bf16[8,8,512]{2,1,0:T(8,128)(2,1)S(1)}, u32[]{:S(2)}, u32[]{:S(2)}) async-start(bf16[8,8,512]{2,1,0:T(8,128)(2,1)} %shard_map.110), calls=%async_computation | async-start | bytes 131072 | tf_op jit(solution)/shard_map/all_to_all | solution.py:275
  21.8 20.2 %collective-permute-start = (bf16[128,2048]{1,0:T(8,128)(2,1)S(1)}, bf16[128,2048]{1,0:T(8,128)(2,1)S(1)}, u32[]{:S(2)}, u32[]{:S(2)}) collective-permute-start(bf16[128,2048]{1,0:T(8,128)(2,1)S(1)} %shard_map.113), channel_id=1, source_target_pairs={{0,128},{128,0},{1,129},{129,1},{2,130},{130,2},{3,131},{131,3},{4... | collective-permute-start | bytes 1572872 | tf_op jit(solution)/shard_map/ppermute | solution.py:267
  25.6 8.0 %copy-start = (bf16[128,4096]{1,0:T(8,128)(2,1)S(1)}, bf16[128,4096]{1,0:T(8,128)(2,1)}, u32[]{:S(2)}) copy-start(bf16[128,4096]{1,0:T(8,128)(2,1)} %queries_ref.1) | copy-start | bytes 3145732
  25.6 8.0 %copy-start.9 = (bf16[128,512]{1,0:T(8,128)(2,1)S(1)}, bf16[128,512]{1,0:T(8,128)(2,1)}, u32[]{:S(2)}) copy-start(bf16[128,512]{1,0:T(8,128)(2,1)} %keys_ref) | copy-start | bytes 393220
  25.6 22.2 %all-to-all-start.1 = ((bf16[16,64,512]{2,1,0:T(8,128)(2,1)}), bf16[16,64,512]{2,1,0:T(8,128)(2,1)S(1)}, u32[]{:S(2)}, u32[]{:S(2)}) async-start(bf16[16,64,512]{2,1,0:T(8,128)(2,1)} %shard_map.111), calls=%async_computation.1 | async-start | bytes 2097152 | tf_op jit(solution)/shard_map/all_to_all | solution.py:275
  42.0 1.0 copy-start.5
  43.0 0.9 copy-start.7
  43.9 8.8 %copy-start.8 = (bf16[128,1024]{1,0:T(8,128)(2,1)S(1)}, bf16[128,1024]{1,0:T(8,128)(2,1)}, u32[]{:S(2)}) copy-start(bf16[128,1024]{1,0:T(8,128)(2,1)} %get-tuple-element.53.near_own_ref.near_ref) | copy-start | bytes 786436
  47.8 7.2 %collective-permute-start.1 = (bf16[1024,512]{1,0:T(8,128)(2,1)S(1)}, bf16[1024,512]{1,0:T(8,128)(2,1)S(1)}, u32[]{:S(2)}, u32[]{:S(2)}) collective-permute-start(bf16[1024,512]{1,0:T(8,128)(2,1)S(1)} %bitcast.8), channel_id=1, source_target_pairs={{0,16},{16,0},{1,17},{17,1},{2,18},{18,2},{3,19},{19,3},{4,20},{20... | collective-permute-start | bytes 3145736 | tf_op jit(solution)/shard_map/ppermute | solution.py:263
  55.0 3.1 %copy-start.6 = (bf16[128,1024]{1,0:T(8,128)(2,1)S(1)}, bf16[128,1024]{1,0:T(8,128)(2,1)}, u32[]{:S(2)}) copy-start(bf16[128,1024]{1,0:T(8,128)(2,1)} %get-tuple-element.51.near_other_ref.rows_ref) | copy-start | bytes 786436
  55.0 7.1 %copy-start.2 = (bf16[4,128,1024]{2,1,0:T(8,128)(2,1)S(1)}, bf16[4,128,1024]{2,1,0:T(8,128)(2,1)}, u32[]{:S(2)}) copy-start(bf16[4,128,1024]{2,1,0:T(8,128)(2,1)} %get-tuple-element.58.turned_ref) | copy-start | bytes 3145732
  55.3 6.8 %copy-start.1 = (bf16[4,1024,128]{2,1,0:T(8,128)(2,1)S(1)}, bf16[4,1024,128]{2,1,0:T(8,128)(2,1)}, u32[]{:S(2)}) copy-start(bf16[4,1024,128]{2,1,0:T(8,128)(2,1)} %get-tuple-element.57.probs_ref) | copy-start | bytes 3145732
  55.3 6.7 %collective-permute-start.2 = (bf16[128,512]{1,0:T(8,128)(2,1)S(1)}, bf16[128,512]{1,0:T(8,128)(2,1)S(1)}, u32[]{:S(2)}, u32[]{:S(2)}) collective-permute-start(bf16[128,512]{1,0:T(8,128)(2,1)S(1)} %shard_map.118), channel_id=1, source_target_pairs={{0,128},{128,0},{1,129},{129,1},{2,130},{130,2},{3,131},{131,3},{4... | collective-permute-start | bytes 393224 | tf_op jit(solution)/shard_map/ppermute | solution.py:267
  58.4 10.8 %copy-start.3 = (bf16[1024,256]{1,0:T(8,128)(2,1)S(1)}, bf16[1024,256]{1,0:T(8,128)(2,1)}, u32[]{:S(2)}) copy-start(bf16[1024,256]{1,0:T(8,128)(2,1)} %get-tuple-element.62.hidden_ref) | copy-start | bytes 1572868
  63.5 5.7 %collective-permute-start.3 = (bf16[128,512]{1,0:T(8,128)(2,1)S(1)}, bf16[128,512]{1,0:T(8,128)(2,1)S(1)}, u32[]{:S(2)}, u32[]{:S(2)}) collective-permute-start(bf16[128,512]{1,0:T(8,128)(2,1)S(1)} %get-tuple-element.61.near_ref), channel_id=1, source_target_pairs={{0,128},{128,0},{1,129},{129,1},{2,130},{130,2},{3,131},{131,3},{4... | collective-permute-start | bytes 393224 | tf_op jit(solution)/shard_map/ppermute | solution.py:267
  69.6 6.7 %copy-start.4 = (bf16[1024,256]{1,0:T(8,128)(2,1)S(1)}, bf16[1024,256]{1,0:T(8,128)(2,1)}, u32[]{:S(2)}) copy-start(bf16[1024,256]{1,0:T(8,128)(2,1)} %get-tuple-element.60.hidden_ref) | copy-start | bytes 1572868
  69.6 6.7 %collective-permute-start.4 = (bf16[1024,512]{1,0:T(8,128)(2,1)S(1)}, bf16[1024,512]{1,0:T(8,128)(2,1)S(1)}, u32[]{:S(2)}, u32[]{:S(2)}) collective-permute-start(bf16[1024,512]{1,0:T(8,128)(2,1)S(1)} %shard_map.120), channel_id=1, source_target_pairs={{0,16},{16,0},{1,17},{17,1},{2,18},{18,2},{3,19},{19,3},{4,20},{20... | collective-permute-start | bytes 3145736 | tf_op jit(solution)/shard_map/ppermute | solution.py:263
  77.5 6.5 %copy-start.10 = (f32[8,512]{1,0:T(8,128)S(1)}, f32[8,512]{1,0:T(8,128)}, u32[]{:S(2)}) copy-start(f32[8,512]{1,0:T(8,128)} %master_ref.2) | copy-start | bytes 49156
  77.6 6.5 %copy-start.11 = (f32[8,512]{1,0:T(8,128)S(1)}, f32[8,512]{1,0:T(8,128)}, u32[]{:S(2)}) copy-start(f32[8,512]{1,0:T(8,128)} %moment_ref) | copy-start | bytes 49156
  77.6 6.5 %copy-start.12 = (f32[8,512]{1,0:T(8,128)S(1)}, f32[8,512]{1,0:T(8,128)}, u32[]{:S(2)}) copy-start(f32[8,512]{1,0:T(8,128)} %second_ref) | copy-start | bytes 49156
  77.6 20.8 %all-to-all-start.2 = ((bf16[16,64,512]{2,1,0:T(8,128)(2,1)}), bf16[16,64,512]{2,1,0:T(8,128)(2,1)S(1)}, u32[]{:S(2)}, u32[]{:S(2)}) async-start(bf16[16,64,512]{2,1,0:T(8,128)(2,1)} %shard_map.121), calls=%async_computation.2 | async-start | bytes 2097152 | tf_op jit(solution)/shard_map/all_to_all | solution.py:275
  81.4 29.3 %collective-permute-start.5 = (bf16[128,2048]{1,0:T(8,128)(2,1)S(1)}, bf16[128,2048]{1,0:T(8,128)(2,1)S(1)}, u32[]{:S(2)}, u32[]{:S(2)}) collective-permute-start(bf16[128,2048]{1,0:T(8,128)(2,1)S(1)} %get-tuple-element.66), channel_id=1, source_target_pairs={{0,128},{128,0},{1,129},{129,1},{2,130},{130,2},{3,131},{131,3},{4... | collective-permute-start | bytes 1572872 | tf_op jit(solution)/shard_map/ppermute | solution.py:267
  84.1 26.6 %copy-start.13 = (bf16[128,2048]{1,0:T(8,128)(2,1)S(1)}, bf16[128,2048]{1,0:T(8,128)(2,1)}, u32[]{:S(2)}) copy-start(bf16[128,2048]{1,0:T(8,128)(2,1)} %get-tuple-element.65.keep_ref) | copy-start | bytes 1572868
  99.2 14.4 %all-to-all-start.3 = ((bf16[8,8,512]{2,1,0:T(8,128)(2,1)}), bf16[8,8,512]{2,1,0:T(8,128)(2,1)S(1)}, u32[]{:S(2)}, u32[]{:S(2)}) async-start(bf16[8,8,512]{2,1,0:T(8,128)(2,1)} %shard_map.125), calls=%async_computation.3 | async-start | bytes 131072 | tf_op jit(solution)/shard_map/all_to_all | solution.py:275
  (1 other events, 0.7 us)

commit v11 on v10

--- a/solution.py
+++ b/solution.py
@@ -136,20 +136,16 @@
     other_ref[:, tok:] = far_ref[:, half:].T
 
 
-def part_kernel(hidden_ref, near_ref, far_ref, out_ref):
+def fold_kernel(own_ref, more_ref, near_ref, far_ref, near_more_ref, far_more_ref, out_ref, rows_ref, sem_ref):
     grad = jnp.concatenate([near_ref[...], far_ref[...]], axis=0)
-    out_ref[...] = jnp.dot(hidden_ref[...], grad, preferred_element_type=F32).astype(BF16)
-
-
-def fold_kernel(hidden_ref, near_ref, far_ref, sent_ref, out_ref, rows_ref, sem_ref):
-    grad = jnp.concatenate([near_ref[...], far_ref[...]], axis=0)
+    grad_more = jnp.concatenate([near_more_ref[...], far_more_ref[...]], axis=0)
     step = out_ref.shape[1]
     copies = []
     blocks = 4
     for i in range(0, out_ref.shape[0], blocks):
         at = slice(i * step, (i + blocks) * step)
-        part = jnp.dot(hidden_ref[at], grad, preferred_element_type=F32)
-        part = (part + sent_ref[at].astype(F32)).astype(BF16)
+        part = jnp.dot(own_ref[at], grad, preferred_element_type=F32)
+        part = (part + jnp.dot(more_ref[at], grad_more, preferred_element_type=F32)).astype(BF16)
         for j in range(blocks):
             rows_ref[i + j] = part[j * step : (j + 1) * step]
         to = pl.ds(i, blocks)
@@ -181,7 +177,7 @@
         out_ref[z ^ GATHER_FIRST ^ REDUCE_FIRST] = total[z * rows : (z + 1) * rows]
 
 
-def probs_kernel(queries_ref, keys_ref, seg_row_ref, seg_col_ref, out_ref, turned_ref):
+def probs_kernel(queries_ref, keys_ref, seg_row_ref, seg_col_ref, out_ref):
     tok = queries_ref.shape[0]
     rows = lax.broadcasted_iota(jnp.int32, (tok, tok), 0)
     cols = lax.broadcasted_iota(jnp.int32, (tok, tok), 1)
@@ -197,9 +193,7 @@
             scores = jnp.where(allowed, scores * scale, F32(-1000000000.0))
             expos = jnp.exp(scores - jnp.max(scores, axis=-1, keepdims=True))
             total = jnp.sum(expos, axis=-1, keepdims=True)
-            probs = (expos / total).astype(BF16)
-            out_ref[j, h * tok : (h + 1) * tok, :] = probs
-            turned_ref[j, :, h * tok : (h + 1) * tok] = probs.T
+            out_ref[j, h * tok : (h + 1) * tok, :] = (expos / total).astype(BF16)
 
 
 def states_kernel(moment_ref, second_ref, master_ref, moment_out_ref, second_out_ref, master_out_ref, decay_ref):
@@ -209,7 +203,7 @@
     decay_ref[...] = decay_rate * master_ref[...]
 
 
-def attend_kernel(near_ref, sent_ref, probs_ref, turned_ref, attended_ref, grad_ref, rows_ref, sem_ref):
+def attend_kernel(near_ref, sent_ref, probs_ref, attended_ref, grad_ref, rows_ref, sem_ref):
     tok = near_ref.shape[0]
     wide = GROUPS * HD
     copies = []
@@ -223,7 +217,9 @@
             pltpu.make_async_copy(rows_ref.at[j], attended_ref.at[:, j * wide : (j + 1) * wide], sem_ref.at[j])
         )
         copies[-1].start()
-        grad_ref[:, cols] = jnp.dot(turned_ref[j], attended, preferred_element_type=F32).astype(BF16)
+        grad_ref[:, cols] = lax.dot_general(
+            probs_ref[j], attended, (((0,), (0,)), ((), ())), preferred_element_type=F32
+        ).astype(BF16)
     for copy in copies:
         copy.wait()
 
@@ -334,26 +330,24 @@
 
     ends = jnp.cumsum(lengths[0])
     seg = jnp.sum((jnp.arange(tok, dtype=jnp.int32)[:, None] >= ends[None, :]).astype(jnp.int32), axis=1)
-    probs, turned = call(
+    (probs,) = call(
         probs_kernel,
-        (
-            jax.ShapeDtypeStruct((VH, GROUPS * tok, tok), BF16),
-            jax.ShapeDtypeStruct((VH, tok, GROUPS * tok), BF16),
-        ),
+        (jax.ShapeDtypeStruct((VH, GROUPS * tok, tok), BF16),),
         4 * tok * tok * QH * HD,
         8 << 20,
         queries,
         keys,
         seg[None, :],
         seg[:, None],
-        late=(0, 1),
+        late=(0,),
     )
     flipped = jax.ShapeDtypeStruct((feats, 2 * tok), BF16)
     columns_own, columns_other = call(
-        flip_kernel, (flipped, flipped), WEIGHTY // 6, 2 << 20, near_own, near_other, far, late=(0, 1)
-    )
-    weight, near_own, near_other, far, columns_own, columns_other, probs, turned = lax.optimization_barrier(
-        (weight, near_own, near_other, far, columns_own, columns_other, probs, turned)
+        flip_kernel, (flipped, flipped), WEIGHTY // 24, 2 << 20, near_own, near_other, far, late=(0, 1)
+    )
+    columns_more = swap_core(columns_other)
+    weight, near_own, near_other, far, columns_own, columns_more, probs = lax.optimization_barrier(
+        (weight, near_own, near_other, far, columns_own, columns_more, probs)
     )
     weight_other = swap_core(weight)
 
@@ -369,39 +363,31 @@
         near,
         sent,
         probs,
-        turned,
         scratch=[pltpu.VMEM((VH, tok, GROUPS * HD), BF16), copies(VH)],
         out=(HBM, VMEM),
     )
     grad_far = swap_pair(grad)
 
-    part = call(
-        part_kernel,
-        jax.ShapeDtypeStruct((feats, kv), BF16),
-        2 * flops,
-        2 << 20,
-        columns_other,
-        grad,
-        grad_far,
-    )
     part = call(
         fold_kernel,
         jax.ShapeDtypeStruct((PLANE, DEPTH * rows, kv), BF16),
-        2 * flops,
+        4 * flops,
         2 << 20,
         columns_own,
+        columns_more,
         grad,
         grad_far,
-        swap_core(part),
+        swap_core(grad),
+        swap_core(grad_far),
         scratch=[pltpu.VMEM((PLANE, DEPTH * rows, kv), BF16), copies(PLANE // 4)],
         out=HBM,
     )
+    part, grad, grad_far = lax.optimization_barrier((part, grad, grad_far))
+
     keep, send = call(
         back_kernel, (block, block), 8 * tok * feats * kv, 4 << 20, grad, grad_far, weight, weight_other, late=(0,)
     )
-    part, keep, send, moment, second, master = lax.optimization_barrier(
-        (part, keep, send, moment, second, master)
-    )
+    part, moment, second, master = lax.optimization_barrier((part, moment, second, master))
     moment, second, master, decay = call(
         states_kernel, (jax.ShapeDtypeStruct(master.shape, F32),) * 4, 0, 1 << 17, moment, second, master
     )

time: 116 us -> 114 us (0.983)
  waiting for transfers between devices: 26.3 us -> 18.3 us
  starting transfers between devices: 59 us -> 66.1 us
    ppermute x2 -> x4, starting transfers between devices: 9.31 us -> 15.6 us  [swap_core(): return lax.ppermute(array, 'c', [(0, 1), (1, 0)])]
    all_to_all x4, waiting for transfers between devices: 17 us -> 11.9 us  [exchange(): lax.all_to_all(blocks, AXES, split_axis=0, concat_axis=0, axis_index_grou...]
    ppermute x4, waiting for transfers between devices: 6.7 us -> 3.63 us  [swap_pair(): return lax.ppermute(array, 'zll', [(0, 1), (1, 0)])]
    pallas_call x16 -> x15, Pallas kernels: 24.3 us -> 23.3 us  [call(): pl.pallas_call(kernel, out_shape=out_shape, in_specs=specs, out_specs=out...]
    unnamed x30 -> x26, local copies, waits for them, and re-layouts: 2.6 us -> 2.84 us
    ppermute x2 -> x4, waiting for transfers between devices: 2.53 us -> 2.76 us  [swap_core(): return lax.ppermute(array, 'c', [(0, 1), (1, 0)])]
  transfers between devices with their start and end apart: 10 -> 12, of which waited for: 6 -> 4; matrix products, arithmetic and copies ran while one was open for 0% -> 0% of each run, Pallas kernels for 17% -> 17%
where the time goes in v11:
time: 114 us; the launch traced here: 113 us
  starting transfers between devices  66.1 us (58%)
  Pallas kernels  23.3 us (20%)
  waiting for transfers between devices  18.3 us (16%)
  local copies, waits for them, and re-layouts  2.96 us (3%)
    all_to_all x4, starting transfers between devices, exchange(): lax.all_to_all(blocks, AXES, split_axis=0, concat_axis=0, axis_index_grou...  39.8 us
    pallas_call x15, Pallas kernels, call(): pl.pallas_call(kernel, out_shape=out_shape, in_specs=specs, out_specs=out...  23.3 us
    ppermute x4, starting transfers between devices, swap_core(): return lax.ppermute(array, 'c', [(0, 1), (1, 0)])  15.6 us
    all_to_all x4, waiting for transfers between devices, exchange(): lax.all_to_all(blocks, AXES, split_axis=0, concat_axis=0, axis_index_grou...  11.9 us
    ppermute x4, starting transfers between devices, swap_pair(): return lax.ppermute(array, 'zll', [(0, 1), (1, 0)])  10.7 us
    ppermute x4, waiting for transfers between devices, swap_pair(): return lax.ppermute(array, 'zll', [(0, 1), (1, 0)])  3.63 us
    unnamed x26, local copies, waits for them, and re-layouts  2.84 us
    ppermute x4, waiting for transfers between devices, swap_core(): return lax.ppermute(array, 'c', [(0, 1), (1, 0)])  2.76 us
  transfers between devices with their start and end apart: 12, of which 4 were waited for; matrix products, arithmetic and copies ran while one was open for 0% of the time, Pallas kernels for 17%

profile of v11, /device:TPU:1, one launch (start us, length us, event | category | flops | bytes accessed | tf_op | source)
XLA Modules:
  0.0 112.6 jit_solution(4392377136326673812)
XLA Ops:
  0.6 1.4 %shard_map.110 = bf16[8,8,512]{2,1,0:T(8,128)(2,1)} custom-call(f32[8,512]{1,0:T(8,128)} %master_ref.2), custom_call_target="tpu_custom_call" | custom-call | bytes 131072 | tf_op jit(solution)/shard_map/pallas_call | solution.py:247
  2.0 16.9 %all-to-all-start = ((bf16[8,8,512]{2,1,0:T(8,128)(2,1)}), bf16[8,8,512]{2,1,0:T(8,128)(2,1)S(1)}, u32[]{:S(2)}, u32[]{:S(2)}) async-start(bf16[8,8,512]{2,1,0:T(8,128)(2,1)} %shard_map.110), calls=%async_computation | async-start | bytes 131072 | tf_op jit(solution)/shard_map/all_to_all | solution.py:271
  18.9 2.9 %shard_map.113 = bf16[128,2048]{1,0:T(8,128)(2,1)S(1)} custom-call(s32[2]{0:T(128)S(1)} %pad_add_fusion.at_ref, bf16[128,4096]{1,0:T(8,128)(2,1)} %hidden_ref.1), custom_call_target="tpu_custom_call" | custom-call | flops 536870912 | bytes 2097152 | tf_op jit(solution)/shard_map/pallas_call | solution.py:247
  21.8 2.6 %collective-permute-start = (bf16[128,2048]{1,0:T(8,128)(2,1)S(1)}, bf16[128,2048]{1,0:T(8,128)(2,1)S(1)}, u32[]{:S(2)}, u32[]{:S(2)}) collective-permute-start(bf16[128,2048]{1,0:T(8,128)(2,1)S(1)} %shard_map.113), channel_id=1, source_target_pairs={{0,128},{128,0},{1,129},{129,1},{2,130},{130,2},{3,131},{131,3},{4... | collective-permute-start | bytes 1572872 | tf_op jit(solution)/shard_map/ppermute | solution.py:263
  25.6 6.8 %all-to-all-start.1 = ((bf16[16,64,512]{2,1,0:T(8,128)(2,1)}), bf16[16,64,512]{2,1,0:T(8,128)(2,1)S(1)}, u32[]{:S(2)}, u32[]{:S(2)}) async-start(bf16[16,64,512]{2,1,0:T(8,128)(2,1)} %shard_map.111), calls=%async_computation.1 | async-start | bytes 2097152 | tf_op jit(solution)/shard_map/all_to_all | solution.py:271
  32.4 3.7 %shard_map.112 = (bf16[128,1024]{1,0:T(8,128)(2,1)}, bf16[128,1024]{1,0:T(8,128)(2,1)}) custom-call(s32[2]{0:T(128)S(1)} %pad_add_fusion.at_ref, bf16[128,4096]{1,0:T(8,128)(2,1)} %hidden_ref.1), custom_call_target="tpu_custom_call" | custom-call | flops 536870912 | bytes 2097152 | tf_op jit(solution)/shard_map/pallas_call | solution.py:247
  37.9 1.2 %shard_map.114 = (bf16[1024,256]{1,0:T(8,128)(2,1)}, bf16[1024,256]{1,0:T(8,128)(2,1)}) custom-call(bf16[128,1024]{1,0:T(8,128)(2,1)S(1)} %copy-done.5, bf16[128,1024]{1,0:T(8,128)(2,1)S(1)} %copy-done.3, bf16[128,2048]{1,0:T(8,128)(2,1)S(1)} %collective-permute-done.far_ref.rows_ref), custom_call_target="tpu_custom_call" | custom-call | flops 1431655808 | bytes 2097152 | tf_op jit(solution)/shard_map/pallas_call | solution.py:247
  39.1 4.0 %collective-permute-start.1 = (bf16[1024,256]{1,0:T(8,128)(2,1)}, bf16[1024,256]{1,0:T(8,128)(2,1)S(1)}, u32[]{:S(2)}, u32[]{:S(2)}) collective-permute-start(bf16[1024,256]{1,0:T(8,128)(2,1)} %get-tuple-element.45), channel_id=1, source_target_pairs={{0,16},{16,0},{1,17},{17,1},{2,18},{18,2},{3,19},{19,3},{4,20},{20... | collective-permute-start | bytes 1572872 | tf_op jit(solution)/shard_map/ppermute | solution.py:259
  44.5 3.8 %shard_map.115.probs_ref = bf16[4,1024,128]{2,1,0:T(8,128)(2,1)} custom-call(bf16[128,4096]{1,0:T(8,128)(2,1)S(1)} %copy-done.1, bf16[128,512]{1,0:T(8,128)(2,1)S(1)} %copy-done.7, s32[1,128]{1,0:T(1,128)S(1)} %bitcast.13, s32[128,1]{1,0:T(8,128)S(1)} %copy.13.seg_col_ref), custom_call_target="tpu_custom_call" | custom-call | flops 268435456 | bytes 8388608 | tf_op jit(solution)/shard_map/pallas_call | solution.py:247
  48.3 4.3 %collective-permute-start.2 = (bf16[1024,512]{1,0:T(8,128)(2,1)S(1)}, bf16[1024,512]{1,0:T(8,128)(2,1)S(1)}, u32[]{:S(2)}, u32[]{:S(2)}) collective-permute-start(bf16[1024,512]{1,0:T(8,128)(2,1)S(1)} %bitcast.8), channel_id=1, source_target_pairs={{0,16},{16,0},{1,17},{17,1},{2,18},{18,2},{3,19},{19,3},{4,20},{20... | collective-permute-start | bytes 3145736 | tf_op jit(solution)/shard_map/ppermute | solution.py:259
  53.0 1.8 %collective-permute-done.2.weight_ref.other_ref = bf16[1024,512]{1,0:T(8,128)(2,1)S(1)} collective-permute-done((bf16[1024,512]{1,0:T(8,128)(2,1)S(1)}, bf16[1024,512]{1,0:T(8,128)(2,1)S(1)}, u32[]{:S(2)}, u32[]{:S(2)}) %collective-permute-start.2) | collective-permute-done | bytes 1048608 | tf_op jit(solution)/shard_map/ppermute | solution.py:259
  55.1 2.8 %collective-permute-start.3 = (bf16[128,512]{1,0:T(8,128)(2,1)S(1)}, bf16[128,512]{1,0:T(8,128)(2,1)S(1)}, u32[]{:S(2)}, u32[]{:S(2)}) collective-permute-start(bf16[128,512]{1,0:T(8,128)(2,1)S(1)} %shard_map.118), channel_id=1, source_target_pairs={{0,128},{128,0},{1,129},{129,1},{2,130},{130,2},{3,131},{131,3},{4... | collective-permute-start | bytes 393224 | tf_op jit(solution)/shard_map/ppermute | solution.py:263
  58.3 3.6 %collective-permute-done.3.sent_ref = bf16[128,512]{1,0:T(8,128)(2,1)S(1)} collective-permute-done((bf16[128,512]{1,0:T(8,128)(2,1)S(1)}, bf16[128,512]{1,0:T(8,128)(2,1)S(1)}, u32[]{:S(2)}, u32[]{:S(2)}) %collective-permute-start.3) | collective-permute-done | bytes 131104 | tf_op jit(solution)/shard_map/ppermute | solution.py:263
  61.9 1.4 %shard_map.119 = (bf16[128,4096]{1,0:T(8,128)(2,1)}, bf16[128,512]{1,0:T(8,128)(2,1)S(1)}) custom-call(f32[128,512]{1,0:T(8,128)S(1)} %shard_map.117.near_ref, bf16[128,512]{1,0:T(8,128)(2,1)S(1)} %collective-permute-done.3.sent_ref, bf16[4,1024,128]{2,1,0:T(8,128)(2,1)S(1)} %copy-done), custom_call_target="tpu_custom_call" | custom-call | flops 268435456 | bytes 4194304 | tf_op jit(solution)/shard_map/pallas_call | solution.py:247
  63.3 2.6 %collective-permute-start.4 = (bf16[128,512]{1,0:T(8,128)(2,1)S(1)}, bf16[128,512]{1,0:T(8,128)(2,1)S(1)}, u32[]{:S(2)}, u32[]{:S(2)}) collective-permute-start(bf16[128,512]{1,0:T(8,128)(2,1)S(1)} %get-tuple-element.58.near_ref), channel_id=1, source_target_pairs={{0,128},{128,0},{1,129},{129,1},{2,130},{130,2},{3,131},{131,3},{4... | collective-permute-start | bytes 393224 | tf_op jit(solution)/shard_map/ppermute | solution.py:263
  66.0 3.4 %collective-permute-start.5 = (bf16[128,512]{1,0:T(8,128)(2,1)S(1)}, bf16[128,512]{1,0:T(8,128)(2,1)S(1)}, u32[]{:S(2)}, u32[]{:S(2)}) collective-permute-start(bf16[128,512]{1,0:T(8,128)(2,1)S(1)} %get-tuple-element.58.near_ref), channel_id=1, source_target_pairs={{0,16},{16,0},{1,17},{17,1},{2,18},{18,2},{3,19},{19,3},{4,20},{20... | collective-permute-start | bytes 393224 | tf_op jit(solution)/shard_map/ppermute | solution.py:259
  69.4 3.9 %collective-permute-start.6 = (bf16[128,512]{1,0:T(8,128)(2,1)S(1)}, bf16[128,512]{1,0:T(8,128)(2,1)S(1)}, u32[]{:S(2)}, u32[]{:S(2)}) collective-permute-start(bf16[128,512]{1,0:T(8,128)(2,1)S(1)} %collective-permute-done.4.far_ref), channel_id=1, source_target_pairs={{0,16},{16,0},{1,17},{17,1},{2,18},{18,2},{3,19},{19,3},{4,20},{20... | collective-permute-start | bytes 393224 | tf_op jit(solution)/shard_map/ppermute | solution.py:259
  74.3 1.4 %shard_map.120 = bf16[16,64,512]{2,1,0:T(8,128)(2,1)} custom-call(bf16[1024,256]{1,0:T(8,128)(2,1)S(1)} %copy-done.2, bf16[1024,256]{1,0:T(8,128)(2,1)S(1)} %collective-permute-done.1.more_ref, bf16[128,512]{1,0:T(8,128)(2,1)S(1)} %get-tuple-element.58.near_ref, bf16[128,512]{1,0:T(8,128)(2,1)S(1)} %collective-permute-done.4.far_ref, ...), custom_call_target="tpu_custom_call" | custom-call | flops 536870912 | bytes 2097152 | tf_op jit(solution)/shard_map/pallas_call | solution.py:247
  75.7 4.8 %all-to-all-start.2 = ((bf16[16,64,512]{2,1,0:T(8,128)(2,1)}), bf16[16,64,512]{2,1,0:T(8,128)(2,1)S(1)}, u32[]{:S(2)}, u32[]{:S(2)}) async-start(bf16[16,64,512]{2,1,0:T(8,128)(2,1)} %shard_map.120), calls=%async_computation.2 | async-start | bytes 2097152 | tf_op jit(solution)/shard_map/all_to_all | solution.py:271
  80.5 1.7 %shard_map.121 = (bf16[128,2048]{1,0:T(8,128)(2,1)}, bf16[128,2048]{1,0:T(8,128)(2,1)}) custom-call(bf16[128,512]{1,0:T(8,128)(2,1)S(1)} %get-tuple-element.58.near_ref, bf16[128,512]{1,0:T(8,128)(2,1)S(1)} %collective-permute-done.4.far_ref, bf16[1024,512]{1,0:T(8,128)(2,1)S(1)} %bitcast.10, bf16[1024,512]{1,0:T(8,128)(2,1)S(1)} %collective-permute-done.2.weight_ref.other_ref), custom_call_target="tpu_custom_call" | custom-call | flops 536870912 | bytes 4194304 | tf_op jit(solution)/shard_map/pallas_call | solution.py:247
  82.2 2.6 %collective-permute-start.7 = (bf16[128,2048]{1,0:T(8,128)(2,1)}, bf16[128,2048]{1,0:T(8,128)(2,1)S(1)}, u32[]{:S(2)}, u32[]{:S(2)}) collective-permute-start(bf16[128,2048]{1,0:T(8,128)(2,1)} %get-tuple-element.61), channel_id=1, source_target_pairs={{0,128},{128,0},{1,129},{129,1},{2,130},{130,2},{3,131},{131,3},{4... | collective-permute-start | bytes 1572872 | tf_op jit(solution)/shard_map/ppermute | solution.py:263
  84.9 11.9 %all-to-all-done.2.parts_ref = bf16[16,64,512]{2,1,0:T(8,128)(2,1)S(1)} async-done(((bf16[16,64,512]{2,1,0:T(8,128)(2,1)}), bf16[16,64,512]{2,1,0:T(8,128)(2,1)S(1)}, u32[]{:S(2)}, u32[]{:S(2)}) %all-to-all-start.2) | async-done | bytes 1048608 | tf_op jit(solution)/shard_map/all_to_all | solution.py:271
  97.6 11.5 %all-to-all-start.3 = ((bf16[8,8,512]{2,1,0:T(8,128)(2,1)}), bf16[8,8,512]{2,1,0:T(8,128)(2,1)S(1)}, u32[]{:S(2)}, u32[]{:S(2)}) async-start(bf16[8,8,512]{2,1,0:T(8,128)(2,1)} %shard_map.124), calls=%async_computation.3 | async-start | bytes 131072 | tf_op jit(solution)/shard_map/all_to_all | solution.py:271
  109.0 2.9 %shard_map.122 = bf16[128,4096]{1,0:T(8,128)(2,1)} custom-call(s32[2]{0:T(128)S(1)} %pad_add_fusion.at_ref, bf16[128,2048]{1,0:T(8,128)(2,1)S(1)} %copy-done.11, bf16[128,2048]{1,0:T(8,128)(2,1)S(1)} %collective-permute-done.7.got_ref), custom_call_target="tpu_custom_call" | custom-call | flops 34359738368 | bytes 2097152 | tf_op jit(solution)/shard_map/pallas_call | solution.py:247
  (47 shorter events, 7.8 us)
Async XLA Ops:
  2.0 22.5 %all-to-all-start = ((bf16[8,8,512]{2,1,0:T(8,128)(2,1)}), bf16[8,8,512]{2,1,0:T(8,128)(2,1)S(1)}, u32[]{:S(2)}, u32[]{:S(2)}) async-start(bf16[8,8,512]{2,1,0:T(8,128)(2,1)} %shard_map.110), calls=%async_computation | async-start | bytes 131072 | tf_op jit(solution)/shard_map/all_to_all | solution.py:271
  21.8 14.2 %collective-permute-start = (bf16[128,2048]{1,0:T(8,128)(2,1)S(1)}, bf16[128,2048]{1,0:T(8,128)(2,1)S(1)}, u32[]{:S(2)}, u32[]{:S(2)}) collective-permute-start(bf16[128,2048]{1,0:T(8,128)(2,1)S(1)} %shard_map.113), channel_id=1, source_target_pairs={{0,128},{128,0},{1,129},{129,1},{2,130},{130,2},{3,131},{131,3},{4... | collective-permute-start | bytes 1572872 | tf_op jit(solution)/shard_map/ppermute | solution.py:263
  25.6 22.7 %all-to-all-start.1 = ((bf16[16,64,512]{2,1,0:T(8,128)(2,1)}), bf16[16,64,512]{2,1,0:T(8,128)(2,1)S(1)}, u32[]{:S(2)}, u32[]{:S(2)}) async-start(bf16[16,64,512]{2,1,0:T(8,128)(2,1)} %shard_map.111), calls=%async_computation.1 | async-start | bytes 2097152 | tf_op jit(solution)/shard_map/all_to_all | solution.py:271
  36.0 1.0 copy-start.3
  37.0 0.9 copy-start.5
  37.9 5.7 %copy-start.1 = (bf16[128,4096]{1,0:T(8,128)(2,1)S(1)}, bf16[128,4096]{1,0:T(8,128)(2,1)}, u32[]{:S(2)}) copy-start(bf16[128,4096]{1,0:T(8,128)(2,1)} %queries_ref.1) | copy-start | bytes 3145732
  39.1 4.1 %copy-start.12 = (s32[1,4]{1,0:T(1,128)S(1)}, s32[1,4]{1,0:T(1,128)}, u32[]{:S(2)}) copy-start(s32[1,4]{1,0:T(1,128)} %param.10) | copy-start | bytes 52
  39.1 9.1 %collective-permute-start.1 = (bf16[1024,256]{1,0:T(8,128)(2,1)}, bf16[1024,256]{1,0:T(8,128)(2,1)S(1)}, u32[]{:S(2)}, u32[]{:S(2)}) collective-permute-start(bf16[1024,256]{1,0:T(8,128)(2,1)} %get-tuple-element.45), channel_id=1, source_target_pairs={{0,16},{16,0},{1,17},{17,1},{2,18},{18,2},{3,19},{19,3},{4,20},{20... | collective-permute-start | bytes 1572872 | tf_op jit(solution)/shard_map/ppermute | solution.py:259
  44.5 8.0 %copy-start.6 = (bf16[128,1024]{1,0:T(8,128)(2,1)S(1)}, bf16[128,1024]{1,0:T(8,128)(2,1)}, u32[]{:S(2)}) copy-start(bf16[128,1024]{1,0:T(8,128)(2,1)} %get-tuple-element.49.near_own_ref.near_ref) | copy-start | bytes 786436
  48.3 6.6 %collective-permute-start.2 = (bf16[1024,512]{1,0:T(8,128)(2,1)S(1)}, bf16[1024,512]{1,0:T(8,128)(2,1)S(1)}, u32[]{:S(2)}, u32[]{:S(2)}) collective-permute-start(bf16[1024,512]{1,0:T(8,128)(2,1)S(1)} %bitcast.8), channel_id=1, source_target_pairs={{0,16},{16,0},{1,17},{17,1},{2,18},{18,2},{3,19},{19,3},{4,20},{20... | collective-permute-start | bytes 3145736 | tf_op jit(solution)/shard_map/ppermute | solution.py:259
  54.8 3.1 %copy-start.4 = (bf16[128,1024]{1,0:T(8,128)(2,1)S(1)}, bf16[128,1024]{1,0:T(8,128)(2,1)}, u32[]{:S(2)}) copy-start(bf16[128,1024]{1,0:T(8,128)(2,1)} %get-tuple-element.47.near_other_ref.rows_ref) | copy-start | bytes 786436
  55.1 6.8 %copy-start = (bf16[4,1024,128]{2,1,0:T(8,128)(2,1)S(1)}, bf16[4,1024,128]{2,1,0:T(8,128)(2,1)}, u32[]{:S(2)}) copy-start(bf16[4,1024,128]{2,1,0:T(8,128)(2,1)} %shard_map.115.probs_ref) | copy-start | bytes 3145732
  55.1 6.7 %collective-permute-start.3 = (bf16[128,512]{1,0:T(8,128)(2,1)S(1)}, bf16[128,512]{1,0:T(8,128)(2,1)S(1)}, u32[]{:S(2)}, u32[]{:S(2)}) collective-permute-start(bf16[128,512]{1,0:T(8,128)(2,1)S(1)} %shard_map.118), channel_id=1, source_target_pairs={{0,128},{128,0},{1,129},{129,1},{2,130},{130,2},{3,131},{131,3},{4... | collective-permute-start | bytes 393224 | tf_op jit(solution)/shard_map/ppermute | solution.py:263
  58.2 16.0 %copy-start.2 = (bf16[1024,256]{1,0:T(8,128)(2,1)S(1)}, bf16[1024,256]{1,0:T(8,128)(2,1)}, u32[]{:S(2)}) copy-start(bf16[1024,256]{1,0:T(8,128)(2,1)} %get-tuple-element.55.own_ref) | copy-start | bytes 1572868
  63.3 6.0 %collective-permute-start.4 = (bf16[128,512]{1,0:T(8,128)(2,1)S(1)}, bf16[128,512]{1,0:T(8,128)(2,1)S(1)}, u32[]{:S(2)}, u32[]{:S(2)}) collective-permute-start(bf16[128,512]{1,0:T(8,128)(2,1)S(1)} %get-tuple-element.58.near_ref), channel_id=1, source_target_pairs={{0,128},{128,0},{1,129},{129,1},{2,130},{130,2},{3,131},{131,3},{4... | collective-permute-start | bytes 393224 | tf_op jit(solution)/shard_map/ppermute | solution.py:263
  66.0 7.3 %collective-permute-start.5 = (bf16[128,512]{1,0:T(8,128)(2,1)S(1)}, bf16[128,512]{1,0:T(8,128)(2,1)S(1)}, u32[]{:S(2)}, u32[]{:S(2)}) collective-permute-start(bf16[128,512]{1,0:T(8,128)(2,1)S(1)} %get-tuple-element.58.near_ref), channel_id=1, source_target_pairs={{0,16},{16,0},{1,17},{17,1},{2,18},{18,2},{3,19},{19,3},{4,20},{20... | collective-permute-start | bytes 393224 | tf_op jit(solution)/shard_map/ppermute | solution.py:259
  69.4 4.9 %collective-permute-start.6 = (bf16[128,512]{1,0:T(8,128)(2,1)S(1)}, bf16[128,512]{1,0:T(8,128)(2,1)S(1)}, u32[]{:S(2)}, u32[]{:S(2)}) collective-permute-start(bf16[128,512]{1,0:T(8,128)(2,1)S(1)} %collective-permute-done.4.far_ref), channel_id=1, source_target_pairs={{0,16},{16,0},{1,17},{17,1},{2,18},{18,2},{3,19},{19,3},{4,20},{20... | collective-permute-start | bytes 393224 | tf_op jit(solution)/shard_map/ppermute | solution.py:259
  75.7 21.1 %all-to-all-start.2 = ((bf16[16,64,512]{2,1,0:T(8,128)(2,1)}), bf16[16,64,512]{2,1,0:T(8,128)(2,1)S(1)}, u32[]{:S(2)}, u32[]{:S(2)}) async-start(bf16[16,64,512]{2,1,0:T(8,128)(2,1)} %shard_map.120), calls=%async_computation.2 | async-start | bytes 2097152 | tf_op jit(solution)/shard_map/all_to_all | solution.py:271
  80.5 4.4 %copy-start.8 = (f32[8,512]{1,0:T(8,128)S(1)}, f32[8,512]{1,0:T(8,128)}, u32[]{:S(2)}) copy-start(f32[8,512]{1,0:T(8,128)} %master_ref.2) | copy-start | bytes 49156
  80.5 4.4 %copy-start.9 = (f32[8,512]{1,0:T(8,128)S(1)}, f32[8,512]{1,0:T(8,128)}, u32[]{:S(2)}) copy-start(f32[8,512]{1,0:T(8,128)} %moment_ref) | copy-start | bytes 49156
  80.5 4.4 %copy-start.10 = (f32[8,512]{1,0:T(8,128)S(1)}, f32[8,512]{1,0:T(8,128)}, u32[]{:S(2)}) copy-start(f32[8,512]{1,0:T(8,128)} %second_ref) | copy-start | bytes 49156
  82.2 26.8 %collective-permute-start.7 = (bf16[128,2048]{1,0:T(8,128)(2,1)}, bf16[128,2048]{1,0:T(8,128)(2,1)S(1)}, u32[]{:S(2)}, u32[]{:S(2)}) collective-permute-start(bf16[128,2048]{1,0:T(8,128)(2,1)} %get-tuple-element.61), channel_id=1, source_target_pairs={{0,128},{128,0},{1,129},{129,1},{2,130},{130,2},{3,131},{131,3},{4... | collective-permute-start | bytes 1572872 | tf_op jit(solution)/shard_map/ppermute | solution.py:263
  84.9 24.1 %copy-start.11 = (bf16[128,2048]{1,0:T(8,128)(2,1)S(1)}, bf16[128,2048]{1,0:T(8,128)(2,1)}, u32[]{:S(2)}) copy-start(bf16[128,2048]{1,0:T(8,128)(2,1)} %get-tuple-element.60.keep_ref) | copy-start | bytes 1572868
  97.6 14.4 %all-to-all-start.3 = ((bf16[8,8,512]{2,1,0:T(8,128)(2,1)}), bf16[8,8,512]{2,1,0:T(8,128)(2,1)S(1)}, u32[]{:S(2)}, u32[]{:S(2)}) async-start(bf16[8,8,512]{2,1,0:T(8,128)(2,1)} %shard_map.124), calls=%async_computation.3 | async-start | bytes 131072 | tf_op jit(solution)/shard_map/all_to_all | solution.py:271
  (1 other events, 0.9 us)

commit v12 on v11

--- a/solution.py
+++ b/solution.py
@@ -93,14 +93,16 @@
     for copy in copies:
         copy.start()
     matrix_ref[...] = order_matrix(at_ref[0] ^ far, at_ref[1])
-    for y in range(4):
-        rows = slice(y * tok, (y + 1) * tok)
-        for copy in copies[y * 4 : y * 4 + 4]:
+    for first in range(0, 4, 2):
+        for copy in copies[first * 4 : first * 4 + 8]:
             copy.wait()
+        rows = slice(first * tok, (first + 2) * tok)
         moved = jnp.dot(cols_ref[rows], matrix_ref[...], preferred_element_type=F32).astype(BF16)
-        for c in range(2):
-            at = (c * half if far else 0) + y * 256
-            out_refs[0 if far else c][:, at : at + 256] = moved[:, c * 256 : (c + 1) * 256]
+        for y in range(first, first + 2):
+            for c in range(2):
+                at = (c * half if far else 0) + y * 256
+                part = moved[(y - first) * tok : (y - first + 1) * tok, c * 256 : (c + 1) * 256]
+                out_refs[0 if far else c][:, at : at + 256] = part
 
 
 def join_kernel(at_ref, keep_ref, got_ref, out_ref, cols_ref, moved_ref, matrix_ref, sem_ref):
@@ -128,12 +130,19 @@
     out_ref[...] = total.astype(out_ref.dtype)
 
 
-def flip_kernel(near_own_ref, near_other_ref, far_ref, own_ref, other_ref):
+def flip_kernel(near_own_ref, near_other_ref, far_ref, own_ref, other_ref, near_ref, sem_ref):
     tok, half = near_own_ref.shape
-    own_ref[:, :tok] = near_own_ref[...].T
+    copies = [
+        pltpu.make_async_copy(ref, near_ref.at[i], sem_ref.at[i]) for i, ref in enumerate((near_own_ref, near_other_ref))
+    ]
+    for copy in copies:
+        copy.start()
     own_ref[:, tok:] = far_ref[:, :half].T
-    other_ref[:, :tok] = near_other_ref[...].T
     other_ref[:, tok:] = far_ref[:, half:].T
+    for copy in copies:
+        copy.wait()
+    own_ref[:, :tok] = near_ref[0].T
+    other_ref[:, :tok] = near_ref[1].T
 
 
 def fold_kernel(own_ref, more_ref, near_ref, far_ref, near_more_ref, far_more_ref, out_ref, rows_ref, sem_ref):
@@ -343,7 +352,8 @@
     )
     flipped = jax.ShapeDtypeStruct((feats, 2 * tok), BF16)
     columns_own, columns_other = call(
-        flip_kernel, (flipped, flipped), WEIGHTY // 24, 2 << 20, near_own, near_other, far, late=(0, 1)
+        flip_kernel, (flipped, flipped), WEIGHTY // 24, 2 << 20, near_own, near_other, far,
+        scratch=[pltpu.VMEM((2, tok, feats), BF16), copies(2)], hbm=(0, 1), late=(0, 1)
     )
     columns_more = swap_core(columns_other)
     weight, near_own, near_other, far, columns_own, columns_more, probs = lax.optimization_barrier(

time: 114 us -> 114 us (level); the launches traced: 113 us -> 111 us
  local copies, waits for them, and re-layouts: 2.96 us -> 1.07 us
    unnamed x26 -> x22, local copies, waits for them, and re-layouts: 2.84 us -> 0.95 us
  transfers between devices with their start and end apart: 12 -> 12, of which waited for: 4 -> 6; matrix products, arithmetic and copies ran while one was open for 0% -> 0% of each run, Pallas kernels for 17% -> 17%
where the time goes in v12:
time: 114 us; the launch traced here: 111 us
  starting transfers between devices  65.9 us (58%)
  Pallas kernels  23.8 us (21%)
  waiting for transfers between devices  18.7 us (16%)
    all_to_all x4, starting transfers between devices, exchange(): lax.all_to_all(blocks, AXES, split_axis=0, concat_axis=0, axis_index_grou...  38.9 us
    pallas_call x15, Pallas kernels, call(): pl.pallas_call(kernel, out_shape=out_shape, in_specs=specs, out_specs=out...  23.8 us
    ppermute x4, starting transfers between devices, swap_core(): return lax.ppermute(array, 'c', [(0, 1), (1, 0)])  16.3 us
    all_to_all x4, waiting for transfers between devices, exchange(): lax.all_to_all(blocks, AXES, split_axis=0, concat_axis=0, axis_index_grou...  12.2 us
    ppermute x4, starting transfers between devices, swap_pair(): return lax.ppermute(array, 'zll', [(0, 1), (1, 0)])  10.7 us
    ppermute x4, waiting for transfers between devices, swap_pair(): return lax.ppermute(array, 'zll', [(0, 1), (1, 0)])  3.73 us
    ppermute x4, waiting for transfers between devices, swap_core(): return lax.ppermute(array, 'c', [(0, 1), (1, 0)])  2.76 us
  transfers between devices with their start and end apart: 12, of which 6 were waited for; matrix products, arithmetic and copies ran while one was open for 0% of the time, Pallas kernels for 17%

profile of v12, /device:TPU:1, one launch (start us, length us, event | category | flops | bytes accessed | tf_op | source)
XLA Modules:
  0.0 111.4 jit_solution(11443592027972743226)
XLA Ops:
  0.6 1.4 %shard_map.110 = bf16[8,8,512]{2,1,0:T(8,128)(2,1)} custom-call(f32[8,512]{1,0:T(8,128)} %master_ref.2), custom_call_target="tpu_custom_call" | custom-call | bytes 131072 | tf_op jit(solution)/shard_map/pallas_call | solution.py:256
  2.0 16.9 %all-to-all-start = ((bf16[8,8,512]{2,1,0:T(8,128)(2,1)}), bf16[8,8,512]{2,1,0:T(8,128)(2,1)S(1)}, u32[]{:S(2)}, u32[]{:S(2)}) async-start(bf16[8,8,512]{2,1,0:T(8,128)(2,1)} %shard_map.110), calls=%async_computation | async-start | bytes 131072 | tf_op jit(solution)/shard_map/all_to_all | solution.py:280
  18.9 2.6 %shard_map.113 = bf16[128,2048]{1,0:T(8,128)(2,1)S(1)} custom-call(s32[2]{0:T(128)S(1)} %pad_add_fusion.at_ref, bf16[128,4096]{1,0:T(8,128)(2,1)} %hidden_ref.1), custom_call_target="tpu_custom_call" | custom-call | flops 536870912 | bytes 2097152 | tf_op jit(solution)/shard_map/pallas_call | solution.py:256
  21.6 2.7 %collective-permute-start = (bf16[128,2048]{1,0:T(8,128)(2,1)S(1)}, bf16[128,2048]{1,0:T(8,128)(2,1)S(1)}, u32[]{:S(2)}, u32[]{:S(2)}) collective-permute-start(bf16[128,2048]{1,0:T(8,128)(2,1)S(1)} %shard_map.113), channel_id=1, source_target_pairs={{0,128},{128,0},{1,129},{129,1},{2,130},{130,2},{3,131},{131,3},{4... | collective-permute-start | bytes 1572872 | tf_op jit(solution)/shard_map/ppermute | solution.py:272
  25.3 6.8 %all-to-all-start.1 = ((bf16[16,64,512]{2,1,0:T(8,128)(2,1)}), bf16[16,64,512]{2,1,0:T(8,128)(2,1)S(1)}, u32[]{:S(2)}, u32[]{:S(2)}) async-start(bf16[16,64,512]{2,1,0:T(8,128)(2,1)} %shard_map.111), calls=%async_computation.1 | async-start | bytes 2097152 | tf_op jit(solution)/shard_map/all_to_all | solution.py:280
  32.1 3.4 %shard_map.112 = (bf16[128,1024]{1,0:T(8,128)(2,1)}, bf16[128,1024]{1,0:T(8,128)(2,1)}) custom-call(s32[2]{0:T(128)S(1)} %pad_add_fusion.at_ref, bf16[128,4096]{1,0:T(8,128)(2,1)} %hidden_ref.1), custom_call_target="tpu_custom_call" | custom-call | flops 536870912 | bytes 2097152 | tf_op jit(solution)/shard_map/pallas_call | solution.py:256
  35.6 2.3 %shard_map.114 = (bf16[1024,256]{1,0:T(8,128)(2,1)}, bf16[1024,256]{1,0:T(8,128)(2,1)}) custom-call(bf16[128,1024]{1,0:T(8,128)(2,1)} %get-tuple-element.49.near_own_ref.near_ref, bf16[128,1024]{1,0:T(8,128)(2,1)} %get-tuple-element.47.near_other_ref.rows_ref, bf16[128,2048]{1,0:T(8,128)(2,1)S(1)} %collective-permute-done.far_ref.rows_ref), custom_call_target="tpu_custom_call" | custom-call | flops 1431655808 | bytes 2097152 | tf_op jit(solution)/shard_map/pallas_call | solution.py:256
  37.9 4.1 %collective-permute-start.1 = (bf16[1024,256]{1,0:T(8,128)(2,1)}, bf16[1024,256]{1,0:T(8,128)(2,1)S(1)}, u32[]{:S(2)}, u32[]{:S(2)}) collective-permute-start(bf16[1024,256]{1,0:T(8,128)(2,1)} %get-tuple-element.45), channel_id=1, source_target_pairs={{0,16},{16,0},{1,17},{17,1},{2,18},{18,2},{3,19},{19,3},{4,20},{20... | collective-permute-start | bytes 1572872 | tf_op jit(solution)/shard_map/ppermute | solution.py:268
  43.3 3.8 %shard_map.115.probs_ref = bf16[4,1024,128]{2,1,0:T(8,128)(2,1)} custom-call(bf16[128,4096]{1,0:T(8,128)(2,1)S(1)} %copy-done.1, bf16[128,512]{1,0:T(8,128)(2,1)S(1)} %copy-done.5, s32[1,128]{1,0:T(1,128)S(1)} %bitcast.13, s32[128,1]{1,0:T(8,128)S(1)} %copy.13.seg_col_ref), custom_call_target="tpu_custom_call" | custom-call | flops 268435456 | bytes 8388608 | tf_op jit(solution)/shard_map/pallas_call | solution.py:256
  47.4 4.9 %collective-permute-start.2 = (bf16[1024,512]{1,0:T(8,128)(2,1)S(1)}, bf16[1024,512]{1,0:T(8,128)(2,1)S(1)}, u32[]{:S(2)}, u32[]{:S(2)}) collective-permute-start(bf16[1024,512]{1,0:T(8,128)(2,1)S(1)} %bitcast.8), channel_id=1, source_target_pairs={{0,16},{16,0},{1,17},{17,1},{2,18},{18,2},{3,19},{19,3},{4,20},{20... | collective-permute-start | bytes 3145736 | tf_op jit(solution)/shard_map/ppermute | solution.py:268
  52.8 1.8 %collective-permute-done.2.weight_ref.other_ref = bf16[1024,512]{1,0:T(8,128)(2,1)S(1)} collective-permute-done((bf16[1024,512]{1,0:T(8,128)(2,1)S(1)}, bf16[1024,512]{1,0:T(8,128)(2,1)S(1)}, u32[]{:S(2)}, u32[]{:S(2)}) %collective-permute-start.2) | collective-permute-done | bytes 1048608 | tf_op jit(solution)/shard_map/ppermute | solution.py:268
  54.9 2.8 %collective-permute-start.3 = (bf16[128,512]{1,0:T(8,128)(2,1)S(1)}, bf16[128,512]{1,0:T(8,128)(2,1)S(1)}, u32[]{:S(2)}, u32[]{:S(2)}) collective-permute-start(bf16[128,512]{1,0:T(8,128)(2,1)S(1)} %shard_map.118), channel_id=1, source_target_pairs={{0,128},{128,0},{1,129},{129,1},{2,130},{130,2},{3,131},{131,3},{4... | collective-permute-start | bytes 393224 | tf_op jit(solution)/shard_map/ppermute | solution.py:272
  58.0 3.6 %collective-permute-done.3.sent_ref = bf16[128,512]{1,0:T(8,128)(2,1)S(1)} collective-permute-done((bf16[128,512]{1,0:T(8,128)(2,1)S(1)}, bf16[128,512]{1,0:T(8,128)(2,1)S(1)}, u32[]{:S(2)}, u32[]{:S(2)}) %collective-permute-start.3) | collective-permute-done | bytes 131104 | tf_op jit(solution)/shard_map/ppermute | solution.py:272
  61.6 1.4 %shard_map.119 = (bf16[128,4096]{1,0:T(8,128)(2,1)}, bf16[128,512]{1,0:T(8,128)(2,1)S(1)}) custom-call(f32[128,512]{1,0:T(8,128)S(1)} %shard_map.117.near_ref, bf16[128,512]{1,0:T(8,128)(2,1)S(1)} %collective-permute-done.3.sent_ref, bf16[4,1024,128]{2,1,0:T(8,128)(2,1)S(1)} %copy-done), custom_call_target="tpu_custom_call" | custom-call | flops 268435456 | bytes 4194304 | tf_op jit(solution)/shard_map/pallas_call | solution.py:256
  63.1 2.6 %collective-permute-start.4 = (bf16[128,512]{1,0:T(8,128)(2,1)S(1)}, bf16[128,512]{1,0:T(8,128)(2,1)S(1)}, u32[]{:S(2)}, u32[]{:S(2)}) collective-permute-start(bf16[128,512]{1,0:T(8,128)(2,1)S(1)} %get-tuple-element.58.near_ref), channel_id=1, source_target_pairs={{0,128},{128,0},{1,129},{129,1},{2,130},{130,2},{3,131},{131,3},{4... | collective-permute-start | bytes 393224 | tf_op jit(solution)/shard_map/ppermute | solution.py:272
  65.7 3.4 %collective-permute-start.5 = (bf16[128,512]{1,0:T(8,128)(2,1)S(1)}, bf16[128,512]{1,0:T(8,128)(2,1)S(1)}, u32[]{:S(2)}, u32[]{:S(2)}) collective-permute-start(bf16[128,512]{1,0:T(8,128)(2,1)S(1)} %get-tuple-element.58.near_ref), channel_id=1, source_target_pairs={{0,16},{16,0},{1,17},{17,1},{2,18},{18,2},{3,19},{19,3},{4,20},{20... | collective-permute-start | bytes 393224 | tf_op jit(solution)/shard_map/ppermute | solution.py:268
  69.1 3.9 %collective-permute-start.6 = (bf16[128,512]{1,0:T(8,128)(2,1)S(1)}, bf16[128,512]{1,0:T(8,128)(2,1)S(1)}, u32[]{:S(2)}, u32[]{:S(2)}) collective-permute-start(bf16[128,512]{1,0:T(8,128)(2,1)S(1)} %collective-permute-done.4.far_ref), channel_id=1, source_target_pairs={{0,16},{16,0},{1,17},{17,1},{2,18},{18,2},{3,19},{19,3},{4,20},{20... | collective-permute-start | bytes 393224 | tf_op jit(solution)/shard_map/ppermute | solution.py:268
  74.0 1.4 %shard_map.120 = bf16[16,64,512]{2,1,0:T(8,128)(2,1)} custom-call(bf16[1024,256]{1,0:T(8,128)(2,1)S(1)} %copy-done.2, bf16[1024,256]{1,0:T(8,128)(2,1)S(1)} %collective-permute-done.1.more_ref, bf16[128,512]{1,0:T(8,128)(2,1)S(1)} %get-tuple-element.58.near_ref, bf16[128,512]{1,0:T(8,128)(2,1)S(1)} %collective-permute-done.4.far_ref, ...), custom_call_target="tpu_custom_call" | custom-call | flops 536870912 | bytes 2097152 | tf_op jit(solution)/shard_map/pallas_call | solution.py:256
  75.5 3.8 %all-to-all-start.2 = ((bf16[16,64,512]{2,1,0:T(8,128)(2,1)}), bf16[16,64,512]{2,1,0:T(8,128)(2,1)S(1)}, u32[]{:S(2)}, u32[]{:S(2)}) async-start(bf16[16,64,512]{2,1,0:T(8,128)(2,1)} %shard_map.120), calls=%async_computation.2 | async-start | bytes 2097152 | tf_op jit(solution)/shard_map/all_to_all | solution.py:280
  79.3 1.7 %shard_map.121 = (bf16[128,2048]{1,0:T(8,128)(2,1)}, bf16[128,2048]{1,0:T(8,128)(2,1)}) custom-call(bf16[128,512]{1,0:T(8,128)(2,1)S(1)} %get-tuple-element.58.near_ref, bf16[128,512]{1,0:T(8,128)(2,1)S(1)} %collective-permute-done.4.far_ref, bf16[1024,512]{1,0:T(8,128)(2,1)S(1)} %bitcast.10, bf16[1024,512]{1,0:T(8,128)(2,1)S(1)} %collective-permute-done.2.weight_ref.other_ref), custom_call_target="tpu_custom_call" | custom-call | flops 536870912 | bytes 4194304 | tf_op jit(solution)/shard_map/pallas_call | solution.py:256
  81.0 2.6 %collective-permute-start.7 = (bf16[128,2048]{1,0:T(8,128)(2,1)}, bf16[128,2048]{1,0:T(8,128)(2,1)S(1)}, u32[]{:S(2)}, u32[]{:S(2)}) collective-permute-start(bf16[128,2048]{1,0:T(8,128)(2,1)} %get-tuple-element.61), channel_id=1, source_target_pairs={{0,128},{128,0},{1,129},{129,1},{2,130},{130,2},{3,131},{131,3},{4... | collective-permute-start | bytes 1572872 | tf_op jit(solution)/shard_map/ppermute | solution.py:272
  83.7 11.9 %all-to-all-done.2.parts_ref = bf16[16,64,512]{2,1,0:T(8,128)(2,1)S(1)} async-done(((bf16[16,64,512]{2,1,0:T(8,128)(2,1)}), bf16[16,64,512]{2,1,0:T(8,128)(2,1)S(1)}, u32[]{:S(2)}, u32[]{:S(2)}) %all-to-all-start.2) | async-done | bytes 1048608 | tf_op jit(solution)/shard_map/all_to_all | solution.py:280
  96.4 11.5 %all-to-all-start.3 = ((bf16[8,8,512]{2,1,0:T(8,128)(2,1)}), bf16[8,8,512]{2,1,0:T(8,128)(2,1)S(1)}, u32[]{:S(2)}, u32[]{:S(2)}) async-start(bf16[8,8,512]{2,1,0:T(8,128)(2,1)} %shard_map.124), calls=%async_computation.3 | async-start | bytes 131072 | tf_op jit(solution)/shard_map/all_to_all | solution.py:280
  107.9 2.9 %shard_map.122 = bf16[128,4096]{1,0:T(8,128)(2,1)} custom-call(s32[2]{0:T(128)S(1)} %pad_add_fusion.at_ref, bf16[128,2048]{1,0:T(8,128)(2,1)S(1)} %copy-done.9, bf16[128,2048]{1,0:T(8,128)(2,1)S(1)} %collective-permute-done.7.got_ref), custom_call_target="tpu_custom_call" | custom-call | flops 34359738368 | bytes 2097152 | tf_op jit(solution)/shard_map/pallas_call | solution.py:256
  (43 shorter events, 6.4 us)
Async XLA Ops:
  2.0 22.2 %all-to-all-start = ((bf16[8,8,512]{2,1,0:T(8,128)(2,1)}), bf16[8,8,512]{2,1,0:T(8,128)(2,1)S(1)}, u32[]{:S(2)}, u32[]{:S(2)}) async-start(bf16[8,8,512]{2,1,0:T(8,128)(2,1)} %shard_map.110), calls=%async_computation | async-start | bytes 131072 | tf_op jit(solution)/shard_map/all_to_all | solution.py:280
  21.6 14.1 %collective-permute-start = (bf16[128,2048]{1,0:T(8,128)(2,1)S(1)}, bf16[128,2048]{1,0:T(8,128)(2,1)S(1)}, u32[]{:S(2)}, u32[]{:S(2)}) collective-permute-start(bf16[128,2048]{1,0:T(8,128)(2,1)S(1)} %shard_map.113), channel_id=1, source_target_pairs={{0,128},{128,0},{1,129},{129,1},{2,130},{130,2},{3,131},{131,3},{4... | collective-permute-start | bytes 1572872 | tf_op jit(solution)/shard_map/ppermute | solution.py:272
  25.3 22.0 %all-to-all-start.1 = ((bf16[16,64,512]{2,1,0:T(8,128)(2,1)}), bf16[16,64,512]{2,1,0:T(8,128)(2,1)S(1)}, u32[]{:S(2)}, u32[]{:S(2)}) async-start(bf16[16,64,512]{2,1,0:T(8,128)(2,1)} %shard_map.111), calls=%async_computation.1 | async-start | bytes 2097152 | tf_op jit(solution)/shard_map/all_to_all | solution.py:280
  35.6 6.8 %copy-start.1 = (bf16[128,4096]{1,0:T(8,128)(2,1)S(1)}, bf16[128,4096]{1,0:T(8,128)(2,1)}, u32[]{:S(2)}) copy-start(bf16[128,4096]{1,0:T(8,128)(2,1)} %queries_ref.1) | copy-start | bytes 3145732
  37.9 4.1 %copy-start.10 = (s32[1,4]{1,0:T(1,128)S(1)}, s32[1,4]{1,0:T(1,128)}, u32[]{:S(2)}) copy-start(s32[1,4]{1,0:T(1,128)} %param.10) | copy-start | bytes 52
  37.9 9.1 %collective-permute-start.1 = (bf16[1024,256]{1,0:T(8,128)(2,1)}, bf16[1024,256]{1,0:T(8,128)(2,1)S(1)}, u32[]{:S(2)}, u32[]{:S(2)}) collective-permute-start(bf16[1024,256]{1,0:T(8,128)(2,1)} %get-tuple-element.45), channel_id=1, source_target_pairs={{0,16},{16,0},{1,17},{17,1},{2,18},{18,2},{3,19},{19,3},{4,20},{20... | collective-permute-start | bytes 1572872 | tf_op jit(solution)/shard_map/ppermute | solution.py:268
  42.4 0.9 copy-start.5
  43.3 9.0 %copy-start.4 = (bf16[128,1024]{1,0:T(8,128)(2,1)S(1)}, bf16[128,1024]{1,0:T(8,128)(2,1)}, u32[]{:S(2)}) copy-start(bf16[128,1024]{1,0:T(8,128)(2,1)} %get-tuple-element.49.near_own_ref.near_ref) | copy-start | bytes 786436
  47.4 7.2 %collective-permute-start.2 = (bf16[1024,512]{1,0:T(8,128)(2,1)S(1)}, bf16[1024,512]{1,0:T(8,128)(2,1)S(1)}, u32[]{:S(2)}, u32[]{:S(2)}) collective-permute-start(bf16[1024,512]{1,0:T(8,128)(2,1)S(1)} %bitcast.8), channel_id=1, source_target_pairs={{0,16},{16,0},{1,17},{17,1},{2,18},{18,2},{3,19},{19,3},{4,20},{20... | collective-permute-start | bytes 3145736 | tf_op jit(solution)/shard_map/ppermute | solution.py:268
  54.6 3.1 %copy-start.3 = (bf16[128,1024]{1,0:T(8,128)(2,1)S(1)}, bf16[128,1024]{1,0:T(8,128)(2,1)}, u32[]{:S(2)}) copy-start(bf16[128,1024]{1,0:T(8,128)(2,1)} %get-tuple-element.47.near_other_ref.rows_ref) | copy-start | bytes 786436
  54.9 6.8 %copy-start = (bf16[4,1024,128]{2,1,0:T(8,128)(2,1)S(1)}, bf16[4,1024,128]{2,1,0:T(8,128)(2,1)}, u32[]{:S(2)}) copy-start(bf16[4,1024,128]{2,1,0:T(8,128)(2,1)} %shard_map.115.probs_ref) | copy-start | bytes 3145732
  54.9 6.7 %collective-permute-start.3 = (bf16[128,512]{1,0:T(8,128)(2,1)S(1)}, bf16[128,512]{1,0:T(8,128)(2,1)S(1)}, u32[]{:S(2)}, u32[]{:S(2)}) collective-permute-start(bf16[128,512]{1,0:T(8,128)(2,1)S(1)} %shard_map.118), channel_id=1, source_target_pairs={{0,128},{128,0},{1,129},{129,1},{2,130},{130,2},{3,131},{131,3},{4... | collective-permute-start | bytes 393224 | tf_op jit(solution)/shard_map/ppermute | solution.py:272
  58.0 16.0 %copy-start.2 = (bf16[1024,256]{1,0:T(8,128)(2,1)S(1)}, bf16[1024,256]{1,0:T(8,128)(2,1)}, u32[]{:S(2)}) copy-start(bf16[1024,256]{1,0:T(8,128)(2,1)} %get-tuple-element.55.own_ref) | copy-start | bytes 1572868
  63.1 6.0 %collective-permute-start.4 = (bf16[128,512]{1,0:T(8,128)(2,1)S(1)}, bf16[128,512]{1,0:T(8,128)(2,1)S(1)}, u32[]{:S(2)}, u32[]{:S(2)}) collective-permute-start(bf16[128,512]{1,0:T(8,128)(2,1)S(1)} %get-tuple-element.58.near_ref), channel_id=1, source_target_pairs={{0,128},{128,0},{1,129},{129,1},{2,130},{130,2},{3,131},{131,3},{4... | collective-permute-start | bytes 393224 | tf_op jit(solution)/shard_map/ppermute | solution.py:272
  65.7 7.3 %collective-permute-start.5 = (bf16[128,512]{1,0:T(8,128)(2,1)S(1)}, bf16[128,512]{1,0:T(8,128)(2,1)S(1)}, u32[]{:S(2)}, u32[]{:S(2)}) collective-permute-start(bf16[128,512]{1,0:T(8,128)(2,1)S(1)} %get-tuple-element.58.near_ref), channel_id=1, source_target_pairs={{0,16},{16,0},{1,17},{17,1},{2,18},{18,2},{3,19},{19,3},{4,20},{20... | collective-permute-start | bytes 393224 | tf_op jit(solution)/shard_map/ppermute | solution.py:268
  69.1 4.9 %collective-permute-start.6 = (bf16[128,512]{1,0:T(8,128)(2,1)S(1)}, bf16[128,512]{1,0:T(8,128)(2,1)S(1)}, u32[]{:S(2)}, u32[]{:S(2)}) collective-permute-start(bf16[128,512]{1,0:T(8,128)(2,1)S(1)} %collective-permute-done.4.far_ref), channel_id=1, source_target_pairs={{0,16},{16,0},{1,17},{17,1},{2,18},{18,2},{3,19},{19,3},{4,20},{20... | collective-permute-start | bytes 393224 | tf_op jit(solution)/shard_map/ppermute | solution.py:268
  75.5 20.2 %all-to-all-start.2 = ((bf16[16,64,512]{2,1,0:T(8,128)(2,1)}), bf16[16,64,512]{2,1,0:T(8,128)(2,1)S(1)}, u32[]{:S(2)}, u32[]{:S(2)}) async-start(bf16[16,64,512]{2,1,0:T(8,128)(2,1)} %shard_map.120), calls=%async_computation.2 | async-start | bytes 2097152 | tf_op jit(solution)/shard_map/all_to_all | solution.py:280
  79.3 4.4 %copy-start.6 = (f32[8,512]{1,0:T(8,128)S(1)}, f32[8,512]{1,0:T(8,128)}, u32[]{:S(2)}) copy-start(f32[8,512]{1,0:T(8,128)} %master_ref.2) | copy-start | bytes 49156
  79.3 4.4 %copy-start.7 = (f32[8,512]{1,0:T(8,128)S(1)}, f32[8,512]{1,0:T(8,128)}, u32[]{:S(2)}) copy-start(f32[8,512]{1,0:T(8,128)} %moment_ref) | copy-start | bytes 49156
  79.3 4.4 %copy-start.8 = (f32[8,512]{1,0:T(8,128)S(1)}, f32[8,512]{1,0:T(8,128)}, u32[]{:S(2)}) copy-start(f32[8,512]{1,0:T(8,128)} %second_ref) | copy-start | bytes 49156
  81.0 26.8 %collective-permute-start.7 = (bf16[128,2048]{1,0:T(8,128)(2,1)}, bf16[128,2048]{1,0:T(8,128)(2,1)S(1)}, u32[]{:S(2)}, u32[]{:S(2)}) collective-permute-start(bf16[128,2048]{1,0:T(8,128)(2,1)} %get-tuple-element.61), channel_id=1, source_target_pairs={{0,128},{128,0},{1,129},{129,1},{2,130},{130,2},{3,131},{131,3},{4... | collective-permute-start | bytes 1572872 | tf_op jit(solution)/shard_map/ppermute | solution.py:272
  83.7 24.1 %copy-start.9 = (bf16[128,2048]{1,0:T(8,128)(2,1)S(1)}, bf16[128,2048]{1,0:T(8,128)(2,1)}, u32[]{:S(2)}) copy-start(bf16[128,2048]{1,0:T(8,128)(2,1)} %get-tuple-element.60.keep_ref) | copy-start | bytes 1572868
  96.4 14.4 %all-to-all-start.3 = ((bf16[8,8,512]{2,1,0:T(8,128)(2,1)}), bf16[8,8,512]{2,1,0:T(8,128)(2,1)S(1)}, u32[]{:S(2)}, u32[]{:S(2)}) async-start(bf16[8,8,512]{2,1,0:T(8,128)(2,1)} %shard_map.124), calls=%async_computation.3 | async-start | bytes 131072 | tf_op jit(solution)/shard_map/all_to_all | solution.py:280

commit v13 on v12

--- a/solution.py
+++ b/solution.py
@@ -27,7 +27,7 @@
 DEPTH = 8
 PLANE = 16
 GATHER_FIRST = 6
-REDUCE_FIRST = 2
+REDUCE_FIRST = 1
 
 F32 = jnp.float32
 BF16 = jnp.bfloat16

time: 114 us -> 117 us (1.026)
  waiting for transfers between devices: 18.7 us -> 23.5 us
  starting transfers between devices: 65.9 us -> 64.4 us
    all_to_all x4, waiting for transfers between devices: 12.2 us -> 17 us  [exchange(): lax.all_to_all(blocks, AXES, split_axis=0, concat_axis=0, axis_index_grou...]
    all_to_all x4, starting transfers between devices: 38.9 us -> 37.4 us  [exchange(): lax.all_to_all(blocks, AXES, split_axis=0, concat_axis=0, axis_index_grou...]
  transfers between devices with their start and end apart: 12 -> 12, of which waited for: 6 -> 7; matrix products, arithmetic and copies ran while one was open for 0% -> 0% of each run, Pallas kernels for 17% -> 17%
where the time goes in v13:
time: 117 us; the launch traced here: 115 us
  starting transfers between devices  64.4 us (55%)
  Pallas kernels  23.8 us (20%)
  waiting for transfers between devices  23.5 us (20%)
    all_to_all x4, starting transfers between devices, exchange(): lax.all_to_all(blocks, AXES, split_axis=0, concat_axis=0, axis_index_grou...  37.4 us
    pallas_call x15, Pallas kernels, call(): pl.pallas_call(kernel, out_shape=out_shape, in_specs=specs, out_specs=out...  23.8 us
    all_to_all x4, waiting for transfers between devices, exchange(): lax.all_to_all(blocks, AXES, split_axis=0, concat_axis=0, axis_index_grou...  17 us
    ppermute x4, starting transfers between devices, swap_core(): return lax.ppermute(array, 'c', [(0, 1), (1, 0)])  16.3 us
    ppermute x4, starting transfers between devices, swap_pair(): return lax.ppermute(array, 'zll', [(0, 1), (1, 0)])  10.7 us
    ppermute x4, waiting for transfers between devices, swap_pair(): return lax.ppermute(array, 'zll', [(0, 1), (1, 0)])  3.73 us
    ppermute x4, waiting for transfers between devices, swap_core(): return lax.ppermute(array, 'c', [(0, 1), (1, 0)])  2.76 us
  transfers between devices with their start and end apart: 12, of which 7 were waited for; matrix products, arithmetic and copies ran while one was open for 0% of the time, Pallas kernels for 17%

profile of v13, /device:TPU:1, one launch (start us, length us, event | category | flops | bytes accessed | tf_op | source)
XLA Modules:
  0.0 114.7 jit_solution(12872971499948904195)
XLA Ops:
  2.0 16.9 %all-to-all-start = ((bf16[8,8,512]{2,1,0:T(8,128)(2,1)}), bf16[8,8,512]{2,1,0:T(8,128)(2,1)S(1)}, u32[]{:S(2)}, u32[]{:S(2)}) async-start(bf16[8,8,512]{2,1,0:T(8,128)(2,1)} %shard_map.110), calls=%async_computation | async-start | bytes 131072 | tf_op jit(solution)/shard_map/all_to_all | solution.py:280
  18.9 2.6 %shard_map.113 = bf16[128,2048]{1,0:T(8,128)(2,1)S(1)} custom-call(s32[2]{0:T(128)S(1)} %pad_add_fusion.at_ref, bf16[128,4096]{1,0:T(8,128)(2,1)} %hidden_ref.1), custom_call_target="tpu_custom_call" | custom-call | flops 536870912 | bytes 2097152 | tf_op jit(solution)/shard_map/pallas_call | solution.py:256
  21.6 2.7 %collective-permute-start = (bf16[128,2048]{1,0:T(8,128)(2,1)S(1)}, bf16[128,2048]{1,0:T(8,128)(2,1)S(1)}, u32[]{:S(2)}, u32[]{:S(2)}) collective-permute-start(bf16[128,2048]{1,0:T(8,128)(2,1)S(1)} %shard_map.113), channel_id=1, source_target_pairs={{0,128},{128,0},{1,129},{129,1},{2,130},{130,2},{3,131},{131,3},{4... | collective-permute-start | bytes 1572872 | tf_op jit(solution)/shard_map/ppermute | solution.py:272
  25.3 6.8 %all-to-all-start.1 = ((bf16[16,64,512]{2,1,0:T(8,128)(2,1)}), bf16[16,64,512]{2,1,0:T(8,128)(2,1)S(1)}, u32[]{:S(2)}, u32[]{:S(2)}) async-start(bf16[16,64,512]{2,1,0:T(8,128)(2,1)} %shard_map.111), calls=%async_computation.1 | async-start | bytes 2097152 | tf_op jit(solution)/shard_map/all_to_all | solution.py:280
  32.1 3.4 %shard_map.112 = (bf16[128,1024]{1,0:T(8,128)(2,1)}, bf16[128,1024]{1,0:T(8,128)(2,1)}) custom-call(s32[2]{0:T(128)S(1)} %pad_add_fusion.at_ref, bf16[128,4096]{1,0:T(8,128)(2,1)} %hidden_ref.1), custom_call_target="tpu_custom_call" | custom-call | flops 536870912 | bytes 2097152 | tf_op jit(solution)/shard_map/pallas_call | solution.py:256
  35.6 2.3 %shard_map.114 = (bf16[1024,256]{1,0:T(8,128)(2,1)}, bf16[1024,256]{1,0:T(8,128)(2,1)}) custom-call(bf16[128,1024]{1,0:T(8,128)(2,1)} %get-tuple-element.49.near_own_ref.near_ref, bf16[128,1024]{1,0:T(8,128)(2,1)} %get-tuple-element.47.near_other_ref.rows_ref, bf16[128,2048]{1,0:T(8,128)(2,1)S(1)} %collective-permute-done.far_ref.rows_ref), custom_call_target="tpu_custom_call" | custom-call | flops 1431655808 | bytes 2097152 | tf_op jit(solution)/shard_map/pallas_call | solution.py:256
  37.9 4.1 %collective-permute-start.1 = (bf16[1024,256]{1,0:T(8,128)(2,1)}, bf16[1024,256]{1,0:T(8,128)(2,1)S(1)}, u32[]{:S(2)}, u32[]{:S(2)}) collective-permute-start(bf16[1024,256]{1,0:T(8,128)(2,1)} %get-tuple-element.45), channel_id=1, source_target_pairs={{0,16},{16,0},{1,17},{17,1},{2,18},{18,2},{3,19},{19,3},{4,20},{20... | collective-permute-start | bytes 1572872 | tf_op jit(solution)/shard_map/ppermute | solution.py:268
  43.3 3.8 %shard_map.115.probs_ref = bf16[4,1024,128]{2,1,0:T(8,128)(2,1)} custom-call(bf16[128,4096]{1,0:T(8,128)(2,1)S(1)} %copy-done.1, bf16[128,512]{1,0:T(8,128)(2,1)S(1)} %copy-done.5, s32[1,128]{1,0:T(1,128)S(1)} %bitcast.13, s32[128,1]{1,0:T(8,128)S(1)} %copy.13.seg_col_ref), custom_call_target="tpu_custom_call" | custom-call | flops 268435456 | bytes 8388608 | tf_op jit(solution)/shard_map/pallas_call | solution.py:256
  47.4 4.9 %collective-permute-start.2 = (bf16[1024,512]{1,0:T(8,128)(2,1)S(1)}, bf16[1024,512]{1,0:T(8,128)(2,1)S(1)}, u32[]{:S(2)}, u32[]{:S(2)}) collective-permute-start(bf16[1024,512]{1,0:T(8,128)(2,1)S(1)} %bitcast.8), channel_id=1, source_target_pairs={{0,16},{16,0},{1,17},{17,1},{2,18},{18,2},{3,19},{19,3},{4,20},{20... | collective-permute-start | bytes 3145736 | tf_op jit(solution)/shard_map/ppermute | solution.py:268
  52.8 1.8 %collective-permute-done.2.weight_ref.other_ref = bf16[1024,512]{1,0:T(8,128)(2,1)S(1)} collective-permute-done((bf16[1024,512]{1,0:T(8,128)(2,1)S(1)}, bf16[1024,512]{1,0:T(8,128)(2,1)S(1)}, u32[]{:S(2)}, u32[]{:S(2)}) %collective-permute-start.2) | collective-permute-done | bytes 1048608 | tf_op jit(solution)/shard_map/ppermute | solution.py:268
  54.9 2.8 %collective-permute-start.3 = (bf16[128,512]{1,0:T(8,128)(2,1)S(1)}, bf16[128,512]{1,0:T(8,128)(2,1)S(1)}, u32[]{:S(2)}, u32[]{:S(2)}) collective-permute-start(bf16[128,512]{1,0:T(8,128)(2,1)S(1)} %shard_map.118), channel_id=1, source_target_pairs={{0,128},{128,0},{1,129},{129,1},{2,130},{130,2},{3,131},{131,3},{4... | collective-permute-start | bytes 393224 | tf_op jit(solution)/shard_map/ppermute | solution.py:272
  58.0 3.6 %collective-permute-done.3.sent_ref = bf16[128,512]{1,0:T(8,128)(2,1)S(1)} collective-permute-done((bf16[128,512]{1,0:T(8,128)(2,1)S(1)}, bf16[128,512]{1,0:T(8,128)(2,1)S(1)}, u32[]{:S(2)}, u32[]{:S(2)}) %collective-permute-start.3) | collective-permute-done | bytes 131104 | tf_op jit(solution)/shard_map/ppermute | solution.py:272
  61.6 1.4 %shard_map.119 = (bf16[128,4096]{1,0:T(8,128)(2,1)}, bf16[128,512]{1,0:T(8,128)(2,1)S(1)}) custom-call(f32[128,512]{1,0:T(8,128)S(1)} %shard_map.117.near_ref, bf16[128,512]{1,0:T(8,128)(2,1)S(1)} %collective-permute-done.3.sent_ref, bf16[4,1024,128]{2,1,0:T(8,128)(2,1)S(1)} %copy-done), custom_call_target="tpu_custom_call" | custom-call | flops 268435456 | bytes 4194304 | tf_op jit(solution)/shard_map/pallas_call | solution.py:256
  63.1 2.6 %collective-permute-start.4 = (bf16[128,512]{1,0:T(8,128)(2,1)S(1)}, bf16[128,512]{1,0:T(8,128)(2,1)S(1)}, u32[]{:S(2)}, u32[]{:S(2)}) collective-permute-start(bf16[128,512]{1,0:T(8,128)(2,1)S(1)} %get-tuple-element.58.near_ref), channel_id=1, source_target_pairs={{0,128},{128,0},{1,129},{129,1},{2,130},{130,2},{3,131},{131,3},{4... | collective-permute-start | bytes 393224 | tf_op jit(solution)/shard_map/ppermute | solution.py:272
  65.7 3.4 %collective-permute-start.5 = (bf16[128,512]{1,0:T(8,128)(2,1)S(1)}, bf16[128,512]{1,0:T(8,128)(2,1)S(1)}, u32[]{:S(2)}, u32[]{:S(2)}) collective-permute-start(bf16[128,512]{1,0:T(8,128)(2,1)S(1)} %get-tuple-element.58.near_ref), channel_id=1, source_target_pairs={{0,16},{16,0},{1,17},{17,1},{2,18},{18,2},{3,19},{19,3},{4,20},{20... | collective-permute-start | bytes 393224 | tf_op jit(solution)/shard_map/ppermute | solution.py:268
  69.1 3.9 %collective-permute-start.6 = (bf16[128,512]{1,0:T(8,128)(2,1)S(1)}, bf16[128,512]{1,0:T(8,128)(2,1)S(1)}, u32[]{:S(2)}, u32[]{:S(2)}) collective-permute-start(bf16[128,512]{1,0:T(8,128)(2,1)S(1)} %collective-permute-done.4.far_ref), channel_id=1, source_target_pairs={{0,16},{16,0},{1,17},{17,1},{2,18},{18,2},{3,19},{19,3},{4,20},{20... | collective-permute-start | bytes 393224 | tf_op jit(solution)/shard_map/ppermute | solution.py:268
  74.0 1.4 %shard_map.120 = bf16[16,64,512]{2,1,0:T(8,128)(2,1)} custom-call(bf16[1024,256]{1,0:T(8,128)(2,1)S(1)} %copy-done.2, bf16[1024,256]{1,0:T(8,128)(2,1)S(1)} %collective-permute-done.1.more_ref, bf16[128,512]{1,0:T(8,128)(2,1)S(1)} %get-tuple-element.58.near_ref, bf16[128,512]{1,0:T(8,128)(2,1)S(1)} %collective-permute-done.4.far_ref, ...), custom_call_target="tpu_custom_call" | custom-call | flops 536870912 | bytes 2097152 | tf_op jit(solution)/shard_map/pallas_call | solution.py:256
  75.5 3.8 %all-to-all-start.2 = ((bf16[16,64,512]{2,1,0:T(8,128)(2,1)}), bf16[16,64,512]{2,1,0:T(8,128)(2,1)S(1)}, u32[]{:S(2)}, u32[]{:S(2)}) async-start(bf16[16,64,512]{2,1,0:T(8,128)(2,1)} %shard_map.120), calls=%async_computation.2 | async-start | bytes 2097152 | tf_op jit(solution)/shard_map/all_to_all | solution.py:280
  79.3 1.7 %shard_map.121 = (bf16[128,2048]{1,0:T(8,128)(2,1)}, bf16[128,2048]{1,0:T(8,128)(2,1)}) custom-call(bf16[128,512]{1,0:T(8,128)(2,1)S(1)} %get-tuple-element.58.near_ref, bf16[128,512]{1,0:T(8,128)(2,1)S(1)} %collective-permute-done.4.far_ref, bf16[1024,512]{1,0:T(8,128)(2,1)S(1)} %bitcast.10, bf16[1024,512]{1,0:T(8,128)(2,1)S(1)} %collective-permute-done.2.weight_ref.other_ref), custom_call_target="tpu_custom_call" | custom-call | flops 536870912 | bytes 4194304 | tf_op jit(solution)/shard_map/pallas_call | solution.py:256
  81.0 2.6 %collective-permute-start.7 = (bf16[128,2048]{1,0:T(8,128)(2,1)}, bf16[128,2048]{1,0:T(8,128)(2,1)S(1)}, u32[]{:S(2)}, u32[]{:S(2)}) collective-permute-start(bf16[128,2048]{1,0:T(8,128)(2,1)} %get-tuple-element.61), channel_id=1, source_target_pairs={{0,128},{128,0},{1,129},{129,1},{2,130},{130,2},{3,131},{131,3},{4... | collective-permute-start | bytes 1572872 | tf_op jit(solution)/shard_map/ppermute | solution.py:272
  83.7 11.9 %all-to-all-done.2.parts_ref = bf16[16,64,512]{2,1,0:T(8,128)(2,1)S(1)} async-done(((bf16[16,64,512]{2,1,0:T(8,128)(2,1)}), bf16[16,64,512]{2,1,0:T(8,128)(2,1)S(1)}, u32[]{:S(2)}, u32[]{:S(2)}) %all-to-all-start.2) | async-done | bytes 1048608 | tf_op jit(solution)/shard_map/all_to_all | solution.py:280
  96.4 9.9 %all-to-all-start.3 = ((bf16[8,8,512]{2,1,0:T(8,128)(2,1)}), bf16[8,8,512]{2,1,0:T(8,128)(2,1)S(1)}, u32[]{:S(2)}, u32[]{:S(2)}) async-start(bf16[8,8,512]{2,1,0:T(8,128)(2,1)} %shard_map.124), calls=%async_computation.3 | async-start | bytes 131072 | tf_op jit(solution)/shard_map/all_to_all | solution.py:280
  106.3 2.9 %shard_map.122 = bf16[128,4096]{1,0:T(8,128)(2,1)} custom-call(s32[2]{0:T(128)S(1)} %pad_add_fusion.at_ref, bf16[128,2048]{1,0:T(8,128)(2,1)S(1)} %copy-done.9, bf16[128,2048]{1,0:T(8,128)(2,1)S(1)} %collective-permute-done.7.got_ref), custom_call_target="tpu_custom_call" | custom-call | flops 34359738368 | bytes 2097152 | tf_op jit(solution)/shard_map/pallas_call | solution.py:256
  109.3 4.8 %all-to-all-done.3 = bf16[8,8,512]{2,1,0:T(8,128)(2,1)S(1)} async-done(((bf16[8,8,512]{2,1,0:T(8,128)(2,1)}), bf16[8,8,512]{2,1,0:T(8,128)(2,1)S(1)}, u32[]{:S(2)}, u32[]{:S(2)}) %all-to-all-start.3) | async-done | bytes 65568 | tf_op jit(solution)/shard_map/all_to_all | solution.py:280
  (43 shorter events, 7.7 us)
Async XLA Ops:
  2.0 22.2 %all-to-all-start = ((bf16[8,8,512]{2,1,0:T(8,128)(2,1)}), bf16[8,8,512]{2,1,0:T(8,128)(2,1)S(1)}, u32[]{:S(2)}, u32[]{:S(2)}) async-start(bf16[8,8,512]{2,1,0:T(8,128)(2,1)} %shard_map.110), calls=%async_computation | async-start | bytes 131072 | tf_op jit(solution)/shard_map/all_to_all | solution.py:280
  21.6 14.1 %collective-permute-start = (bf16[128,2048]{1,0:T(8,128)(2,1)S(1)}, bf16[128,2048]{1,0:T(8,128)(2,1)S(1)}, u32[]{:S(2)}, u32[]{:S(2)}) collective-permute-start(bf16[128,2048]{1,0:T(8,128)(2,1)S(1)} %shard_map.113), channel_id=1, source_target_pairs={{0,128},{128,0},{1,129},{129,1},{2,130},{130,2},{3,131},{131,3},{4... | collective-permute-start | bytes 1572872 | tf_op jit(solution)/shard_map/ppermute | solution.py:272
  25.3 22.0 %all-to-all-start.1 = ((bf16[16,64,512]{2,1,0:T(8,128)(2,1)}), bf16[16,64,512]{2,1,0:T(8,128)(2,1)S(1)}, u32[]{:S(2)}, u32[]{:S(2)}) async-start(bf16[16,64,512]{2,1,0:T(8,128)(2,1)} %shard_map.111), calls=%async_computation.1 | async-start | bytes 2097152 | tf_op jit(solution)/shard_map/all_to_all | solution.py:280
  35.6 6.8 %copy-start.1 = (bf16[128,4096]{1,0:T(8,128)(2,1)S(1)}, bf16[128,4096]{1,0:T(8,128)(2,1)}, u32[]{:S(2)}) copy-start(bf16[128,4096]{1,0:T(8,128)(2,1)} %queries_ref.1) | copy-start | bytes 3145732
  37.9 4.1 %copy-start.10 = (s32[1,4]{1,0:T(1,128)S(1)}, s32[1,4]{1,0:T(1,128)}, u32[]{:S(2)}) copy-start(s32[1,4]{1,0:T(1,128)} %param.10) | copy-start | bytes 52
  37.9 9.1 %collective-permute-start.1 = (bf16[1024,256]{1,0:T(8,128)(2,1)}, bf16[1024,256]{1,0:T(8,128)(2,1)S(1)}, u32[]{:S(2)}, u32[]{:S(2)}) collective-permute-start(bf16[1024,256]{1,0:T(8,128)(2,1)} %get-tuple-element.45), channel_id=1, source_target_pairs={{0,16},{16,0},{1,17},{17,1},{2,18},{18,2},{3,19},{19,3},{4,20},{20... | collective-permute-start | bytes 1572872 | tf_op jit(solution)/shard_map/ppermute | solution.py:268
  42.4 0.9 copy-start.5
  43.3 9.0 %copy-start.4 = (bf16[128,1024]{1,0:T(8,128)(2,1)S(1)}, bf16[128,1024]{1,0:T(8,128)(2,1)}, u32[]{:S(2)}) copy-start(bf16[128,1024]{1,0:T(8,128)(2,1)} %get-tuple-element.49.near_own_ref.near_ref) | copy-start | bytes 786436
  47.4 7.2 %collective-permute-start.2 = (bf16[1024,512]{1,0:T(8,128)(2,1)S(1)}, bf16[1024,512]{1,0:T(8,128)(2,1)S(1)}, u32[]{:S(2)}, u32[]{:S(2)}) collective-permute-start(bf16[1024,512]{1,0:T(8,128)(2,1)S(1)} %bitcast.8), channel_id=1, source_target_pairs={{0,16},{16,0},{1,17},{17,1},{2,18},{18,2},{3,19},{19,3},{4,20},{20... | collective-permute-start | bytes 3145736 | tf_op jit(solution)/shard_map/ppermute | solution.py:268
  54.6 3.1 %copy-start.3 = (bf16[128,1024]{1,0:T(8,128)(2,1)S(1)}, bf16[128,1024]{1,0:T(8,128)(2,1)}, u32[]{:S(2)}) copy-start(bf16[128,1024]{1,0:T(8,128)(2,1)} %get-tuple-element.47.near_other_ref.rows_ref) | copy-start | bytes 786436
  54.9 6.8 %copy-start = (bf16[4,1024,128]{2,1,0:T(8,128)(2,1)S(1)}, bf16[4,1024,128]{2,1,0:T(8,128)(2,1)}, u32[]{:S(2)}) copy-start(bf16[4,1024,128]{2,1,0:T(8,128)(2,1)} %shard_map.115.probs_ref) | copy-start | bytes 3145732
  54.9 6.7 %collective-permute-start.3 = (bf16[128,512]{1,0:T(8,128)(2,1)S(1)}, bf16[128,512]{1,0:T(8,128)(2,1)S(1)}, u32[]{:S(2)}, u32[]{:S(2)}) collective-permute-start(bf16[128,512]{1,0:T(8,128)(2,1)S(1)} %shard_map.118), channel_id=1, source_target_pairs={{0,128},{128,0},{1,129},{129,1},{2,130},{130,2},{3,131},{131,3},{4... | collective-permute-start | bytes 393224 | tf_op jit(solution)/shard_map/ppermute | solution.py:272
  58.0 16.0 %copy-start.2 = (bf16[1024,256]{1,0:T(8,128)(2,1)S(1)}, bf16[1024,256]{1,0:T(8,128)(2,1)}, u32[]{:S(2)}) copy-start(bf16[1024,256]{1,0:T(8,128)(2,1)} %get-tuple-element.55.own_ref) | copy-start | bytes 1572868
  63.1 6.0 %collective-permute-start.4 = (bf16[128,512]{1,0:T(8,128)(2,1)S(1)}, bf16[128,512]{1,0:T(8,128)(2,1)S(1)}, u32[]{:S(2)}, u32[]{:S(2)}) collective-permute-start(bf16[128,512]{1,0:T(8,128)(2,1)S(1)} %get-tuple-element.58.near_ref), channel_id=1, source_target_pairs={{0,128},{128,0},{1,129},{129,1},{2,130},{130,2},{3,131},{131,3},{4... | collective-permute-start | bytes 393224 | tf_op jit(solution)/shard_map/ppermute | solution.py:272
  65.7 7.3 %collective-permute-start.5 = (bf16[128,512]{1,0:T(8,128)(2,1)S(1)}, bf16[128,512]{1,0:T(8,128)(2,1)S(1)}, u32[]{:S(2)}, u32[]{:S(2)}) collective-permute-start(bf16[128,512]{1,0:T(8,128)(2,1)S(1)} %get-tuple-element.58.near_ref), channel_id=1, source_target_pairs={{0,16},{16,0},{1,17},{17,1},{2,18},{18,2},{3,19},{19,3},{4,20},{20... | collective-permute-start | bytes 393224 | tf_op jit(solution)/shard_map/ppermute | solution.py:268
  69.1 4.9 %collective-permute-start.6 = (bf16[128,512]{1,0:T(8,128)(2,1)S(1)}, bf16[128,512]{1,0:T(8,128)(2,1)S(1)}, u32[]{:S(2)}, u32[]{:S(2)}) collective-permute-start(bf16[128,512]{1,0:T(8,128)(2,1)S(1)} %collective-permute-done.4.far_ref), channel_id=1, source_target_pairs={{0,16},{16,0},{1,17},{17,1},{2,18},{18,2},{3,19},{19,3},{4,20},{20... | collective-permute-start | bytes 393224 | tf_op jit(solution)/shard_map/ppermute | solution.py:268
  75.5 20.2 %all-to-all-start.2 = ((bf16[16,64,512]{2,1,0:T(8,128)(2,1)}), bf16[16,64,512]{2,1,0:T(8,128)(2,1)S(1)}, u32[]{:S(2)}, u32[]{:S(2)}) async-start(bf16[16,64,512]{2,1,0:T(8,128)(2,1)} %shard_map.120), calls=%async_computation.2 | async-start | bytes 2097152 | tf_op jit(solution)/shard_map/all_to_all | solution.py:280
  79.3 4.4 %copy-start.6 = (f32[8,512]{1,0:T(8,128)S(1)}, f32[8,512]{1,0:T(8,128)}, u32[]{:S(2)}) copy-start(f32[8,512]{1,0:T(8,128)} %master_ref.2) | copy-start | bytes 49156
  79.3 4.4 %copy-start.7 = (f32[8,512]{1,0:T(8,128)S(1)}, f32[8,512]{1,0:T(8,128)}, u32[]{:S(2)}) copy-start(f32[8,512]{1,0:T(8,128)} %moment_ref) | copy-start | bytes 49156
  79.3 4.4 %copy-start.8 = (f32[8,512]{1,0:T(8,128)S(1)}, f32[8,512]{1,0:T(8,128)}, u32[]{:S(2)}) copy-start(f32[8,512]{1,0:T(8,128)} %second_ref) | copy-start | bytes 49156
  81.0 25.3 %collective-permute-start.7 = (bf16[128,2048]{1,0:T(8,128)(2,1)}, bf16[128,2048]{1,0:T(8,128)(2,1)S(1)}, u32[]{:S(2)}, u32[]{:S(2)}) collective-permute-start(bf16[128,2048]{1,0:T(8,128)(2,1)} %get-tuple-element.61), channel_id=1, source_target_pairs={{0,128},{128,0},{1,129},{129,1},{2,130},{130,2},{3,131},{131,3},{4... | collective-permute-start | bytes 1572872 | tf_op jit(solution)/shard_map/ppermute | solution.py:272
  83.7 22.6 %copy-start.9 = (bf16[128,2048]{1,0:T(8,128)(2,1)S(1)}, bf16[128,2048]{1,0:T(8,128)(2,1)}, u32[]{:S(2)}) copy-start(bf16[128,2048]{1,0:T(8,128)(2,1)} %get-tuple-element.60.keep_ref) | copy-start | bytes 1572868
  96.4 17.6 %all-to-all-start.3 = ((bf16[8,8,512]{2,1,0:T(8,128)(2,1)}), bf16[8,8,512]{2,1,0:T(8,128)(2,1)S(1)}, u32[]{:S(2)}, u32[]{:S(2)}) async-start(bf16[8,8,512]{2,1,0:T(8,128)(2,1)} %shard_map.124), calls=%async_computation.3 | async-start | bytes 131072 | tf_op jit(solution)/shard_map/all_to_all | solution.py:280
